TPU v7x, 32 devices: a whole 2x2x4 slice. The times are simulated.
32 devices in a mesh: groups: 2 (over x), pos: 8 (over z, y), mp: 2 (over core).
Axes of the slice: x: 2, y: 2, z: 4, core: 2. Of those that a mesh axis runs over, the one named last changes fastest.
Arguments:
- gate_stream: bfloat16 [8192, 4096], P(('groups', 'pos'), 'mp'), parts along dimension 0, may hold values from -6 to 6
- key_stream: bfloat16 [8192, 4096], P(('groups', 'pos'), 'mp'), parts along dimension 0, may hold values from -6 to 6
- value_stream: bfloat16 [8192, 4096], P(('groups', 'pos'), 'mp'), parts along dimension 0, may hold values from -6 to 6
- filters: float32 [4096, 128], P('mp')
- temps: float32 [32], P('mp'), may hold values from 4 to 24
- queries: bfloat16 [32, 256, 4096], P('groups', 'pos', 'mp'), parts along dimension 0, may hold values from -6 to 6
- blocks: int32 [32], P('groups'), parts along dimension 0, may hold values from 0 to 7, as said below
- sites: int32 [32], P('groups'), parts along dimension 0, may hold values from 128 to 4095, as said below
Outputs:
- hyena_out: bfloat16 [8192, 4096], P(('groups', 'pos'), 'mp'), parts along dimension 0
- attended: bfloat16 [32, 256, 4096], P('groups', 'pos', 'mp'), parts along dimension 0
There are 2 independent parts, one for each index of `groups`. A program takes and returns all parts, laid end to end along the dimension named above; an argument that names none is the same for every part. Nothing has to cross between parts.
Inputs may be any that keep to these rules, and one draw needn't show every extreme that they name: `blocks`: A block is the 512 reference positions of one index of pos. Exactly one block is named by exactly 4 windows; every other block by at most two windows, and some block by exactly two. sites[w] - 512 * blocks[w] lies from 128 to 511.
All inputs are finite; a program needn't handle non-finite values.
Results may differ from a plain program's by a relative error of at most 0.01.
Values may be sent and summed in bfloat16 or wider, within the bound.
No kernel may reach another device: no remote copies, remote signals or barrier semaphores. Data moves between devices by JAX's collectives and lax.ppermute only.
A program may use at most 128 MiB of HBM per device.

v0:
```python
import jax
import jax.numpy as jnp
from jax import lax
from jax.sharding import PartitionSpec as P

HEAD_DIM = 128
HOT = 4


def shifted(value, axis, by):
    peers = lax.axis_size(axis)
    pairs = [(i, i + by) for i in range(peers) if 0 <= i + by < peers]
    return lax.ppermute(value, axis, pairs)


def causal_mix(extended, filters):
    kernel = jnp.flip(filters.T, 0)[:, None, :]
    mixed = lax.conv_general_dilated(
        extended.astype(jnp.float32)[None],
        kernel,
        (1,),
        "VALID",
        dimension_numbers=("NWC", "WIO", "NWC"),
        feature_group_count=filters.shape[0],
        precision=lax.Precision.HIGHEST,
    )
    return mixed[0]


def head_norm(block, heads):
    shaped = block.astype(jnp.float32).reshape(block.shape[:-1] + (heads, HEAD_DIM))
    scale = lax.rsqrt(jnp.mean(shaped * shaped, axis=-1, keepdims=True) + 1e-06)
    return (shaped * scale).reshape(block.shape).astype(jnp.bfloat16)


def attend_slot(query_rows, key_rows, value_rows, offset, temps):
    heads = temps.shape[0]
    length = query_rows.shape[0]
    positions = key_rows.shape[0]
    qnorm = head_norm(query_rows, heads).reshape(length, heads, HEAD_DIM)
    keyed = key_rows.reshape(positions, heads, HEAD_DIM)
    valued = value_rows.reshape(positions, heads, HEAD_DIM)
    scores = (
        jnp.einsum("qhd,khd->hqk", qnorm, keyed, preferred_element_type=jnp.float32)
        * (temps / HEAD_DIM)[:, None, None]
    )
    live = lax.broadcasted_iota(jnp.int32, (1, 1, positions), 2) < offset
    weights = jnp.where(live, jnp.exp(scores), 0.0)
    total = jnp.sum(weights, axis=-1)
    numer = jnp.einsum(
        "hqk,khd->qhd", weights.astype(jnp.bfloat16), valued, preferred_element_type=jnp.float32
    )
    return (numer / total.T[:, :, None]).reshape(length, heads * HEAD_DIM).astype(jnp.bfloat16)


def shards(gate_stream, key_stream, value_stream, filters, temps, queries, blocks, sites):
    rows, chans = gate_stream.shape
    taps = filters.shape[1]
    product = (key_stream.astype(jnp.float32) * value_stream.astype(jnp.float32)).astype(
        jnp.bfloat16
    )
    earlier = shifted(product[rows - taps :], "pos", 1)
    extended = jnp.concatenate([earlier[1:], product], 0)
    mixed = causal_mix(extended, filters)
    hyena_out = (gate_stream.astype(jnp.float32) * mixed).astype(jnp.bfloat16)
    keys = head_norm(hyena_out, temps.shape[0])
    count = lax.axis_size("pos")
    me = lax.axis_index("pos")
    windows = blocks.shape[0]
    order = jnp.arange(windows)
    before = order[None, :] < order[:, None]
    same = (blocks[:, None] == blocks[None, :]) & before
    within = jnp.sum(same, axis=1)
    slot_count = HOT
    slot_ids = jnp.arange(slot_count)
    tok_rows = queries.shape[1]
    select = (blocks[None, None, :] == jnp.arange(count)[None, :, None]) & (
        within[None, None, :] == slot_ids[:, None, None]
    )
    outgoing = jnp.dot(
        select.reshape(slot_count * count, windows).astype(jnp.bfloat16),
        queries.reshape(windows, tok_rows * chans),
        preferred_element_type=jnp.float32,
    )
    outgoing = outgoing.astype(jnp.bfloat16).reshape(slot_count, count * tok_rows, chans)
    arrived = lax.all_to_all(outgoing, "pos", split_axis=1, concat_axis=1, tiled=True)
    mine = (blocks == me)[None, :] & (within[None, :] == slot_ids[:, None])
    offsets = jnp.sum(jnp.where(mine, sites[None, :] - blocks[None, :] * rows, 0), axis=1)
    offsets = jnp.where(jnp.any(mine, axis=1), offsets, rows)

    def one_slot(item):
        return attend_slot(item[0], keys, hyena_out, item[1], temps)

    results = lax.map(one_slot, (arrived, offsets))
    returned = lax.all_to_all(results, "pos", split_axis=1, concat_axis=0, tiled=True)
    pick = blocks[:, None] * slot_count + within[:, None] == jnp.arange(count * slot_count)[None, :]
    attended = jnp.dot(
        pick.astype(jnp.bfloat16),
        returned.reshape(count * slot_count, tok_rows * chans),
        preferred_element_type=jnp.float32,
    )
    attended = attended.astype(jnp.bfloat16).reshape(windows, tok_rows, chans)
    return (hyena_out, attended)


def solution(mesh):
    placed = (
        P(("groups", "pos"), "mp"),
        P(("groups", "pos"), "mp"),
        P(("groups", "pos"), "mp"),
        P("mp", None),
        P("mp"),
        P("groups", "pos", "mp"),
        P("groups"),
        P("groups"),
    )
    return jax.shard_map(
        shards,
        mesh=mesh,
        in_specs=placed,
        out_specs=(P(("groups", "pos"), "mp"), P("groups", "pos", "mp")),
        check_vma=False,
    )
```

profile of v0, /device:TPU:0, one launch (start us, length us, event | category | flops | bytes accessed | tf_op | source)
XLA Modules:
  0.0 292.1 jit_solution(6040972376619216045)
XLA Ops:
  0.6 3.0 %multiply_convert_fusion.1 = bf16[512,2048]{1,0:T(8,128)(2,1)S(1)} fusion(bf16[512,2048]{1,0:T(8,128)(2,1)} %param.12, bf16[512,2048]{1,0:T(8,128)(2,1)} %param.11), kind=kLoop, calls=%fused_computation.31 | loop fusion | flops 4194304 | bytes 6291456 | tf_op jit(solution)/shard_map/convert_element_type | solution.py:59
  4.5 5.7 %collective-permute-start = (bf16[128,2048]{1,0:T(8,128)(2,1)}, bf16[128,2048]{1,0:T(8,128)(2,1)}, u32[]{:S(2)}, u32[]{:S(2)}) collective-permute-start(bf16[128,2048]{1,0:T(8,128)(2,1)} %slice.8), channel_id=1, source_target_pairs={{0,2},{2,4},{4,6},{6,8},{8,10},{10,12},{12,14},{1,3},{3,5},{5,7},{... | collective-permute-start | bytes 1572872 | tf_op jit(solution)/shard_map/ppermute | solution.py:13
  10.4 2.7 copy.71
  13.3 3.2 %convolution_convert_fusion = bf16[32,65536]{1,0:T(8,128)(2,1)} fusion(bf16[16,65536]{1,0:T(8,128)(2,1)S(1)} %bitcast.84, pred[4,16]{1,0:T(4,128)(4,1)S(1)} %get-tuple-element.102, pred[8,16]{1,0:T(8,128)(4,1)S(1)} %iota_compare_fusion.4), kind=kOutput, calls=%fused_computation.21 | convolution fusion | flops 69206528 | bytes 6291648 | tf_op jit(solution)/shard_map/dot_general | solution.py:80
  16.4 5.6 %reshape.143 = bf16[4,256,2048]{2,1,0:T(8,128)(2,1)} reshape(bf16[32,65536]{1,0:T(8,128)(2,1)} %convolution_convert_fusion) | data formatting | bytes 8388608 | tf_op jit(solution)/shard_map/reshape | solution.py:85
  22.0 7.3 %copy.60 = bf16[4,256,2048]{2,0,1:T(4,128)(2,1)} copy(bf16[4,256,2048]{2,1,0:T(8,128)(2,1)} %reshape.143) | data formatting | bytes 8388608 | tf_op jit(solution)/shard_map/reshape | solution.py:85
  29.4 4.8 %all-to-all-start = ((bf16[4,256,2048]{2,0,1:T(4,128)(2,1)}), bf16[4,256,2048]{2,0,1:T(4,128)(2,1)}, u32[]{:S(2)}, u32[]{:S(2)}) async-start(bf16[4,256,2048]{2,0,1:T(4,128)(2,1)} %copy.60), calls=%async_computation | async-start | bytes 8388608 | tf_op jit(solution)/shard_map/all_to_all | solution.py:86
  34.2 7.5 %rev.4 = f32[128,2048]{0,1:T(8,128)S(1)} reverse(f32[128,2048]{0,1:T(8,128)} %bitcast.89), dimensions={0} | reverse | bytes 2097152 | tf_op jit(solution)/shard_map/jit(_flip)/rev | solution.py:17
  41.7 1.9 copy.59
  46.1 45.5 %fusion.15 = f32[1,512,2048]{2,0,1:T(1,128)S(1)} fusion(f32[128,1,2048]{2,1,0:T(1,128)S(1)} %copy-done.3, bf16[1,639,2048]{2,1,0:T(8,128)(2,1)S(1)} %maximum_bitcast_fusion), kind=kOutput, calls=%fused_computation.25 | convolution fusion | flops 1610612736 | bytes 7860224 | tf_op jit(solution)/shard_map/conv_general_dilated | solution.py:18
  91.6 2.3 fusion.17
  93.9 2.9 copy.72
  96.8 3.4 %reduce_sum.47 = f32[512,16]{1,0:T(8,128)S(1)} reduce(f32[512,16,128]{2,1,0:T(8,128)} %bitcast.79, f32[]{:T(128)} %constant.41.clone.1), dimensions={2}, to_apply=%region_3.4 | reduce | flops 1040384 | bytes 4227076 | tf_op jit(solution)/shard_map/reduce_sum | solution.py:32
  100.4 2.6 copy.64
  104.1 3.1 %fusion.18 = bf16[512,2048]{1,0:T(8,128)(2,1)} fusion(bf16[512,2048]{1,0:T(8,128)(2,1)S(1)} %get-tuple-element.97, f32[64,8,16,128]{3,2,1,0:T(8,128)S(1)} %bitcast.80), kind=kLoop, calls=%fused_computation.28 | loop fusion | flops 3145728 | bytes 8388608 | tf_op jit(solution)/shard_map/convert_element_type | solution.py:33
  107.2 20.0 %all-to-all-done = bf16[4,256,2048]{2,0,1:T(4,128)(2,1)} async-done(((bf16[4,256,2048]{2,0,1:T(4,128)(2,1)}), bf16[4,256,2048]{2,0,1:T(4,128)(2,1)}, u32[]{:S(2)}, u32[]{:S(2)}) %all-to-all-start) | async-done | bytes 4194336 | tf_op jit(solution)/shard_map/all_to_all | solution.py:86
  127.2 6.4 %copy.63 = bf16[4,256,2048]{2,1,0:T(8,128)(2,1)} copy(bf16[4,256,2048]{2,0,1:T(4,128)(2,1)} %all-to-all-done) | data formatting | bytes 8388608 | tf_op jit(solution)/shard_map/while | solution.py:94
  133.6 45.2 %while.10 = (s32[]{:T(128)}, bf16[4,256,2048]{1,2,0:T(8,128)(2,1)}, s32[4]{0:T(128)S(1)}, bf16[4,256,2048]{2,1,0:T(8,128)(2,1)}, bf16[512,2048]{1,0:T(8,128)(2,1...) while((s32[]{:T(128)}, bf16[4,256,2048]{1,2,0:T(8,128)(2,1)}, s32[4]{0:T(128)S(1)}, ...), condition=%wide.region_7.8_spmd, body=%wide.region_4.7_spmd.sunk | while | flops 1089995264 | bytes 46303620 | solution.py:94
  133.6 1.5 convert_bitcast_fusion.2
  138.4 3.6 %fusion.40 = (f32[16,256]{1,0:T(8,128)S(1)}, f32[16,256,512]{2,1,0:T(8,128)S(1)}) fusion(f32[16]{0:T(128)S(1)} %broadcast_multiply_fusion.2, pred[512]{0:T(512)(128)(4,1)S(1)} %iota_compare_fusion.7, bf16[256,16,128]{2,1,0:T(8,128)(2,1)S(1)} %multiply_convert_fusion.3, bf16[512,2048]{1,0:T(8,128)(2,1)} %get-tuple-element.171), kind=kOutput, calls=%fused_computation.1.clone.1 | convolution fusion | flops 543158272 | bytes 11551296 | tf_op jit(solution)/shard_map/while/body/eval_jaxpr/qhd,khd->hqk/dot_general | solution.py:44
  142.1 1.7 fusion.41
  149.7 3.6 %fusion.40 = (f32[16,256]{1,0:T(8,128)S(1)}, f32[16,256,512]{2,1,0:T(8,128)S(1)}) fusion(f32[16]{0:T(128)S(1)} %broadcast_multiply_fusion.2, pred[512]{0:T(512)(128)(4,1)S(1)} %iota_compare_fusion.7, bf16[256,16,128]{2,1,0:T(8,128)(2,1)S(1)} %multiply_convert_fusion.3, bf16[512,2048]{1,0:T(8,128)(2,1)} %get-tuple-element.171), kind=kOutput, calls=%fused_computation.1.clone.1 | convolution fusion | flops 543158272 | bytes 11551296 | tf_op jit(solution)/shard_map/while/body/eval_jaxpr/qhd,khd->hqk/dot_general | solution.py:44
  153.3 1.7 fusion.41
  161.0 3.6 %fusion.40 = (f32[16,256]{1,0:T(8,128)S(1)}, f32[16,256,512]{2,1,0:T(8,128)S(1)}) fusion(f32[16]{0:T(128)S(1)} %broadcast_multiply_fusion.2, pred[512]{0:T(512)(128)(4,1)S(1)} %iota_compare_fusion.7, bf16[256,16,128]{2,1,0:T(8,128)(2,1)S(1)} %multiply_convert_fusion.3, bf16[512,2048]{1,0:T(8,128)(2,1)} %get-tuple-element.171), kind=kOutput, calls=%fused_computation.1.clone.1 | convolution fusion | flops 543158272 | bytes 11551296 | tf_op jit(solution)/shard_map/while/body/eval_jaxpr/qhd,khd->hqk/dot_general | solution.py:44
  164.7 1.7 fusion.41
  172.3 3.6 %fusion.40 = (f32[16,256]{1,0:T(8,128)S(1)}, f32[16,256,512]{2,1,0:T(8,128)S(1)}) fusion(f32[16]{0:T(128)S(1)} %broadcast_multiply_fusion.2, pred[512]{0:T(512)(128)(4,1)S(1)} %iota_compare_fusion.7, bf16[256,16,128]{2,1,0:T(8,128)(2,1)S(1)} %multiply_convert_fusion.3, bf16[512,2048]{1,0:T(8,128)(2,1)} %get-tuple-element.171), kind=kOutput, calls=%fused_computation.1.clone.1 | convolution fusion | flops 543158272 | bytes 11551296 | tf_op jit(solution)/shard_map/while/body/eval_jaxpr/qhd,khd->hqk/dot_general | solution.py:44
  176.0 1.7 fusion.41
  178.8 8.0 %copy.65 = bf16[4,256,2048]{2,0,1:T(4,128)(2,1)} copy(bf16[4,256,2048]{1,2,0:T(8,128)(2,1)} %get-tuple-element.39) | data formatting | bytes 8388608 | tf_op jit(solution)/shard_map/while | solution.py:94
  186.7 96.9 %all_to_all.20 = bf16[4,256,2048]{2,0,1:T(4,128)(2,1)S(1)} all-to-all(bf16[4,256,2048]{2,0,1:T(4,128)(2,1)} %copy.65), channel_id=1, replica_groups=mesh['groups'=2,'pos'=8,'mp'=2] {'pos'}, dimensions={1} | all-to-all | bytes 8388608 | tf_op jit(solution)/shard_map/all_to_all | solution.py:95
  283.6 2.3 copy.66
  286.5 2.3 copy.74
  289.7 2.5 copy.75
  (83 shorter events, 28.3 us)
Async XLA Ops:
  0.6 9.6 %copy-start.5 = (s32[16]{0:T(128)S(1)}, s32[16]{0:T(128)}, u32[]{:S(2)}) copy-start(s32[16]{0:T(128)} %param.16) | copy-start | bytes 196
  4.5 39.7 %collective-permute-start = (bf16[128,2048]{1,0:T(8,128)(2,1)}, bf16[128,2048]{1,0:T(8,128)(2,1)}, u32[]{:S(2)}, u32[]{:S(2)}) collective-permute-start(bf16[128,2048]{1,0:T(8,128)(2,1)} %slice.8), channel_id=1, source_target_pairs={{0,2},{2,4},{4,6},{6,8},{8,10},{10,12},{12,14},{1,3},{3,5},{5,7},{... | collective-permute-start | bytes 1572872 | tf_op jit(solution)/shard_map/ppermute | solution.py:13
  29.4 97.8 %all-to-all-start = ((bf16[4,256,2048]{2,0,1:T(4,128)(2,1)}), bf16[4,256,2048]{2,0,1:T(4,128)(2,1)}, u32[]{:S(2)}, u32[]{:S(2)}) async-start(bf16[4,256,2048]{2,0,1:T(4,128)(2,1)} %copy.60), calls=%async_computation | async-start | bytes 8388608 | tf_op jit(solution)/shard_map/all_to_all | solution.py:86
  34.2 9.4 %copy-start.6 = (s32[16]{0:T(128)S(1)}, s32[16]{0:T(128)}, u32[]{:S(2)}) copy-start(s32[16]{0:T(128)} %param.17) | copy-start | bytes 196
  43.6 2.5 copy-start.3
  46.1 45.5 %copy-start.2 = (bf16[512,2048]{1,0:T(8,128)(2,1)S(1)}, bf16[512,2048]{1,0:T(8,128)(2,1)}, u32[]{:S(2)}) copy-start(bf16[512,2048]{1,0:T(8,128)(2,1)} %param.10) | copy-start | bytes 6291460
  93.9 10.2 %copy-start = (bf16[512,2048]{1,0:T(8,128)(2,1)}, bf16[512,2048]{1,0:T(8,128)(2,1)S(1)}, u32[]{:S(2)}) copy-start(bf16[512,2048]{1,0:T(8,128)(2,1)S(1)} %get-tuple-element.97) | copy-start | bytes 6291460
  107.2 26.4 %copy-start.7 = (f32[16]{0:T(128)S(1)}, f32[16]{0:T(128)}, u32[]{:S(2)}) copy-start(f32[16]{0:T(128)} %param.14) | copy-start | bytes 196
  138.4 3.6 %copy-start.1 = (bf16[512,2048]{0,1:T(8,128)(2,1)S(1)}, bf16[512,2048]{0,1:T(8,128)(2,1)}, u32[]{:S(2)}) copy-start(bf16[512,2048]{0,1:T(8,128)(2,1)} %get-tuple-element.173) | copy-start | bytes 6291460 | tf_op jit(solution)/shard_map/while
  149.7 3.6 %copy-start.1 = (bf16[512,2048]{0,1:T(8,128)(2,1)S(1)}, bf16[512,2048]{0,1:T(8,128)(2,1)}, u32[]{:S(2)}) copy-start(bf16[512,2048]{0,1:T(8,128)(2,1)} %get-tuple-element.173) | copy-start | bytes 6291460 | tf_op jit(solution)/shard_map/while
  161.0 3.6 %copy-start.1 = (bf16[512,2048]{0,1:T(8,128)(2,1)S(1)}, bf16[512,2048]{0,1:T(8,128)(2,1)}, u32[]{:S(2)}) copy-start(bf16[512,2048]{0,1:T(8,128)(2,1)} %get-tuple-element.173) | copy-start | bytes 6291460 | tf_op jit(solution)/shard_map/while
  172.3 3.6 %copy-start.1 = (bf16[512,2048]{0,1:T(8,128)(2,1)S(1)}, bf16[512,2048]{0,1:T(8,128)(2,1)}, u32[]{:S(2)}) copy-start(bf16[512,2048]{0,1:T(8,128)(2,1)} %get-tuple-element.173) | copy-start | bytes 6291460 | tf_op jit(solution)/shard_map/while
  286.5 2.4 copy-start.4
where the time goes:
time: 293 us; the launch traced here: 292 us
  blocking collectives  96.9 us (33%)
  matrix products  70.8 us (24%)
  local copies, waits for them, and re-layouts  65.1 us (22%)
  other arithmetic  27.7 us (9%)
  waiting for transfers between devices  20 us (7%)
  starting transfers between devices  10.5 us (4%)
    all_to_all x1, blocking collectives, shards(): lax.all_to_all(results, 'pos', split_axis=1, concat_axis=0, tiled=True)  96.9 us
    conv_general_dilated x1, matrix products, causal_mix(): lax.conv_general_dilated(extended.astype(jnp.float32)[None], kernel, (1,)...  45.5 us
    all_to_all x1, waiting for transfers between devices, shards(): lax.all_to_all(outgoing, 'pos', split_axis=1, concat_axis=1, tiled=True)  20 us
    while x3, local copies, waits for them, and re-layouts, shards(): results = lax.map(one_slot, (arrived, offsets))  16.9 us
    dot_general x4, matrix products, attend_slot(): jnp.einsum('qhd,khd->hqk', qnorm, keyed, preferred_element_type=jnp.float32)  14.5 us
    reshape x2, local copies, waits for them, and re-layouts, shards(): outgoing.astype(jnp.bfloat16).reshape(slot_count, count * tok_rows, chans)  13 us
    unnamed x18, local copies, waits for them, and re-layouts  10.5 us
    rev x1, local copies, waits for them, and re-layouts, causal_mix(): kernel = jnp.flip(filters.T, 0)[:, None, :]  7.5 us
  transfers between devices with their start and end apart: 2, of which 1 were waited for; matrix products, arithmetic and copies ran while one was open for 32% of the time, Pallas kernels for 0%

commit v1 on v0

v1 whole, which is shorter than its diff:
```python
import functools

import jax
import jax.numpy as jnp
import numpy as np
from jax import lax
from jax.experimental import pallas as pl
from jax.experimental.pallas import tpu as pltpu
from jax.sharding import PartitionSpec as P

HEAD_DIM = 128
HOT = 4
EPS = 1e-06
LOG2E = 1.4426950408889634
MIB = 1 << 20


def halves(array):
    high = array.astype(jnp.bfloat16)
    low = (array - high.astype(jnp.float32)).astype(jnp.bfloat16)
    return high, low


def transforms(taps):
    size = 2 * taps
    odd = 2 * np.arange(taps) + 1
    angle = np.pi / size * ((odd[:, None] * np.arange(size)[None, :]) % (2 * size))
    forward = np.concatenate([np.cos(angle), -np.sin(angle)], 0)
    inverse = forward.T[taps:] * (2.0 / size)
    out = []
    for matrix in (forward, inverse):
        high = matrix.astype(jnp.bfloat16)
        low = (matrix - high.astype(np.float64)).astype(jnp.bfloat16)
        out.append(np.concatenate([high, low], 0))
    return out


def unit(block):
    return block * lax.rsqrt(jnp.mean(block * block, axis=-1, keepdims=True) + EPS)


def mix_kernel(gate, key, value, earlier, filters, forward, inverse, out, rows_of, keys_of):
    rows, wide = gate.shape
    taps = filters.shape[1]
    size = 2 * taps
    f32 = jnp.float32
    fwd = forward[...]
    inv = inverse[...]
    high, low = halves(filters[...])
    across = (((1,), (1,)), ((), ()))
    both = lax.dot_general(fwd[:, :taps], high, across, preferred_element_type=f32)
    spectrum = both[:size] + both[size:]
    spectrum += lax.dot_general(fwd[:size, :taps], low, across, preferred_element_type=f32)
    hr, hi = spectrum[:taps], spectrum[taps:]
    before = earlier[...]
    for start in range(0, rows, taps):
        part = slice(start, start + taps)
        now = (key[part, :].astype(f32) * value[part, :].astype(f32)).astype(jnp.bfloat16)
        both = jnp.dot(fwd, jnp.concatenate([before, now], 0), preferred_element_type=f32)
        seen = both[:size] + both[size:]
        xr, xi = seen[:taps], seen[taps:]
        product = jnp.concatenate([xr * hr - xi * hi, xr * hi + xi * hr], 0)
        high, low = halves(product)
        both = jnp.dot(inv, high, preferred_element_type=f32)
        mixed = both[:taps] + both[taps:]
        mixed += jnp.dot(inv[:taps], low, preferred_element_type=f32)
        result = (gate[part, :].astype(f32) * mixed).astype(jnp.bfloat16)
        out[part, :] = result
        for head in range(wide // HEAD_DIM):
            piece = result[:, head * HEAD_DIM : (head + 1) * HEAD_DIM]
            rows_of[head, part, :] = piece
            keys_of[head, part, :] = unit(piece.astype(f32)).astype(jnp.bfloat16)
        before = now


def mix(gate, key, value, earlier, filters):
    rows, chans = gate.shape
    taps = filters.shape[1]
    heads = chans // HEAD_DIM
    wide = 2 * HEAD_DIM
    each = wide // HEAD_DIM
    forward, inverse = (jnp.asarray(matrix) for matrix in transforms(taps))
    stream = pl.BlockSpec((rows, wide), lambda i: (0, i))
    by_head = pl.BlockSpec((each, rows, HEAD_DIM), lambda i: (i, 0, 0))
    whole = lambda array: pl.BlockSpec(array.shape, lambda i: (0, 0))
    per_head = jax.ShapeDtypeStruct((heads, rows, HEAD_DIM), jnp.bfloat16)
    return pl.pallas_call(
        mix_kernel,
        grid=(chans // wide,),
        in_specs=[
            stream,
            stream,
            stream,
            pl.BlockSpec((taps, wide), lambda i: (0, i)),
            pl.BlockSpec((wide, taps), lambda i: (i, 0)),
            whole(forward),
            whole(inverse),
        ],
        out_specs=[stream, by_head, by_head],
        out_shape=[jax.ShapeDtypeStruct((rows, chans), jnp.bfloat16), per_head, per_head],
        compiler_params=pltpu.CompilerParams(vmem_limit_bytes=32 * MIB),
        cost_estimate=pl.CostEstimate(
            flops=16 * rows * taps * chans, bytes_accessed=14 * rows * chans, transcendentals=0
        ),
        name="mix",
    )(gate, key, value, earlier, filters, forward, inverse)


def softened(query, keys, rows, heat, live):
    f32 = jnp.float32
    query = unit(query).astype(jnp.bfloat16)
    scores = lax.dot_general(query, keys, (((1,), (1,)), ((), ())), preferred_element_type=f32)
    weights = jnp.where(live, jnp.exp2(scores * heat), 0.0)
    total = jnp.sum(weights, axis=-1, keepdims=True)
    return jnp.dot(weights.astype(jnp.bfloat16), rows, preferred_element_type=f32) / total


def masks(offsets, first, slots, tokens, positions):
    place = lax.broadcasted_iota(jnp.int32, (tokens, positions), 1)
    return jnp.concatenate([place < offsets[first + slot] for slot in range(slots)], 0)


def attend_kernel(offsets, temps, queries, keys, rows, out):
    slots, tokens, wide = queries.shape
    f32 = jnp.float32
    live = masks(offsets, 0, slots, tokens, keys.shape[1])
    each = wide // HEAD_DIM
    base = pl.program_id(0) * each
    for head in range(each):
        cols = slice(head * HEAD_DIM, (head + 1) * HEAD_DIM)
        query = queries[:, :, cols].astype(f32).reshape(slots * tokens, HEAD_DIM)
        heat = temps[base + head] * (LOG2E / HEAD_DIM)
        done = softened(query, keys[head], rows[head], heat, live)
        out[:, :, cols] = done.reshape(slots, tokens, HEAD_DIM).astype(jnp.bfloat16)


def attend(offsets, temps, message, keys, rows):
    heads, positions, _ = keys.shape
    slots, tokens, _ = message.shape
    each = 4
    wide = each * HEAD_DIM
    scalars = pl.BlockSpec(memory_space=pltpu.SMEM)
    block = pl.BlockSpec((slots, tokens, wide), lambda i: (0, 0, i))
    by_head = pl.BlockSpec((each, positions, HEAD_DIM), lambda i: (i, 0, 0))
    work = slots * tokens * positions * heads
    return pl.pallas_call(
        attend_kernel,
        grid=(heads // each,),
        in_specs=[scalars, scalars, block, by_head, by_head],
        out_specs=block,
        out_shape=jax.ShapeDtypeStruct((slots, tokens, heads * HEAD_DIM), jnp.bfloat16),
        compiler_params=pltpu.CompilerParams(vmem_limit_bytes=24 * MIB),
        cost_estimate=pl.CostEstimate(
            flops=4 * work * HEAD_DIM, bytes_accessed=4 * keys.size, transcendentals=work
        ),
        name="attend",
    )(offsets, temps, message, keys, rows)


def extra_kernel(offsets, temps, place, rows, *refs):
    queries, out = refs[:-1], refs[-1]
    extras, tokens, wide = queries[0].shape
    f32 = jnp.float32
    me = place[0]
    live = masks(offsets, 0, extras, tokens, rows.shape[1])
    for head in range(wide // HEAD_DIM):
        cols = slice(head * HEAD_DIM, (head + 1) * HEAD_DIM)
        valued = rows[head]
        keyed = unit(valued.astype(f32)).astype(jnp.bfloat16)
        heat = temps[place[1] * (wide // HEAD_DIM) + head] * (LOG2E / HEAD_DIM)
        for step, source in enumerate(queries):
            query = source[:, :, cols].astype(f32).reshape(extras * tokens, HEAD_DIM)
            done = softened(query, keyed, valued, heat, live)
            done = done.reshape(1, extras, tokens, HEAD_DIM).astype(jnp.bfloat16)
            out[pl.ds(jnp.bitwise_xor(me, step), 1), :, :, cols] = done


def attend_extra(offsets, temps, place, rows, messages, chans):
    peers = len(messages)
    extras, tokens, _ = messages[0].shape
    wide = chans // peers
    scalars = pl.BlockSpec(memory_space=pltpu.SMEM)
    positions = rows.shape[1]
    work = extras * tokens * positions * peers * wide // HEAD_DIM
    return pl.pallas_call(
        extra_kernel,
        grid=(1,),
        in_specs=[scalars, scalars, scalars, pl.BlockSpec(rows.shape, lambda i: (0, 0, 0))]
        + [pl.BlockSpec((extras, tokens, wide), lambda i: (0, 0, chans // wide))] * peers,
        out_specs=pl.BlockSpec((peers, extras, tokens, wide), lambda i: (0, 0, 0, 0)),
        out_shape=jax.ShapeDtypeStruct((peers, extras, tokens, wide), jnp.bfloat16),
        compiler_params=pltpu.CompilerParams(vmem_limit_bytes=24 * MIB),
        cost_estimate=pl.CostEstimate(
            flops=4 * work * HEAD_DIM, bytes_accessed=2 * MIB, transcendentals=work
        ),
        name="attend_extra",
    )(offsets, temps, place, rows, *messages)


def mirrored(index, peers):
    result = 0
    for bit in range(peers.bit_length() - 1):
        result = result * 2 + jnp.bitwise_and(lax.shift_right_logical(index, bit), 1)
    return result


def pack_kernel(slots, place, table, queries, *refs):
    outs, sems = refs[:-1], refs[-1]
    peers = len(outs)
    chans = queries.shape[2]
    wide = outs[0].shape[2] - chans
    extras = HOT - slots if wide else 0
    copies = []
    for step, out in enumerate(outs):
        peer = jnp.bitwise_xor(place[0], step)
        for slot in range(slots):
            window = jnp.maximum(table[peer * HOT + slot], 0)
            target = out.at[slot, :, pl.ds(0, chans)] if wide else out.at[slot]
            copies.append((queries.at[window], target))
        if extras:
            start = pl.multiple_of(mirrored(peer, peers) * wide, wide)
        for extra in range(extras):
            window = table[place[2] * HOT + slots + extra]
            copies.append(
                (queries.at[window, :, pl.ds(start, wide)], out.at[extra, :, pl.ds(chans, wide)])
            )
    copies = [pltpu.make_async_copy(*pair, sems.at[i]) for i, pair in enumerate(copies)]
    for copy in copies:
        copy.start()
    for copy in copies:
        copy.wait()


def pack(place, table, queries, peers, slots, wide):
    _, tokens, chans = queries.shape
    scalars = pl.BlockSpec(memory_space=pltpu.SMEM)
    anywhere = pl.BlockSpec(memory_space=pl.ANY)
    extras = HOT - slots if wide else 0
    return pl.pallas_call(
        functools.partial(pack_kernel, slots),
        in_specs=[scalars, scalars, anywhere],
        out_specs=[anywhere] * peers,
        out_shape=[jax.ShapeDtypeStruct((slots, tokens, chans + wide), queries.dtype)] * peers,
        scratch_shapes=[pltpu.SemaphoreType.DMA((peers * (slots + extras),))],
        name="pack",
    )(place, table, queries)


def unpack_kernel(slots, peers, place, table, *refs):
    results, extra_results = refs[:peers], refs[peers:-2]
    out, sems = refs[-2:]
    copies = []
    for step, source in enumerate(results):
        peer = jnp.bitwise_xor(place[0], step)
        for slot in range(slots):
            window = table[peer * HOT + slot]
            copies.append((window, source.at[slot], out.at[jnp.maximum(window, 0)]))
    for source in extra_results:
        _, extras, _, wide = source.shape
        for peer in range(peers):
            start = pl.multiple_of(mirrored(jnp.int32(peer), peers) * wide, wide)
            for extra in range(extras):
                window = table[place[2] * HOT + slots + extra]
                target = out.at[jnp.maximum(window, 0), :, pl.ds(start, wide)]
                copies.append((window, source.at[peer, extra], target))

    def each(act):
        for i, (window, source, target) in enumerate(copies):
            copy = pltpu.make_async_copy(source, target, sems.at[i])
            pl.when(window >= 0)(functools.partial(act, copy))

    each(lambda copy: copy.start())
    each(lambda copy: copy.wait())


def unpack(place, table, results, extra_results, windows):
    peers = len(results)
    slots, tokens, chans = results[0].shape
    scalars = pl.BlockSpec(memory_space=pltpu.SMEM)
    anywhere = pl.BlockSpec(memory_space=pl.ANY)
    count = peers * slots + sum(array.shape[0] * array.shape[1] for array in extra_results)
    return pl.pallas_call(
        functools.partial(unpack_kernel, slots, peers),
        in_specs=[scalars, scalars] + [anywhere] * (peers + len(extra_results)),
        out_specs=anywhere,
        out_shape=jax.ShapeDtypeStruct((windows, tokens, chans), results[0].dtype),
        scratch_shapes=[pltpu.SemaphoreType.DMA((count,))],
        name="unpack",
    )(place, table, *results, *extra_results)


def exchanged(value, step):
    peers = lax.axis_size("pos")
    if step == 0:
        return value
    return lax.ppermute(value, "pos", [(i, i ^ step) for i in range(peers)])


def spread(rows, me, hot, peers):
    held = rows
    for bit in range(peers.bit_length() - 1):
        count = held.shape[0] // 2
        mine = jnp.bitwise_and(lax.shift_right_logical(me, bit), 1)
        sent = lax.dynamic_slice_in_dim(held, (1 - mine) * count, count, 0)
        kept = lax.dynamic_slice_in_dim(held, mine * count, count, 0)
        arrived = exchanged(sent, 1 << bit)
        have = lax.shift_right_logical(me, bit) == lax.shift_right_logical(hot, bit)
        held = jnp.where(have, kept, arrived)
    return held


def shards(gate_stream, key_stream, value_stream, filters, temps, queries, blocks, sites):
    rows, chans = gate_stream.shape
    taps = filters.shape[1]
    peers = lax.axis_size("pos")
    me = lax.axis_index("pos").astype(jnp.int32)
    windows = blocks.shape[0]
    heads = chans // HEAD_DIM
    extras = 2 if heads % peers == 0 else 0
    slots = HOT - extras
    wide = chans // peers if extras else 0

    last = slice(rows - taps, rows)
    product = key_stream[last].astype(jnp.float32) * value_stream[last].astype(jnp.float32)
    earlier = lax.ppermute(
        product.astype(jnp.bfloat16), "pos", [(i, i + 1) for i in range(peers - 1)]
    )

    order = jnp.arange(windows)
    same = (blocks[:, None] == blocks[None, :]) & (order[None, :] < order[:, None])
    within = jnp.sum(same, axis=1)
    hot = jnp.sum(jnp.where(within == HOT - 1, blocks, 0))
    named = jnp.arange(peers * HOT)[:, None] == (blocks * HOT + within)[None, :]
    table = (jnp.sum(jnp.where(named, order[None, :] + 1, 0), axis=1) - 1).astype(jnp.int32)
    offset = jnp.sum(jnp.where(named, (sites - blocks * rows)[None, :], 0), axis=1)
    offset = jnp.where(table >= 0, offset, rows).astype(jnp.int32)
    mine = lax.dynamic_slice_in_dim(offset, me * HOT, HOT, 0)
    place = jnp.stack([me, mirrored(me, peers), hot]).astype(jnp.int32)

    messages = pack(place, table, queries, peers, slots, wide)
    arrived = [exchanged(message, step) for step, message in enumerate(messages)]
    hyena_out, valued, keyed = mix(gate_stream, key_stream, value_stream, earlier, filters)
    results = [attend(mine, temps, message, keyed, valued) for message in arrived]
    returned = [exchanged(result, step) for step, result in enumerate(results)]
    extra_results = []
    if extras:
        share = spread(valued, me, hot, peers)
        theirs = lax.dynamic_slice_in_dim(offset, hot * HOT + slots, extras, 0)
        result = attend_extra(theirs, temps, place, share, arrived, chans)
        extra_results.append(lax.all_to_all(result, "pos", 0, 0, tiled=True))
    attended = unpack(place, table, returned, extra_results, windows)
    return (hyena_out, attended)


def solution(mesh):
    placed = (
        P(("groups", "pos"), "mp"),
        P(("groups", "pos"), "mp"),
        P(("groups", "pos"), "mp"),
        P("mp", None),
        P("mp"),
        P("groups", "pos", "mp"),
        P("groups"),
        P("groups"),
    )
    return jax.shard_map(
        shards,
        mesh=mesh,
        in_specs=placed,
        out_specs=(P(("groups", "pos"), "mp"), P("groups", "pos", "mp")),
        check_vma=False,
    )
```

time: 293 us -> 340 us (1.16)
  Pallas kernels: 0 us -> 191 us
  blocking collectives: 96.9 us -> 0 us
  matrix products: 70.8 us -> 0 us
  starting transfers between devices: 10.5 us -> 68.3 us
  local copies, waits for them, and re-layouts: 65.1 us -> 19 us
  waiting for transfers between devices: 20 us -> 49.1 us
  other arithmetic: 27.7 us -> 7.77 us
    pallas_call x0 -> x12, Pallas kernels: none -> 191 us  [the longest x1 73.7 us: pack(): pl.pallas_call(functools.partial(pack_kernel, slots), in_specs=[scalars,...]
    all_to_all x1 -> x0, blocking collectives: 96.9 us -> none  [shards(): lax.all_to_all(results, 'pos', split_axis=1, concat_axis=0, tiled=True)]
    ppermute x1 -> x18, starting transfers between devices: 5.69 us -> 64.2 us  [the longest x17 59.3 us: exchanged(): return lax.ppermute(value, 'pos', [(i, i ^ step) for i in range(peers)])]
    ppermute x1 -> x18, waiting for transfers between devices: 0.01 us -> 49.1 us  [the longest x17 38 us: exchanged(): return lax.ppermute(value, 'pos', [(i, i ^ step) for i in range(peers)])]
    conv_general_dilated x1 -> x0, matrix products: 45.5 us -> none  [causal_mix(): lax.conv_general_dilated(extended.astype(jnp.float32)[None], kernel, (1,)...]
    dot_general x10 -> x0, matrix products: 25.4 us -> none  [the longest x4 14.5 us: attend_slot(): jnp.einsum('qhd,khd->hqk', qnorm, keyed, preferred_element_type=jnp.float32)]
    all_to_all x1, waiting for transfers between devices: 20 us -> 0.01 us  [shards(): extra_results.append(lax.all_to_all(result, 'pos', 0, 0, tiled=True))]
    while x15 -> x0, local copies, waits for them, and re-layouts: 18.5 us -> none  [the longest x3 16.9 us: shards(): results = lax.map(one_slot, (arrived, offsets))]
  transfers between devices with their start and end apart: 2 -> 19, of which waited for: 1 -> 6; matrix products, arithmetic and copies ran while one was open for 32% -> 2% of each run, Pallas kernels for 0% -> 33%
where the time goes in v1:
time: 340 us; the launch traced here: 339 us
  Pallas kernels  191 us (56%)
  starting transfers between devices  68.3 us (20%)
  waiting for transfers between devices  49.1 us (14%)
  local copies, waits for them, and re-layouts  19 us (6%)
  other arithmetic  7.77 us (2%)
  between operations  3.67 us (1%)
    pallas_call x1, Pallas kernels, pack(): pl.pallas_call(functools.partial(pack_kernel, slots), in_specs=[scalars,...  73.7 us
    pallas_call x1, Pallas kernels, unpack(): pl.pallas_call(functools.partial(unpack_kernel, slots, peers), in_specs=[...  65.6 us
    ppermute x17, starting transfers between devices, exchanged(): return lax.ppermute(value, 'pos', [(i, i ^ step) for i in range(peers)])  59.3 us
    ppermute x17, waiting for transfers between devices, exchanged(): return lax.ppermute(value, 'pos', [(i, i ^ step) for i in range(peers)])  38 us
    pallas_call x8, Pallas kernels, attend(): pl.pallas_call(attend_kernel, grid=(heads // each,), in_specs=[scalars, s...  35 us
    unnamed x50, local copies, waits for them, and re-layouts  17.1 us
    pallas_call x1, Pallas kernels, mix(): pl.pallas_call(mix_kernel, grid=(chans // wide,), in_specs=[stream, strea...  12.5 us
    ppermute x1, waiting for transfers between devices, shards(): lax.ppermute(product.astype(jnp.bfloat16), 'pos', [(i, i + 1) for i in ra...  11.1 us
  transfers between devices with their start and end apart: 19, of which 6 were waited for; matrix products, arithmetic and copies ran while one was open for 2% of the time, Pallas kernels for 33%

profile of v1, /device:TPU:0, one launch (start us, length us, event | category | flops | bytes accessed | tf_op | source)
XLA Modules:
  0.0 339.1 jit_solution(15102094577203784578)
XLA Ops:
  2.0 4.9 %collective-permute-start = (bf16[128,2048]{1,0:T(8,128)(2,1)S(1)}, bf16[128,2048]{1,0:T(8,128)(2,1)S(1)}, u32[]{:S(2)}, u32[]{:S(2)}) collective-permute-start(bf16[128,2048]{1,0:T(8,128)(2,1)S(1)} %multiply_convert_fusion), channel_id=1, source_target_pairs={{0,2},{2,4},{4,6},{6,8},{8,10},{10,12},{12,14},{1,3},{3,5},{5,7},{... | collective-permute-start | bytes 1572872 | tf_op jit(solution)/shard_map/ppermute | solution.py:325
  6.9 11.1 %collective-permute-done.earlier = bf16[128,2048]{1,0:T(8,128)(2,1)S(1)} collective-permute-done((bf16[128,2048]{1,0:T(8,128)(2,1)S(1)}, bf16[128,2048]{1,0:T(8,128)(2,1)S(1)}, u32[]{:S(2)}, u32[]{:S(2)}) %collective-permute-start) | collective-permute-done | bytes 524320 | tf_op jit(solution)/shard_map/ppermute | solution.py:325
  18.0 1.6 copy-done.3
  19.6 1.6 copy-done.4
  25.9 12.5 %mix.1 = (bf16[512,2048]{1,0:T(8,128)(2,1)}, bf16[16,512,128]{2,1,0:T(8,128)(2,1)S(1)}, bf16[16,512,128]{2,1,0:T(8,128)(2,1)S(1)}) custom-call(bf16[512,2048]{1,0:T(8,128)(2,1)S(1)} %copy-done.5, bf16[512,2048]{1,0:T(8,128)(2,1)S(1)} %copy-done.3, bf16[512,2048]{1,0:T(8,128)(2,1)S(1)} %copy-done.4, bf16[128,2048]{1,0:T(8,128)(2,1)S(1)} %collective-permute-done.earlier, ...), custom_call_target="tpu_custom_call" | custom-call | flops 2147483648 | bytes 14680064 | tf_op jit(solution)/shard_map/mix/pallas_call | solution.py:87
  39.8 2.5 collective-permute-start.15
  43.9 20.8 %collective-permute-done.15 = bf16[8,512,128]{2,1,0:T(8,128)(2,1)} collective-permute-done((bf16[8,512,128]{2,1,0:T(8,128)(2,1)S(1)}, bf16[8,512,128]{2,1,0:T(8,128)(2,1)}, u32[]{:S(2)}, u32[]{:S(2)}) %collective-permute-start.15) | collective-permute-done | bytes 1048608 | tf_op jit(solution)/shard_map/ppermute | solution.py:296
  67.9 2.7 collective-permute-start.16
  72.5 73.7 %pack.1 = (bf16[2,32,2304]{2,1,0:T(8,128)(2,1)}, bf16[2,32,2304]{2,1,0:T(8,128)(2,1)}, bf16[2,32,2304]{2,1,0:T(8,128)(2,1)}, bf16[2,32,2304]{2,1,0:T(8,128)(2,1)...) custom-call(s32[3]{0:T(128)} %pad_add_fusion.place, ...), custom_call_target="tpu_custom_call" | custom-call | tf_op jit(solution)/shard_map/pack/pallas_call | solution.py:239
  146.9 2.5 collective-permute-start.11
  149.4 2.2 collective-permute-start.13
  154.3 2.4 collective-permute-start.17
  158.9 13.6 %collective-permute-start.7 = (bf16[2,32,2304]{2,1,0:T(8,128)(2,1)}, bf16[2,32,2304]{2,1,0:T(8,128)(2,1)}, u32[]{:S(2)}, u32[]{:S(2)}) collective-permute-start(bf16[2,32,2304]{2,1,0:T(8,128)(2,1)} %get-tuple-element.20), channel_id=1, source_target_pairs={{0,8},{2,10},{4,12},{6,14},{8,0},{10,2},{12,4},{14,6},{1,9},{3,11}... | collective-permute-start | bytes 884744 | tf_op jit(solution)/shard_map/ppermute | solution.py:296
  172.5 19.5 %collective-permute-start.9 = (bf16[2,32,2304]{2,1,0:T(8,128)(2,1)}, bf16[2,32,2304]{2,1,0:T(8,128)(2,1)}, u32[]{:S(2)}, u32[]{:S(2)}) collective-permute-start(bf16[2,32,2304]{2,1,0:T(8,128)(2,1)} %get-tuple-element.21), channel_id=1, source_target_pairs={{0,10},{2,8},{4,14},{6,12},{8,2},{10,0},{12,6},{14,4},{1,11},{3,9}... | collective-permute-start | bytes 884744 | tf_op jit(solution)/shard_map/ppermute | solution.py:296
  193.5 1.6 copy-done.1
  195.1 4.8 %attend.15 = bf16[2,32,2048]{2,1,0:T(8,128)(2,1)} custom-call(s32[4]{0:T(128)S(1)} %dynamic_slice.24.offsets, f32[16]{0:T(128)S(1)} %copy-done.13, bf16[2,32,2304]{2,1,0:T(8,128)(2,1)S(1)} %collective-permute-done.13.queries.refs_7_, bf16[16,512,128]{2,1,0:T(8,128)(2,1)S(1)} %copy-done.1, bf16[16,512,128]{2,1,0:T(8,128)(2,1)S(1)} %get-tuple-element.16.rows), custom_call_target="tpu_custom_call" | custom-call | flops 268435456 | bytes 4194304 | tf_op jit(solution)/shard_map/attend/pallas_call | solution.py:146
  200.7 4.2 %attend.14 = bf16[2,32,2048]{2,1,0:T(8,128)(2,1)S(1)} custom-call(s32[4]{0:T(128)S(1)} %dynamic_slice.24.offsets, f32[16]{0:T(128)S(1)} %copy-done.13, bf16[2,32,2304]{2,1,0:T(8,128)(2,1)S(1)} %collective-permute-done.11.queries.refs_6_, bf16[16,512,128]{2,1,0:T(8,128)(2,1)S(1)} %copy-done.1, bf16[16,512,128]{2,1,0:T(8,128)(2,1)S(1)} %get-tuple-element.16.rows), custom_call_target="tpu_custom_call" | custom-call | flops 268435456 | bytes 4194304 | tf_op jit(solution)/shard_map/attend/pallas_call | solution.py:146
  204.9 2.3 collective-permute-start.14
  207.2 2.3 collective-permute-start.12
  210.5 12.6 %collective-permute-done.9.queries.refs_5_ = bf16[2,32,2304]{2,1,0:T(8,128)(2,1)} collective-permute-done((bf16[2,32,2304]{2,1,0:T(8,128)(2,1)}, bf16[2,32,2304]{2,1,0:T(8,128)(2,1)}, u32[]{:S(2)}, u32[]{:S(2)}) %collective-permute-start.9) | collective-permute-done | bytes 294944 | tf_op jit(solution)/shard_map/ppermute | solution.py:296
  224.1 4.5 %attend_extra.1 = bf16[8,2,32,256]{3,2,1,0:T(8,128)(2,1)} custom-call(s32[2]{0:T(128)S(1)} %dynamic_slice.25.offsets, f32[16]{0:T(128)S(1)} %copy-done.13, s32[3]{0:T(128)S(1)} %copy-done.14, bf16[2,512,128]{2,1,0:T(8,128)(2,1)S(1)} %dynamic-slice_select_fusion.2.rows, bf16[2,32,2304]{2,1,0:T(8,128)(2,1)S(1)} %copy-done.6, ...), custom_call_target="tpu_custom_call" | custom-call | flops 268435456 | bytes 2097152 | tf_op jit(solution)/shard_map/attend_extra/pallas_call | solution.py:185
  228.6 4.1 %all-to-all-start = ((bf16[8,2,32,256]{3,2,1,0:T(8,128)(2,1)}), bf16[8,2,32,256]{3,2,1,0:T(8,128)(2,1)}, u32[]{:S(2)}, u32[]{:S(2)}) async-start(bf16[8,2,32,256]{3,2,1,0:T(8,128)(2,1)} %attend_extra.1), calls=%async_computation | async-start | bytes 524288 | tf_op jit(solution)/shard_map/all_to_all | solution.py:350
  234.2 4.4 %attend.13 = bf16[2,32,2048]{2,1,0:T(8,128)(2,1)S(1)} custom-call(s32[4]{0:T(128)S(1)} %dynamic_slice.24.offsets, f32[16]{0:T(128)S(1)} %copy-done.13, bf16[2,32,2304]{2,1,0:T(8,128)(2,1)} %collective-permute-done.9.queries.refs_5_, bf16[16,512,128]{2,1,0:T(8,128)(2,1)S(1)} %copy-done.2, bf16[16,512,128]{2,1,0:T(8,128)(2,1)S(1)} %get-tuple-element.16.rows), custom_call_target="tpu_custom_call" | custom-call | flops 268435456 | bytes 4194304 | tf_op jit(solution)/shard_map/attend/pallas_call | solution.py:146
  238.7 3.8 %collective-permute-start.10 = (bf16[2,32,2048]{2,1,0:T(8,128)(2,1)S(1)}, bf16[2,32,2048]{2,1,0:T(8,128)(2,1)S(1)}, u32[]{:S(2)}, u32[]{:S(2)}) collective-permute-start(bf16[2,32,2048]{2,1,0:T(8,128)(2,1)S(1)} %attend.13), channel_id=1, source_target_pairs={{0,10},{2,8},{4,14},{6,12},{8,2},{10,0},{12,6},{14,4},{1,11},{3,9}... | collective-permute-start | bytes 786440 | tf_op jit(solution)/shard_map/ppermute | solution.py:296
  242.5 4.4 %attend.12 = bf16[2,32,2048]{2,1,0:T(8,128)(2,1)S(1)} custom-call(s32[4]{0:T(128)S(1)} %dynamic_slice.24.offsets, f32[16]{0:T(128)S(1)} %copy-done.13, bf16[2,32,2304]{2,1,0:T(8,128)(2,1)} %collective-permute-done.7.queries.refs_4_, bf16[16,512,128]{2,1,0:T(8,128)(2,1)S(1)} %copy-done.2, bf16[16,512,128]{2,1,0:T(8,128)(2,1)S(1)} %get-tuple-element.16.rows), custom_call_target="tpu_custom_call" | custom-call | flops 268435456 | bytes 4194304 | tf_op jit(solution)/shard_map/attend/pallas_call | solution.py:146
  247.5 4.4 %attend.11 = bf16[2,32,2048]{2,1,0:T(8,128)(2,1)S(1)} custom-call(s32[4]{0:T(128)S(1)} %dynamic_slice.24.offsets, f32[16]{0:T(128)S(1)} %copy-done.13, bf16[2,32,2304]{2,1,0:T(8,128)(2,1)} %collective-permute-done.5.queries.refs_3_, bf16[16,512,128]{2,1,0:T(8,128)(2,1)S(1)} %copy-done.2, bf16[16,512,128]{2,1,0:T(8,128)(2,1)S(1)} %get-tuple-element.16.rows), custom_call_target="tpu_custom_call" | custom-call | flops 268435456 | bytes 4194304 | tf_op jit(solution)/shard_map/attend/pallas_call | solution.py:146
  253.5 4.2 %attend.10 = bf16[2,32,2048]{2,1,0:T(8,128)(2,1)S(1)} custom-call(s32[4]{0:T(128)S(1)} %dynamic_slice.24.offsets, f32[16]{0:T(128)S(1)} %copy-done.13, bf16[2,32,2304]{2,1,0:T(8,128)(2,1)S(1)} %collective-permute-done.3.queries.refs_2_, bf16[16,512,128]{2,1,0:T(8,128)(2,1)S(1)} %copy-done.2, bf16[16,512,128]{2,1,0:T(8,128)(2,1)S(1)} %get-tuple-element.16.rows), custom_call_target="tpu_custom_call" | custom-call | flops 268435456 | bytes 4194304 | tf_op jit(solution)/shard_map/attend/pallas_call | solution.py:146
  257.7 4.3 %attend.9 = bf16[2,32,2048]{2,1,0:T(8,128)(2,1)S(1)} custom-call(s32[4]{0:T(128)S(1)} %dynamic_slice.24.offsets, f32[16]{0:T(128)S(1)} %copy-done.13, bf16[2,32,2304]{2,1,0:T(8,128)(2,1)S(1)} %collective-permute-done.1.queries.refs_1_, bf16[16,512,128]{2,1,0:T(8,128)(2,1)S(1)} %copy-done.2, bf16[16,512,128]{2,1,0:T(8,128)(2,1)S(1)} %get-tuple-element.16.rows), custom_call_target="tpu_custom_call" | custom-call | flops 268435456 | bytes 4194304 | tf_op jit(solution)/shard_map/attend/pallas_call | solution.py:146
  262.2 1.9 collective-permute-start.2
  264.1 4.2 %attend.8.refs_0_ = bf16[2,32,2048]{2,1,0:T(8,128)(2,1)S(1)} custom-call(s32[4]{0:T(128)S(1)} %dynamic_slice.24.offsets, f32[16]{0:T(128)S(1)} %copy-done.13, bf16[2,32,2304]{2,1,0:T(8,128)(2,1)S(1)} %copy-done.6, bf16[16,512,128]{2,1,0:T(8,128)(2,1)S(1)} %copy-done.2, bf16[16,512,128]{2,1,0:T(8,128)(2,1)S(1)} %get-tuple-element.16.rows), custom_call_target="tpu_custom_call" | custom-call | flops 268435456 | bytes 4194304 | tf_op jit(solution)/shard_map/attend/pallas_call | solution.py:146
  269.3 2.7 collective-permute-done.4.refs_2_
  273.5 65.6 %unpack.1 = bf16[16,32,2048]{2,1,0:T(8,128)(2,1)} custom-call(s32[3]{0:T(128)} %pad_add_fusion.place, s32[32]{0:T(128)} %get-tuple-element.29.table, bf16[2,32,2048]{2,1,0:T(8,128)(2,1)} %copy-done.10, bf16[2,32,2048]{2,1,0:T(8,128)(2,1)} %copy-done.22, bf16[2,32,2048]{2,1,0:T(8,128)(2,1)} %copy-done.21, bf16[2,32,2048]{2,1,0:T(8,128)(2,1)} %copy-done.20, ...), custom_call_target="tpu_custom_call" | custom-call | tf_op jit(solution)/shard_map/unpack/pallas_call | solution.py:282
  (82 shorter events, 27.5 us)
Async XLA Ops:
  2.0 16.0 %collective-permute-start = (bf16[128,2048]{1,0:T(8,128)(2,1)S(1)}, bf16[128,2048]{1,0:T(8,128)(2,1)S(1)}, u32[]{:S(2)}, u32[]{:S(2)}) collective-permute-start(bf16[128,2048]{1,0:T(8,128)(2,1)S(1)} %multiply_convert_fusion), channel_id=1, source_target_pairs={{0,2},{2,4},{4,6},{6,8},{8,10},{10,12},{12,14},{1,3},{3,5},{5,7},{... | collective-permute-start | bytes 1572872 | tf_op jit(solution)/shard_map/ppermute | solution.py:325
  18.0 1.6 copy-start.3
  39.7 2.6 copy-start.23
  39.7 2.8 copy-start.24
  39.8 24.9 %collective-permute-start.15 = (bf16[8,512,128]{2,1,0:T(8,128)(2,1)S(1)}, bf16[8,512,128]{2,1,0:T(8,128)(2,1)}, u32[]{:S(2)}, u32[]{:S(2)}) collective-permute-start(bf16[8,512,128]{2,1,0:T(8,128)(2,1)S(1)} %constant_dynamic-slice_fusion.2), channel_id=1, source_target_pairs={{0,2},{2,0},{4,6},{6,4},{8,10},{10,8},{12,14},{14,12},{1,3},{3,1},... | collective-permute-start | bytes 3145736 | tf_op jit(solution)/shard_map/ppermute | solution.py:296
  67.9 84.4 %collective-permute-start.16 = (bf16[4,512,128]{2,1,0:T(8,128)(2,1)}, bf16[4,512,128]{2,1,0:T(8,128)(2,1)}, u32[]{:S(2)}, u32[]{:S(2)}) collective-permute-start(bf16[4,512,128]{2,1,0:T(8,128)(2,1)} %constant_dynamic-slice_fusion.1), channel_id=1, source_target_pairs={{0,4},{2,6},{4,0},{6,2},{8,12},{10,14},{12,8},{14,10},{1,5},{3,7},... | collective-permute-start | bytes 1572872 | tf_op jit(solution)/shard_map/ppermute | solution.py:296
  72.5 121.0 %copy-start.13 = (f32[16]{0:T(128)S(1)}, f32[16]{0:T(128)}, u32[]{:S(2)}) copy-start(f32[16]{0:T(128)} %temps.17) | copy-start | bytes 196
  146.2 10.6 %collective-permute-start.1 = (bf16[2,32,2304]{2,1,0:T(8,128)(2,1)}, bf16[2,32,2304]{2,1,0:T(8,128)(2,1)S(1)}, u32[]{:S(2)}, u32[]{:S(2)}) collective-permute-start(bf16[2,32,2304]{2,1,0:T(8,128)(2,1)} %get-tuple-element.17), channel_id=1, source_target_pairs={{0,2},{2,0},{4,6},{6,4},{8,10},{10,8},{12,14},{14,12},{1,3},{3,1},... | collective-permute-start | bytes 884744 | tf_op jit(solution)/shard_map/ppermute | solution.py:296
  146.9 12.0 %collective-permute-start.11 = (bf16[2,32,2304]{2,1,0:T(8,128)(2,1)}, bf16[2,32,2304]{2,1,0:T(8,128)(2,1)S(1)}, u32[]{:S(2)}, u32[]{:S(2)}) collective-permute-start(bf16[2,32,2304]{2,1,0:T(8,128)(2,1)} %get-tuple-element.22), channel_id=1, source_target_pairs={{0,12},{2,14},{4,8},{6,10},{8,4},{10,6},{12,0},{14,2},{1,13},{3,15... | collective-permute-start | bytes 884744 | tf_op jit(solution)/shard_map/ppermute | solution.py:296
  149.4 23.1 %collective-permute-start.13 = (bf16[2,32,2304]{2,1,0:T(8,128)(2,1)}, bf16[2,32,2304]{2,1,0:T(8,128)(2,1)S(1)}, u32[]{:S(2)}, u32[]{:S(2)}) collective-permute-start(bf16[2,32,2304]{2,1,0:T(8,128)(2,1)} %get-tuple-element.23), channel_id=1, source_target_pairs={{0,14},{2,12},{4,10},{6,8},{8,6},{10,4},{12,2},{14,0},{1,15},{3,13... | collective-permute-start | bytes 884744 | tf_op jit(solution)/shard_map/ppermute | solution.py:296
  151.6 53.4 %collective-permute-start.3 = (bf16[2,32,2304]{2,1,0:T(8,128)(2,1)}, bf16[2,32,2304]{2,1,0:T(8,128)(2,1)S(1)}, u32[]{:S(2)}, u32[]{:S(2)}) collective-permute-start(bf16[2,32,2304]{2,1,0:T(8,128)(2,1)} %get-tuple-element.18), channel_id=1, source_target_pairs={{0,4},{2,6},{4,0},{6,2},{8,12},{10,14},{12,8},{14,10},{1,5},{3,7},... | collective-permute-start | bytes 884744 | tf_op jit(solution)/shard_map/ppermute | solution.py:296
  153.5 18.9 %copy-start.16 = (bf16[4,512,128]{2,1,0:T(8,128)(2,1)}, bf16[4,512,128]{2,1,0:T(8,128)(2,1)S(1)}, u32[]{:S(2)}) copy-start(bf16[4,512,128]{2,1,0:T(8,128)(2,1)S(1)} %dynamic-slice_select_fusion.1) | copy-start | bytes 1572868
  154.3 52.9 %collective-permute-start.17 = (bf16[2,512,128]{2,1,0:T(8,128)(2,1)}, bf16[2,512,128]{2,1,0:T(8,128)(2,1)}, u32[]{:S(2)}, u32[]{:S(2)}) collective-permute-start(bf16[2,512,128]{2,1,0:T(8,128)(2,1)} %constant_dynamic-slice_fusion), channel_id=1, source_target_pairs={{0,8},{2,10},{4,12},{6,14},{8,0},{10,2},{12,4},{14,6},{1,9},{3,11}... | collective-permute-start | bytes 786440 | tf_op jit(solution)/shard_map/ppermute | solution.py:296
  156.8 53.7 %collective-permute-start.5 = (bf16[2,32,2304]{2,1,0:T(8,128)(2,1)}, bf16[2,32,2304]{2,1,0:T(8,128)(2,1)}, u32[]{:S(2)}, u32[]{:S(2)}) collective-permute-start(bf16[2,32,2304]{2,1,0:T(8,128)(2,1)} %get-tuple-element.19), channel_id=1, source_target_pairs={{0,6},{2,4},{4,2},{6,0},{8,14},{10,12},{12,10},{14,8},{1,7},{3,5},... | collective-permute-start | bytes 884744 | tf_op jit(solution)/shard_map/ppermute | solution.py:296
  158.9 51.6 %collective-permute-start.7 = (bf16[2,32,2304]{2,1,0:T(8,128)(2,1)}, bf16[2,32,2304]{2,1,0:T(8,128)(2,1)}, u32[]{:S(2)}, u32[]{:S(2)}) collective-permute-start(bf16[2,32,2304]{2,1,0:T(8,128)(2,1)} %get-tuple-element.20), channel_id=1, source_target_pairs={{0,8},{2,10},{4,12},{6,14},{8,0},{10,2},{12,4},{14,6},{1,9},{3,11}... | collective-permute-start | bytes 884744 | tf_op jit(solution)/shard_map/ppermute | solution.py:296
  172.5 50.6 %collective-permute-start.9 = (bf16[2,32,2304]{2,1,0:T(8,128)(2,1)}, bf16[2,32,2304]{2,1,0:T(8,128)(2,1)}, u32[]{:S(2)}, u32[]{:S(2)}) collective-permute-start(bf16[2,32,2304]{2,1,0:T(8,128)(2,1)} %get-tuple-element.21), channel_id=1, source_target_pairs={{0,10},{2,8},{4,14},{6,12},{8,2},{10,0},{12,6},{14,4},{1,11},{3,9}... | collective-permute-start | bytes 884744 | tf_op jit(solution)/shard_map/ppermute | solution.py:296
  193.5 1.6 copy-start.1
  200.7 8.8 %copy-start.17 = (bf16[4,512,128]{2,1,0:T(8,128)(2,1)S(1)}, bf16[4,512,128]{2,1,0:T(8,128)(2,1)}, u32[]{:S(2)}) copy-start(bf16[4,512,128]{2,1,0:T(8,128)(2,1)} %copy-done.16) | copy-start | bytes 1572868
  200.7 22.4 %copy-start.6 = (bf16[2,32,2304]{2,1,0:T(8,128)(2,1)S(1)}, bf16[2,32,2304]{2,1,0:T(8,128)(2,1)}, u32[]{:S(2)}) copy-start(bf16[2,32,2304]{2,1,0:T(8,128)(2,1)} %get-tuple-element.14.queries.refs_0_) | copy-start | bytes 884740
  200.7 22.4 %copy-start.14 = (s32[3]{0:T(128)S(1)}, s32[3]{0:T(128)}, u32[]{:S(2)}) copy-start(s32[3]{0:T(128)} %pad_add_fusion.place) | copy-start | bytes 40
  204.9 57.0 %collective-permute-start.14 = (bf16[2,32,2048]{2,1,0:T(8,128)(2,1)}, bf16[2,32,2048]{2,1,0:T(8,128)(2,1)}, u32[]{:S(2)}, u32[]{:S(2)}) collective-permute-start(bf16[2,32,2048]{2,1,0:T(8,128)(2,1)} %attend.15), channel_id=1, source_target_pairs={{0,14},{2,12},{4,10},{6,8},{8,6},{10,4},{12,2},{14,0},{1,15},{3,13... | collective-permute-start | bytes 786440 | tf_op jit(solution)/shard_map/ppermute | solution.py:296
  207.2 55.0 %collective-permute-start.12 = (bf16[2,32,2048]{2,1,0:T(8,128)(2,1)S(1)}, bf16[2,32,2048]{2,1,0:T(8,128)(2,1)}, u32[]{:S(2)}, u32[]{:S(2)}) collective-permute-start(bf16[2,32,2048]{2,1,0:T(8,128)(2,1)S(1)} %attend.14), channel_id=1, source_target_pairs={{0,12},{2,14},{4,8},{6,10},{8,4},{10,6},{12,0},{14,2},{1,13},{3,15... | collective-permute-start | bytes 786440 | tf_op jit(solution)/shard_map/ppermute | solution.py:296
  228.6 44.3 %all-to-all-start = ((bf16[8,2,32,256]{3,2,1,0:T(8,128)(2,1)}), bf16[8,2,32,256]{3,2,1,0:T(8,128)(2,1)}, u32[]{:S(2)}, u32[]{:S(2)}) async-start(bf16[8,2,32,256]{3,2,1,0:T(8,128)(2,1)} %attend_extra.1), calls=%async_computation | async-start | bytes 524288 | tf_op jit(solution)/shard_map/all_to_all | solution.py:350
  232.6 1.6 copy-start.2
  238.7 30.3 %collective-permute-start.10 = (bf16[2,32,2048]{2,1,0:T(8,128)(2,1)S(1)}, bf16[2,32,2048]{2,1,0:T(8,128)(2,1)S(1)}, u32[]{:S(2)}, u32[]{:S(2)}) collective-permute-start(bf16[2,32,2048]{2,1,0:T(8,128)(2,1)S(1)} %attend.13), channel_id=1, source_target_pairs={{0,10},{2,8},{4,14},{6,12},{8,2},{10,0},{12,6},{14,4},{1,11},{3,9}... | collective-permute-start | bytes 786440 | tf_op jit(solution)/shard_map/ppermute | solution.py:296
  246.9 22.1 %collective-permute-start.8 = (bf16[2,32,2048]{2,1,0:T(8,128)(2,1)S(1)}, bf16[2,32,2048]{2,1,0:T(8,128)(2,1)S(1)}, u32[]{:S(2)}, u32[]{:S(2)}) collective-permute-start(bf16[2,32,2048]{2,1,0:T(8,128)(2,1)S(1)} %attend.12), channel_id=1, source_target_pairs={{0,8},{2,10},{4,12},{6,14},{8,0},{10,2},{12,4},{14,6},{1,9},{3,11}... | collective-permute-start | bytes 786440 | tf_op jit(solution)/shard_map/ppermute | solution.py:296
  252.0 17.4 %collective-permute-start.6 = (bf16[2,32,2048]{2,1,0:T(8,128)(2,1)S(1)}, bf16[2,32,2048]{2,1,0:T(8,128)(2,1)S(1)}, u32[]{:S(2)}, u32[]{:S(2)}) collective-permute-start(bf16[2,32,2048]{2,1,0:T(8,128)(2,1)S(1)} %attend.11), channel_id=1, source_target_pairs={{0,6},{2,4},{4,2},{6,0},{8,14},{10,12},{12,10},{14,8},{1,7},{3,5},... | collective-permute-start | bytes 786440 | tf_op jit(solution)/shard_map/ppermute | solution.py:296
  262.0 10.1 %collective-permute-start.4 = (bf16[2,32,2048]{2,1,0:T(8,128)(2,1)S(1)}, bf16[2,32,2048]{2,1,0:T(8,128)(2,1)S(1)}, u32[]{:S(2)}, u32[]{:S(2)}) collective-permute-start(bf16[2,32,2048]{2,1,0:T(8,128)(2,1)S(1)} %attend.10), channel_id=1, source_target_pairs={{0,4},{2,6},{4,0},{6,2},{8,12},{10,14},{12,8},{14,10},{1,5},{3,7},... | collective-permute-start | bytes 786440 | tf_op jit(solution)/shard_map/ppermute | solution.py:296
  262.2 10.6 %collective-permute-start.2 = (bf16[2,32,2048]{2,1,0:T(8,128)(2,1)S(1)}, bf16[2,32,2048]{2,1,0:T(8,128)(2,1)S(1)}, u32[]{:S(2)}, u32[]{:S(2)}) collective-permute-start(bf16[2,32,2048]{2,1,0:T(8,128)(2,1)S(1)} %attend.9), channel_id=1, source_target_pairs={{0,2},{2,0},{4,6},{6,4},{8,10},{10,8},{12,14},{14,12},{1,3},{3,1},... | collective-permute-start | bytes 786440 | tf_op jit(solution)/shard_map/ppermute | solution.py:296
  269.0 3.1 copy-start.18
  269.0 3.1 copy-start.19
  269.3 2.7 copy-start.20
  (12 other events, 12.4 us)

commit v2 on v1

v2 whole, which is shorter than its diff:
```python
import functools

import jax
import jax.numpy as jnp
import numpy as np
from jax import lax
from jax.experimental import pallas as pl
from jax.experimental.pallas import tpu as pltpu
from jax.sharding import PartitionSpec as P

HEAD_DIM = 128
HOT = 4
EPS = 1e-06
LOG2E = 1.4426950408889634
MIB = 1 << 20
AHEAD = 16
SMALL = pl.CostEstimate(flops=1000, bytes_accessed=1000, transcendentals=0)


def halves(array):
    high = array.astype(jnp.bfloat16)
    low = (array - high.astype(jnp.float32)).astype(jnp.bfloat16)
    return high, low


def transforms(taps):
    size = 2 * taps
    odd = 2 * np.arange(taps) + 1
    angle = np.pi / size * ((odd[:, None] * np.arange(size)[None, :]) % (2 * size))
    forward = np.concatenate([np.cos(angle), -np.sin(angle)], 0)
    inverse = forward.T[taps:] * (2.0 / size)
    out = []
    for matrix in (forward, inverse):
        high = matrix.astype(jnp.bfloat16)
        low = (matrix - high.astype(np.float64)).astype(jnp.bfloat16)
        out.append(np.concatenate([high, low], 0))
    return out


def unit(block):
    return block * lax.rsqrt(jnp.mean(block * block, axis=-1, keepdims=True) + EPS)


def mix_kernel(gate, key, value, earlier, filters, forward, inverse, out, rows_of, keys_of):
    rows, wide = gate.shape
    taps = filters.shape[1]
    size = 2 * taps
    f32 = jnp.float32
    fwd = forward[...]
    inv = inverse[...]
    high, low = halves(filters[...])
    across = (((1,), (1,)), ((), ()))
    both = lax.dot_general(fwd[:, :taps], high, across, preferred_element_type=f32)
    spectrum = both[:size] + both[size:]
    spectrum += lax.dot_general(fwd[:size, :taps], low, across, preferred_element_type=f32)
    hr, hi = spectrum[:taps], spectrum[taps:]
    before = earlier[...]
    for start in range(0, rows, taps):
        part = slice(start, start + taps)
        now = (key[part, :].astype(f32) * value[part, :].astype(f32)).astype(jnp.bfloat16)
        both = jnp.dot(fwd, jnp.concatenate([before, now], 0), preferred_element_type=f32)
        seen = both[:size] + both[size:]
        xr, xi = seen[:taps], seen[taps:]
        product = jnp.concatenate([xr * hr - xi * hi, xr * hi + xi * hr], 0)
        high, low = halves(product)
        both = jnp.dot(inv, high, preferred_element_type=f32)
        mixed = both[:taps] + both[taps:]
        mixed += jnp.dot(inv[:taps], low, preferred_element_type=f32)
        result = (gate[part, :].astype(f32) * mixed).astype(jnp.bfloat16)
        out[part, :] = result
        for head in range(wide // HEAD_DIM):
            piece = result[:, head * HEAD_DIM : (head + 1) * HEAD_DIM]
            rows_of[head, part, :] = piece
            keys_of[head, :, part] = unit(piece.astype(f32)).astype(jnp.bfloat16).T
        before = now


def mix(gate, key, value, earlier, filters):
    rows, chans = gate.shape
    taps = filters.shape[1]
    heads = chans // HEAD_DIM
    wide = 2 * HEAD_DIM
    each = wide // HEAD_DIM
    forward, inverse = (jnp.asarray(matrix) for matrix in transforms(taps))
    stream = pl.BlockSpec((rows, wide), lambda i: (0, i))
    by_head = pl.BlockSpec((each, rows, HEAD_DIM), lambda i: (i, 0, 0))
    whole = lambda array: pl.BlockSpec(array.shape, lambda i: (0, 0))
    turned = pl.BlockSpec((each, HEAD_DIM, rows), lambda i: (i, 0, 0))
    per_head = jax.ShapeDtypeStruct((heads, rows, HEAD_DIM), jnp.bfloat16)
    per_head_turned = jax.ShapeDtypeStruct((heads, HEAD_DIM, rows), jnp.bfloat16)
    return pl.pallas_call(
        mix_kernel,
        grid=(chans // wide,),
        in_specs=[
            stream,
            stream,
            stream,
            pl.BlockSpec((taps, wide), lambda i: (0, i)),
            pl.BlockSpec((wide, taps), lambda i: (i, 0)),
            whole(forward),
            whole(inverse),
        ],
        out_specs=[stream, by_head, turned],
        out_shape=[jax.ShapeDtypeStruct((rows, chans), jnp.bfloat16), per_head, per_head_turned],
        compiler_params=pltpu.CompilerParams(vmem_limit_bytes=32 * MIB),
        cost_estimate=SMALL,
        name="mix",
    )(gate, key, value, earlier, filters, forward, inverse)


def softened(query, keys, rows, heat, live):
    f32 = jnp.float32
    query = unit(query).astype(jnp.bfloat16)
    scores = jnp.dot(query, keys, preferred_element_type=f32)
    weights = jnp.where(live, jnp.exp2(scores * heat), 0.0)
    total = jnp.sum(weights, axis=-1, keepdims=True)
    return jnp.dot(weights.astype(jnp.bfloat16), rows, preferred_element_type=f32) / total


def masks(offsets, first, slots, tokens, positions):
    place = lax.broadcasted_iota(jnp.int32, (tokens, positions), 1)
    return jnp.concatenate([place < offsets[first + slot] for slot in range(slots)], 0)


def attend_kernel(info, temps, queries, keys, rows, out):
    slots, tokens, _ = queries.shape
    heads, _, positions = keys.shape
    live = masks(info, info.shape[0] - AHEAD, slots, tokens, positions)

    def one(head, carry):
        cols = pl.ds(pl.multiple_of(head * HEAD_DIM, HEAD_DIM), HEAD_DIM)
        query = queries[:, :, cols].astype(jnp.float32).reshape(slots * tokens, HEAD_DIM)
        heat = temps[head] * (LOG2E / HEAD_DIM)
        done = softened(query, keys[head], rows[head], heat, live)
        out[:, :, cols] = done.reshape(slots, tokens, HEAD_DIM).astype(jnp.bfloat16)
        return carry

    lax.fori_loop(0, heads, one, 0, unroll=4)


def attend(info, temps, message, keys, rows):
    heads, positions, _ = rows.shape
    slots, tokens, _ = message.shape
    scalars = pl.BlockSpec(memory_space=pltpu.SMEM)
    vector = pl.BlockSpec(memory_space=pltpu.VMEM)
    return pl.pallas_call(
        attend_kernel,
        in_specs=[scalars, scalars, vector, vector, vector],
        out_specs=vector,
        out_shape=jax.ShapeDtypeStruct((slots, tokens, heads * HEAD_DIM), jnp.bfloat16),
        compiler_params=pltpu.CompilerParams(vmem_limit_bytes=24 * MIB),
        cost_estimate=SMALL,
        name="attend",
    )(info, temps, message, keys, rows)


def extra_kernel(info, temps, rows, *refs):
    queries, out = refs[:-1], refs[-1]
    extras, tokens, wide = queries[0].shape
    me = lax.axis_index("pos")
    share = mirrored(me, len(queries)) * (wide // HEAD_DIM)
    live = masks(info, info.shape[0] - AHEAD + HOT, extras, tokens, rows.shape[1])
    for head in range(wide // HEAD_DIM):
        cols = slice(head * HEAD_DIM, (head + 1) * HEAD_DIM)
        valued = rows[head]
        keyed = unit(valued.astype(jnp.float32)).astype(jnp.bfloat16).T
        heat = temps[share + head] * (LOG2E / HEAD_DIM)
        for step, source in enumerate(queries):
            query = source[:, :, cols].astype(jnp.float32).reshape(extras * tokens, HEAD_DIM)
            done = softened(query, keyed, valued, heat, live)
            done = done.reshape(1, extras, tokens, HEAD_DIM).astype(jnp.bfloat16)
            out[pl.ds(jnp.bitwise_xor(me, step), 1), :, :, cols] = done


def attend_extra(info, temps, rows, messages, chans):
    peers = len(messages)
    extras, tokens, _ = messages[0].shape
    wide = chans // peers
    scalars = pl.BlockSpec(memory_space=pltpu.SMEM)
    return pl.pallas_call(
        extra_kernel,
        grid=(1,),
        in_specs=[scalars, scalars, pl.BlockSpec(rows.shape, lambda i: (0, 0, 0))]
        + [pl.BlockSpec((extras, tokens, wide), lambda i: (0, 0, chans // wide))] * peers,
        out_specs=pl.BlockSpec((peers, extras, tokens, wide), lambda i: (0, 0, 0, 0)),
        out_shape=jax.ShapeDtypeStruct((peers, extras, tokens, wide), jnp.bfloat16),
        compiler_params=pltpu.CompilerParams(vmem_limit_bytes=24 * MIB),
        cost_estimate=SMALL,
        name="attend_extra",
    )(info, temps, rows, *messages)


def mirrored_number(index, peers):
    bits = peers.bit_length() - 1
    return sum(((index >> bit) & 1) << (bits - 1 - bit) for bit in range(bits))


def mirrored(index, peers):
    result = jnp.int32(0)
    for bit in range(peers.bit_length() - 1):
        result = result * 2 + jnp.bitwise_and(lax.shift_right_logical(index, bit), 1)
    return result


def pack_kernel(slots, rows, blocks, sites, queries, key, value, info, tail, *outs):
    peers = len(outs)
    windows, _, chans = queries.shape
    wide = outs[0].shape[2] - chans
    extras = HOT - slots if wide else 0
    me = lax.axis_index("pos")
    ahead = info.shape[0] - AHEAD
    hot_at = info.shape[0] - 1

    def clear(at, carry):
        info[at] = -1
        return carry

    lax.fori_loop(0, info.shape[0], clear, 0)
    for window in range(windows):
        block = blocks[window]
        count = jnp.int32(0)
        for slot in range(HOT - 1):
            count += (info[block * HOT + slot] >= 0).astype(jnp.int32)
        info[block * HOT + count] = window

        @pl.when(count == HOT - 1)
        def _():
            info[hot_at] = block

    hot = info[hot_at]

    def offset(entry):
        window = info[entry]
        site = sites[jnp.maximum(window, 0)]
        return jnp.where(window >= 0, site - rows * (entry // HOT), rows)

    for slot in range(HOT):
        info[ahead + slot] = offset(me * HOT + slot)
    for extra in range(extras):
        info[ahead + HOT + extra] = offset(hot * HOT + slots + extra)

    tail[...] = (key[...].astype(jnp.float32) * value[...].astype(jnp.float32)).astype(jnp.bfloat16)
    for step, out in enumerate(outs):
        peer = jnp.bitwise_xor(me, step)
        for slot in range(slots):
            window = jnp.maximum(info[peer * HOT + slot], 0)
            out[slot, :, :chans] = queries[window]
        if extras:
            start = pl.multiple_of(mirrored(peer, peers) * wide, wide)
        for extra in range(extras):
            window = info[hot * HOT + slots + extra]
            out[extra, :, chans:] = queries[window, :, pl.ds(start, wide)]


def pack(blocks, sites, queries, key, value, taps, peers, slots, wide):
    _, tokens, chans = queries.shape
    rows = key.shape[0]
    scalars = pl.BlockSpec(memory_space=pltpu.SMEM)
    vector = pl.BlockSpec(memory_space=pltpu.VMEM)
    last = pl.BlockSpec((taps, chans), lambda i: (rows // taps - 1, 0))
    whole = pl.BlockSpec(queries.shape, lambda i: (0, 0, 0))
    message = jax.ShapeDtypeStruct((slots, tokens, chans + wide), queries.dtype)
    info, tail, *messages = pl.pallas_call(
        functools.partial(pack_kernel, slots, rows),
        grid=(1,),
        in_specs=[scalars, scalars, whole, last, last],
        out_specs=[scalars, vector] + [vector] * peers,
        out_shape=[
            jax.ShapeDtypeStruct((peers * HOT + AHEAD,), jnp.int32),
            jax.ShapeDtypeStruct((taps, chans), jnp.bfloat16),
        ]
        + [message] * peers,
        compiler_params=pltpu.CompilerParams(vmem_limit_bytes=24 * MIB),
        cost_estimate=SMALL,
        name="pack",
    )(blocks, sites, queries, key, value)
    return info, tail, messages


def unpack_kernel(slots, peers, info, *refs):
    results, extra_results, out = refs[:peers], refs[peers:-1], refs[-1]
    me = lax.axis_index("pos")
    hot = info[info.shape[0] - 1]
    for step, source in enumerate(results):
        peer = jnp.bitwise_xor(me, step)
        for slot in range(slots):
            window = info[peer * HOT + slot]

            @pl.when(window >= 0)
            def _():
                out[pl.ds(window, 1)] = source[slot : slot + 1]

    for source in extra_results:
        _, extras, _, wide = source.shape
        for extra in range(extras):
            window = info[hot * HOT + slots + extra]
            for peer in range(peers):
                start = int(mirrored_number(peer, peers)) * wide
                out[pl.ds(window, 1), :, start : start + wide] = source[peer, extra : extra + 1]


def unpack(info, results, extra_results, windows):
    peers = len(results)
    slots, tokens, chans = results[0].shape
    scalars = pl.BlockSpec(memory_space=pltpu.SMEM)
    vector = pl.BlockSpec(memory_space=pltpu.VMEM)
    return pl.pallas_call(
        functools.partial(unpack_kernel, slots, peers),
        in_specs=[scalars] + [vector] * (peers + len(extra_results)),
        out_specs=vector,
        out_shape=jax.ShapeDtypeStruct((windows, tokens, chans), results[0].dtype),
        compiler_params=pltpu.CompilerParams(vmem_limit_bytes=24 * MIB),
        cost_estimate=SMALL,
        name="unpack",
    )(info, *results, *extra_results)


def exchanged(value, step):
    peers = lax.axis_size("pos")
    if step == 0:
        return value
    return lax.ppermute(value, "pos", [(i, i ^ step) for i in range(peers)])


def spread(rows, me, hot, peers):
    held = rows
    for bit in range(peers.bit_length() - 1):
        count = held.shape[0] // 2
        mine = jnp.bitwise_and(lax.shift_right_logical(me, bit), 1)
        sent = lax.dynamic_slice_in_dim(held, (1 - mine) * count, count, 0)
        kept = lax.dynamic_slice_in_dim(held, mine * count, count, 0)
        arrived = exchanged(sent, 1 << bit)
        have = lax.shift_right_logical(me, bit) == lax.shift_right_logical(hot, bit)
        held = jnp.where(have, kept, arrived)
    return held


def shards(gate_stream, key_stream, value_stream, filters, temps, queries, blocks, sites):
    rows, chans = gate_stream.shape
    taps = filters.shape[1]
    peers = lax.axis_size("pos")
    me = lax.axis_index("pos").astype(jnp.int32)
    windows = blocks.shape[0]
    heads = chans // HEAD_DIM
    extras = 2 if heads % peers == 0 else 0
    slots = HOT - extras
    wide = chans // peers if extras else 0

    info, tail, messages = pack(
        blocks, sites, queries, key_stream, value_stream, taps, peers, slots, wide
    )
    earlier = lax.ppermute(tail, "pos", [(i, i + 1) for i in range(peers - 1)])
    arrived = [exchanged(message, step) for step, message in enumerate(messages)]
    hyena_out, valued, keyed = mix(gate_stream, key_stream, value_stream, earlier, filters)
    results = [attend(info, temps, message, keyed, valued) for message in arrived]
    returned = [exchanged(result, step) for step, result in enumerate(results)]
    extra_results = []
    if extras:
        share = spread(valued, me, info[-1], peers)
        result = attend_extra(info, temps, share, arrived, chans)
        extra_results.append(lax.all_to_all(result, "pos", 0, 0, tiled=True))
    attended = unpack(info, returned, extra_results, windows)
    return (hyena_out, attended)


def solution(mesh):
    placed = (
        P(("groups", "pos"), "mp"),
        P(("groups", "pos"), "mp"),
        P(("groups", "pos"), "mp"),
        P("mp", None),
        P("mp"),
        P("groups", "pos", "mp"),
        P("groups"),
        P("groups"),
    )
    return jax.shard_map(
        shards,
        mesh=mesh,
        in_specs=placed,
        out_specs=(P(("groups", "pos"), "mp"), P("groups", "pos", "mp")),
        check_vma=False,
    )
```

time: 340 us -> 214 us (0.63)
  Pallas kernels: 191 us -> 57.1 us
  waiting for transfers between devices: 49.1 us -> 63.7 us
  local copies, waits for them, and re-layouts: 19 us -> 29.8 us
  starting transfers between devices: 68.3 us -> 57.5 us
  other arithmetic: 7.77 us -> 2.57 us
    pallas_call x10, Pallas kernels: 113 us -> 41.2 us  [the longest x8 34.2 us: attend(): pl.pallas_call(attend_kernel, in_specs=[scalars, scalars, vector, vector,...]
    pallas_call x1, Pallas kernels: 65.6 us -> 2.53 us  [unpack(): pl.pallas_call(functools.partial(unpack_kernel, slots, peers), in_specs=[...]
    ppermute x17, waiting for transfers between devices: 38 us -> 52.6 us  [exchanged(): return lax.ppermute(value, 'pos', [(i, i ^ step) for i in range(peers)])]
    ppermute x17, starting transfers between devices: 59.3 us -> 46.3 us  [exchanged(): return lax.ppermute(value, 'pos', [(i, i ^ step) for i in range(peers)])]
    unnamed x50 -> x62, local copies, waits for them, and re-layouts: 17.1 us -> 27.3 us
  transfers between devices with their start and end apart: 19 -> 19, of which waited for: 6 -> 5; matrix products, arithmetic and copies ran while one was open for 2% -> 1% of each run, Pallas kernels for 33% -> 18%
where the time goes in v2:
time: 214 us
  waiting for transfers between devices  63.7 us (30%)
  starting transfers between devices  57.5 us (27%)
  Pallas kernels  57.1 us (27%)
  local copies, waits for them, and re-layouts  29.8 us (14%)
  between operations  2.84 us (1%)
  other arithmetic  2.57 us (1%)
    ppermute x17, waiting for transfers between devices, exchanged(): return lax.ppermute(value, 'pos', [(i, i ^ step) for i in range(peers)])  52.6 us
    ppermute x17, starting transfers between devices, exchanged(): return lax.ppermute(value, 'pos', [(i, i ^ step) for i in range(peers)])  46.3 us
    pallas_call x8, Pallas kernels, attend(): pl.pallas_call(attend_kernel, in_specs=[scalars, scalars, vector, vector,...  34.2 us
    unnamed x62, local copies, waits for them, and re-layouts  27.3 us
    pallas_call x1, Pallas kernels, mix(): pl.pallas_call(mix_kernel, grid=(chans // wide,), in_specs=[stream, strea...  13.3 us
    ppermute x1, waiting for transfers between devices, shards(): earlier = lax.ppermute(tail, 'pos', [(i, i + 1) for i in range(peers - 1)])  11.1 us
    all_to_all x1, starting transfers between devices, shards(): extra_results.append(lax.all_to_all(result, 'pos', 0, 0, tiled=True))  6.33 us
    ppermute x1, starting transfers between devices, shards(): earlier = lax.ppermute(tail, 'pos', [(i, i + 1) for i in range(peers - 1)])  4.9 us
  transfers between devices with their start and end apart: 19, of which 5 were waited for; matrix products, arithmetic and copies ran while one was open for 1% of the time, Pallas kernels for 18%

profile of v2, /device:TPU:0, one launch (start us, length us, event | category | flops | bytes accessed | tf_op | source)
XLA Modules:
  0.0 213.5 jit_solution(1510338010961459691)
XLA Ops:
  2.2 1.6 copy-done.6
  3.8 1.6 copy-done.8
  6.7 2.5 %pack.1 = (s32[48]{0:T(128)S(1)}, bf16[128,2048]{1,0:T(8,128)(2,1)S(1)}, bf16[2,32,2304]{2,1,0:T(8,128)(2,1)S(1)}, bf16[2,32,2304]{2,1,0:T(8,128)(2,1)}, bf16[2,...) custom-call(s32[16]{0:T(128)S(1)} %copy-done.26, ...), custom_call_target="tpu_custom_call" | custom-call | flops 1000 | bytes 1000 | tf_op jit(solution)/shard_map/pack/pallas_call | solution.py:263
  9.3 4.9 %collective-permute-start = (bf16[128,2048]{1,0:T(8,128)(2,1)S(1)}, bf16[128,2048]{1,0:T(8,128)(2,1)S(1)}, u32[]{:S(2)}, u32[]{:S(2)}) collective-permute-start(bf16[128,2048]{1,0:T(8,128)(2,1)S(1)} %get-tuple-element.15), channel_id=1, source_target_pairs={{0,2},{2,4},{4,6},{6,8},{8,10},{10,12},{12,14},{1,3},{3,5},{5,7},{... | collective-permute-start | bytes 1572872 | tf_op jit(solution)/shard_map/ppermute | solution.py:352
  14.2 11.1 %collective-permute-done.earlier = bf16[128,2048]{1,0:T(8,128)(2,1)S(1)} collective-permute-done((bf16[128,2048]{1,0:T(8,128)(2,1)S(1)}, bf16[128,2048]{1,0:T(8,128)(2,1)S(1)}, u32[]{:S(2)}, u32[]{:S(2)}) %collective-permute-start) | collective-permute-done | bytes 524320 | tf_op jit(solution)/shard_map/ppermute | solution.py:352
  26.1 1.6 copy-done.5
  33.8 13.3 %mix.1 = (bf16[512,2048]{1,0:T(8,128)(2,1)}, bf16[16,512,128]{2,1,0:T(8,128)(2,1)S(1)}, bf16[16,128,512]{2,1,0:T(8,128)(2,1)S(1)}) custom-call(bf16[512,2048]{1,0:T(8,128)(2,1)S(1)} %copy-done.9, bf16[512,2048]{1,0:T(8,128)(2,1)S(1)} %copy-done.5, bf16[512,2048]{1,0:T(8,128)(2,1)S(1)} %copy-done.7, bf16[128,2048]{1,0:T(8,128)(2,1)S(1)} %copy-done.12, ...), custom_call_target="tpu_custom_call" | custom-call | flops 1000 | bytes 1000 | tf_op jit(solution)/shard_map/mix/pallas_call | solution.py:91
  48.5 2.5 %collective-permute-start.15 = (bf16[8,512,128]{2,1,0:T(8,128)(2,1)S(1)}, bf16[8,512,128]{2,1,0:T(8,128)(2,1)}, u32[]{:S(2)}, u32[]{:S(2)}) collective-permute-start(bf16[8,512,128]{2,1,0:T(8,128)(2,1)S(1)} %constant_dynamic-slice_fusion.2), channel_id=1, source_target_pairs={{0,2},{2,0},{4,6},{6,4},{8,10},{10,8},{12,14},{14,12},{1,3},{3,1},... | collective-permute-start | bytes 3145736 | tf_op jit(solution)/shard_map/ppermute | solution.py:322
  52.4 21.1 %collective-permute-done.15 = bf16[8,512,128]{2,1,0:T(8,128)(2,1)} collective-permute-done((bf16[8,512,128]{2,1,0:T(8,128)(2,1)S(1)}, bf16[8,512,128]{2,1,0:T(8,128)(2,1)}, u32[]{:S(2)}, u32[]{:S(2)}) %collective-permute-start.15) | collective-permute-done | bytes 1048608 | tf_op jit(solution)/shard_map/ppermute | solution.py:322
  75.8 2.7 %collective-permute-start.16 = (bf16[4,512,128]{2,1,0:T(8,128)(2,1)}, bf16[4,512,128]{2,1,0:T(8,128)(2,1)}, u32[]{:S(2)}, u32[]{:S(2)}) collective-permute-start(bf16[4,512,128]{2,1,0:T(8,128)(2,1)} %constant_dynamic-slice_fusion.1), channel_id=1, source_target_pairs={{0,4},{2,6},{4,0},{6,2},{8,12},{10,14},{12,8},{14,10},{1,5},{3,7},... | collective-permute-start | bytes 1572872 | tf_op jit(solution)/shard_map/ppermute | solution.py:322
  79.1 2.5 %collective-permute-start.11 = (bf16[2,32,2304]{2,1,0:T(8,128)(2,1)}, bf16[2,32,2304]{2,1,0:T(8,128)(2,1)S(1)}, u32[]{:S(2)}, u32[]{:S(2)}) collective-permute-start(bf16[2,32,2304]{2,1,0:T(8,128)(2,1)} %get-tuple-element.26), channel_id=1, source_target_pairs={{0,12},{2,14},{4,8},{6,10},{8,4},{10,6},{12,0},{14,2},{1,13},{3,15... | collective-permute-start | bytes 884744 | tf_op jit(solution)/shard_map/ppermute | solution.py:322
  81.6 2.2 %collective-permute-start.13 = (bf16[2,32,2304]{2,1,0:T(8,128)(2,1)}, bf16[2,32,2304]{2,1,0:T(8,128)(2,1)}, u32[]{:S(2)}, u32[]{:S(2)}) collective-permute-start(bf16[2,32,2304]{2,1,0:T(8,128)(2,1)} %get-tuple-element.27), channel_id=1, source_target_pairs={{0,14},{2,12},{4,10},{6,8},{8,6},{10,4},{12,2},{14,0},{1,15},{3,13... | collective-permute-start | bytes 884744 | tf_op jit(solution)/shard_map/ppermute | solution.py:322
  84.5 20.3 %collective-permute-done.16 = bf16[4,512,128]{2,1,0:T(8,128)(2,1)} collective-permute-done((bf16[4,512,128]{2,1,0:T(8,128)(2,1)}, bf16[4,512,128]{2,1,0:T(8,128)(2,1)}, u32[]{:S(2)}, u32[]{:S(2)}) %collective-permute-start.16) | collective-permute-done | bytes 524320 | tf_op jit(solution)/shard_map/ppermute | solution.py:322
  106.6 3.7 %collective-permute-start.17 = (bf16[2,512,128]{2,1,0:T(8,128)(2,1)}, bf16[2,512,128]{2,1,0:T(8,128)(2,1)}, u32[]{:S(2)}, u32[]{:S(2)}) collective-permute-start(bf16[2,512,128]{2,1,0:T(8,128)(2,1)} %constant_dynamic-slice_fusion), channel_id=1, source_target_pairs={{0,8},{2,10},{4,12},{6,14},{8,0},{10,2},{12,4},{14,6},{1,9},{3,11}... | collective-permute-start | bytes 786440 | tf_op jit(solution)/shard_map/ppermute | solution.py:322
  110.3 2.7 %collective-permute-start.5 = (bf16[2,32,2304]{2,1,0:T(8,128)(2,1)}, bf16[2,32,2304]{2,1,0:T(8,128)(2,1)}, u32[]{:S(2)}, u32[]{:S(2)}) collective-permute-start(bf16[2,32,2304]{2,1,0:T(8,128)(2,1)} %get-tuple-element.23), channel_id=1, source_target_pairs={{0,6},{2,4},{4,2},{6,0},{8,14},{10,12},{12,10},{14,8},{1,7},{3,5},... | collective-permute-start | bytes 884744 | tf_op jit(solution)/shard_map/ppermute | solution.py:322
  113.0 3.9 %collective-permute-start.9 = (bf16[2,32,2304]{2,1,0:T(8,128)(2,1)}, bf16[2,32,2304]{2,1,0:T(8,128)(2,1)}, u32[]{:S(2)}, u32[]{:S(2)}) collective-permute-start(bf16[2,32,2304]{2,1,0:T(8,128)(2,1)} %get-tuple-element.25), channel_id=1, source_target_pairs={{0,10},{2,8},{4,14},{6,12},{8,2},{10,0},{12,6},{14,4},{1,11},{3,9}... | collective-permute-start | bytes 884744 | tf_op jit(solution)/shard_map/ppermute | solution.py:322
  119.2 5.0 %attend.15 = bf16[2,32,2048]{2,1,0:T(8,128)(2,1)} custom-call(s32[48]{0:T(128)S(1)} %get-tuple-element.17.info, f32[16]{0:T(128)S(1)} %copy-done.25, bf16[2,32,2304]{2,1,0:T(8,128)(2,1)} %collective-permute-done.13.queries.refs_7_, bf16[16,128,512]{2,1,0:T(8,128)(2,1)S(1)} %copy-done.1, bf16[16,512,128]{2,1,0:T(8,128)(2,1)S(1)} %get-tuple-element.20.rows), custom_call_target="tpu_custom_call" | custom-call | flops 1000 | bytes 1000 | tf_op jit(solution)/shard_map/attend/pallas_call | solution.py:146
  124.2 4.6 %attend.14 = bf16[2,32,2048]{2,1,0:T(8,128)(2,1)} custom-call(s32[48]{0:T(128)S(1)} %get-tuple-element.17.info, f32[16]{0:T(128)S(1)} %copy-done.25, bf16[2,32,2304]{2,1,0:T(8,128)(2,1)S(1)} %collective-permute-done.11.queries.refs_6_, bf16[16,128,512]{2,1,0:T(8,128)(2,1)S(1)} %copy-done.1, bf16[16,512,128]{2,1,0:T(8,128)(2,1)S(1)} %get-tuple-element.20.rows), custom_call_target="tpu_custom_call" | custom-call | flops 1000 | bytes 1000 | tf_op jit(solution)/shard_map/attend/pallas_call | solution.py:146
  128.8 17.4 %collective-permute-start.12 = (bf16[2,32,2048]{2,1,0:T(8,128)(2,1)}, bf16[2,32,2048]{2,1,0:T(8,128)(2,1)}, u32[]{:S(2)}, u32[]{:S(2)}) collective-permute-start(bf16[2,32,2048]{2,1,0:T(8,128)(2,1)} %attend.14), channel_id=1, source_target_pairs={{0,12},{2,14},{4,8},{6,10},{8,4},{10,6},{12,0},{14,2},{1,13},{3,15... | collective-permute-start | bytes 786440 | tf_op jit(solution)/shard_map/ppermute | solution.py:322
  146.3 4.9 %collective-permute-done.7.queries.refs_4_ = bf16[2,32,2304]{2,1,0:T(8,128)(2,1)} collective-permute-done((bf16[2,32,2304]{2,1,0:T(8,128)(2,1)}, bf16[2,32,2304]{2,1,0:T(8,128)(2,1)}, u32[]{:S(2)}, u32[]{:S(2)}) %collective-permute-start.7) | collective-permute-done | bytes 294944 | tf_op jit(solution)/shard_map/ppermute | solution.py:322
  151.2 6.3 %collective-permute-done.9.queries.refs_5_ = bf16[2,32,2304]{2,1,0:T(8,128)(2,1)} collective-permute-done((bf16[2,32,2304]{2,1,0:T(8,128)(2,1)}, bf16[2,32,2304]{2,1,0:T(8,128)(2,1)}, u32[]{:S(2)}, u32[]{:S(2)}) %collective-permute-start.9) | collective-permute-done | bytes 294944 | tf_op jit(solution)/shard_map/ppermute | solution.py:322
  157.5 4.5 %attend_extra.1 = bf16[8,2,32,256]{3,2,1,0:T(8,128)(2,1)} custom-call(s32[48]{0:T(128)S(1)} %get-tuple-element.17.info, f32[16]{0:T(128)S(1)} %copy-done.25, bf16[2,512,128]{2,1,0:T(8,128)(2,1)S(1)} %dynamic-slice_select_fusion.2.rows, bf16[2,32,2304]{2,1,0:T(8,128)(2,1)S(1)} %get-tuple-element.18.queries.refs_0_, ...), custom_call_target="tpu_custom_call" | custom-call | flops 1000 | bytes 1000 | tf_op jit(solution)/shard_map/attend_extra/pallas_call | solution.py:180
  162.0 6.3 %all-to-all-start = ((bf16[8,2,32,256]{3,2,1,0:T(8,128)(2,1)}), bf16[8,2,32,256]{3,2,1,0:T(8,128)(2,1)S(1)}, u32[]{:S(2)}, u32[]{:S(2)}) async-start(bf16[8,2,32,256]{3,2,1,0:T(8,128)(2,1)} %attend_extra.1), calls=%async_computation | async-start | bytes 524288 | tf_op jit(solution)/shard_map/all_to_all | solution.py:361
  169.9 4.3 %attend.13 = bf16[2,32,2048]{2,1,0:T(8,128)(2,1)S(1)} custom-call(s32[48]{0:T(128)S(1)} %get-tuple-element.17.info, f32[16]{0:T(128)S(1)} %copy-done.25, bf16[2,32,2304]{2,1,0:T(8,128)(2,1)} %collective-permute-done.9.queries.refs_5_, bf16[16,128,512]{2,1,0:T(8,128)(2,1)S(1)} %copy-done.2, bf16[16,512,128]{2,1,0:T(8,128)(2,1)S(1)} %get-tuple-element.20.rows), custom_call_target="tpu_custom_call" | custom-call | flops 1000 | bytes 1000 | tf_op jit(solution)/shard_map/attend/pallas_call | solution.py:146
  174.2 3.9 %collective-permute-start.10 = (bf16[2,32,2048]{2,1,0:T(8,128)(2,1)S(1)}, bf16[2,32,2048]{2,1,0:T(8,128)(2,1)S(1)}, u32[]{:S(2)}, u32[]{:S(2)}) collective-permute-start(bf16[2,32,2048]{2,1,0:T(8,128)(2,1)S(1)} %attend.13), channel_id=1, source_target_pairs={{0,10},{2,8},{4,14},{6,12},{8,2},{10,0},{12,6},{14,4},{1,11},{3,9}... | collective-permute-start | bytes 786440 | tf_op jit(solution)/shard_map/ppermute | solution.py:322
  178.1 4.3 %attend.12 = bf16[2,32,2048]{2,1,0:T(8,128)(2,1)S(1)} custom-call(s32[48]{0:T(128)S(1)} %get-tuple-element.17.info, f32[16]{0:T(128)S(1)} %copy-done.25, bf16[2,32,2304]{2,1,0:T(8,128)(2,1)} %collective-permute-done.7.queries.refs_4_, bf16[16,128,512]{2,1,0:T(8,128)(2,1)S(1)} %copy-done.2, bf16[16,512,128]{2,1,0:T(8,128)(2,1)S(1)} %get-tuple-element.20.rows), custom_call_target="tpu_custom_call" | custom-call | flops 1000 | bytes 1000 | tf_op jit(solution)/shard_map/attend/pallas_call | solution.py:146
  183.1 4.3 %attend.11 = bf16[2,32,2048]{2,1,0:T(8,128)(2,1)S(1)} custom-call(s32[48]{0:T(128)S(1)} %get-tuple-element.17.info, f32[16]{0:T(128)S(1)} %copy-done.25, bf16[2,32,2304]{2,1,0:T(8,128)(2,1)} %collective-permute-done.5.queries.refs_3_, bf16[16,128,512]{2,1,0:T(8,128)(2,1)S(1)} %copy-done.2, bf16[16,512,128]{2,1,0:T(8,128)(2,1)S(1)} %get-tuple-element.20.rows), custom_call_target="tpu_custom_call" | custom-call | flops 1000 | bytes 1000 | tf_op jit(solution)/shard_map/attend/pallas_call | solution.py:146
  188.9 3.9 %attend.10 = bf16[2,32,2048]{2,1,0:T(8,128)(2,1)S(1)} custom-call(s32[48]{0:T(128)S(1)} %get-tuple-element.17.info, f32[16]{0:T(128)S(1)} %copy-done.25, bf16[2,32,2304]{2,1,0:T(8,128)(2,1)S(1)} %collective-permute-done.3.queries.refs_2_, bf16[16,128,512]{2,1,0:T(8,128)(2,1)S(1)} %copy-done.2, bf16[16,512,128]{2,1,0:T(8,128)(2,1)S(1)} %get-tuple-element.20.rows), custom_call_target="tpu_custom_call" | custom-call | flops 1000 | bytes 1000 | tf_op jit(solution)/shard_map/attend/pallas_call | solution.py:146
  192.8 3.9 %attend.9 = bf16[2,32,2048]{2,1,0:T(8,128)(2,1)S(1)} custom-call(s32[48]{0:T(128)S(1)} %get-tuple-element.17.info, f32[16]{0:T(128)S(1)} %copy-done.25, bf16[2,32,2304]{2,1,0:T(8,128)(2,1)S(1)} %collective-permute-done.1.queries.refs_1_, bf16[16,128,512]{2,1,0:T(8,128)(2,1)S(1)} %copy-done.2, bf16[16,512,128]{2,1,0:T(8,128)(2,1)S(1)} %get-tuple-element.20.rows), custom_call_target="tpu_custom_call" | custom-call | flops 1000 | bytes 1000 | tf_op jit(solution)/shard_map/attend/pallas_call | solution.py:146
  196.8 2.0 collective-permute-start.2
  198.8 3.9 %attend.8.refs_0_ = bf16[2,32,2048]{2,1,0:T(8,128)(2,1)S(1)} custom-call(s32[48]{0:T(128)S(1)} %get-tuple-element.17.info, f32[16]{0:T(128)S(1)} %copy-done.25, bf16[2,32,2304]{2,1,0:T(8,128)(2,1)S(1)} %get-tuple-element.18.queries.refs_0_, bf16[16,128,512]{2,1,0:T(8,128)(2,1)S(1)} %copy-done.3, bf16[16,512,128]{2,1,0:T(8,128)(2,1)S(1)} %get-tuple-element.20.rows), custom_call_target="tpu_custom_call" | custom-call | flops 1000 | bytes 1000 | tf_op jit(solution)/shard_map/attend/pallas_call | solution.py:146
  211.0 2.5 %unpack.1 = bf16[16,32,2048]{2,1,0:T(8,128)(2,1)} custom-call(s32[48]{0:T(128)S(1)} %get-tuple-element.17.info, bf16[2,32,2048]{2,1,0:T(8,128)(2,1)S(1)} %attend.8.refs_0_, bf16[2,32,2048]{2,1,0:T(8,128)(2,1)S(1)} %copy-done.23, bf16[2,32,2048]{2,1,0:T(8,128)(2,1)S(1)} %copy-done.21, bf16[2,32,2048]{2,1,0:T(8,128)(2,1)S(1)} %copy-done.18, ...), custom_call_target="tpu_custom_call" | custom-call | flops 1000 | bytes 1000 | tf_op jit(solution)/shard_map/unpack/pallas_call | solution.py:307
  (87 shorter events, 30.5 us)
Async XLA Ops:
  0.6 1.6 copy-start.4
  2.2 1.6 copy-start.6
  3.8 1.6 copy-start.8
  6.7 19.4 %copy-start.10 = (f32[2048,128]{1,0:T(8,128)S(1)}, f32[2048,128]{1,0:T(8,128)}, u32[]{:S(2)}) copy-start(f32[2048,128]{1,0:T(8,128)} %filters.1) | copy-start | bytes 3145732
  9.3 16.0 %collective-permute-start = (bf16[128,2048]{1,0:T(8,128)(2,1)S(1)}, bf16[128,2048]{1,0:T(8,128)(2,1)S(1)}, u32[]{:S(2)}, u32[]{:S(2)}) collective-permute-start(bf16[128,2048]{1,0:T(8,128)(2,1)S(1)} %get-tuple-element.15), channel_id=1, source_target_pairs={{0,2},{2,4},{4,6},{6,8},{8,10},{10,12},{12,14},{1,3},{3,5},{5,7},{... | collective-permute-start | bytes 1572872 | tf_op jit(solution)/shard_map/ppermute | solution.py:352
  26.1 1.6 copy-start.5
  27.7 1.6 copy-start.7
  29.3 1.6 copy-start.9
  48.5 24.9 %collective-permute-start.15 = (bf16[8,512,128]{2,1,0:T(8,128)(2,1)S(1)}, bf16[8,512,128]{2,1,0:T(8,128)(2,1)}, u32[]{:S(2)}, u32[]{:S(2)}) collective-permute-start(bf16[8,512,128]{2,1,0:T(8,128)(2,1)S(1)} %constant_dynamic-slice_fusion.2), channel_id=1, source_target_pairs={{0,2},{2,0},{4,6},{6,4},{8,10},{10,8},{12,14},{14,12},{1,3},{3,1},... | collective-permute-start | bytes 3145736 | tf_op jit(solution)/shard_map/ppermute | solution.py:322
  74.9 8.9 %copy-start.28 = (bf16[8,512,128]{2,1,0:T(8,128)(2,1)}, bf16[8,512,128]{2,1,0:T(8,128)(2,1)S(1)}, u32[]{:S(2)}) copy-start(bf16[8,512,128]{2,1,0:T(8,128)(2,1)S(1)} %dynamic-slice_select_fusion) | copy-start | bytes 3145732
  74.9 42.7 %copy-start.25 = (f32[16]{0:T(128)S(1)}, f32[16]{0:T(128)}, u32[]{:S(2)}) copy-start(f32[16]{0:T(128)} %temps.17) | copy-start | bytes 196
  75.8 28.9 %collective-permute-start.16 = (bf16[4,512,128]{2,1,0:T(8,128)(2,1)}, bf16[4,512,128]{2,1,0:T(8,128)(2,1)}, u32[]{:S(2)}, u32[]{:S(2)}) collective-permute-start(bf16[4,512,128]{2,1,0:T(8,128)(2,1)} %constant_dynamic-slice_fusion.1), channel_id=1, source_target_pairs={{0,4},{2,6},{4,0},{6,2},{8,12},{10,14},{12,8},{14,10},{1,5},{3,7},... | collective-permute-start | bytes 1572872 | tf_op jit(solution)/shard_map/ppermute | solution.py:322
  78.5 31.8 %collective-permute-start.1 = (bf16[2,32,2304]{2,1,0:T(8,128)(2,1)}, bf16[2,32,2304]{2,1,0:T(8,128)(2,1)S(1)}, u32[]{:S(2)}, u32[]{:S(2)}) collective-permute-start(bf16[2,32,2304]{2,1,0:T(8,128)(2,1)} %get-tuple-element.21), channel_id=1, source_target_pairs={{0,2},{2,0},{4,6},{6,4},{8,10},{10,8},{12,14},{14,12},{1,3},{3,1},... | collective-permute-start | bytes 884744 | tf_op jit(solution)/shard_map/ppermute | solution.py:322
  79.1 33.9 %collective-permute-start.11 = (bf16[2,32,2304]{2,1,0:T(8,128)(2,1)}, bf16[2,32,2304]{2,1,0:T(8,128)(2,1)S(1)}, u32[]{:S(2)}, u32[]{:S(2)}) collective-permute-start(bf16[2,32,2304]{2,1,0:T(8,128)(2,1)} %get-tuple-element.26), channel_id=1, source_target_pairs={{0,12},{2,14},{4,8},{6,10},{8,4},{10,6},{12,0},{14,2},{1,13},{3,15... | collective-permute-start | bytes 884744 | tf_op jit(solution)/shard_map/ppermute | solution.py:322
  81.6 31.4 %collective-permute-start.13 = (bf16[2,32,2304]{2,1,0:T(8,128)(2,1)}, bf16[2,32,2304]{2,1,0:T(8,128)(2,1)}, u32[]{:S(2)}, u32[]{:S(2)}) collective-permute-start(bf16[2,32,2304]{2,1,0:T(8,128)(2,1)} %get-tuple-element.27), channel_id=1, source_target_pairs={{0,14},{2,12},{4,10},{6,8},{8,6},{10,4},{12,2},{14,0},{1,15},{3,13... | collective-permute-start | bytes 884744 | tf_op jit(solution)/shard_map/ppermute | solution.py:322
  83.8 45.0 %collective-permute-start.3 = (bf16[2,32,2304]{2,1,0:T(8,128)(2,1)}, bf16[2,32,2304]{2,1,0:T(8,128)(2,1)S(1)}, u32[]{:S(2)}, u32[]{:S(2)}) collective-permute-start(bf16[2,32,2304]{2,1,0:T(8,128)(2,1)} %get-tuple-element.22), channel_id=1, source_target_pairs={{0,4},{2,6},{4,0},{6,2},{8,12},{10,14},{12,8},{14,10},{1,5},{3,7},... | collective-permute-start | bytes 884744 | tf_op jit(solution)/shard_map/ppermute | solution.py:322
  105.8 7.1 %copy-start.29 = (bf16[4,512,128]{2,1,0:T(8,128)(2,1)}, bf16[4,512,128]{2,1,0:T(8,128)(2,1)S(1)}, u32[]{:S(2)}) copy-start(bf16[4,512,128]{2,1,0:T(8,128)(2,1)S(1)} %dynamic-slice_select_fusion.1) | copy-start | bytes 1572868
  106.6 22.1 %collective-permute-start.17 = (bf16[2,512,128]{2,1,0:T(8,128)(2,1)}, bf16[2,512,128]{2,1,0:T(8,128)(2,1)}, u32[]{:S(2)}, u32[]{:S(2)}) collective-permute-start(bf16[2,512,128]{2,1,0:T(8,128)(2,1)} %constant_dynamic-slice_fusion), channel_id=1, source_target_pairs={{0,8},{2,10},{4,12},{6,14},{8,0},{10,2},{12,4},{14,6},{1,9},{3,11}... | collective-permute-start | bytes 786440 | tf_op jit(solution)/shard_map/ppermute | solution.py:322
  110.3 35.9 %collective-permute-start.5 = (bf16[2,32,2304]{2,1,0:T(8,128)(2,1)}, bf16[2,32,2304]{2,1,0:T(8,128)(2,1)}, u32[]{:S(2)}, u32[]{:S(2)}) collective-permute-start(bf16[2,32,2304]{2,1,0:T(8,128)(2,1)} %get-tuple-element.23), channel_id=1, source_target_pairs={{0,6},{2,4},{4,2},{6,0},{8,14},{10,12},{12,10},{14,8},{1,7},{3,5},... | collective-permute-start | bytes 884744 | tf_op jit(solution)/shard_map/ppermute | solution.py:322
  113.0 38.2 %collective-permute-start.7 = (bf16[2,32,2304]{2,1,0:T(8,128)(2,1)}, bf16[2,32,2304]{2,1,0:T(8,128)(2,1)}, u32[]{:S(2)}, u32[]{:S(2)}) collective-permute-start(bf16[2,32,2304]{2,1,0:T(8,128)(2,1)} %get-tuple-element.24), channel_id=1, source_target_pairs={{0,8},{2,10},{4,12},{6,14},{8,0},{10,2},{12,4},{14,6},{1,9},{3,11}... | collective-permute-start | bytes 884744 | tf_op jit(solution)/shard_map/ppermute | solution.py:322
  113.0 44.5 %collective-permute-start.9 = (bf16[2,32,2304]{2,1,0:T(8,128)(2,1)}, bf16[2,32,2304]{2,1,0:T(8,128)(2,1)}, u32[]{:S(2)}, u32[]{:S(2)}) collective-permute-start(bf16[2,32,2304]{2,1,0:T(8,128)(2,1)} %get-tuple-element.25), channel_id=1, source_target_pairs={{0,10},{2,8},{4,14},{6,12},{8,2},{10,0},{12,6},{14,4},{1,11},{3,9}... | collective-permute-start | bytes 884744 | tf_op jit(solution)/shard_map/ppermute | solution.py:322
  117.6 1.6 copy-start.1
  124.2 22.0 %copy-start.30 = (bf16[4,512,128]{2,1,0:T(8,128)(2,1)S(1)}, bf16[4,512,128]{2,1,0:T(8,128)(2,1)}, u32[]{:S(2)}) copy-start(bf16[4,512,128]{2,1,0:T(8,128)(2,1)} %copy-done.29) | copy-start | bytes 1572868
  128.8 67.9 %collective-permute-start.14 = (bf16[2,32,2048]{2,1,0:T(8,128)(2,1)}, bf16[2,32,2048]{2,1,0:T(8,128)(2,1)S(1)}, u32[]{:S(2)}, u32[]{:S(2)}) collective-permute-start(bf16[2,32,2048]{2,1,0:T(8,128)(2,1)} %attend.15), channel_id=1, source_target_pairs={{0,14},{2,12},{4,10},{6,8},{8,6},{10,4},{12,2},{14,0},{1,15},{3,13... | collective-permute-start | bytes 786440 | tf_op jit(solution)/shard_map/ppermute | solution.py:322
  128.8 68.0 %collective-permute-start.12 = (bf16[2,32,2048]{2,1,0:T(8,128)(2,1)}, bf16[2,32,2048]{2,1,0:T(8,128)(2,1)}, u32[]{:S(2)}, u32[]{:S(2)}) collective-permute-start(bf16[2,32,2048]{2,1,0:T(8,128)(2,1)} %attend.14), channel_id=1, source_target_pairs={{0,12},{2,14},{4,8},{6,10},{8,4},{10,6},{12,0},{14,2},{1,13},{3,15... | collective-permute-start | bytes 786440 | tf_op jit(solution)/shard_map/ppermute | solution.py:322
  162.0 44.3 %all-to-all-start = ((bf16[8,2,32,256]{3,2,1,0:T(8,128)(2,1)}), bf16[8,2,32,256]{3,2,1,0:T(8,128)(2,1)S(1)}, u32[]{:S(2)}, u32[]{:S(2)}) async-start(bf16[8,2,32,256]{3,2,1,0:T(8,128)(2,1)} %attend_extra.1), calls=%async_computation | async-start | bytes 524288 | tf_op jit(solution)/shard_map/all_to_all | solution.py:361
  174.2 28.4 %collective-permute-start.10 = (bf16[2,32,2048]{2,1,0:T(8,128)(2,1)S(1)}, bf16[2,32,2048]{2,1,0:T(8,128)(2,1)S(1)}, u32[]{:S(2)}, u32[]{:S(2)}) collective-permute-start(bf16[2,32,2048]{2,1,0:T(8,128)(2,1)S(1)} %attend.13), channel_id=1, source_target_pairs={{0,10},{2,8},{4,14},{6,12},{8,2},{10,0},{12,6},{14,4},{1,11},{3,9}... | collective-permute-start | bytes 786440 | tf_op jit(solution)/shard_map/ppermute | solution.py:322
  182.4 21.0 %collective-permute-start.8 = (bf16[2,32,2048]{2,1,0:T(8,128)(2,1)S(1)}, bf16[2,32,2048]{2,1,0:T(8,128)(2,1)S(1)}, u32[]{:S(2)}, u32[]{:S(2)}) collective-permute-start(bf16[2,32,2048]{2,1,0:T(8,128)(2,1)S(1)} %attend.12), channel_id=1, source_target_pairs={{0,8},{2,10},{4,12},{6,14},{8,0},{10,2},{12,4},{14,6},{1,9},{3,11}... | collective-permute-start | bytes 786440 | tf_op jit(solution)/shard_map/ppermute | solution.py:322
  187.4 16.8 %collective-permute-start.6 = (bf16[2,32,2048]{2,1,0:T(8,128)(2,1)S(1)}, bf16[2,32,2048]{2,1,0:T(8,128)(2,1)S(1)}, u32[]{:S(2)}, u32[]{:S(2)}) collective-permute-start(bf16[2,32,2048]{2,1,0:T(8,128)(2,1)S(1)} %attend.11), channel_id=1, source_target_pairs={{0,6},{2,4},{4,2},{6,0},{8,14},{10,12},{12,10},{14,8},{1,7},{3,5},... | collective-permute-start | bytes 786440 | tf_op jit(solution)/shard_map/ppermute | solution.py:322
  192.8 6.0 %copy-start.3 = (bf16[16,128,512]{2,1,0:T(8,128)(2,1)S(1)}, bf16[16,128,512]{2,1,0:T(8,128)(2,1)}, u32[]{:S(2)}) copy-start(bf16[16,128,512]{2,1,0:T(8,128)(2,1)} %copy-done) | copy-start | bytes 6291460
  196.7 8.1 %collective-permute-start.4 = (bf16[2,32,2048]{2,1,0:T(8,128)(2,1)S(1)}, bf16[2,32,2048]{2,1,0:T(8,128)(2,1)S(1)}, u32[]{:S(2)}, u32[]{:S(2)}) collective-permute-start(bf16[2,32,2048]{2,1,0:T(8,128)(2,1)S(1)} %attend.10), channel_id=1, source_target_pairs={{0,4},{2,6},{4,0},{6,2},{8,12},{10,14},{12,8},{14,10},{1,5},{3,7},... | collective-permute-start | bytes 786440 | tf_op jit(solution)/shard_map/ppermute | solution.py:322
  196.8 8.8 %collective-permute-start.2 = (bf16[2,32,2048]{2,1,0:T(8,128)(2,1)S(1)}, bf16[2,32,2048]{2,1,0:T(8,128)(2,1)S(1)}, u32[]{:S(2)}, u32[]{:S(2)}) collective-permute-start(bf16[2,32,2048]{2,1,0:T(8,128)(2,1)S(1)} %attend.9), channel_id=1, source_target_pairs={{0,2},{2,0},{4,6},{6,4},{8,10},{10,8},{12,14},{14,12},{1,3},{3,1},... | collective-permute-start | bytes 786440 | tf_op jit(solution)/shard_map/ppermute | solution.py:322
  (18 other events, 16.2 us)

commit v3 on v2

v3 whole, which is shorter than its diff:
```python
import functools

import jax
import jax.numpy as jnp
import numpy as np
from jax import lax
from jax.experimental import pallas as pl
from jax.experimental.pallas import tpu as pltpu
from jax.sharding import PartitionSpec as P

HEAD_DIM = 128
HOT = 4
EPS = 1e-06
LOG2E = 1.4426950408889634
MIB = 1 << 20
AHEAD = 16
CUT_FLOPS = 2 << 30
ATTEND_FLOPS = 20 << 30
MIX_FLOPS = 100 << 30
PACK_FLOPS = 20 << 30


def cost(flops):
    return pl.CostEstimate(flops=flops, bytes_accessed=1000, transcendentals=0)


def halves(array):
    high = array.astype(jnp.bfloat16)
    low = (array - high.astype(jnp.float32)).astype(jnp.bfloat16)
    return high, low


def transforms(taps):
    size = 2 * taps
    odd = 2 * np.arange(taps) + 1
    angle = np.pi / size * ((odd[:, None] * np.arange(size)[None, :]) % (2 * size))
    forward = np.concatenate([np.cos(angle), -np.sin(angle)], 0)
    inverse = forward.T[taps:] * (2.0 / size)
    out = []
    for matrix in (forward, inverse):
        high = matrix.astype(jnp.bfloat16)
        low = (matrix - high.astype(np.float64)).astype(jnp.bfloat16)
        out.append(np.concatenate([high, low], 0))
    return out


def unit(block):
    return block * lax.rsqrt(jnp.mean(block * block, axis=-1, keepdims=True) + EPS)


def mix_kernel(gate, key, value, earlier, filters, forward, inverse, out, rows_of, keys_of):
    rows, wide = gate.shape
    taps = filters.shape[1]
    size = 2 * taps
    f32 = jnp.float32
    fwd = forward[...]
    inv = inverse[...]
    high, low = halves(filters[...])
    across = (((1,), (1,)), ((), ()))
    both = lax.dot_general(fwd[:, :taps], high, across, preferred_element_type=f32)
    spectrum = both[:size] + both[size:]
    spectrum += lax.dot_general(fwd[:size, :taps], low, across, preferred_element_type=f32)
    hr, hi = spectrum[:taps], spectrum[taps:]
    before = earlier[...]
    for start in range(0, rows, taps):
        part = slice(start, start + taps)
        now = (key[part, :].astype(f32) * value[part, :].astype(f32)).astype(jnp.bfloat16)
        both = jnp.dot(fwd, jnp.concatenate([before, now], 0), preferred_element_type=f32)
        seen = both[:size] + both[size:]
        xr, xi = seen[:taps], seen[taps:]
        product = jnp.concatenate([xr * hr - xi * hi, xr * hi + xi * hr], 0)
        high, low = halves(product)
        both = jnp.dot(inv, high, preferred_element_type=f32)
        mixed = both[:taps] + both[taps:]
        mixed += jnp.dot(inv[:taps], low, preferred_element_type=f32)
        result = (gate[part, :].astype(f32) * mixed).astype(jnp.bfloat16)
        out[part, :] = result
        for head in range(wide // HEAD_DIM):
            piece = result[:, head * HEAD_DIM : (head + 1) * HEAD_DIM]
            rows_of[head, part, :] = piece
            keys_of[head, :, part] = unit(piece.astype(f32)).astype(jnp.bfloat16).T
        before = now


def mix(gate, key, value, earlier, filters):
    rows, chans = gate.shape
    taps = filters.shape[1]
    heads = chans // HEAD_DIM
    wide = 2 * HEAD_DIM
    each = wide // HEAD_DIM
    forward, inverse = (jnp.asarray(matrix) for matrix in transforms(taps))
    stream = pl.BlockSpec((rows, wide), lambda i: (0, i))
    by_head = pl.BlockSpec((each, rows, HEAD_DIM), lambda i: (i, 0, 0))
    whole = lambda array: pl.BlockSpec(array.shape, lambda i: (0, 0))
    turned = pl.BlockSpec((each, HEAD_DIM, rows), lambda i: (i, 0, 0))
    per_head = jax.ShapeDtypeStruct((heads, rows, HEAD_DIM), jnp.bfloat16)
    per_head_turned = jax.ShapeDtypeStruct((heads, HEAD_DIM, rows), jnp.bfloat16)
    return pl.pallas_call(
        mix_kernel,
        grid=(chans // wide,),
        in_specs=[
            stream,
            stream,
            stream,
            pl.BlockSpec((taps, wide), lambda i: (0, i)),
            pl.BlockSpec((wide, taps), lambda i: (i, 0)),
            whole(forward),
            whole(inverse),
        ],
        out_specs=[stream, by_head, turned],
        out_shape=[jax.ShapeDtypeStruct((rows, chans), jnp.bfloat16), per_head, per_head_turned],
        compiler_params=pltpu.CompilerParams(vmem_limit_bytes=48 * MIB),
        cost_estimate=cost(MIX_FLOPS),
        name="mix",
    )(gate, key, value, earlier, filters, forward, inverse)


def softened(query, keys, rows, heat, live):
    f32 = jnp.float32
    query = unit(query).astype(jnp.bfloat16)
    scores = jnp.dot(query, keys, preferred_element_type=f32)
    weights = jnp.where(live, jnp.exp2(scores * heat), 0.0)
    total = jnp.sum(weights, axis=-1, keepdims=True)
    return jnp.dot(weights.astype(jnp.bfloat16), rows, preferred_element_type=f32) / total


def masks(offsets, first, slots, tokens, positions):
    place = lax.broadcasted_iota(jnp.int32, (tokens, positions), 1)
    return jnp.concatenate([place < offsets[first + slot] for slot in range(slots)], 0)


def attend_kernel(count, info, temps, keys, rows, _, *refs):
    sources, outs = refs[:count], refs[count:]
    heads, _, positions = keys.shape
    slots, tokens, _ = sources[0].shape[-3:]
    places = []
    for source, out in zip(sources, outs):
        whole = len(source.shape) == 3
        places += [(source, out, () if whole else (at,)) for at in range(1 if whole else source.shape[0])]
    each = slots * tokens
    live = masks(info, info.shape[0] - AHEAD, slots, tokens, positions)
    live = jnp.concatenate([live] * len(places), 0)
    every = (slice(None), slice(None))

    def one(head, carry):
        cols = pl.ds(pl.multiple_of(head * HEAD_DIM, HEAD_DIM), HEAD_DIM)
        query = [source[at + every + (cols,)].astype(jnp.float32) for source, _, at in places]
        query = [part.reshape(each, HEAD_DIM) for part in query]
        heat = temps[head] * (LOG2E / HEAD_DIM)
        done = softened(jnp.concatenate(query, 0), keys[head], rows[head], heat, live)
        for place, (_, out, at) in enumerate(places):
            part = done[place * each : (place + 1) * each].reshape(slots, tokens, HEAD_DIM)
            out[at + every + (cols,)] = part.astype(jnp.bfloat16)
        return carry

    lax.fori_loop(0, heads, one, 0, unroll=4 if len(places) <= 4 else 1)


def attend(info, temps, keys, rows, after, messages):
    chans = rows.shape[0] * HEAD_DIM
    scalars = pl.BlockSpec(memory_space=pltpu.SMEM)
    vector = pl.BlockSpec(memory_space=pltpu.VMEM)
    anywhere = pl.BlockSpec(memory_space=pl.ANY)
    return pl.pallas_call(
        functools.partial(attend_kernel, len(messages)),
        in_specs=[scalars, scalars, vector, vector, anywhere] + [vector] * len(messages),
        out_specs=[vector] * len(messages),
        out_shape=[
            jax.ShapeDtypeStruct(message.shape[:-1] + (chans,), jnp.bfloat16)
            for message in messages
        ],
        compiler_params=pltpu.CompilerParams(vmem_limit_bytes=16 * MIB),
        cost_estimate=cost(ATTEND_FLOPS),
        name="attend",
    )(info, temps, keys, rows, after, *messages)


def cut_kernel(bit, info, held, *refs):
    sent, kept = refs[-2:]
    me = lax.axis_index("pos")
    count = sent.shape[0]
    mine = jnp.bitwise_and(lax.shift_right_logical(me, bit), 1)
    if bit:
        hot = info[info.shape[0] - 1]
        before = bit - 1
        have = lax.shift_right_logical(me, before) == lax.shift_right_logical(hot, before)
        arrived = refs[0]

        @pl.when(have)
        def _():
            sent[...] = held[pl.ds((1 - mine) * count, count)]
            kept[...] = held[pl.ds(mine * count, count)]

        @pl.when(jnp.logical_not(have))
        def _():
            sent[...] = arrived[pl.ds((1 - mine) * count, count)]
            kept[...] = arrived[pl.ds(mine * count, count)]
    else:
        sent[...] = held[pl.ds((1 - mine) * count, count)]
        kept[...] = held[pl.ds(mine * count, count)]


def cut(bit, info, held, arrived, after):
    count, positions, wide = held.shape
    half = jax.ShapeDtypeStruct((count // 2, positions, wide), held.dtype)
    vector = pl.BlockSpec(memory_space=pltpu.VMEM)
    return pl.pallas_call(
        functools.partial(cut_kernel, bit),
        in_specs=[pl.BlockSpec(memory_space=pltpu.SMEM), vector]
        + [vector] * len(arrived)
        + [pl.BlockSpec(memory_space=pl.ANY)],
        out_specs=[vector] * 2,
        out_shape=[half] * 2,
        compiler_params=pltpu.CompilerParams(vmem_limit_bytes=16 * MIB),
        cost_estimate=cost(CUT_FLOPS),
        name="cut",
    )(info, held, *arrived, after)


def extra_kernel(info, temps, kept, fresh, _, near, *refs):
    far, out = refs[:-1], refs[-1]
    half, extras, tokens, wide = near.shape
    peers = 2 * half
    me = lax.axis_index("pos")
    share = mirrored(me, peers) * (wide // HEAD_DIM)
    live = masks(info, info.shape[0] - AHEAD + HOT, extras, tokens, kept.shape[1])
    before = peers.bit_length() - 2
    hot = info[info.shape[0] - 1]
    have = lax.shift_right_logical(me, before) == lax.shift_right_logical(hot, before)
    base = jnp.bitwise_and(me, half)
    sources = [(base + at, near[at]) for at in range(half)]
    sources += [(jnp.bitwise_xor(me, half + at), source[...]) for at, source in enumerate(far)]
    for head in range(wide // HEAD_DIM):
        cols = slice(head * HEAD_DIM, (head + 1) * HEAD_DIM)
        valued = jnp.where(have, kept[head], fresh[head])
        keyed = unit(valued.astype(jnp.float32)).astype(jnp.bfloat16).T
        heat = temps[share + head] * (LOG2E / HEAD_DIM)
        for peer, source in sources:
            query = source[:, :, cols].astype(jnp.float32)
            query = query.reshape(extras * tokens, HEAD_DIM)
            done = softened(query, keyed, valued, heat, live)
            done = done.reshape(1, extras, tokens, HEAD_DIM).astype(jnp.bfloat16)
            out[pl.ds(peer, 1), :, :, cols] = done


def attend_extra(info, temps, kept, fresh, after, near, far, wide):
    half, extras, tokens, held = near.shape
    scalars = pl.BlockSpec(memory_space=pltpu.SMEM)
    rows = pl.BlockSpec(kept.shape, lambda i: (0, 0, 0))
    return pl.pallas_call(
        extra_kernel,
        grid=(1,),
        in_specs=[
            scalars,
            scalars,
            rows,
            rows,
            pl.BlockSpec(memory_space=pl.ANY),
            pl.BlockSpec((half, extras, tokens, wide), lambda i: (0, 0, 0, held // wide - 1)),
        ]
        + [pl.BlockSpec((extras, tokens, wide), lambda i: (0, 0, held // wide - 1))] * half,
        out_specs=pl.BlockSpec((2 * half, extras, tokens, wide), lambda i: (0, 0, 0, 0)),
        out_shape=jax.ShapeDtypeStruct((2 * half, extras, tokens, wide), jnp.bfloat16),
        compiler_params=pltpu.CompilerParams(vmem_limit_bytes=16 * MIB),
        cost_estimate=cost(ATTEND_FLOPS),
        name="attend_extra",
    )(info, temps, kept, fresh, after, near, *far)


def mirrored_number(index, peers):
    bits = peers.bit_length() - 1
    return sum(((index >> bit) & 1) << (bits - 1 - bit) for bit in range(bits))


def mirrored(index, peers):
    result = jnp.int32(0)
    for bit in range(peers.bit_length() - 1):
        result = result * 2 + jnp.bitwise_and(lax.shift_right_logical(index, bit), 1)
    return result


def route(info, peers, slots, extras, rows, blocks, sites):
    me = lax.axis_index("pos")
    ahead = info.shape[0] - AHEAD
    hot_at = info.shape[0] - 1

    def clear(at, carry):
        info[at] = -1
        return carry

    lax.fori_loop(0, info.shape[0], clear, 0)
    for window in range(blocks.shape[0]):
        block = blocks[window]
        count = jnp.int32(0)
        for slot in range(HOT - 1):
            count += (info[block * HOT + slot] >= 0).astype(jnp.int32)
        info[block * HOT + count] = window

        @pl.when(count == HOT - 1)
        def _():
            info[hot_at] = block

    hot = info[hot_at]

    def offset(entry):
        window = info[entry]
        site = sites[jnp.maximum(window, 0)]
        return jnp.where(window >= 0, site - rows * (entry // HOT), rows)

    for slot in range(HOT):
        info[ahead + slot] = offset(me * HOT + slot)
    for extra in range(extras):
        info[ahead + HOT + extra] = offset(hot * HOT + slots + extra)


def deliver(info, queries, targets, sems, slots, extras, peers):
    chans = queries.shape[2]
    hot = info[info.shape[0] - 1]
    copies = []
    for peer, out in targets:
        held = out.shape[2]
        for slot in range(slots):
            window = jnp.maximum(info[peer * HOT + slot], 0)
            copies.append((queries.at[window], out.at[slot, :, pl.ds(0, chans)]))
        for extra in range(extras):
            wide = held - chans
            share = pl.multiple_of(mirrored(peer, peers) * wide, wide)
            window = info[hot * HOT + slots + extra]
            target = out.at[extra, :, pl.ds(chans, wide)]
            copies.append((queries.at[window, :, pl.ds(share, wide)], target))
    copies = [pltpu.make_async_copy(*pair, sems.at[at]) for at, pair in enumerate(copies)]
    for copy in copies:
        copy.start()
    for copy in copies:
        copy.wait()


def near_kernel(extras, rows, blocks, sites, queries, _, info, near, sems, blocks_held, sites_held, pair):
    half, slots, _, _ = near.shape
    loads = [
        pltpu.make_async_copy(blocks, blocks_held, pair.at[0]),
        pltpu.make_async_copy(sites, sites_held, pair.at[1]),
    ]
    for load in loads:
        load.start()
    for load in loads:
        load.wait()
    route(info, 2 * half, slots, extras, rows, blocks_held, sites_held)
    base = jnp.bitwise_and(lax.axis_index("pos"), half)
    targets = [(base + at, near.at[at]) for at in range(half)]
    deliver(info, queries, targets, sems, slots, extras, 2 * half)


def far_kernel(extras, info, queries, _, *refs):
    far, sems = refs[:-1], refs[-1]
    half = len(far)
    me = lax.axis_index("pos")
    targets = [(jnp.bitwise_xor(me, half + at), out) for at, out in enumerate(far)]
    deliver(info, queries, targets, sems, far[0].shape[0], extras, 2 * half)


def pack(blocks, sites, queries, tail, rows, peers, slots):
    windows, tokens, chans = queries.shape
    extras = HOT - slots
    half = peers // 2
    held = chans + (chans // peers if extras else 0)
    scalars = pl.BlockSpec(memory_space=pltpu.SMEM)
    vector = pl.BlockSpec(memory_space=pltpu.VMEM)
    anywhere = pl.BlockSpec(memory_space=pl.ANY)
    hbm = pl.BlockSpec(memory_space=pltpu.HBM)
    message = jax.ShapeDtypeStruct((slots, tokens, held), queries.dtype)
    params = dict(
        compiler_params=pltpu.CompilerParams(vmem_limit_bytes=16 * MIB),
        cost_estimate=cost(PACK_FLOPS),
    )
    sems = pltpu.SemaphoreType.DMA((half * (slots + extras),))
    info, near = pl.pallas_call(
        functools.partial(near_kernel, extras, rows),
        in_specs=[hbm, hbm, hbm, anywhere],
        out_specs=[scalars, vector],
        out_shape=[
            jax.ShapeDtypeStruct((peers * HOT + AHEAD,), jnp.int32),
            jax.ShapeDtypeStruct((half,) + message.shape, queries.dtype),
        ],
        scratch_shapes=[
            sems,
            pltpu.SMEM((windows,), jnp.int32),
            pltpu.SMEM((windows,), jnp.int32),
            pltpu.SemaphoreType.DMA((2,)),
        ],
        name="pack_near",
        **params,
    )(blocks, sites, queries, tail)
    far = pl.pallas_call(
        functools.partial(far_kernel, extras),
        in_specs=[scalars, hbm, anywhere],
        out_specs=[vector] * half,
        out_shape=[message] * half,
        scratch_shapes=[sems],
        name="pack_far",
        **params,
    )(info, queries, near)
    return info, near, far


def unpack_kernel(steps, info, *refs):
    results, out, sems = refs[: len(steps)], refs[-2], refs[-1]
    me = lax.axis_index("pos")
    pieces = []
    for step, result in zip(steps, results):
        if len(result.shape) == 3:
            pieces.append((jnp.bitwise_xor(me, step), result))
        else:
            base = jnp.bitwise_and(me, result.shape[0])
            pieces += [(base + at, result.at[at]) for at in range(result.shape[0])]

    def each(act):
        at = 0
        for peer, result in pieces:
            for slot in range(result.shape[0]):
                window = info[peer * HOT + slot]
                target = out.at[jnp.maximum(window, 0)]
                copy = pltpu.make_async_copy(result.at[slot], target, sems.at[at])
                pl.when(window >= 0)(functools.partial(act, copy))
                at += 1

    each(lambda copy: copy.start())
    each(lambda copy: copy.wait())


def unpack(steps, info, results, so_far, shape, after):
    anywhere = pl.BlockSpec(memory_space=pl.ANY)
    count = len(steps)
    copies = sum(result.size // (shape[1] * shape[2]) for result in results)
    return pl.pallas_call(
        functools.partial(unpack_kernel, steps),
        in_specs=[pl.BlockSpec(memory_space=pltpu.SMEM)]
        + [pl.BlockSpec(memory_space=pltpu.VMEM)] * count
        + [anywhere] * (len(so_far) + 1),
        out_specs=anywhere,
        out_shape=jax.ShapeDtypeStruct(shape, results[0].dtype),
        input_output_aliases={1 + count: 0} if so_far else {},
        scratch_shapes=[pltpu.SemaphoreType.DMA((copies,))],
        compiler_params=pltpu.CompilerParams(vmem_limit_bytes=16 * MIB),
        cost_estimate=cost(CUT_FLOPS),
        name="unpack",
    )(info, *results, *so_far, after)


def unpack_extra_kernel(slots, info, results, _, out, held, sems):
    peers, extras, _, wide = results.shape
    hot = info[info.shape[0] - 1]
    copies = []
    for extra in range(extras):
        for peer in range(peers):
            start = mirrored_number(peer, peers) * wide
            held[extra, :, start : start + wide] = results[peer, extra]
        window = info[hot * HOT + slots + extra]
        copies.append(pltpu.make_async_copy(held.at[extra], out.at[window], sems.at[extra]))
        copies[-1].start()
    for copy in copies:
        copy.wait()


def unpack_extra(info, results, so_far, slots):
    _, extras, tokens, _ = results.shape
    scalars = pl.BlockSpec(memory_space=pltpu.SMEM)
    vector = pl.BlockSpec(memory_space=pltpu.VMEM)
    anywhere = pl.BlockSpec(memory_space=pl.ANY)
    return pl.pallas_call(
        functools.partial(unpack_extra_kernel, slots),
        in_specs=[scalars, vector, anywhere],
        out_specs=anywhere,
        out_shape=jax.ShapeDtypeStruct(so_far.shape, so_far.dtype),
        input_output_aliases={2: 0},
        scratch_shapes=[
            pltpu.VMEM((extras, tokens, so_far.shape[2]), so_far.dtype),
            pltpu.SemaphoreType.DMA((extras,)),
        ],
        compiler_params=pltpu.CompilerParams(vmem_limit_bytes=24 * MIB),
        cost_estimate=cost(1000),
        name="unpack_extra",
    )(info, results, so_far)


def exchanged(value, step):
    peers = lax.axis_size("pos")
    if step == 0:
        return value
    return lax.ppermute(value, "pos", [(i, i ^ step) for i in range(peers)])


def exchanged_near(value):
    peers = lax.axis_size("pos")
    half = peers // 2
    groups = [list(range(half)), list(range(half, peers))]
    return lax.all_to_all(value, "pos", 0, 0, axis_index_groups=groups, tiled=True)


def shards(gate_stream, key_stream, value_stream, filters, temps, queries, blocks, sites):
    rows, chans = gate_stream.shape
    taps = filters.shape[1]
    peers = lax.axis_size("pos")
    me = lax.axis_index("pos").astype(jnp.int32)
    windows = blocks.shape[0]
    heads = chans // HEAD_DIM
    extras = 2 if heads % peers == 0 else 0
    slots = HOT - extras
    wide = chans // peers

    last = slice(rows - taps, rows)
    tail = key_stream[last].astype(jnp.float32) * value_stream[last].astype(jnp.float32)
    tail = tail.astype(jnp.bfloat16)
    earlier = lax.ppermute(tail, "pos", [(i, i + 1) for i in range(peers - 1)])
    info, near, far = pack(blocks, sites, queries, tail, rows, peers, slots)
    half = peers // 2
    far = [exchanged(message, half + at) for at, message in enumerate(far)]
    near = exchanged_near(near)
    hyena_out, valued, keyed = mix(gate_stream, key_stream, value_stream, earlier, filters)

    def attended_far(first, count, after):
        results = attend(info, temps, keyed, valued, after, far[first : first + count])
        moved = [exchanged(result, half + first + at) for at, result in enumerate(results)]
        return moved, results[0]

    bits = peers.bit_length() - 1 if extras else 0
    kept, fresh, after = valued, [], valued
    returned, so_far, done = [], [], 0
    for bit in range(min(bits, 1)):
        sent, kept = cut(bit, info, kept, fresh, after)
        fresh, after = [exchanged(sent, 1 << bit)], sent
    (result,) = attend(info, temps, keyed, valued, after, [near])
    returned_near, after = exchanged_near(result), result
    first = 0
    for place in range(half):
        if first >= half:
            break
        count = 1 if place < 2 else 2
        moved, after = attended_far(first, count, after)
        returned += moved
        first += count
        bit = place + 1
        if bit < bits:
            sent, kept = cut(bit, info, kept, fresh, after)
            fresh, after = [exchanged(sent, 1 << bit)], sent
        if place >= 2:
            early = list(range(half + done, half + done + 2))
            arrivals = returned[done : done + 2]
            so_far = [unpack(early, info, arrivals, so_far, queries.shape, after)]
            after = so_far[0]
            done += 2
    extra_results = []
    if extras:
        result = attend_extra(info, temps, kept, fresh[0], after, near, far, wide)
        extra_results.append(lax.all_to_all(result, "pos", 0, 0, tiled=True))
        after = result
    so_far = [unpack([0], info, [returned_near], so_far, queries.shape, after)]
    late = list(range(half + done, peers))
    so_far = [unpack(late, info, returned[done:], so_far, queries.shape, info)]
    attended = so_far[0]
    for result in extra_results:
        attended = unpack_extra(info, result, attended, slots)
    return (hyena_out, attended)


def solution(mesh):
    placed = (
        P(("groups", "pos"), "mp"),
        P(("groups", "pos"), "mp"),
        P(("groups", "pos"), "mp"),
        P("mp", None),
        P("mp"),
        P("groups", "pos", "mp"),
        P("groups"),
        P("groups"),
    )
    return jax.shard_map(
        shards,
        mesh=mesh,
        in_specs=placed,
        out_specs=(P(("groups", "pos"), "mp"), P("groups", "pos", "mp")),
        check_vma=False,
    )
```

time: 214 us -> 150 us (0.70)
  waiting for transfers between devices: 63.7 us -> 36.4 us
  local copies, waits for them, and re-layouts: 29.8 us -> 13.5 us
  starting transfers between devices: 57.5 us -> 46 us
  Pallas kernels: 57.1 us -> 51.1 us
    ppermute x17 -> x11, waiting for transfers between devices: 52.6 us -> 31.1 us  [exchanged(): return lax.ppermute(value, 'pos', [(i, i ^ step) for i in range(peers)])]
    ppermute x17 -> x11, starting transfers between devices: 46.3 us -> 26 us  [exchanged(): return lax.ppermute(value, 'pos', [(i, i ^ step) for i in range(peers)])]
    unnamed x62 -> x36, local copies, waits for them, and re-layouts: 27.3 us -> 13.5 us
    ppermute x1, waiting for transfers between devices: 11.1 us -> 0.01 us  [shards(): earlier = lax.ppermute(tail, 'pos', [(i, i + 1) for i in range(peers - 1)])]
    all_to_all x0 -> x2, starting transfers between devices: none -> 7.3 us  [exchanged_near(): lax.all_to_all(value, 'pos', 0, 0, axis_index_groups=groups, tiled=True)]
    pallas_call x11 -> x14, Pallas kernels: 43.8 us -> 37.7 us  [the longest x4 19.5 us: attend(): pl.pallas_call(functools.partial(attend_kernel, len(messages)), in_specs=...]
    all_to_all x1, waiting for transfers between devices: 0.01 us -> 5.27 us  [shards(): extra_results.append(lax.all_to_all(result, 'pos', 0, 0, tiled=True))]
    select_n x3 -> x0, other arithmetic: 2.57 us -> none  [spread(): held = jnp.where(have, kept, arrived)]
  transfers between devices with their start and end apart: 19 -> 15, of which waited for: 5 -> 5; matrix products, arithmetic and copies ran while one was open for 1% -> 0% of each run, Pallas kernels for 18% -> 33%
where the time goes in v3:
time: 150 us; the launch traced here: 149 us
  Pallas kernels  51.1 us (34%)
  starting transfers between devices  46 us (31%)
  waiting for transfers between devices  36.4 us (24%)
  local copies, waits for them, and re-layouts  13.5 us (9%)
    ppermute x11, waiting for transfers between devices, exchanged(): return lax.ppermute(value, 'pos', [(i, i ^ step) for i in range(peers)])  31.1 us
    ppermute x11, starting transfers between devices, exchanged(): return lax.ppermute(value, 'pos', [(i, i ^ step) for i in range(peers)])  26 us
    pallas_call x4, Pallas kernels, attend(): pl.pallas_call(functools.partial(attend_kernel, len(messages)), in_specs=...  19.5 us
    unnamed x36, local copies, waits for them, and re-layouts  13.5 us
    pallas_call x1, Pallas kernels, mix(): pl.pallas_call(mix_kernel, grid=(chans // wide,), in_specs=[stream, strea...  13.3 us
    all_to_all x1, starting transfers between devices, shards(): extra_results.append(lax.all_to_all(result, 'pos', 0, 0, tiled=True))  7.75 us
    all_to_all x2, starting transfers between devices, exchanged_near(): lax.all_to_all(value, 'pos', 0, 0, axis_index_groups=groups, tiled=True)  7.3 us
    all_to_all x1, waiting for transfers between devices, shards(): extra_results.append(lax.all_to_all(result, 'pos', 0, 0, tiled=True))  5.27 us
  transfers between devices with their start and end apart: 15, of which 5 were waited for; matrix products, arithmetic and copies ran while one was open for 0% of the time, Pallas kernels for 33%

profile of v3, /device:TPU:0, one launch (start us, length us, event | category | flops | bytes accessed | tf_op | source)
XLA Modules:
  0.0 149.1 jit_solution(6714769569909816538)
XLA Ops:
  2.0 4.9 %collective-permute-start = (bf16[128,2048]{1,0:T(8,128)(2,1)S(1)}, bf16[128,2048]{1,0:T(8,128)(2,1)S(1)}, u32[]{:S(2)}, u32[]{:S(2)}) collective-permute-start(bf16[128,2048]{1,0:T(8,128)(2,1)S(1)} %multiply_convert_fusion._), channel_id=1, source_target_pairs={{0,2},{2,4},{4,6},{6,8},{8,10},{10,12},{12,14},{1,3},{3,5},{5,7},{... | collective-permute-start | bytes 1572872 | tf_op jit(solution)/shard_map/ppermute | solution.py:514
  6.9 1.6 %copy-done.1 = bf16[16,32,2048]{2,1,0:T(8,128)(2,1)S(1)} copy-done((bf16[16,32,2048]{2,1,0:T(8,128)(2,1)S(1)}, bf16[16,32,2048]{2,1,0:T(8,128)(2,1)}, u32[]{:S(2)}) %copy-start.1) | copy-done | bytes 2097176
  9.8 2.7 %pack_near.1 = (s32[48]{0:T(128)S(1)}, bf16[4,2,32,2304]{3,2,1,0:T(8,128)(2,1)}) custom-call(s32[16]{0:T(128)S(1)} %copy-done.4, s32[16]{0:T(128)S(1)} %copy-done.5, bf16[16,32,2048]{2,1,0:T(8,128)(2,1)S(1)} %copy-done.1, bf16[128,2048]{1,0:T(8,128)(2,1)S(1)} %multiply_convert_fusion._), custom_call_target="tpu_custom_call" | custom-call | flops 21474836480 | bytes 1000 | tf_op jit(solution)/shard_map/pack_near/pallas_call | solution.py:377
  12.5 3.8 %all-to-all-start = ((bf16[4,2,32,2304]{3,2,1,0:T(8,128)(2,1)}), bf16[4,2,32,2304]{3,2,1,0:T(8,128)(2,1)S(1)}, u32[]{:S(2)}, u32[]{:S(2)}) async-start(bf16[4,2,32,2304]{3,2,1,0:T(8,128)(2,1)} %get-tuple-element.25._), calls=%async_computation | async-start | bytes 2359296 | tf_op jit(solution)/shard_map/all_to_all | solution.py:497
  16.3 1.6 %copy-done.2 = bf16[16,32,2048]{2,1,0:T(8,128)(2,1)S(1)} copy-done((bf16[16,32,2048]{2,1,0:T(8,128)(2,1)S(1)}, bf16[16,32,2048]{2,1,0:T(8,128)(2,1)}, u32[]{:S(2)}) %copy-start.2) | copy-done | bytes 2097176
  17.9 2.1 %pack_far.1 = (bf16[2,32,2304]{2,1,0:T(8,128)(2,1)}, bf16[2,32,2304]{2,1,0:T(8,128)(2,1)}, bf16[2,32,2304]{2,1,0:T(8,128)(2,1)}, bf16[2,32,2304]{2,1,0:T(8,128)(2,1)}) custom-call(s32[48]{0:T(128)S(1)} %get-tuple-element.20.info.refs_3_, bf16[16,32,2048]{2,1,0:T(8,128)(2,1)S(1)} %copy-done.2, bf16[4,2,32,2304]{3,2,1,0:T(8,128)(2,1)} %get-tuple-element.25._), custom_call_target="tpu_custom_call" | custom-call | flops 21474836480 | bytes 1000 | tf_op jit(solution)/shard_map/pack_far/pallas_call | solution.py:394
  20.0 2.4 %collective-permute-start.2 = (bf16[2,32,2304]{2,1,0:T(8,128)(2,1)}, bf16[2,32,2304]{2,1,0:T(8,128)(2,1)}, u32[]{:S(2)}, u32[]{:S(2)}) collective-permute-start(bf16[2,32,2304]{2,1,0:T(8,128)(2,1)} %get-tuple-element.26), channel_id=1, source_target_pairs={{0,8},{2,10},{4,12},{6,14},{8,0},{10,2},{12,4},{14,6},{1,9},{3,11}... | collective-permute-start | bytes 884744 | tf_op jit(solution)/shard_map/ppermute | solution.py:490
  22.4 2.1 %collective-permute-start.4 = (bf16[2,32,2304]{2,1,0:T(8,128)(2,1)}, bf16[2,32,2304]{2,1,0:T(8,128)(2,1)}, u32[]{:S(2)}, u32[]{:S(2)}) collective-permute-start(bf16[2,32,2304]{2,1,0:T(8,128)(2,1)} %get-tuple-element.29), channel_id=1, source_target_pairs={{0,10},{2,8},{4,14},{6,12},{8,2},{10,0},{12,6},{14,4},{1,11},{3,9}... | collective-permute-start | bytes 884744 | tf_op jit(solution)/shard_map/ppermute | solution.py:490
  24.5 3.2 %collective-permute-start.8 = (bf16[2,32,2304]{2,1,0:T(8,128)(2,1)}, bf16[2,32,2304]{2,1,0:T(8,128)(2,1)}, u32[]{:S(2)}, u32[]{:S(2)}) collective-permute-start(bf16[2,32,2304]{2,1,0:T(8,128)(2,1)} %get-tuple-element.32), channel_id=1, source_target_pairs={{0,12},{2,14},{4,8},{6,10},{8,4},{10,6},{12,0},{14,2},{1,13},{3,15... | collective-permute-start | bytes 884744 | tf_op jit(solution)/shard_map/ppermute | solution.py:490
  27.7 13.3 %mix.1 = (bf16[512,2048]{1,0:T(8,128)(2,1)}, bf16[16,512,128]{2,1,0:T(8,128)(2,1)S(1)}, bf16[16,128,512]{2,1,0:T(8,128)(2,1)S(1)}) custom-call(bf16[512,2048]{1,0:T(8,128)(2,1)} %gate.1, bf16[512,2048]{1,0:T(8,128)(2,1)} %key.1, bf16[512,2048]{1,0:T(8,128)(2,1)} %value.1, bf16[128,2048]{1,0:T(8,128)(2,1)S(1)} %collective-permute-done.earlier, ...), custom_call_target="tpu_custom_call" | custom-call | flops 107374182400 | bytes 1000 | tf_op jit(solution)/shard_map/mix/pallas_call | solution.py:98
  41.1 2.2 %cut.3 = (bf16[8,512,128]{2,1,0:T(8,128)(2,1)}, bf16[8,512,128]{2,1,0:T(8,128)(2,1)S(1)}) custom-call(s32[48]{0:T(128)S(1)} %get-tuple-element.20.info.refs_3_, bf16[16,512,128]{2,1,0:T(8,128)(2,1)S(1)} %get-tuple-element.21.held.refs_0_.rows, bf16[16,512,128]{2,1,0:T(8,128)(2,1)S(1)} %get-tuple-element.21.held.refs_0_.rows), custom_call_target="tpu_custom_call" | custom-call | flops 2147483648 | bytes 1000 | tf_op jit(solution)/shard_map/cut/pallas_call | solution.py:207
  43.4 2.0 %collective-permute-start.1 = (bf16[8,512,128]{2,1,0:T(8,128)(2,1)}, bf16[8,512,128]{2,1,0:T(8,128)(2,1)S(1)}, u32[]{:S(2)}, u32[]{:S(2)}) collective-permute-start(bf16[8,512,128]{2,1,0:T(8,128)(2,1)} %get-tuple-element.23._), channel_id=1, source_target_pairs={{0,2},{2,0},{4,6},{6,4},{8,10},{10,8},{12,14},{14,12},{1,3},{3,1},... | collective-permute-start | bytes 3145736 | tf_op jit(solution)/shard_map/ppermute | solution.py:490
  45.4 1.6 %copy-done.10 = bf16[16,512,128]{2,1,0:T(8,128)(2,1)S(1)} copy-done((bf16[16,512,128]{2,1,0:T(8,128)(2,1)S(1)}, bf16[16,512,128]{2,1,0:T(8,128)(2,1)}, u32[]{:S(2)}) %copy-start.10) | copy-done | bytes 2097176
  47.0 1.6 %copy-done.16 = bf16[16,128,512]{2,1,0:T(8,128)(2,1)S(1)} copy-done((bf16[16,128,512]{2,1,0:T(8,128)(2,1)S(1)}, bf16[16,128,512]{2,1,0:T(8,128)(2,1)}, u32[]{:S(2)}) %copy-start.16) | copy-done | bytes 2097176
  48.6 6.0 %attend.4._ = bf16[4,2,32,2048]{3,2,1,0:T(8,128)(2,1)} custom-call(s32[48]{0:T(128)S(1)} %get-tuple-element.20.info.refs_3_, f32[16]{0:T(128)S(1)} %copy-done.6, bf16[16,128,512]{2,1,0:T(8,128)(2,1)S(1)} %copy-done.16, bf16[16,512,128]{2,1,0:T(8,128)(2,1)S(1)} %copy-done.10, bf16[8,512,128]{2,1,0:T(8,128)(2,1)} %get-tuple-element.23._, ...), custom_call_target="tpu_custom_call" | custom-call | flops 21474836480 | bytes 1000 | tf_op jit(solution)/shard_map/attend/pallas_call | solution.py:164
  54.6 3.5 %all-to-all-start.2 = ((bf16[4,2,32,2048]{3,2,1,0:T(8,128)(2,1)}), bf16[4,2,32,2048]{3,2,1,0:T(8,128)(2,1)S(1)}, u32[]{:S(2)}, u32[]{:S(2)}) async-start(bf16[4,2,32,2048]{3,2,1,0:T(8,128)(2,1)} %attend.4._), calls=%async_computation.2 | async-start | bytes 2097152 | tf_op jit(solution)/shard_map/all_to_all | solution.py:497
  58.1 1.6 %copy-done.11 = bf16[16,512,128]{2,1,0:T(8,128)(2,1)S(1)} copy-done((bf16[16,512,128]{2,1,0:T(8,128)(2,1)S(1)}, bf16[16,512,128]{2,1,0:T(8,128)(2,1)}, u32[]{:S(2)}) %copy-start.11) | copy-done | bytes 2097176
  59.7 1.6 %copy-done.17 = bf16[16,128,512]{2,1,0:T(8,128)(2,1)S(1)} copy-done((bf16[16,128,512]{2,1,0:T(8,128)(2,1)S(1)}, bf16[16,128,512]{2,1,0:T(8,128)(2,1)}, u32[]{:S(2)}) %copy-start.17) | copy-done | bytes 2097176
  61.3 4.4 %attend.5.refs_1_ = bf16[2,32,2048]{2,1,0:T(8,128)(2,1)S(1)} custom-call(s32[48]{0:T(128)S(1)} %get-tuple-element.20.info.refs_3_, f32[16]{0:T(128)S(1)} %copy-done.6, bf16[16,128,512]{2,1,0:T(8,128)(2,1)S(1)} %copy-done.17, bf16[16,512,128]{2,1,0:T(8,128)(2,1)S(1)} %copy-done.11, bf16[4,2,32,2048]{3,2,1,0:T(8,128)(2,1)} %attend.4._, ...), custom_call_target="tpu_custom_call" | custom-call | flops 21474836480 | bytes 1000 | tf_op jit(solution)/shard_map/attend/pallas_call | solution.py:164
  65.7 1.6 %collective-permute-start.6 = (bf16[2,32,2048]{2,1,0:T(8,128)(2,1)S(1)}, bf16[2,32,2048]{2,1,0:T(8,128)(2,1)S(1)}, u32[]{:S(2)}, u32[]{:S(2)}) collective-permute-start(bf16[2,32,2048]{2,1,0:T(8,128)(2,1)S(1)} %attend.5.refs_1_), channel_id=1, source_target_pairs={{0,8},{2,10},{4,12},{6,14},{8,0},{10,2},{12,4},{14,6},{1,9},{3,11}... | collective-permute-start | bytes 786440 | tf_op jit(solution)/shard_map/ppermute | solution.py:490
  67.3 16.6 %collective-permute-done.1.refs_0_ = bf16[8,512,128]{2,1,0:T(8,128)(2,1)S(1)} collective-permute-done((bf16[8,512,128]{2,1,0:T(8,128)(2,1)}, bf16[8,512,128]{2,1,0:T(8,128)(2,1)S(1)}, u32[]{:S(2)}, u32[]{:S(2)}) %collective-permute-start.1) | collective-permute-done | bytes 1048608 | tf_op jit(solution)/shard_map/ppermute | solution.py:490
  85.4 4.3 %attend.6.refs_1_ = bf16[2,32,2048]{2,1,0:T(8,128)(2,1)S(1)} custom-call(s32[48]{0:T(128)S(1)} %get-tuple-element.20.info.refs_3_, f32[16]{0:T(128)S(1)} %copy-done.6, bf16[16,128,512]{2,1,0:T(8,128)(2,1)S(1)} %copy-done.17, bf16[16,512,128]{2,1,0:T(8,128)(2,1)S(1)} %copy-done.12, bf16[4,512,128]{2,1,0:T(8,128)(2,1)S(1)} %get-tuple-element.28._, ...), custom_call_target="tpu_custom_call" | custom-call | flops 21474836480 | bytes 1000 | tf_op jit(solution)/shard_map/attend/pallas_call | solution.py:164
  89.7 7.5 %collective-permute-start.7 = (bf16[2,32,2048]{2,1,0:T(8,128)(2,1)S(1)}, bf16[2,32,2048]{2,1,0:T(8,128)(2,1)S(1)}, u32[]{:S(2)}, u32[]{:S(2)}) collective-permute-start(bf16[2,32,2048]{2,1,0:T(8,128)(2,1)S(1)} %attend.6.refs_1_), channel_id=1, source_target_pairs={{0,10},{2,8},{4,14},{6,12},{8,2},{10,0},{12,6},{14,4},{1,11},{3,9}... | collective-permute-start | bytes 786440 | tf_op jit(solution)/shard_map/ppermute | solution.py:490
  97.3 4.6 %collective-permute-done.3.refs_0_ = bf16[4,512,128]{2,1,0:T(8,128)(2,1)S(1)} collective-permute-done((bf16[4,512,128]{2,1,0:T(8,128)(2,1)S(1)}, bf16[4,512,128]{2,1,0:T(8,128)(2,1)S(1)}, u32[]{:S(2)}, u32[]{:S(2)}) %collective-permute-start.3) | collective-permute-done | bytes 524320 | tf_op jit(solution)/shard_map/ppermute | solution.py:490
  102.6 4.8 %attend.7 = (bf16[2,32,2048]{2,1,0:T(8,128)(2,1)S(1)}, bf16[2,32,2048]{2,1,0:T(8,128)(2,1)S(1)}) custom-call(s32[48]{0:T(128)S(1)} %get-tuple-element.20.info.refs_3_, f32[16]{0:T(128)S(1)} %copy-done.6, bf16[16,128,512]{2,1,0:T(8,128)(2,1)S(1)} %copy-done.17, bf16[16,512,128]{2,1,0:T(8,128)(2,1)S(1)} %copy-done.12, ...), custom_call_target="tpu_custom_call" | custom-call | flops 21474836480 | bytes 1000 | tf_op jit(solution)/shard_map/attend/pallas_call | solution.py:164
  107.5 2.0 %collective-permute-start.10 = (bf16[2,32,2048]{2,1,0:T(8,128)(2,1)S(1)}, bf16[2,32,2048]{2,1,0:T(8,128)(2,1)S(1)}, u32[]{:S(2)}, u32[]{:S(2)}) collective-permute-start(bf16[2,32,2048]{2,1,0:T(8,128)(2,1)S(1)} %get-tuple-element.34.refs_2_), channel_id=1, source_target_pairs={{0,12},{2,14},{4,8},{6,10},{8,4},{10,6},{12,0},{14,2},{1,13},{3,15... | collective-permute-start | bytes 786440 | tf_op jit(solution)/shard_map/ppermute | solution.py:490
  109.4 5.0 %collective-permute-start.11 = (bf16[2,32,2048]{2,1,0:T(8,128)(2,1)S(1)}, bf16[2,32,2048]{2,1,0:T(8,128)(2,1)S(1)}, u32[]{:S(2)}, u32[]{:S(2)}) collective-permute-start(bf16[2,32,2048]{2,1,0:T(8,128)(2,1)S(1)} %get-tuple-element.35), channel_id=1, source_target_pairs={{0,14},{2,12},{4,10},{6,8},{8,6},{10,4},{12,2},{14,0},{1,15},{3,13... | collective-permute-start | bytes 786440 | tf_op jit(solution)/shard_map/ppermute | solution.py:490
  114.5 8.9 %collective-permute-done.7.refs_1_ = bf16[2,32,2048]{2,1,0:T(8,128)(2,1)S(1)} collective-permute-done((bf16[2,32,2048]{2,1,0:T(8,128)(2,1)S(1)}, bf16[2,32,2048]{2,1,0:T(8,128)(2,1)S(1)}, u32[]{:S(2)}, u32[]{:S(2)}) %collective-permute-start.7) | collective-permute-done | bytes 262176 | tf_op jit(solution)/shard_map/ppermute | solution.py:490
  125.7 1.6 %copy-done = bf16[16,32,2048]{2,1,0:T(8,128)(2,1)S(1)} copy-done((bf16[16,32,2048]{2,1,0:T(8,128)(2,1)S(1)}, bf16[16,32,2048]{2,1,0:T(8,128)(2,1)}, u32[]{:S(2)}) %copy-start) | copy-done | bytes 2097176
  127.3 4.5 %attend_extra.1.refs_2_ = bf16[8,2,32,256]{3,2,1,0:T(8,128)(2,1)} custom-call(s32[48]{0:T(128)S(1)} %get-tuple-element.20.info.refs_3_, f32[16]{0:T(128)S(1)} %copy-done.6, bf16[2,512,128]{2,1,0:T(8,128)(2,1)S(1)} %get-tuple-element.30.kept, bf16[2,512,128]{2,1,0:T(8,128)(2,1)S(1)} %collective-permute-done.5.fresh, bf16[16,32,2048]{2,1,0:T(8,128)(2,1)S(1)} %copy-done, ...), custom_call_target="tpu_custom_call" | custom-call | flops 21474836480 | bytes 1000 | tf_op jit(solution)/shard_map/attend_extra/pallas_call | solution.py:250
  131.8 7.7 %all-to-all-start.1 = ((bf16[8,2,32,256]{3,2,1,0:T(8,128)(2,1)}), bf16[8,2,32,256]{3,2,1,0:T(8,128)(2,1)S(1)}, u32[]{:S(2)}, u32[]{:S(2)}) async-start(bf16[8,2,32,256]{3,2,1,0:T(8,128)(2,1)} %attend_extra.1.refs_2_), calls=%async_computation.1 | async-start | bytes 524288 | tf_op jit(solution)/shard_map/all_to_all | solution.py:555
  142.5 5.3 %all-to-all-done.1.results = bf16[8,2,32,256]{3,2,1,0:T(8,128)(2,1)S(1)} async-done(((bf16[8,2,32,256]{3,2,1,0:T(8,128)(2,1)}), bf16[8,2,32,256]{3,2,1,0:T(8,128)(2,1)S(1)}, u32[]{:S(2)}, u32[]{:S(2)}) %all-to-all-start.1) | async-done | bytes 262176 | tf_op jit(solution)/shard_map/all_to_all | solution.py:555
  (50 shorter events, 11.7 us)
Async XLA Ops:
  2.0 25.8 %collective-permute-start = (bf16[128,2048]{1,0:T(8,128)(2,1)S(1)}, bf16[128,2048]{1,0:T(8,128)(2,1)S(1)}, u32[]{:S(2)}, u32[]{:S(2)}) collective-permute-start(bf16[128,2048]{1,0:T(8,128)(2,1)S(1)} %multiply_convert_fusion._), channel_id=1, source_target_pairs={{0,2},{2,4},{4,6},{6,8},{8,10},{10,12},{12,14},{1,3},{3,5},{5,7},{... | collective-permute-start | bytes 1572872 | tf_op jit(solution)/shard_map/ppermute | solution.py:514
  6.9 1.6 %copy-start.1 = (bf16[16,32,2048]{2,1,0:T(8,128)(2,1)S(1)}, bf16[16,32,2048]{2,1,0:T(8,128)(2,1)}, u32[]{:S(2)}) copy-start(bf16[16,32,2048]{2,1,0:T(8,128)(2,1)} %queries.3) | copy-start | bytes 6291460
  8.5 0.7 copy-start.4
  12.5 32.9 %all-to-all-start = ((bf16[4,2,32,2304]{3,2,1,0:T(8,128)(2,1)}), bf16[4,2,32,2304]{3,2,1,0:T(8,128)(2,1)S(1)}, u32[]{:S(2)}, u32[]{:S(2)}) async-start(bf16[4,2,32,2304]{3,2,1,0:T(8,128)(2,1)} %get-tuple-element.25._), calls=%async_computation | async-start | bytes 2359296 | tf_op jit(solution)/shard_map/all_to_all | solution.py:497
  16.3 1.6 %copy-start.2 = (bf16[16,32,2048]{2,1,0:T(8,128)(2,1)S(1)}, bf16[16,32,2048]{2,1,0:T(8,128)(2,1)}, u32[]{:S(2)}) copy-start(bf16[16,32,2048]{2,1,0:T(8,128)(2,1)} %queries.3) | copy-start | bytes 6291460
  17.8 9.9 %copy-start.3 = (f32[2048,128]{1,0:T(8,128)S(1)}, f32[2048,128]{1,0:T(8,128)}, u32[]{:S(2)}) copy-start(f32[2048,128]{1,0:T(8,128)} %filters.1) | copy-start | bytes 3145732
  17.9 9.9 %copy-start.7 = (bf16[512,256]{1,0:T(8,128)(2,1)S(1)}, bf16[512,256]{1,0:T(8,128)(2,1)}, u32[]{:S(2)}) copy-start(bf16[512,256]{1,0:T(8,128)(2,1)} %constant.4.clone.forward) | copy-start | bytes 786436
  17.9 9.9 %copy-start.8 = (bf16[256,256]{1,0:T(8,128)(2,1)S(1)}, bf16[256,256]{1,0:T(8,128)(2,1)}, u32[]{:S(2)}) copy-start(bf16[256,256]{1,0:T(8,128)(2,1)} %constant.5.clone.inverse) | copy-start | bytes 393220
  20.0 38.1 %collective-permute-start.2 = (bf16[2,32,2304]{2,1,0:T(8,128)(2,1)}, bf16[2,32,2304]{2,1,0:T(8,128)(2,1)}, u32[]{:S(2)}, u32[]{:S(2)}) collective-permute-start(bf16[2,32,2304]{2,1,0:T(8,128)(2,1)} %get-tuple-element.26), channel_id=1, source_target_pairs={{0,8},{2,10},{4,12},{6,14},{8,0},{10,2},{12,4},{14,6},{1,9},{3,11}... | collective-permute-start | bytes 884744 | tf_op jit(solution)/shard_map/ppermute | solution.py:490
  22.4 62.1 %collective-permute-start.4 = (bf16[2,32,2304]{2,1,0:T(8,128)(2,1)}, bf16[2,32,2304]{2,1,0:T(8,128)(2,1)}, u32[]{:S(2)}, u32[]{:S(2)}) collective-permute-start(bf16[2,32,2304]{2,1,0:T(8,128)(2,1)} %get-tuple-element.29), channel_id=1, source_target_pairs={{0,10},{2,8},{4,14},{6,12},{8,2},{10,0},{12,6},{14,4},{1,11},{3,9}... | collective-permute-start | bytes 884744 | tf_op jit(solution)/shard_map/ppermute | solution.py:490
  24.5 78.2 %collective-permute-start.8 = (bf16[2,32,2304]{2,1,0:T(8,128)(2,1)}, bf16[2,32,2304]{2,1,0:T(8,128)(2,1)}, u32[]{:S(2)}, u32[]{:S(2)}) collective-permute-start(bf16[2,32,2304]{2,1,0:T(8,128)(2,1)} %get-tuple-element.32), channel_id=1, source_target_pairs={{0,12},{2,14},{4,8},{6,10},{8,4},{10,6},{12,0},{14,2},{1,13},{3,15... | collective-permute-start | bytes 884744 | tf_op jit(solution)/shard_map/ppermute | solution.py:490
  27.6 75.0 %collective-permute-start.9 = (bf16[2,32,2304]{2,1,0:T(8,128)(2,1)}, bf16[2,32,2304]{2,1,0:T(8,128)(2,1)}, u32[]{:S(2)}, u32[]{:S(2)}) collective-permute-start(bf16[2,32,2304]{2,1,0:T(8,128)(2,1)} %get-tuple-element.33), channel_id=1, source_target_pairs={{0,14},{2,12},{4,10},{6,8},{8,6},{10,4},{12,2},{14,0},{1,15},{3,13... | collective-permute-start | bytes 884744 | tf_op jit(solution)/shard_map/ppermute | solution.py:490
  41.1 2.2 %copy-start.9 = (bf16[16,512,128]{2,1,0:T(8,128)(2,1)}, bf16[16,512,128]{2,1,0:T(8,128)(2,1)S(1)}, u32[]{:S(2)}) copy-start(bf16[16,512,128]{2,1,0:T(8,128)(2,1)S(1)} %get-tuple-element.21.held.refs_0_.rows) | copy-start | bytes 6291460
  41.1 2.3 %copy-start.15 = (bf16[16,128,512]{2,1,0:T(8,128)(2,1)}, bf16[16,128,512]{2,1,0:T(8,128)(2,1)S(1)}, u32[]{:S(2)}) copy-start(bf16[16,128,512]{2,1,0:T(8,128)(2,1)S(1)} %get-tuple-element.24.keys) | copy-start | bytes 6291460
  41.1 4.4 %copy-start.6 = (f32[16]{0:T(128)S(1)}, f32[16]{0:T(128)}, u32[]{:S(2)}) copy-start(f32[16]{0:T(128)} %temps.9) | copy-start | bytes 196
  43.4 11.2 %copy-start.13 = (bf16[8,512,128]{2,1,0:T(8,128)(2,1)}, bf16[8,512,128]{2,1,0:T(8,128)(2,1)S(1)}, u32[]{:S(2)}) copy-start(bf16[8,512,128]{2,1,0:T(8,128)(2,1)S(1)} %get-tuple-element.22.held) | copy-start | bytes 3145732
  43.4 40.4 %collective-permute-start.1 = (bf16[8,512,128]{2,1,0:T(8,128)(2,1)}, bf16[8,512,128]{2,1,0:T(8,128)(2,1)S(1)}, u32[]{:S(2)}, u32[]{:S(2)}) collective-permute-start(bf16[8,512,128]{2,1,0:T(8,128)(2,1)} %get-tuple-element.23._), channel_id=1, source_target_pairs={{0,2},{2,0},{4,6},{6,4},{8,10},{10,8},{12,14},{14,12},{1,3},{3,1},... | collective-permute-start | bytes 3145736 | tf_op jit(solution)/shard_map/ppermute | solution.py:490
  45.4 1.6 %copy-start.10 = (bf16[16,512,128]{2,1,0:T(8,128)(2,1)S(1)}, bf16[16,512,128]{2,1,0:T(8,128)(2,1)}, u32[]{:S(2)}) copy-start(bf16[16,512,128]{2,1,0:T(8,128)(2,1)} %copy-done.9) | copy-start | bytes 6291460
  47.0 1.6 %copy-start.16 = (bf16[16,128,512]{2,1,0:T(8,128)(2,1)S(1)}, bf16[16,128,512]{2,1,0:T(8,128)(2,1)}, u32[]{:S(2)}) copy-start(bf16[16,128,512]{2,1,0:T(8,128)(2,1)} %copy-done.15) | copy-start | bytes 6291460
  54.6 77.2 %all-to-all-start.2 = ((bf16[4,2,32,2048]{3,2,1,0:T(8,128)(2,1)}), bf16[4,2,32,2048]{3,2,1,0:T(8,128)(2,1)S(1)}, u32[]{:S(2)}, u32[]{:S(2)}) async-start(bf16[4,2,32,2048]{3,2,1,0:T(8,128)(2,1)} %attend.4._), calls=%async_computation.2 | async-start | bytes 2097152 | tf_op jit(solution)/shard_map/all_to_all | solution.py:497
  58.1 1.6 %copy-start.11 = (bf16[16,512,128]{2,1,0:T(8,128)(2,1)S(1)}, bf16[16,512,128]{2,1,0:T(8,128)(2,1)}, u32[]{:S(2)}) copy-start(bf16[16,512,128]{2,1,0:T(8,128)(2,1)} %copy-done.9) | copy-start | bytes 6291460
  59.7 1.6 %copy-start.17 = (bf16[16,128,512]{2,1,0:T(8,128)(2,1)S(1)}, bf16[16,128,512]{2,1,0:T(8,128)(2,1)}, u32[]{:S(2)}) copy-start(bf16[16,128,512]{2,1,0:T(8,128)(2,1)} %copy-done.15) | copy-start | bytes 6291460
  61.3 22.5 %copy-start.14 = (bf16[8,512,128]{2,1,0:T(8,128)(2,1)S(1)}, bf16[8,512,128]{2,1,0:T(8,128)(2,1)}, u32[]{:S(2)}) copy-start(bf16[8,512,128]{2,1,0:T(8,128)(2,1)} %copy-done.13) | copy-start | bytes 3145732
  65.7 48.8 %collective-permute-start.6 = (bf16[2,32,2048]{2,1,0:T(8,128)(2,1)S(1)}, bf16[2,32,2048]{2,1,0:T(8,128)(2,1)S(1)}, u32[]{:S(2)}, u32[]{:S(2)}) collective-permute-start(bf16[2,32,2048]{2,1,0:T(8,128)(2,1)S(1)} %attend.5.refs_1_), channel_id=1, source_target_pairs={{0,8},{2,10},{4,12},{6,14},{8,0},{10,2},{12,4},{14,6},{1,9},{3,11}... | collective-permute-start | bytes 786440 | tf_op jit(solution)/shard_map/ppermute | solution.py:490
  83.8 1.6 %copy-start.12 = (bf16[16,512,128]{2,1,0:T(8,128)(2,1)S(1)}, bf16[16,512,128]{2,1,0:T(8,128)(2,1)}, u32[]{:S(2)}) copy-start(bf16[16,512,128]{2,1,0:T(8,128)(2,1)} %copy-done.9) | copy-start | bytes 6291460
  84.5 17.5 %collective-permute-start.3 = (bf16[4,512,128]{2,1,0:T(8,128)(2,1)S(1)}, bf16[4,512,128]{2,1,0:T(8,128)(2,1)S(1)}, u32[]{:S(2)}, u32[]{:S(2)}) collective-permute-start(bf16[4,512,128]{2,1,0:T(8,128)(2,1)S(1)} %get-tuple-element.28._), channel_id=1, source_target_pairs={{0,4},{2,6},{4,0},{6,2},{8,12},{10,14},{12,8},{14,10},{1,5},{3,7},... | collective-permute-start | bytes 1572872 | tf_op jit(solution)/shard_map/ppermute | solution.py:490
  89.7 33.7 %collective-permute-start.7 = (bf16[2,32,2048]{2,1,0:T(8,128)(2,1)S(1)}, bf16[2,32,2048]{2,1,0:T(8,128)(2,1)S(1)}, u32[]{:S(2)}, u32[]{:S(2)}) collective-permute-start(bf16[2,32,2048]{2,1,0:T(8,128)(2,1)S(1)} %attend.6.refs_1_), channel_id=1, source_target_pairs={{0,10},{2,8},{4,14},{6,12},{8,2},{10,0},{12,6},{14,4},{1,11},{3,9}... | collective-permute-start | bytes 786440 | tf_op jit(solution)/shard_map/ppermute | solution.py:490
  102.5 23.2 %collective-permute-start.5 = (bf16[2,512,128]{2,1,0:T(8,128)(2,1)S(1)}, bf16[2,512,128]{2,1,0:T(8,128)(2,1)S(1)}, u32[]{:S(2)}, u32[]{:S(2)}) collective-permute-start(bf16[2,512,128]{2,1,0:T(8,128)(2,1)S(1)} %get-tuple-element.31._), channel_id=1, source_target_pairs={{0,8},{2,10},{4,12},{6,14},{8,0},{10,2},{12,4},{14,6},{1,9},{3,11}... | collective-permute-start | bytes 786440 | tf_op jit(solution)/shard_map/ppermute | solution.py:490
  107.5 33.7 %collective-permute-start.10 = (bf16[2,32,2048]{2,1,0:T(8,128)(2,1)S(1)}, bf16[2,32,2048]{2,1,0:T(8,128)(2,1)S(1)}, u32[]{:S(2)}, u32[]{:S(2)}) collective-permute-start(bf16[2,32,2048]{2,1,0:T(8,128)(2,1)S(1)} %get-tuple-element.34.refs_2_), channel_id=1, source_target_pairs={{0,12},{2,14},{4,8},{6,10},{8,4},{10,6},{12,0},{14,2},{1,13},{3,15... | collective-permute-start | bytes 786440 | tf_op jit(solution)/shard_map/ppermute | solution.py:490
  109.4 31.7 %collective-permute-start.11 = (bf16[2,32,2048]{2,1,0:T(8,128)(2,1)S(1)}, bf16[2,32,2048]{2,1,0:T(8,128)(2,1)S(1)}, u32[]{:S(2)}, u32[]{:S(2)}) collective-permute-start(bf16[2,32,2048]{2,1,0:T(8,128)(2,1)S(1)} %get-tuple-element.35), channel_id=1, source_target_pairs={{0,14},{2,12},{4,10},{6,8},{8,6},{10,4},{12,2},{14,0},{1,15},{3,13... | collective-permute-start | bytes 786440 | tf_op jit(solution)/shard_map/ppermute | solution.py:490
  125.7 1.6 %copy-start = (bf16[16,32,2048]{2,1,0:T(8,128)(2,1)S(1)}, bf16[16,32,2048]{2,1,0:T(8,128)(2,1)}, u32[]{:S(2)}) copy-start(bf16[16,32,2048]{2,1,0:T(8,128)(2,1)} %unpack.3._.refs_1_) | copy-start | bytes 6291460
  131.8 16.0 %all-to-all-start.1 = ((bf16[8,2,32,256]{3,2,1,0:T(8,128)(2,1)}), bf16[8,2,32,256]{3,2,1,0:T(8,128)(2,1)S(1)}, u32[]{:S(2)}, u32[]{:S(2)}) async-start(bf16[8,2,32,256]{3,2,1,0:T(8,128)(2,1)} %attend_extra.1.refs_2_), calls=%async_computation.1 | async-start | bytes 524288 | tf_op jit(solution)/shard_map/all_to_all | solution.py:555
  (1 other events, 0.7 us)

commit v4 on v2

v4 whole, which is shorter than its diff:
```python
import functools

import jax
import jax.numpy as jnp
import numpy as np
from jax import lax
from jax.experimental import pallas as pl
from jax.experimental.pallas import tpu as pltpu
from jax.sharding import PartitionSpec as P

HEAD_DIM = 128
HOT = 4
EPS = 1e-06
LOG2E = 1.4426950408889634
MIB = 1 << 20
AHEAD = 16
PACK_VMEM = 60
ATTEND_FLOPS = 20 << 30
MIX_FLOPS = 100 << 30
PACK_FLOPS = 20 << 30


def cost(flops):
    return pl.CostEstimate(flops=flops, bytes_accessed=1000, transcendentals=0)


def halves(array):
    high = array.astype(jnp.bfloat16)
    low = (array - high.astype(jnp.float32)).astype(jnp.bfloat16)
    return high, low


def transforms(taps):
    size = 2 * taps
    odd = 2 * np.arange(taps) + 1
    angle = np.pi / size * ((odd[:, None] * np.arange(size)[None, :]) % (2 * size))
    forward = np.concatenate([np.cos(angle), -np.sin(angle)], 0)
    inverse = forward.T[taps:] * (2.0 / size)
    out = []
    for matrix in (forward, inverse):
        high = matrix.astype(jnp.bfloat16)
        low = (matrix - high.astype(np.float64)).astype(jnp.bfloat16)
        out.append(np.concatenate([high, low], 0))
    return out


def unit(block):
    return block * lax.rsqrt(jnp.mean(block * block, axis=-1, keepdims=True) + EPS)


def mix_kernel(gate, key, value, earlier, filters, forward, inverse, _, out, rows_of, keys_of):
    rows, wide = gate.shape
    taps = filters.shape[1]
    size = 2 * taps
    f32 = jnp.float32
    fwd = forward[...]
    inv = inverse[...]
    high, low = halves(filters[...])
    across = (((1,), (1,)), ((), ()))
    both = lax.dot_general(fwd[:, :taps], high, across, preferred_element_type=f32)
    spectrum = both[:size] + both[size:]
    spectrum += lax.dot_general(fwd[:size, :taps], low, across, preferred_element_type=f32)
    hr, hi = spectrum[:taps], spectrum[taps:]
    before = earlier[...]
    for start in range(0, rows, taps):
        part = slice(start, start + taps)
        now = (key[part, :].astype(f32) * value[part, :].astype(f32)).astype(jnp.bfloat16)
        both = jnp.dot(fwd, jnp.concatenate([before, now], 0), preferred_element_type=f32)
        seen = both[:size] + both[size:]
        xr, xi = seen[:taps], seen[taps:]
        product = jnp.concatenate([xr * hr - xi * hi, xr * hi + xi * hr], 0)
        high, low = halves(product)
        both = jnp.dot(inv, high, preferred_element_type=f32)
        mixed = both[:taps] + both[taps:]
        mixed += jnp.dot(inv[:taps], low, preferred_element_type=f32)
        result = (gate[part, :].astype(f32) * mixed).astype(jnp.bfloat16)
        out[part, :] = result
        for head in range(wide // HEAD_DIM):
            piece = result[:, head * HEAD_DIM : (head + 1) * HEAD_DIM]
            rows_of[head, part, :] = piece
            keys_of[head, :, part] = unit(piece.astype(f32)).astype(jnp.bfloat16).T
        before = now


def mix(gate, key, value, earlier, filters, after):
    rows, chans = gate.shape
    taps = filters.shape[1]
    heads = chans // HEAD_DIM
    wide = 2 * HEAD_DIM
    each = wide // HEAD_DIM
    forward, inverse = (jnp.asarray(matrix) for matrix in transforms(taps))
    stream = pl.BlockSpec((rows, wide), lambda i: (0, i))
    by_head = pl.BlockSpec((each, rows, HEAD_DIM), lambda i: (i, 0, 0))
    whole = lambda array: pl.BlockSpec(array.shape, lambda i: (0, 0))
    turned = pl.BlockSpec((each, HEAD_DIM, rows), lambda i: (i, 0, 0))
    per_head = jax.ShapeDtypeStruct((heads, rows, HEAD_DIM), jnp.bfloat16)
    per_head_turned = jax.ShapeDtypeStruct((heads, HEAD_DIM, rows), jnp.bfloat16)
    return pl.pallas_call(
        mix_kernel,
        grid=(chans // wide,),
        in_specs=[
            stream,
            stream,
            stream,
            pl.BlockSpec((taps, wide), lambda i: (0, i)),
            pl.BlockSpec((wide, taps), lambda i: (i, 0)),
            whole(forward),
            whole(inverse),
            pl.BlockSpec(memory_space=pl.ANY),
        ],
        out_specs=[stream, by_head, turned],
        out_shape=[jax.ShapeDtypeStruct((rows, chans), jnp.bfloat16), per_head, per_head_turned],
        compiler_params=pltpu.CompilerParams(vmem_limit_bytes=48 * MIB),
        cost_estimate=cost(MIX_FLOPS),
        name="mix",
    )(gate, key, value, earlier, filters, forward, inverse, after)


def softened(query, keys, rows, heat, live):
    f32 = jnp.float32
    query = unit(query).astype(jnp.bfloat16)
    scores = jnp.dot(query, keys, preferred_element_type=f32)
    weights = jnp.where(live, jnp.exp2(scores * heat), 0.0)
    total = jnp.sum(weights, axis=-1, keepdims=True)
    return jnp.dot(weights.astype(jnp.bfloat16), rows, preferred_element_type=f32) / total


def masks(offsets, first, slots, tokens, positions):
    place = lax.broadcasted_iota(jnp.int32, (tokens, positions), 1)
    return jnp.concatenate([place < offsets[first + slot] for slot in range(slots)], 0)


def attend_heads(info, temps, keys, rows, places, first, last):
    positions = keys.shape[2]
    slots, tokens = places[0][:2]
    each = slots * tokens
    live = masks(info, info.shape[0] - AHEAD, slots, tokens, positions)
    live = jnp.concatenate([live] * len(places), 0)

    def one(head, carry):
        query = [load(head).astype(jnp.float32).reshape(each, HEAD_DIM) for _, _, load, _ in places]
        heat = temps[head] * (LOG2E / HEAD_DIM)
        done = softened(jnp.concatenate(query, 0), keys[head], rows[head], heat, live)
        for place, (_, _, _, store) in enumerate(places):
            part = done[place * each : (place + 1) * each].reshape(slots, tokens, HEAD_DIM)
            store(head, part.astype(jnp.bfloat16))
        return carry

    lax.fori_loop(first, last, one, 0, unroll=2 if (last - first) % 2 == 0 else 1)


def columns(head):
    return pl.ds(pl.multiple_of(head * HEAD_DIM, HEAD_DIM), HEAD_DIM)


def loader(ref, shift, *at):
    return lambda head: ref[at + (slice(None), slice(None), columns(head - shift))]


def storer(ref, shift, *at):
    def store(head, block):
        ref[at + (slice(None), slice(None), columns(head - shift))] = block

    return store


def near_kernel(info, temps, keys, rows, _, near, out):
    half, slots, tokens, _ = near.shape
    places = [(slots, tokens, loader(near, 0, at), storer(out, 0, at)) for at in range(half)]
    attend_heads(info, temps, keys, rows, places, 0, keys.shape[0])


def first_kernel(tail, info, temps, keys, rows, _, queries, rest, out, kept):
    slots, tokens, _ = queries.shape
    heads = keys.shape[0]
    split = heads - 2 * tail
    for_out = [(slots, tokens, loader(queries, 0), storer(out, 0))]
    attend_heads(info, temps, keys, rows, for_out, 0, split)
    for_kept = [(slots, tokens, loader(queries, 0), storer(kept, split))]
    attend_heads(info, temps, keys, rows, for_kept, split, heads - tail)
    part = slice(split * HEAD_DIM, (split + tail) * HEAD_DIM)
    home = on_hot_half(info, out_peers(heads, tail))

    @pl.when(home)
    def _():
        out[:, :, part] = kept[...]

    @pl.when(jnp.logical_not(home))
    def _():
        out[:, :, part] = rest[...]


def second_kernel(tail, step, info, temps, keys, rows, extra, _, queries, later, kept, out, held):
    slots, tokens, _ = queries.shape
    heads = keys.shape[0]
    split = heads - 2 * tail
    home = on_hot_half(info, out_peers(heads, tail))

    @pl.when(home)
    def _():
        held[...] = later[:, :, split * HEAD_DIM :]

    @pl.when(jnp.logical_not(home))
    def _():
        held[...] = queries[:, :, (split + tail) * HEAD_DIM :]

    places = [(slots, tokens, loader(held, heads - tail), storer(out, heads - tail))]
    attend_heads(info, temps, keys, rows, places, heads - tail, heads)
    part = slice(tail * HEAD_DIM, 2 * tail * HEAD_DIM)

    @pl.when(home)
    def _():
        out[:, :, part] = extra[jnp.bitwise_xor(lax.axis_index("pos"), step)]

    @pl.when(jnp.logical_not(home))
    def _():
        out[:, :, part] = kept[...]


def out_peers(heads, tail):
    return 2 * (heads // tail)


def on_hot_half(info, peers):
    half = peers // 2
    return (lax.axis_index("pos") >= half) == (info[info.shape[0] - 1] >= half)


def attend(kernel, name, widths, info, temps, keys, rows, refs, unread, arrays, scratch=()):
    scalars = pl.BlockSpec(memory_space=pltpu.SMEM)
    vector = pl.BlockSpec(memory_space=pltpu.VMEM)
    anywhere = pl.BlockSpec(memory_space=pl.ANY)
    leading = arrays[0].shape[:-1]
    return pl.pallas_call(
        kernel,
        in_specs=[scalars, scalars, vector, vector]
        + [vector] * len(refs)
        + [anywhere]
        + [vector] * len(arrays),
        out_specs=[vector] * len(widths),
        out_shape=[
            jax.ShapeDtypeStruct(leading + (width * HEAD_DIM,), jnp.bfloat16) for width in widths
        ],
        scratch_shapes=list(scratch),
        compiler_params=pltpu.CompilerParams(vmem_limit_bytes=16 * MIB),
        cost_estimate=cost(ATTEND_FLOPS),
        name=name,
    )(info, temps, keys, rows, *refs, unread, *arrays)


def finish_kernel(extra, near, out):
    half, _, _, chans = near.shape
    base = jnp.bitwise_and(lax.axis_index("pos"), half)
    out[:, :, :, :chans] = near[...]
    for at in range(half):
        out[at, :, :, chans:] = extra[base + at]


def finish(extra, near):
    vector = pl.BlockSpec(memory_space=pltpu.VMEM)
    held = near.shape[3] + extra.shape[3]
    return pl.pallas_call(
        finish_kernel,
        in_specs=[vector] * 2,
        out_specs=vector,
        out_shape=jax.ShapeDtypeStruct(near.shape[:3] + (held,), jnp.bfloat16),
        compiler_params=pltpu.CompilerParams(vmem_limit_bytes=24 * MIB),
        cost_estimate=cost(1000),
        name="finish",
    )(extra, near)


def extra_kernel(info, temps, rows, _, near, *refs):
    far, out = refs[:-1], refs[-1]
    half, extras, tokens, wide = near.shape
    me = lax.axis_index("pos")
    hot = jnp.bitwise_and(info[info.shape[0] - 1], half - 1)
    each = wide // HEAD_DIM
    first = jnp.bitwise_and(me, half - 1) * each
    live = masks(info, info.shape[0] - AHEAD + HOT, extras, tokens, rows.shape[2])
    live = jnp.concatenate([live] * half, 0)
    base = jnp.bitwise_and(me, half)
    for head in range(each):
        cols = slice(head * HEAD_DIM, (head + 1) * HEAD_DIM)
        valued = rows[hot, head]
        keyed = unit(valued.astype(jnp.float32)).astype(jnp.bfloat16).T
        heat = temps[first + head] * (LOG2E / HEAD_DIM)
        for side in range(2):
            query = [source[:, :, cols] for source in far] if side else [near[:, :, :, cols]]
            query = [part.astype(jnp.float32).reshape(-1, HEAD_DIM) for part in query]
            done = softened(jnp.concatenate(query, 0), keyed, valued, heat, live)
            done = done.reshape(half, extras, tokens, HEAD_DIM).astype(jnp.bfloat16)
            for at in range(half):
                peer = jnp.bitwise_xor(me, half + at) if side else base + at
                out[pl.ds(peer, 1), :, :, cols] = done[at : at + 1]


def attend_extra(info, temps, rows, after, near, far, wide):
    half, extras, tokens, held = near.shape
    scalars = pl.BlockSpec(memory_space=pltpu.SMEM)
    return pl.pallas_call(
        extra_kernel,
        grid=(1,),
        in_specs=[
            scalars,
            scalars,
            pl.BlockSpec(rows.shape, lambda i: (0, 0, 0, 0)),
            pl.BlockSpec(memory_space=pl.ANY),
            pl.BlockSpec((half, extras, tokens, wide), lambda i: (0, 0, 0, held // wide - 1)),
        ]
        + [pl.BlockSpec((extras, tokens, wide), lambda i: (0, 0, held // wide - 2))] * half,
        out_specs=pl.BlockSpec((2 * half, extras, tokens, wide), lambda i: (0, 0, 0, 0)),
        out_shape=jax.ShapeDtypeStruct((2 * half, extras, tokens, wide), jnp.bfloat16),
        compiler_params=pltpu.CompilerParams(vmem_limit_bytes=16 * MIB),
        cost_estimate=cost(ATTEND_FLOPS),
        name="attend_extra",
    )(info, temps, rows, after, near, *far)


def route(info, peers, slots, extras, rows, blocks, sites):
    me = lax.axis_index("pos")
    ahead = info.shape[0] - AHEAD
    hot_at = info.shape[0] - 1

    def clear(at, carry):
        info[at] = -1
        return carry

    lax.fori_loop(0, info.shape[0], clear, 0)
    for window in range(blocks.shape[0]):
        block = blocks[window]
        count = jnp.int32(0)
        for slot in range(HOT - 1):
            count += (info[block * HOT + slot] >= 0).astype(jnp.int32)
        info[block * HOT + count] = window

        @pl.when(count == HOT - 1)
        def _():
            info[hot_at] = block

    hot = info[hot_at]

    def offset(entry):
        window = info[entry]
        site = sites[jnp.maximum(window, 0)]
        return jnp.where(window >= 0, site - rows * (entry // HOT), rows)

    for slot in range(HOT):
        info[ahead + slot] = offset(me * HOT + slot)
    for extra in range(extras):
        info[ahead + HOT + extra] = offset(hot * HOT + slots + extra)


def copied(copies, sems):
    copies = [pltpu.make_async_copy(*pair, sems.at[at]) for at, pair in enumerate(copies)]
    for copy in copies:
        copy.start()
    for copy in copies:
        copy.wait()


def message(info, queries, peer, out, wide, extras, start, count, with_extras):
    slots, _, held = out.shape
    hot = info[info.shape[0] - 1]
    copies = []
    for slot in range(slots):
        window = jnp.maximum(info[peer * HOT + slot], 0)
        source = queries.at[window, :, pl.ds(start, count)]
        copies.append((source, out.at[slot, :, pl.ds(0, count)]))
    half = queries.shape[2] // wide
    share = pl.multiple_of(jnp.bitwise_and(peer, half - 1) * wide, wide)
    for extra in range(extras if held > count else 0):
        window = info[hot * HOT + slots + extra]
        column = share
        if with_extras is not None:
            window = jnp.where(with_extras, window, jnp.maximum(info[peer * HOT + extra], 0))
            column = pl.multiple_of(jnp.where(with_extras, share, start + count), wide)
        source = queries.at[window, :, pl.ds(column, wide)]
        copies.append((source, out.at[extra, :, pl.ds(count, wide)]))
    return copies


def far_copies(info, queries, steps, far, rest, wide, extras):
    half = queries.shape[2] // wide
    me = lax.axis_index("pos")
    away = jnp.logical_not(on_hot_half(info, 2 * half))
    chans = queries.shape[2]
    copies = []
    for step, out, other in zip(steps, far, rest):
        peer = jnp.bitwise_xor(me, step)
        copies += message(info, queries, peer, out, wide, extras, 0, chans - wide, away)
        copies += message(info, queries, peer, other, wide, extras, chans - wide, wide, None)
    return copies


def pack_kernel(extras, rows, wide, blocks, sites, queries, _, info, near, *refs):
    half, slots, _, _ = near.shape
    outs, (sems, blocks_held, sites_held, pair) = refs[:-4], refs[-4:]
    count = len(outs) // 2
    copied([(blocks, blocks_held), (sites, sites_held)], pair)
    route(info, 2 * half, slots, extras, rows, blocks_held, sites_held)
    base = jnp.bitwise_and(lax.axis_index("pos"), half)
    chans = queries.shape[2]
    steps = range(half, half + count)
    copies = far_copies(info, queries, steps, outs[:count], outs[count:], wide, extras)
    for at in range(half):
        copies += message(info, queries, base + at, near.at[at], wide, extras, 0, chans, None)
    copied(copies, sems)


def pack_later_kernel(extras, wide, steps, info, queries, _, *refs):
    outs, sems = refs[:-1], refs[-1]
    count = len(outs) // 2
    copied(far_copies(info, queries, steps, outs[:count], outs[count:], wide, extras), sems)


def far_shapes(queries, slots, wide, count):
    _, tokens, chans = queries.shape
    return [jax.ShapeDtypeStruct((slots, tokens, chans), queries.dtype)] * count + [
        jax.ShapeDtypeStruct((slots, tokens, wide), queries.dtype)
    ] * count


def pack(blocks, sites, queries, tail, rows, half, slots, extras, wide, count):
    windows, tokens, chans = queries.shape
    scalars = pl.BlockSpec(memory_space=pltpu.SMEM)
    vector = pl.BlockSpec(memory_space=pltpu.VMEM)
    anywhere = pl.BlockSpec(memory_space=pl.ANY)
    info, near, *far = pl.pallas_call(
        functools.partial(pack_kernel, extras, rows, wide),
        in_specs=[anywhere] * 4,
        out_specs=[scalars] + [vector] * (1 + 2 * count),
        out_shape=[
            jax.ShapeDtypeStruct((2 * half * HOT + AHEAD,), jnp.int32),
            jax.ShapeDtypeStruct((half, slots, tokens, chans + wide), queries.dtype),
        ]
        + far_shapes(queries, slots, wide, count),
        scratch_shapes=[
            pltpu.SemaphoreType.DMA(((half + count) * (slots + extras) + count * slots,)),
            pltpu.SMEM((windows,), jnp.int32),
            pltpu.SMEM((windows,), jnp.int32),
            pltpu.SemaphoreType.DMA((2,)),
        ],
        compiler_params=pltpu.CompilerParams(vmem_limit_bytes=PACK_VMEM * MIB),
        cost_estimate=cost(PACK_FLOPS),
        name="pack",
    )(blocks, sites, queries, tail)
    return info, near, far[:count], far[count:]


def pack_later(info, queries, after, steps, slots, extras, wide):
    count = len(steps)
    vector = pl.BlockSpec(memory_space=pltpu.VMEM)
    anywhere = pl.BlockSpec(memory_space=pl.ANY)
    far = pl.pallas_call(
        functools.partial(pack_later_kernel, extras, wide, steps),
        in_specs=[pl.BlockSpec(memory_space=pltpu.SMEM), anywhere, anywhere],
        out_specs=[vector] * (2 * count),
        out_shape=far_shapes(queries, slots, wide, count),
        scratch_shapes=[pltpu.SemaphoreType.DMA((count * (2 * slots + extras),))],
        compiler_params=pltpu.CompilerParams(vmem_limit_bytes=PACK_VMEM * MIB),
        cost_estimate=cost(1000),
        name="pack_later",
    )(info, queries, after)
    return far[:count], far[count:]


def placed(info, out, sems, pieces):
    def each(act):
        at = 0
        for peer, result, start, count, column, whether in pieces:
            for slot in range(result.shape[0]):
                window = info[peer * HOT + slot]
                source = result.at[slot, :, pl.ds(start, count)]
                target = out.at[jnp.maximum(window, 0), :, pl.ds(column, count)]
                copy = pltpu.make_async_copy(source, target, sems.at[at])
                pl.when(jnp.logical_and(window >= 0, whether))(functools.partial(act, copy))
                at += 1

    each(lambda copy: copy.start())
    return lambda: each(lambda copy: copy.wait())


def unpack_early_kernel(wide, info, *refs):
    results, out, sems = refs[:-3], refs[-2], refs[-1]
    half = len(results)
    me = lax.axis_index("pos")
    home = on_hot_half(info, 2 * half)
    split = out.shape[2] - 2 * wide
    pieces = []
    for at, result in enumerate(results):
        peer = jnp.bitwise_xor(me, half + at)
        pieces.append((peer, result, 0, split, 0, True))
        pieces.append((peer, result, split, wide, split, jnp.logical_not(home)))
    placed(info, out, sems, pieces)()


def unpack_early(info, results, after, shape, wide):
    anywhere = pl.BlockSpec(memory_space=pl.ANY)
    count = len(results)
    return pl.pallas_call(
        functools.partial(unpack_early_kernel, wide),
        in_specs=[pl.BlockSpec(memory_space=pltpu.SMEM)]
        + [pl.BlockSpec(memory_space=pltpu.VMEM)] * count
        + [anywhere],
        out_specs=anywhere,
        out_shape=jax.ShapeDtypeStruct(shape, results[0].dtype),
        scratch_shapes=[pltpu.SemaphoreType.DMA((2 * count * results[0].shape[0],))],
        compiler_params=pltpu.CompilerParams(vmem_limit_bytes=16 * MIB),
        cost_estimate=cost(1000),
        name="unpack_early",
    )(info, *results, after)


def unpack_kernel(wide, info, near, *refs):
    half, slots, _, _ = near.shape
    far, (_, out, own, far_sems, near_sems, own_sems) = refs[:half], refs[half:]
    chans = out.shape[2]
    split = chans - 2 * wide
    me = lax.axis_index("pos")
    base = jnp.bitwise_and(me, half)
    hot = info[info.shape[0] - 1]
    home = on_hot_half(info, 2 * half)
    pieces = []
    for at, result in enumerate(far):
        peer = jnp.bitwise_xor(me, half + at)
        pieces.append((peer, result, 0, wide, split + wide, True))
        pieces.append((peer, result, wide, wide, split, home))
    far_wait = placed(info, out, far_sems, pieces)
    pieces = [(base + at, near.at[at], 0, chans, 0, True) for at in range(half)]
    near_wait = placed(info, out, near_sems, pieces)
    copies = []
    for extra in range(own.shape[0]):

        @pl.when(home)
        def _():
            for at in range(half):
                own[extra, :, at * wide : (at + 1) * wide] = near[at, extra, :, chans:]

        @pl.when(jnp.logical_not(home))
        def _():
            for at, result in enumerate(far):
                share = jnp.bitwise_and(jnp.bitwise_xor(me, at), half - 1)
                cols = pl.ds(pl.multiple_of(share * wide, wide), wide)
                own[extra, :, cols] = result[extra, :, wide:]

        window = info[hot * HOT + slots + extra]
        copies.append(pltpu.make_async_copy(own.at[extra], out.at[window], own_sems.at[extra]))
        copies[-1].start()
    far_wait()
    near_wait()
    for copy in copies:
        copy.wait()


def unpack(info, near, far, so_far, extras, wide):
    half, slots, tokens, _ = near.shape
    anywhere = pl.BlockSpec(memory_space=pl.ANY)
    return pl.pallas_call(
        functools.partial(unpack_kernel, wide),
        in_specs=[pl.BlockSpec(memory_space=pltpu.SMEM)]
        + [pl.BlockSpec(memory_space=pltpu.VMEM)] * (1 + half)
        + [anywhere],
        out_specs=anywhere,
        out_shape=jax.ShapeDtypeStruct(so_far.shape, so_far.dtype),
        input_output_aliases={2 + half: 0},
        scratch_shapes=[
            pltpu.VMEM((extras, tokens, so_far.shape[2]), so_far.dtype),
            pltpu.SemaphoreType.DMA((2 * half * slots,)),
            pltpu.SemaphoreType.DMA((half * slots,)),
            pltpu.SemaphoreType.DMA((extras,)),
        ],
        compiler_params=pltpu.CompilerParams(vmem_limit_bytes=24 * MIB),
        cost_estimate=cost(1000),
        name="unpack",
    )(info, near, *far, so_far)


def wait_kernel(*_):
    pass


def once(value, after):
    anywhere = pl.BlockSpec(memory_space=pl.ANY)
    return pl.pallas_call(
        wait_kernel,
        in_specs=[anywhere] * 2,
        out_specs=anywhere,
        out_shape=jax.ShapeDtypeStruct(value.shape, value.dtype),
        input_output_aliases={0: 0},
        cost_estimate=cost(1000),
        name="once",
    )(value, after)


def exchanged(value, step):
    peers = lax.axis_size("pos")
    if step == 0:
        return value
    return lax.ppermute(value, "pos", [(i, i ^ step) for i in range(peers)])


def exchanged_near(value):
    peers = lax.axis_size("pos")
    half = peers // 2
    groups = [list(range(half)), list(range(half, peers))]
    return lax.all_to_all(value, "pos", 0, 0, axis_index_groups=groups, tiled=True)


def shards(gate_stream, key_stream, value_stream, filters, temps, queries, blocks, sites):
    rows, chans = gate_stream.shape
    taps = filters.shape[1]
    peers = lax.axis_size("pos")
    me = lax.axis_index("pos").astype(jnp.int32)
    windows = blocks.shape[0]
    heads = chans // HEAD_DIM
    extras = 2
    slots = HOT - extras
    half = peers // 2

    last = slice(rows - taps, rows)
    tail = key_stream[last].astype(jnp.float32) * value_stream[last].astype(jnp.float32)
    tail = tail.astype(jnp.bfloat16)
    earlier = lax.ppermute(tail, "pos", [(i, i + 1) for i in range(peers - 1)])
    wide = chans // half
    share = heads // half
    ahead = half // 2
    info, near, far, rest = pack(
        blocks, sites, queries, tail, rows, half, slots, extras, wide, ahead
    )
    far = [exchanged(sent, half + at) for at, sent in enumerate(far)]
    near = exchanged_near(near)
    hyena_out, valued, keyed = mix(
        gate_stream, key_stream, value_stream, earlier, filters, info
    )
    valued = once(valued, near)
    hot_rows = exchanged_near(valued).reshape((half, share) + valued.shape[1:])
    steps = range(half + ahead, peers)
    far_later, rest_later = pack_later(info, queries, valued, steps, slots, extras, wide)
    far += [exchanged(sent, step) for step, sent in zip(steps, far_later)]
    rest += rest_later

    own = (info, temps, keyed, valued)
    (near_results,) = attend(near_kernel, "attend_near", [heads], *own, [], valued, [near])
    sent, kept, after = [], [], near_results
    for at in range(half):
        kernel = functools.partial(first_kernel, share)
        result, back = attend(
            kernel, "attend_first", [heads - share, share], *own, [], after, [far[at], rest[at]]
        )
        sent.append(exchanged(result, half + at))
        kept.append(back)
        after = result
    extra = attend_extra(info, temps, hot_rows, after, near, far, wide)
    near_out = exchanged_near(finish(extra, near_results))
    late, after = [], extra
    for at in range(half):
        kernel = functools.partial(second_kernel, share, half + at)
        arrays = [far[at], sent[at], kept[at]]
        scratch = [pltpu.VMEM(kept[at].shape, jnp.bfloat16)]
        (result,) = attend(
            kernel, "attend_second", [2 * share], *own, [extra], after, arrays, scratch
        )
        late.append(exchanged(result, half + at))
        after = result
    so_far = unpack_early(info, sent, after, queries.shape, wide)
    return (hyena_out, unpack(info, near_out, late, so_far, extras, wide))


def solution(mesh):
    placed = (
        P(("groups", "pos"), "mp"),
        P(("groups", "pos"), "mp"),
        P(("groups", "pos"), "mp"),
        P("mp", None),
        P("mp"),
        P("groups", "pos", "mp"),
        P("groups"),
        P("groups"),
    )
    return jax.shard_map(
        shards,
        mesh=mesh,
        in_specs=placed,
        out_specs=(P(("groups", "pos"), "mp"), P("groups", "pos", "mp")),
        check_vma=False,
    )
```

time: 214 us -> 148 us (0.69)
  waiting for transfers between devices: 63.7 us -> 23.2 us
  local copies, waits for them, and re-layouts: 29.8 us -> 12 us
  starting transfers between devices: 57.5 us -> 46.2 us
  Pallas kernels: 57.1 us -> 62.9 us
    ppermute x17 -> x12, waiting for transfers between devices: 52.6 us -> 16.3 us  [exchanged(): return lax.ppermute(value, 'pos', [(i, i ^ step) for i in range(peers)])]
    ppermute x17 -> x12, starting transfers between devices: 46.3 us -> 29.2 us  [exchanged(): return lax.ppermute(value, 'pos', [(i, i ^ step) for i in range(peers)])]
    unnamed x62, local copies, waits for them, and re-layouts: 27.3 us -> 12 us
    ppermute x1, waiting for transfers between devices: 11.1 us -> 0.94 us  [shards(): earlier = lax.ppermute(tail, 'pos', [(i, i + 1) for i in range(peers - 1)])]
    pallas_call x10 -> x15, Pallas kernels: 39.3 us -> 45.6 us  [the longest x9 32.9 us: attend(): pl.pallas_call(kernel, in_specs=[scalars, scalars, vector, vector] + [vec...]
    all_to_all x1 -> x3, waiting for transfers between devices: 0.01 us -> 5.96 us  [exchanged_near(): lax.all_to_all(value, 'pos', 0, 0, axis_index_groups=groups, tiled=True)]
    all_to_all x1 -> x3, starting transfers between devices: 6.33 us -> 12.1 us  [exchanged_near(): lax.all_to_all(value, 'pos', 0, 0, axis_index_groups=groups, tiled=True)]
    select_n x3 -> x0, other arithmetic: 2.57 us -> none  [spread(): held = jnp.where(have, kept, arrived)]
  transfers between devices with their start and end apart: 19 -> 16, of which waited for: 5 -> 6; matrix products, arithmetic and copies ran while one was open for 1% -> 0% of each run, Pallas kernels for 18% -> 41%
where the time goes in v4:
time: 148 us; the launch traced here: 147 us
  Pallas kernels  62.9 us (42%)
  starting transfers between devices  46.2 us (31%)
  waiting for transfers between devices  23.2 us (16%)
  local copies, waits for them, and re-layouts  12 us (8%)
  other arithmetic  2.12 us (1%)
    pallas_call x9, Pallas kernels, attend(): pl.pallas_call(kernel, in_specs=[scalars, scalars, vector, vector] + [vec...  32.9 us
    ppermute x12, starting transfers between devices, exchanged(): return lax.ppermute(value, 'pos', [(i, i ^ step) for i in range(peers)])  29.2 us
    ppermute x12, waiting for transfers between devices, exchanged(): return lax.ppermute(value, 'pos', [(i, i ^ step) for i in range(peers)])  16.3 us
    pallas_call x1, Pallas kernels, mix(): pl.pallas_call(mix_kernel, grid=(chans // wide,), in_specs=[stream, strea...  13.5 us
    all_to_all x3, starting transfers between devices, exchanged_near(): lax.all_to_all(value, 'pos', 0, 0, axis_index_groups=groups, tiled=True)  12.1 us
    unnamed x62, local copies, waits for them, and re-layouts  12 us
    all_to_all x3, waiting for transfers between devices, exchanged_near(): lax.all_to_all(value, 'pos', 0, 0, axis_index_groups=groups, tiled=True)  5.96 us
    ppermute x1, starting transfers between devices, shards(): earlier = lax.ppermute(tail, 'pos', [(i, i + 1) for i in range(peers - 1)])  4.89 us
  transfers between devices with their start and end apart: 16, of which 6 were waited for; matrix products, arithmetic and copies ran while one was open for 0% of the time, Pallas kernels for 41%

profile of v4, /device:TPU:0, one launch (start us, length us, event | category | flops | bytes accessed | tf_op | source)
XLA Modules:
  0.0 147.4 jit_solution(7212662661781746832)
XLA Ops:
  0.6 2.1 %multiply_convert_fusion._ = bf16[128,2048]{1,0:T(8,128)(2,1)} fusion(bf16[512,2048]{1,0:T(8,128)(2,1)} %value.1, bf16[512,2048]{1,0:T(8,128)(2,1)} %key.1), kind=kLoop, calls=%fused_computation | loop fusion | flops 1048576 | bytes 1572864 | tf_op jit(solution)/shard_map/convert_element_type | solution.py:623
  2.8 4.9 %collective-permute-start = (bf16[128,2048]{1,0:T(8,128)(2,1)}, bf16[128,2048]{1,0:T(8,128)(2,1)S(1)}, u32[]{:S(2)}, u32[]{:S(2)}) collective-permute-start(bf16[128,2048]{1,0:T(8,128)(2,1)} %multiply_convert_fusion._), channel_id=1, source_target_pairs={{0,2},{2,4},{4,6},{6,8},{8,10},{10,12},{12,14},{1,3},{3,5},{5,7},{... | collective-permute-start | bytes 1572872 | tf_op jit(solution)/shard_map/ppermute | solution.py:624
  7.7 4.4 %pack.1 = (s32[48]{0:T(128)}, bf16[4,2,32,2560]{3,2,1,0:T(8,128)(2,1)}, bf16[2,32,2048]{2,1,0:T(8,128)(2,1)}, bf16[2,32,2048]{2,1,0:T(8,128)(2,1)}, bf16[2,32,51...) custom-call(s32[16]{0:T(128)} %blocks.1, s32[16]{0:T(128)} %sites.1, bf16[16,32,2048]{2,1,0:T(8,128)(2,1)} %queries.3, ...), custom_call_target="tpu_custom_call" | custom-call | flops 21474836480 | bytes 1000 | tf_op jit(solution)/shard_map/pack/pallas_call | solution.py:429
  12.1 3.9 %all-to-all-start = ((bf16[4,2,32,2560]{3,2,1,0:T(8,128)(2,1)}), bf16[4,2,32,2560]{3,2,1,0:T(8,128)(2,1)S(1)}, u32[]{:S(2)}, u32[]{:S(2)}) async-start(bf16[4,2,32,2560]{3,2,1,0:T(8,128)(2,1)} %get-tuple-element.26), calls=%async_computation | async-start | bytes 2621440 | tf_op jit(solution)/shard_map/all_to_all | solution.py:607
  16.0 2.4 %collective-permute-start.1 = (bf16[2,32,2048]{2,1,0:T(8,128)(2,1)}, bf16[2,32,2048]{2,1,0:T(8,128)(2,1)}, u32[]{:S(2)}, u32[]{:S(2)}) collective-permute-start(bf16[2,32,2048]{2,1,0:T(8,128)(2,1)} %get-tuple-element.28), channel_id=1, source_target_pairs={{0,8},{2,10},{4,12},{6,14},{8,0},{10,2},{12,4},{14,6},{1,9},{3,11}... | collective-permute-start | bytes 786440 | tf_op jit(solution)/shard_map/ppermute | solution.py:600
  18.4 2.0 %collective-permute-start.2 = (bf16[2,32,2048]{2,1,0:T(8,128)(2,1)}, bf16[2,32,2048]{2,1,0:T(8,128)(2,1)}, u32[]{:S(2)}, u32[]{:S(2)}) collective-permute-start(bf16[2,32,2048]{2,1,0:T(8,128)(2,1)} %get-tuple-element.31), channel_id=1, source_target_pairs={{0,10},{2,8},{4,14},{6,12},{8,2},{10,0},{12,6},{14,4},{1,11},{3,9}... | collective-permute-start | bytes 786440 | tf_op jit(solution)/shard_map/ppermute | solution.py:600
  21.3 13.5 %mix.1 = (bf16[512,2048]{1,0:T(8,128)(2,1)}, bf16[16,512,128]{2,1,0:T(8,128)(2,1)S(1)}, bf16[16,128,512]{2,1,0:T(8,128)(2,1)S(1)}) custom-call(bf16[512,2048]{1,0:T(8,128)(2,1)} %gate.1, bf16[512,2048]{1,0:T(8,128)(2,1)} %key.1, bf16[512,2048]{1,0:T(8,128)(2,1)} %value.1, bf16[128,2048]{1,0:T(8,128)(2,1)S(1)} %collective-permute-done.earlier, ...), custom_call_target="tpu_custom_call" | custom-call | flops 107374182400 | bytes 1000 | tf_op jit(solution)/shard_map/mix/pallas_call | solution.py:98
  37.5 6.0 %all-to-all-done.__1_.near = bf16[4,2,32,2560]{3,2,1,0:T(8,128)(2,1)S(1)} async-done(((bf16[4,2,32,2560]{3,2,1,0:T(8,128)(2,1)}), bf16[4,2,32,2560]{3,2,1,0:T(8,128)(2,1)S(1)}, u32[]{:S(2)}, u32[]{:S(2)}) %all-to-all-start) | async-done | bytes 1310752 | tf_op jit(solution)/shard_map/all_to_all | solution.py:607
  44.5 4.7 %all-to-all-start.1 = ((bf16[16,512,128]{2,1,0:T(8,128)(2,1)}), bf16[16,512,128]{2,1,0:T(8,128)(2,1)}, u32[]{:S(2)}, u32[]{:S(2)}) async-start(bf16[16,512,128]{2,1,0:T(8,128)(2,1)} %once.1.rows._), calls=%async_computation.1 | async-start | bytes 4194304 | tf_op jit(solution)/shard_map/all_to_all | solution.py:607
  49.2 3.1 %pack_later.1 = (bf16[2,32,2048]{2,1,0:T(8,128)(2,1)}, bf16[2,32,2048]{2,1,0:T(8,128)(2,1)}, bf16[2,32,512]{2,1,0:T(8,128)(2,1)}, bf16[2,32,512]{2,1,0:T(8,128)(2,1)}) custom-call(s32[48]{0:T(128)} %get-tuple-element.23._.info, bf16[16,32,2048]{2,1,0:T(8,128)(2,1)} %queries.3, bf16[16,512,128]{2,1,0:T(8,128)(2,1)} %once.1.rows._), custom_call_target="tpu_custom_call" | custom-call | flops 1000 | bytes 1000 | tf_op jit(solution)/shard_map/pack_later/pallas_call | solution.py:455
  52.3 9.6 %collective-permute-start.3 = (bf16[2,32,2048]{2,1,0:T(8,128)(2,1)}, bf16[2,32,2048]{2,1,0:T(8,128)(2,1)S(1)}, u32[]{:S(2)}, u32[]{:S(2)}) collective-permute-start(bf16[2,32,2048]{2,1,0:T(8,128)(2,1)} %get-tuple-element.34), channel_id=1, source_target_pairs={{0,12},{2,14},{4,8},{6,10},{8,4},{10,6},{12,0},{14,2},{1,13},{3,15... | collective-permute-start | bytes 786440 | tf_op jit(solution)/shard_map/ppermute | solution.py:600
  63.5 5.9 %attend_near.1._.near = bf16[4,2,32,2048]{3,2,1,0:T(8,128)(2,1)S(1)} custom-call(s32[48]{0:T(128)S(1)} %copy-done.9, f32[16]{0:T(128)S(1)} %copy-done.19, bf16[16,128,512]{2,1,0:T(8,128)(2,1)S(1)} %copy-done.23, bf16[16,512,128]{2,1,0:T(8,128)(2,1)S(1)} %copy-done.1, bf16[16,512,128]{2,1,0:T(8,128)(2,1)S(1)} %copy-done.1, bf16[4,2,32,2560]{3,2,1,0:T(8,128)(2,1)S(1)} %copy-done.3), custom_call_target="tpu_custom_call" | custom-call | flops 21474836480 | bytes 1000 | tf_op jit(solution)/shard_map/attend_near/pallas_call | solution.py:234
  69.4 5.1 %attend_first.4 = (bf16[2,32,1536]{2,1,0:T(8,128)(2,1)}, bf16[2,32,512]{2,1,0:T(8,128)(2,1)S(1)}) custom-call(s32[48]{0:T(128)S(1)} %copy-done.9, f32[16]{0:T(128)S(1)} %copy-done.19, bf16[16,128,512]{2,1,0:T(8,128)(2,1)S(1)} %copy-done.23, bf16[16,512,128]{2,1,0:T(8,128)(2,1)S(1)} %copy-done.1, bf16[4,2,32,2048]{3,2,1,0:T(8,128)(2,1)S(1)} %attend_near.1._.near, ...), custom_call_target="tpu_custom_call" | custom-call | flops 21474836480 | bytes 1000 | tf_op jit(solution)/shard_map/attend_first/pallas_call | solution.py:234
  75.4 4.8 %attend_first.5 = (bf16[2,32,1536]{2,1,0:T(8,128)(2,1)}, bf16[2,32,512]{2,1,0:T(8,128)(2,1)S(1)}) custom-call(s32[48]{0:T(128)S(1)} %copy-done.9, f32[16]{0:T(128)S(1)} %copy-done.19, bf16[16,128,512]{2,1,0:T(8,128)(2,1)S(1)} %copy-done.23, bf16[16,512,128]{2,1,0:T(8,128)(2,1)S(1)} %copy-done.1, bf16[2,32,1536]{2,1,0:T(8,128)(2,1)} %get-tuple-element.30._, ...), custom_call_target="tpu_custom_call" | custom-call | flops 21474836480 | bytes 1000 | tf_op jit(solution)/shard_map/attend_first/pallas_call | solution.py:234
  80.2 3.0 %collective-permute-start.7 = (bf16[2,32,1536]{2,1,0:T(8,128)(2,1)}, bf16[2,32,1536]{2,1,0:T(8,128)(2,1)}, u32[]{:S(2)}, u32[]{:S(2)}) collective-permute-start(bf16[2,32,1536]{2,1,0:T(8,128)(2,1)} %get-tuple-element.33._), channel_id=1, source_target_pairs={{0,10},{2,8},{4,14},{6,12},{8,2},{10,0},{12,6},{14,4},{1,11},{3,9}... | collective-permute-start | bytes 589832 | tf_op jit(solution)/shard_map/ppermute | solution.py:600
  83.3 5.3 %collective-permute-done.3.queries.refs_2_ = bf16[2,32,2048]{2,1,0:T(8,128)(2,1)S(1)} collective-permute-done((bf16[2,32,2048]{2,1,0:T(8,128)(2,1)}, bf16[2,32,2048]{2,1,0:T(8,128)(2,1)S(1)}, u32[]{:S(2)}, u32[]{:S(2)}) %collective-permute-start.3) | collective-permute-done | bytes 262176 | tf_op jit(solution)/shard_map/ppermute | solution.py:600
  88.6 4.4 %attend_first.6 = (bf16[2,32,1536]{2,1,0:T(8,128)(2,1)}, bf16[2,32,512]{2,1,0:T(8,128)(2,1)S(1)}) custom-call(s32[48]{0:T(128)S(1)} %copy-done.9, f32[16]{0:T(128)S(1)} %copy-done.19, bf16[16,128,512]{2,1,0:T(8,128)(2,1)S(1)} %copy-done.23, bf16[16,512,128]{2,1,0:T(8,128)(2,1)S(1)} %copy-done.1, bf16[2,32,1536]{2,1,0:T(8,128)(2,1)} %get-tuple-element.33._, ...), custom_call_target="tpu_custom_call" | custom-call | flops 21474836480 | bytes 1000 | tf_op jit(solution)/shard_map/attend_first/pallas_call | solution.py:234
  93.6 4.4 %attend_first.7 = (bf16[2,32,1536]{2,1,0:T(8,128)(2,1)}, bf16[2,32,512]{2,1,0:T(8,128)(2,1)S(1)}) custom-call(s32[48]{0:T(128)S(1)} %copy-done.9, f32[16]{0:T(128)S(1)} %copy-done.19, bf16[16,128,512]{2,1,0:T(8,128)(2,1)S(1)} %copy-done.23, bf16[16,512,128]{2,1,0:T(8,128)(2,1)S(1)} %copy-done.1, bf16[2,32,1536]{2,1,0:T(8,128)(2,1)} %get-tuple-element.36._, ...), custom_call_target="tpu_custom_call" | custom-call | flops 21474836480 | bytes 1000 | tf_op jit(solution)/shard_map/attend_first/pallas_call | solution.py:234
  100.5 3.8 %attend_extra.1.extra._ = bf16[8,2,32,512]{3,2,1,0:T(8,128)(2,1)S(1)} custom-call(s32[48]{0:T(128)S(1)} %copy-done.9, f32[16]{0:T(128)S(1)} %copy-done.19, bf16[4,4,512,128]{3,2,1,0:T(8,128)(2,1)} %bitcast.rows, bf16[2,32,1536]{2,1,0:T(8,128)(2,1)} %get-tuple-element.39._, bf16[4,2,32,2560]{3,2,1,0:T(8,128)(2,1)S(1)} %copy-done.3, ...), custom_call_target="tpu_custom_call" | custom-call | flops 21474836480 | bytes 1000 | tf_op jit(solution)/shard_map/attend_extra/pallas_call | solution.py:301
  104.4 3.7 %collective-permute-start.9 = (bf16[2,32,1536]{2,1,0:T(8,128)(2,1)}, bf16[2,32,1536]{2,1,0:T(8,128)(2,1)}, u32[]{:S(2)}, u32[]{:S(2)}) collective-permute-start(bf16[2,32,1536]{2,1,0:T(8,128)(2,1)} %get-tuple-element.36._), channel_id=1, source_target_pairs={{0,12},{2,14},{4,8},{6,10},{8,4},{10,6},{12,0},{14,2},{1,13},{3,15... | collective-permute-start | bytes 589832 | tf_op jit(solution)/shard_map/ppermute | solution.py:600
  110.0 3.5 %all-to-all-start.2 = ((bf16[4,2,32,2560]{3,2,1,0:T(8,128)(2,1)}), bf16[4,2,32,2560]{3,2,1,0:T(8,128)(2,1)S(1)}, u32[]{:S(2)}, u32[]{:S(2)}) async-start(bf16[4,2,32,2560]{3,2,1,0:T(8,128)(2,1)} %finish.1), calls=%async_computation.2 | async-start | bytes 2621440 | tf_op jit(solution)/shard_map/all_to_all | solution.py:607
  114.6 1.6 %copy-done.24 = bf16[16,128,512]{2,1,0:T(8,128)(2,1)S(1)} copy-done((bf16[16,128,512]{2,1,0:T(8,128)(2,1)S(1)}, bf16[16,128,512]{2,1,0:T(8,128)(2,1)}, u32[]{:S(2)}) %copy-start.24) | copy-done | bytes 2097176
  116.2 2.1 %attend_second.4._ = bf16[2,32,1024]{2,1,0:T(8,128)(2,1)S(1)} custom-call(s32[48]{0:T(128)S(1)} %copy-done.9, f32[16]{0:T(128)S(1)} %copy-done.19, bf16[16,128,512]{2,1,0:T(8,128)(2,1)S(1)} %copy-done.24, bf16[16,512,128]{2,1,0:T(8,128)(2,1)S(1)} %copy-done.1, bf16[8,2,32,512]{3,2,1,0:T(8,128)(2,1)S(1)} %copy-done.7, bf16[8,2,32,512]{3,2,1,0:T(8,128)(2,1)S(1)} %copy-done.7, ...), custom_call_target="tpu_custom_call" | custom-call | flops 21474836480 | bytes 1000 | tf_op jit(solution)/shard_map/attend_second/pallas_call | solution.py:234
  118.3 2.1 %attend_second.5._ = bf16[2,32,1024]{2,1,0:T(8,128)(2,1)S(1)} custom-call(s32[48]{0:T(128)S(1)} %copy-done.9, f32[16]{0:T(128)S(1)} %copy-done.19, bf16[16,128,512]{2,1,0:T(8,128)(2,1)S(1)} %copy-done.24, bf16[16,512,128]{2,1,0:T(8,128)(2,1)S(1)} %copy-done.1, bf16[8,2,32,512]{3,2,1,0:T(8,128)(2,1)S(1)} %copy-done.7, ...), custom_call_target="tpu_custom_call" | custom-call | flops 21474836480 | bytes 1000 | tf_op jit(solution)/shard_map/attend_second/pallas_call | solution.py:234
  120.5 2.1 %attend_second.6._ = bf16[2,32,1024]{2,1,0:T(8,128)(2,1)S(1)} custom-call(s32[48]{0:T(128)S(1)} %copy-done.9, f32[16]{0:T(128)S(1)} %copy-done.19, bf16[16,128,512]{2,1,0:T(8,128)(2,1)S(1)} %copy-done.24, bf16[16,512,128]{2,1,0:T(8,128)(2,1)S(1)} %copy-done.1, bf16[8,2,32,512]{3,2,1,0:T(8,128)(2,1)S(1)} %copy-done.7, ...), custom_call_target="tpu_custom_call" | custom-call | flops 21474836480 | bytes 1000 | tf_op jit(solution)/shard_map/attend_second/pallas_call | solution.py:234
  122.6 2.0 %attend_second.7.refs_4_ = bf16[2,32,1024]{2,1,0:T(8,128)(2,1)S(1)} custom-call(s32[48]{0:T(128)S(1)} %copy-done.9, f32[16]{0:T(128)S(1)} %copy-done.19, bf16[16,128,512]{2,1,0:T(8,128)(2,1)S(1)} %copy-done.24, bf16[16,512,128]{2,1,0:T(8,128)(2,1)S(1)} %copy-done.1, bf16[8,2,32,512]{3,2,1,0:T(8,128)(2,1)S(1)} %copy-done.7, ...), custom_call_target="tpu_custom_call" | custom-call | flops 21474836480 | bytes 1000 | tf_op jit(solution)/shard_map/attend_second/pallas_call | solution.py:234
  124.6 1.8 %collective-permute-start.12 = (bf16[2,32,1024]{2,1,0:T(8,128)(2,1)S(1)}, bf16[2,32,1024]{2,1,0:T(8,128)(2,1)S(1)}, u32[]{:S(2)}, u32[]{:S(2)}) collective-permute-start(bf16[2,32,1024]{2,1,0:T(8,128)(2,1)S(1)} %attend_second.7.refs_4_), channel_id=1, source_target_pairs={{0,14},{2,12},{4,10},{6,8},{8,6},{10,4},{12,2},{14,0},{1,15},{3,13... | collective-permute-start | bytes 393224 | tf_op jit(solution)/shard_map/ppermute | solution.py:600
  126.5 3.5 %collective-permute-start.10 = (bf16[2,32,1024]{2,1,0:T(8,128)(2,1)S(1)}, bf16[2,32,1024]{2,1,0:T(8,128)(2,1)S(1)}, u32[]{:S(2)}, u32[]{:S(2)}) collective-permute-start(bf16[2,32,1024]{2,1,0:T(8,128)(2,1)S(1)} %attend_second.6._), channel_id=1, source_target_pairs={{0,12},{2,14},{4,8},{6,10},{8,4},{10,6},{12,0},{14,2},{1,13},{3,15... | collective-permute-start | bytes 393224 | tf_op jit(solution)/shard_map/ppermute | solution.py:600
  129.9 2.4 %collective-permute-start.6 = (bf16[2,32,1024]{2,1,0:T(8,128)(2,1)S(1)}, bf16[2,32,1024]{2,1,0:T(8,128)(2,1)S(1)}, u32[]{:S(2)}, u32[]{:S(2)}) collective-permute-start(bf16[2,32,1024]{2,1,0:T(8,128)(2,1)S(1)} %attend_second.4._), channel_id=1, source_target_pairs={{0,8},{2,10},{4,12},{6,14},{8,0},{10,2},{12,4},{14,6},{1,9},{3,11}... | collective-permute-start | bytes 393224 | tf_op jit(solution)/shard_map/ppermute | solution.py:600
  132.3 2.1 %unpack_early.1.refs_4_ = bf16[16,32,2048]{2,1,0:T(8,128)(2,1)} custom-call(s32[48]{0:T(128)S(1)} %copy-done.9, bf16[2,32,1536]{2,1,0:T(8,128)(2,1)} %collective-permute-done.5.later.refs_0_, bf16[2,32,1536]{2,1,0:T(8,128)(2,1)} %collective-permute-done.7.later.refs_1_, bf16[2,32,1536]{2,1,0:T(8,128)(2,1)} %collective-permute-done.9.later.refs_2_, ...), custom_call_target="tpu_custom_call" | custom-call | flops 1000 | bytes 1000 | tf_op jit(solution)/shard_map/unpack_early/pallas_call | solution.py:501
  134.7 10.2 %collective-permute-done.8.refs_1_ = bf16[2,32,1024]{2,1,0:T(8,128)(2,1)S(1)} collective-permute-done((bf16[2,32,1024]{2,1,0:T(8,128)(2,1)S(1)}, bf16[2,32,1024]{2,1,0:T(8,128)(2,1)S(1)}, u32[]{:S(2)}, u32[]{:S(2)}) %collective-permute-start.8) | collective-permute-done | bytes 131104 | tf_op jit(solution)/shard_map/ppermute | solution.py:600
  145.5 1.9 %unpack.1 = bf16[16,32,2048]{2,1,0:T(8,128)(2,1)} custom-call(s32[48]{0:T(128)S(1)} %copy-done.9, bf16[4,2,32,2560]{3,2,1,0:T(8,128)(2,1)S(1)} %all-to-all-done.2.near, bf16[2,32,1024]{2,1,0:T(8,128)(2,1)S(1)} %collective-permute-done.6.refs_0_, bf16[2,32,1024]{2,1,0:T(8,128)(2,1)S(1)} %collective-permute-done.8.refs_1_, ...), custom_call_target="tpu_custom_call", output_to_operand_aliasing={{}: (6, {})} | custom-call | flops 1000 | bytes 1000 | tf_op jit(solution)/shard_map/unpack/pallas_call | solution.py:559
  (80 shorter events, 14.1 us)
Async XLA Ops:
  2.8 18.6 %collective-permute-start = (bf16[128,2048]{1,0:T(8,128)(2,1)}, bf16[128,2048]{1,0:T(8,128)(2,1)S(1)}, u32[]{:S(2)}, u32[]{:S(2)}) collective-permute-start(bf16[128,2048]{1,0:T(8,128)(2,1)} %multiply_convert_fusion._), channel_id=1, source_target_pairs={{0,2},{2,4},{4,6},{6,8},{8,10},{10,12},{12,14},{1,3},{3,5},{5,7},{... | collective-permute-start | bytes 1572872 | tf_op jit(solution)/shard_map/ppermute | solution.py:624
  12.0 9.3 %copy-start.8 = (s32[48]{0:T(128)S(1)}, s32[48]{0:T(128)}, u32[]{:S(2)}) copy-start(s32[48]{0:T(128)} %get-tuple-element.23._.info) | copy-start | bytes 580
  12.0 9.3 %copy-start.10 = (f32[2048,128]{1,0:T(8,128)S(1)}, f32[2048,128]{1,0:T(8,128)}, u32[]{:S(2)}) copy-start(f32[2048,128]{1,0:T(8,128)} %filters.1) | copy-start | bytes 3145732
  12.0 9.3 %copy-start.20 = (bf16[512,256]{1,0:T(8,128)(2,1)S(1)}, bf16[512,256]{1,0:T(8,128)(2,1)}, u32[]{:S(2)}) copy-start(bf16[512,256]{1,0:T(8,128)(2,1)} %constant.4.clone.forward) | copy-start | bytes 786436
  12.1 9.3 %copy-start.21 = (bf16[256,256]{1,0:T(8,128)(2,1)S(1)}, bf16[256,256]{1,0:T(8,128)(2,1)}, u32[]{:S(2)}) copy-start(bf16[256,256]{1,0:T(8,128)(2,1)} %constant.5.clone.inverse) | copy-start | bytes 393220
  12.1 31.4 %all-to-all-start = ((bf16[4,2,32,2560]{3,2,1,0:T(8,128)(2,1)}), bf16[4,2,32,2560]{3,2,1,0:T(8,128)(2,1)S(1)}, u32[]{:S(2)}, u32[]{:S(2)}) async-start(bf16[4,2,32,2560]{3,2,1,0:T(8,128)(2,1)} %get-tuple-element.26), calls=%async_computation | async-start | bytes 2621440 | tf_op jit(solution)/shard_map/all_to_all | solution.py:607
  16.0 53.4 %collective-permute-start.1 = (bf16[2,32,2048]{2,1,0:T(8,128)(2,1)}, bf16[2,32,2048]{2,1,0:T(8,128)(2,1)}, u32[]{:S(2)}, u32[]{:S(2)}) collective-permute-start(bf16[2,32,2048]{2,1,0:T(8,128)(2,1)} %get-tuple-element.28), channel_id=1, source_target_pairs={{0,8},{2,10},{4,12},{6,14},{8,0},{10,2},{12,4},{14,6},{1,9},{3,11}... | collective-permute-start | bytes 786440 | tf_op jit(solution)/shard_map/ppermute | solution.py:600
  18.4 57.0 %collective-permute-start.2 = (bf16[2,32,2048]{2,1,0:T(8,128)(2,1)}, bf16[2,32,2048]{2,1,0:T(8,128)(2,1)}, u32[]{:S(2)}, u32[]{:S(2)}) collective-permute-start(bf16[2,32,2048]{2,1,0:T(8,128)(2,1)} %get-tuple-element.31), channel_id=1, source_target_pairs={{0,10},{2,8},{4,14},{6,12},{8,2},{10,0},{12,6},{14,4},{1,11},{3,9}... | collective-permute-start | bytes 786440 | tf_op jit(solution)/shard_map/ppermute | solution.py:600
  44.5 54.1 %all-to-all-start.1 = ((bf16[16,512,128]{2,1,0:T(8,128)(2,1)}), bf16[16,512,128]{2,1,0:T(8,128)(2,1)}, u32[]{:S(2)}, u32[]{:S(2)}) async-start(bf16[16,512,128]{2,1,0:T(8,128)(2,1)} %once.1.rows._), calls=%async_computation.1 | async-start | bytes 4194304 | tf_op jit(solution)/shard_map/all_to_all | solution.py:607
  49.2 12.7 %copy-start.1 = (bf16[16,512,128]{2,1,0:T(8,128)(2,1)S(1)}, bf16[16,512,128]{2,1,0:T(8,128)(2,1)}, u32[]{:S(2)}) copy-start(bf16[16,512,128]{2,1,0:T(8,128)(2,1)} %once.1.rows._) | copy-start | bytes 6291460
  49.2 12.7 %copy-start.3 = (bf16[4,2,32,2560]{3,2,1,0:T(8,128)(2,1)S(1)}, bf16[4,2,32,2560]{3,2,1,0:T(8,128)(2,1)}, u32[]{:S(2)}) copy-start(bf16[4,2,32,2560]{3,2,1,0:T(8,128)(2,1)} %copy-done.2) | copy-start | bytes 3932164
  49.2 12.7 %copy-start.9 = (s32[48]{0:T(128)S(1)}, s32[48]{0:T(128)}, u32[]{:S(2)}) copy-start(s32[48]{0:T(128)} %get-tuple-element.23._.info) | copy-start | bytes 580
  49.2 12.7 %copy-start.19 = (f32[16]{0:T(128)S(1)}, f32[16]{0:T(128)}, u32[]{:S(2)}) copy-start(f32[16]{0:T(128)} %temps.19) | copy-start | bytes 196
  52.3 36.3 %collective-permute-start.3 = (bf16[2,32,2048]{2,1,0:T(8,128)(2,1)}, bf16[2,32,2048]{2,1,0:T(8,128)(2,1)S(1)}, u32[]{:S(2)}, u32[]{:S(2)}) collective-permute-start(bf16[2,32,2048]{2,1,0:T(8,128)(2,1)} %get-tuple-element.34), channel_id=1, source_target_pairs={{0,12},{2,14},{4,8},{6,10},{8,4},{10,6},{12,0},{14,2},{1,13},{3,15... | collective-permute-start | bytes 786440 | tf_op jit(solution)/shard_map/ppermute | solution.py:600
  61.9 31.7 %collective-permute-start.4 = (bf16[2,32,2048]{2,1,0:T(8,128)(2,1)}, bf16[2,32,2048]{2,1,0:T(8,128)(2,1)S(1)}, u32[]{:S(2)}, u32[]{:S(2)}) collective-permute-start(bf16[2,32,2048]{2,1,0:T(8,128)(2,1)} %get-tuple-element.37), channel_id=1, source_target_pairs={{0,14},{2,12},{4,10},{6,8},{8,6},{10,4},{12,2},{14,0},{1,15},{3,13... | collective-permute-start | bytes 786440 | tf_op jit(solution)/shard_map/ppermute | solution.py:600
  63.5 5.9 %copy-start.25 = (bf16[2,32,512]{2,1,0:T(8,128)(2,1)S(1)}, bf16[2,32,512]{2,1,0:T(8,128)(2,1)}, u32[]{:S(2)}) copy-start(bf16[2,32,512]{2,1,0:T(8,128)(2,1)} %get-tuple-element.29.rest) | copy-start | bytes 196612
  69.3 5.2 %copy-start.4 = (bf16[4,2,32,2048]{3,2,1,0:T(8,128)(2,1)}, bf16[4,2,32,2048]{3,2,1,0:T(8,128)(2,1)S(1)}, u32[]{:S(2)}) copy-start(bf16[4,2,32,2048]{3,2,1,0:T(8,128)(2,1)S(1)} %attend_near.1._.near) | copy-start | bytes 3145732
  69.4 6.0 %copy-start.30 = (bf16[2,32,512]{2,1,0:T(8,128)(2,1)S(1)}, bf16[2,32,512]{2,1,0:T(8,128)(2,1)}, u32[]{:S(2)}) copy-start(bf16[2,32,512]{2,1,0:T(8,128)(2,1)} %get-tuple-element.32.rest) | copy-start | bytes 196612
  74.5 39.0 %collective-permute-start.5 = (bf16[2,32,1536]{2,1,0:T(8,128)(2,1)}, bf16[2,32,1536]{2,1,0:T(8,128)(2,1)}, u32[]{:S(2)}, u32[]{:S(2)}) collective-permute-start(bf16[2,32,1536]{2,1,0:T(8,128)(2,1)} %get-tuple-element.30._), channel_id=1, source_target_pairs={{0,8},{2,10},{4,12},{6,14},{8,0},{10,2},{12,4},{14,6},{1,9},{3,11}... | collective-permute-start | bytes 589832 | tf_op jit(solution)/shard_map/ppermute | solution.py:600
  75.4 13.2 %copy-start.18 = (bf16[2,32,512]{2,1,0:T(8,128)(2,1)S(1)}, bf16[2,32,512]{2,1,0:T(8,128)(2,1)}, u32[]{:S(2)}) copy-start(bf16[2,32,512]{2,1,0:T(8,128)(2,1)} %get-tuple-element.35.rest) | copy-start | bytes 196612
  80.2 38.0 %collective-permute-start.7 = (bf16[2,32,1536]{2,1,0:T(8,128)(2,1)}, bf16[2,32,1536]{2,1,0:T(8,128)(2,1)}, u32[]{:S(2)}, u32[]{:S(2)}) collective-permute-start(bf16[2,32,1536]{2,1,0:T(8,128)(2,1)} %get-tuple-element.33._), channel_id=1, source_target_pairs={{0,10},{2,8},{4,14},{6,12},{8,2},{10,0},{12,6},{14,4},{1,11},{3,9}... | collective-permute-start | bytes 589832 | tf_op jit(solution)/shard_map/ppermute | solution.py:600
  88.6 4.4 %copy-start.14 = (bf16[2,32,2048]{2,1,0:T(8,128)(2,1)}, bf16[2,32,2048]{2,1,0:T(8,128)(2,1)S(1)}, u32[]{:S(2)}) copy-start(bf16[2,32,2048]{2,1,0:T(8,128)(2,1)S(1)} %collective-permute-done.3.queries.refs_2_) | copy-start | bytes 786436
  88.6 5.0 %copy-start.17 = (bf16[2,32,512]{2,1,0:T(8,128)(2,1)S(1)}, bf16[2,32,512]{2,1,0:T(8,128)(2,1)}, u32[]{:S(2)}) copy-start(bf16[2,32,512]{2,1,0:T(8,128)(2,1)} %get-tuple-element.38.rest) | copy-start | bytes 196612
  93.6 4.4 %copy-start.11 = (bf16[2,32,2048]{2,1,0:T(8,128)(2,1)}, bf16[2,32,2048]{2,1,0:T(8,128)(2,1)S(1)}, u32[]{:S(2)}) copy-start(bf16[2,32,2048]{2,1,0:T(8,128)(2,1)S(1)} %collective-permute-done.4.queries.refs_3_) | copy-start | bytes 786436
  98.6 24.0 %collective-permute-start.11 = (bf16[2,32,1536]{2,1,0:T(8,128)(2,1)}, bf16[2,32,1536]{2,1,0:T(8,128)(2,1)}, u32[]{:S(2)}, u32[]{:S(2)}) collective-permute-start(bf16[2,32,1536]{2,1,0:T(8,128)(2,1)} %get-tuple-element.39._), channel_id=1, source_target_pairs={{0,14},{2,12},{4,10},{6,8},{8,6},{10,4},{12,2},{14,0},{1,15},{3,13... | collective-permute-start | bytes 589832 | tf_op jit(solution)/shard_map/ppermute | solution.py:600
  100.5 7.5 %copy-start.5 = (bf16[4,2,32,2048]{3,2,1,0:T(8,128)(2,1)S(1)}, bf16[4,2,32,2048]{3,2,1,0:T(8,128)(2,1)}, u32[]{:S(2)}) copy-start(bf16[4,2,32,2048]{3,2,1,0:T(8,128)(2,1)} %copy-done.4) | copy-start | bytes 3145732
  104.4 16.1 %collective-permute-start.9 = (bf16[2,32,1536]{2,1,0:T(8,128)(2,1)}, bf16[2,32,1536]{2,1,0:T(8,128)(2,1)}, u32[]{:S(2)}, u32[]{:S(2)}) collective-permute-start(bf16[2,32,1536]{2,1,0:T(8,128)(2,1)} %get-tuple-element.36._), channel_id=1, source_target_pairs={{0,12},{2,14},{4,8},{6,10},{8,4},{10,6},{12,0},{14,2},{1,13},{3,15... | collective-permute-start | bytes 589832 | tf_op jit(solution)/shard_map/ppermute | solution.py:600
  110.0 35.5 %all-to-all-start.2 = ((bf16[4,2,32,2560]{3,2,1,0:T(8,128)(2,1)}), bf16[4,2,32,2560]{3,2,1,0:T(8,128)(2,1)S(1)}, u32[]{:S(2)}, u32[]{:S(2)}) async-start(bf16[4,2,32,2560]{3,2,1,0:T(8,128)(2,1)} %finish.1), calls=%async_computation.2 | async-start | bytes 2621440 | tf_op jit(solution)/shard_map/all_to_all | solution.py:607
  124.6 9.9 %collective-permute-start.12 = (bf16[2,32,1024]{2,1,0:T(8,128)(2,1)S(1)}, bf16[2,32,1024]{2,1,0:T(8,128)(2,1)S(1)}, u32[]{:S(2)}, u32[]{:S(2)}) collective-permute-start(bf16[2,32,1024]{2,1,0:T(8,128)(2,1)S(1)} %attend_second.7.refs_4_), channel_id=1, source_target_pairs={{0,14},{2,12},{4,10},{6,8},{8,6},{10,4},{12,2},{14,0},{1,15},{3,13... | collective-permute-start | bytes 393224 | tf_op jit(solution)/shard_map/ppermute | solution.py:600
  126.5 8.3 %collective-permute-start.10 = (bf16[2,32,1024]{2,1,0:T(8,128)(2,1)S(1)}, bf16[2,32,1024]{2,1,0:T(8,128)(2,1)S(1)}, u32[]{:S(2)}, u32[]{:S(2)}) collective-permute-start(bf16[2,32,1024]{2,1,0:T(8,128)(2,1)S(1)} %attend_second.6._), channel_id=1, source_target_pairs={{0,12},{2,14},{4,8},{6,10},{8,4},{10,6},{12,0},{14,2},{1,13},{3,15... | collective-permute-start | bytes 393224 | tf_op jit(solution)/shard_map/ppermute | solution.py:600
  129.9 15.0 %collective-permute-start.8 = (bf16[2,32,1024]{2,1,0:T(8,128)(2,1)S(1)}, bf16[2,32,1024]{2,1,0:T(8,128)(2,1)S(1)}, u32[]{:S(2)}, u32[]{:S(2)}) collective-permute-start(bf16[2,32,1024]{2,1,0:T(8,128)(2,1)S(1)} %attend_second.5._), channel_id=1, source_target_pairs={{0,10},{2,8},{4,14},{6,12},{8,2},{10,0},{12,6},{14,4},{1,11},{3,9}... | collective-permute-start | bytes 393224 | tf_op jit(solution)/shard_map/ppermute | solution.py:600
  129.9 15.5 %collective-permute-start.6 = (bf16[2,32,1024]{2,1,0:T(8,128)(2,1)S(1)}, bf16[2,32,1024]{2,1,0:T(8,128)(2,1)S(1)}, u32[]{:S(2)}, u32[]{:S(2)}) collective-permute-start(bf16[2,32,1024]{2,1,0:T(8,128)(2,1)S(1)} %attend_second.4._), channel_id=1, source_target_pairs={{0,8},{2,10},{4,12},{6,14},{8,0},{10,2},{12,4},{14,6},{1,9},{3,11}... | collective-permute-start | bytes 393224 | tf_op jit(solution)/shard_map/ppermute | solution.py:600
  (15 other events, 20.5 us)

commit v5 on v4

v5 whole, which is shorter than its diff:
```python
import functools

import jax
import jax.numpy as jnp
import numpy as np
from jax import lax
from jax.experimental import pallas as pl
from jax.experimental.pallas import tpu as pltpu
from jax.sharding import PartitionSpec as P

HEAD_DIM = 128
HOT = 4
EPS = 1e-06
LOG2E = 1.4426950408889634
MIB = 1 << 20
AHEAD = 16
UNPACK_FLOPS = 20 << 30
PACK_VMEM = 60
ATTEND_FLOPS = 20 << 30
MIX_FLOPS = 100 << 30
PACK_FLOPS = 20 << 30


def cost(flops):
    return pl.CostEstimate(flops=flops, bytes_accessed=1000, transcendentals=0)


def halves(array):
    high = array.astype(jnp.bfloat16)
    low = (array - high.astype(jnp.float32)).astype(jnp.bfloat16)
    return high, low


def transforms(taps):
    size = 2 * taps
    odd = 2 * np.arange(taps) + 1
    angle = np.pi / size * ((odd[:, None] * np.arange(size)[None, :]) % (2 * size))
    forward = np.concatenate([np.cos(angle), -np.sin(angle)], 0)
    inverse = forward.T[taps:] * (2.0 / size)
    out = []
    for matrix in (forward, inverse):
        high = matrix.astype(jnp.bfloat16)
        low = (matrix - high.astype(np.float64)).astype(jnp.bfloat16)
        out.append(np.concatenate([high, low], 0))
    return out


def unit(block):
    return block * lax.rsqrt(jnp.mean(block * block, axis=-1, keepdims=True) + EPS)


def mix_rows(starts, before, gate, key, value, filters, forward, inverse, out, rows_of, keys_of):
    _, wide = gate.shape
    taps = filters.shape[1]
    size = 2 * taps
    f32 = jnp.float32
    fwd = forward[...]
    inv = inverse[...]
    high, low = halves(filters[...])
    across = (((1,), (1,)), ((), ()))
    both = lax.dot_general(fwd[:, :taps], high, across, preferred_element_type=f32)
    spectrum = both[:size] + both[size:]
    spectrum += lax.dot_general(fwd[:size, :taps], low, across, preferred_element_type=f32)
    hr, hi = spectrum[:taps], spectrum[taps:]
    for start in starts:
        part = slice(start, start + taps)
        now = products(key, value, part)
        both = jnp.dot(fwd, jnp.concatenate([before, now], 0), preferred_element_type=f32)
        seen = both[:size] + both[size:]
        xr, xi = seen[:taps], seen[taps:]
        product = jnp.concatenate([xr * hr - xi * hi, xr * hi + xi * hr], 0)
        high, low = halves(product)
        both = jnp.dot(inv, high, preferred_element_type=f32)
        mixed = both[:taps] + both[taps:]
        mixed += jnp.dot(inv[:taps], low, preferred_element_type=f32)
        result = (gate[part, :].astype(f32) * mixed).astype(jnp.bfloat16)
        out[part, :] = result
        for head in range(wide // HEAD_DIM):
            piece = result[:, head * HEAD_DIM : (head + 1) * HEAD_DIM]
            rows_of[head, part, :] = piece
            keys_of[head, :, part] = unit(piece.astype(f32)).astype(jnp.bfloat16).T
        before = now


def products(key, value, part):
    return (key[part, :].astype(jnp.float32) * value[part, :].astype(jnp.float32)).astype(jnp.bfloat16)


def mix_later_kernel(gate, key, value, filters, forward, inverse, _, *outs):
    taps = filters.shape[1]
    before = products(key, value, slice(0, taps))
    starts = range(taps, gate.shape[0], taps)
    mix_rows(starts, before, gate, key, value, filters, forward, inverse, *outs)


def mix_first_kernel(gate, key, value, filters, forward, inverse, earlier, *refs):
    mix_rows([0], earlier[...], gate, key, value, filters, forward, inverse, *refs[-3:])


def mix(gate, key, value, earlier, filters, after):
    rows, chans = gate.shape
    taps = filters.shape[1]
    heads = chans // HEAD_DIM
    wide = 8 * HEAD_DIM
    forward, inverse = (jnp.asarray(matrix) for matrix in transforms(taps))
    anywhere = pl.BlockSpec(memory_space=pl.ANY)
    whole = lambda array: pl.BlockSpec(array.shape, lambda i: (0, 0))
    first = pl.BlockSpec((taps, wide), lambda i: (0, i))

    def specs(high):
        stream = pl.BlockSpec((high, wide), lambda i: (0, i))
        by_head = pl.BlockSpec((wide // HEAD_DIM, high, HEAD_DIM), lambda i: (i, 0, 0))
        turned = pl.BlockSpec((wide // HEAD_DIM, HEAD_DIM, high), lambda i: (i, 0, 0))
        weights = pl.BlockSpec((wide, taps), lambda i: (i, 0))
        return [stream] * 3 + [weights, whole(forward), whole(inverse)], [stream, by_head, turned]

    params = dict(
        grid=(chans // wide,),
        out_shape=[
            jax.ShapeDtypeStruct((rows, chans), jnp.bfloat16),
            jax.ShapeDtypeStruct((heads, rows, HEAD_DIM), jnp.bfloat16),
            jax.ShapeDtypeStruct((heads, HEAD_DIM, rows), jnp.bfloat16),
        ],
        compiler_params=pltpu.CompilerParams(vmem_limit_bytes=48 * MIB),
        cost_estimate=cost(MIX_FLOPS),
    )
    arrays = (gate, key, value, filters, forward, inverse)
    ins, outs = specs(rows)
    mixed = pl.pallas_call(
        mix_later_kernel, in_specs=ins + [anywhere], out_specs=outs, name="mix_later", **params
    )(*arrays, after)
    ins, outs = specs(taps)
    return pl.pallas_call(
        mix_first_kernel,
        in_specs=ins + [first] + [anywhere] * 3,
        out_specs=outs,
        input_output_aliases={7: 0, 8: 1, 9: 2},
        name="mix_first",
        **params,
    )(*arrays, earlier, *mixed)


def softened(queries, keys, rows, heats, live):
    f32 = jnp.float32
    queries = [unit(query).astype(jnp.bfloat16) for query in queries]
    scores = [jnp.dot(*pair, preferred_element_type=f32) for pair in zip(queries, keys)]
    weights = [jnp.where(live, jnp.exp2(s * heat), 0.0) for s, heat in zip(scores, heats)]
    totals = [jnp.sum(weight, axis=-1, keepdims=True) for weight in weights]
    sums = [
        jnp.dot(weight.astype(jnp.bfloat16), rows_of, preferred_element_type=f32)
        for weight, rows_of in zip(weights, rows)
    ]
    return [part / total for part, total in zip(sums, totals)]


def together(count, high):
    most = 8 if high <= 128 else 4
    return max(size for size in range(1, most + 1) if count % size == 0)


def masks(offsets, first, slots, tokens, positions):
    place = lax.broadcasted_iota(jnp.int32, (tokens, positions), 1)
    return jnp.concatenate([place < offsets[first + slot] for slot in range(slots)], 0)


def attend_heads(info, temps, keys, rows, places, first, last):
    positions = keys.shape[2]
    slots, tokens = places[0][:2]
    each = slots * tokens
    live = masks(info, info.shape[0] - AHEAD, slots, tokens, positions)
    live = jnp.concatenate([live] * len(places), 0)

    batch = together(last - first, each * len(places))

    def some(step, carry):
        heads = [first + step * batch + at for at in range(batch)]
        queries = []
        for head in heads:
            parts = [load(head).astype(jnp.float32) for _, _, load, _ in places]
            queries.append(jnp.concatenate([part.reshape(each, HEAD_DIM) for part in parts], 0))
        heats = [temps[head] * (LOG2E / HEAD_DIM) for head in heads]
        done = softened(queries, [keys[h] for h in heads], [rows[h] for h in heads], heats, live)
        for head, block in zip(heads, done):
            for place, (_, _, _, store) in enumerate(places):
                part = block[place * each : (place + 1) * each].reshape(slots, tokens, HEAD_DIM)
                store(head, part.astype(jnp.bfloat16))
        return carry

    lax.fori_loop(0, (last - first) // batch, some, 0)


def columns(head):
    return pl.ds(pl.multiple_of(head * HEAD_DIM, HEAD_DIM), HEAD_DIM)


def loader(ref, shift, *at):
    return lambda head: ref[at + (slice(None), slice(None), columns(head - shift))]


def storer(ref, shift, *at):
    def store(head, block):
        ref[at + (slice(None), slice(None), columns(head - shift))] = block

    return store


def near_kernel(info, temps, keys, rows, _, near, out):
    half, slots, tokens, _ = near.shape
    places = [(slots, tokens, loader(near, 0, at), storer(out, 0, at)) for at in range(half)]
    attend_heads(info, temps, keys, rows, places, 0, keys.shape[0])


def first_kernel(tail, info, temps, keys, rows, _, queries, rest, out, kept):
    slots, tokens, _ = queries.shape
    heads = keys.shape[0]
    split = heads - 2 * tail
    places = [(slots, tokens, loader(queries, 0), storer(out, 0))]
    attend_heads(info, temps, keys, rows, places, 0, heads - tail)
    part = slice(split * HEAD_DIM, (split + tail) * HEAD_DIM)
    home = on_hot_half(info, out_peers(heads, tail))

    kept[...] = out[:, :, part]

    @pl.when(jnp.logical_not(home))
    def _():
        out[:, :, part] = rest[...]


def second_kernel(tail, first, count, info, temps, keys, rows, extra, _, *refs):
    queries, later, kept = (refs[at * count : (at + 1) * count] for at in range(3))
    outs, held = refs[3 * count : 4 * count], refs[-1]
    slots, tokens, _ = queries[0].shape
    heads = keys.shape[0]
    split = heads - 2 * tail
    part = slice(tail * HEAD_DIM, 2 * tail * HEAD_DIM)
    home = on_hot_half(info, out_peers(heads, tail))

    @pl.when(home)
    def _():
        for at in range(count):
            held[at] = later[at][:, :, split * HEAD_DIM :]
            outs[at][:, :, part] = extra[first + at]

    @pl.when(jnp.logical_not(home))
    def _():
        for at in range(count):
            held[at] = queries[at][:, :, (split + tail) * HEAD_DIM :]
            outs[at][:, :, part] = kept[at][...]

    places = [
        (slots, tokens, loader(held, heads - tail, at), storer(outs[at], heads - tail))
        for at in range(count)
    ]
    attend_heads(info, temps, keys, rows, places, heads - tail, heads)


def out_peers(heads, tail):
    return 2 * (heads // tail)


def on_hot_half(info, peers):
    half = peers // 2
    return (lax.axis_index("pos") >= half) == (info[info.shape[0] - 1] >= half)


def attend(kernel, name, widths, info, temps, keys, rows, refs, unread, arrays, scratch=()):
    scalars = pl.BlockSpec(memory_space=pltpu.SMEM)
    vector = pl.BlockSpec(memory_space=pltpu.VMEM)
    anywhere = pl.BlockSpec(memory_space=pl.ANY)
    leading = arrays[0].shape[:-1]
    return pl.pallas_call(
        kernel,
        in_specs=[scalars, scalars, vector, vector]
        + [vector] * len(refs)
        + [anywhere]
        + [vector] * len(arrays),
        out_specs=[vector] * len(widths),
        out_shape=[
            jax.ShapeDtypeStruct(leading + (width * HEAD_DIM,), jnp.bfloat16) for width in widths
        ],
        scratch_shapes=list(scratch),
        compiler_params=pltpu.CompilerParams(vmem_limit_bytes=16 * MIB),
        cost_estimate=cost(ATTEND_FLOPS),
        name=name,
    )(info, temps, keys, rows, *refs, unread, *arrays)


def holds(info, done):
    hot = info[info.shape[0] - 1]
    apart = jnp.bitwise_xor(lax.axis_index("pos"), hot)
    for bit in done:
        apart -= apart // (1 << bit) % 2 * (1 << bit)
    return apart == 0


def cut_kernel(stage, ways, info, *refs):
    sources, (sent, kept) = refs[: -2 * len(ways) - 1], (refs[-2 * len(ways) : -len(ways)], refs[-len(ways) :])
    for at, (start, _, order) in enumerate(ways):
        count = sent[at].shape[0]
        mine = lax.axis_index("pos") // (1 << order[stage]) % 2
        if stage:
            have = holds(info, order[: stage - 1])
            choices = [(have, sources[2 * at]), (jnp.logical_not(have), sources[2 * at + 1])]
            start = 0
        else:
            choices = [(True, sources[0])]
        for whether, source in choices:

            @pl.when(whether)
            def _():
                sent[at][...] = source[pl.ds(start + (1 - mine) * count, count)]
                kept[at][...] = source[pl.ds(start + mine * count, count)]


def cut(stage, ways, info, sources, after):
    _, positions, wide = sources[0].shape
    vector = pl.BlockSpec(memory_space=pltpu.VMEM)
    halves_of = [
        jax.ShapeDtypeStruct((count >> (stage + 1), positions, wide), sources[0].dtype)
        for _, count, _ in ways
    ]
    outs = pl.pallas_call(
        functools.partial(cut_kernel, stage, ways),
        in_specs=[pl.BlockSpec(memory_space=pltpu.SMEM)]
        + [vector] * len(sources)
        + [pl.BlockSpec(memory_space=pl.ANY)],
        out_specs=[vector] * (2 * len(ways)),
        out_shape=halves_of * 2,
        compiler_params=pltpu.CompilerParams(vmem_limit_bytes=16 * MIB),
        cost_estimate=cost(1000),
        name="cut",
    )(info, *sources, after)
    return outs[: len(ways)], outs[len(ways) :]


def extra_kernel(ways, info, temps, *refs):
    rows, near, far = refs[: 2 * len(ways)], refs[2 * len(ways) + 1], refs[2 * len(ways) + 2 : -2]
    near_out, far_out = refs[-2:]
    half, extras, tokens, wide = near.shape
    me = lax.axis_index("pos")
    live = masks(info, info.shape[0] - AHEAD + HOT, extras, tokens, rows[0].shape[1])
    live = jnp.concatenate([live] * half, 0)
    values, heats = [], []
    pieces = share_of(me, half, temps.shape[0])
    for at, ((_, _, order), (first, count)) in enumerate(zip(ways, pieces)):
        have = holds(info, order[:-1])
        for head in range(count):
            values.append(jnp.where(have, rows[2 * at][head], rows[2 * at + 1][head]))
            heats.append(temps[first + head] * (LOG2E / HEAD_DIM))
    keyed = [unit(valued.astype(jnp.float32)).astype(jnp.bfloat16).T for valued in values]
    for side in range(2):
        queries = []
        for head in range(len(values)):
            cols = slice(head * HEAD_DIM, (head + 1) * HEAD_DIM)
            query = [source[:, :, cols] for source in far] if side else [near[:, :, :, cols]]
            query = [part.astype(jnp.float32).reshape(-1, HEAD_DIM) for part in query]
            queries.append(jnp.concatenate(query, 0))
        for head, done in enumerate(softened(queries, keyed, values, heats, live)):
            cols = slice(head * HEAD_DIM, (head + 1) * HEAD_DIM)
            done = done.reshape(half, extras, tokens, HEAD_DIM).astype(jnp.bfloat16)
            (far_out if side else near_out)[:, :, :, cols] = done


def attend_extra(ways, info, temps, rows, after, near, far, wide):
    half, extras, tokens, columns = near.shape
    scalars = pl.BlockSpec(memory_space=pltpu.SMEM)
    return pl.pallas_call(
        functools.partial(extra_kernel, ways),
        grid=(1,),
        in_specs=[
            scalars,
            scalars,
        ]
        + [pl.BlockSpec(array.shape, lambda i: (0, 0, 0)) for array in rows]
        + [
            pl.BlockSpec(memory_space=pl.ANY),
            pl.BlockSpec((half, extras, tokens, wide), lambda i: (0, 0, 0, columns // wide - 1)),
        ]
        + [pl.BlockSpec((extras, tokens, wide), lambda i: (0, 0, columns // wide - 2))] * half,
        out_specs=[pl.BlockSpec((half, extras, tokens, wide), lambda i: (0, 0, 0, 0))] * 2,
        out_shape=[jax.ShapeDtypeStruct((half, extras, tokens, wide), jnp.bfloat16)] * 2,
        compiler_params=pltpu.CompilerParams(vmem_limit_bytes=16 * MIB),
        cost_estimate=cost(ATTEND_FLOPS),
        name="attend_extra",
    )(info, temps, *rows, after, near, *far)


def route(info, peers, slots, extras, rows, blocks, sites):
    me = lax.axis_index("pos")
    ahead = info.shape[0] - AHEAD
    hot_at = info.shape[0] - 1

    def clear(at, carry):
        info[at] = -1
        return carry

    lax.fori_loop(0, info.shape[0], clear, 0)
    for window in range(blocks.shape[0]):
        block = blocks[window]
        count = jnp.int32(0)
        for slot in range(HOT - 1):
            count += (info[block * HOT + slot] >= 0).astype(jnp.int32)
        info[block * HOT + count] = window

        @pl.when(count == HOT - 1)
        def _():
            info[hot_at] = block

    hot = info[hot_at]

    def offset(entry):
        window = info[entry]
        site = sites[jnp.maximum(window, 0)]
        return jnp.where(window >= 0, site - rows * (entry // HOT), rows)

    for slot in range(HOT):
        info[ahead + slot] = offset(me * HOT + slot)
    for extra in range(extras):
        info[ahead + HOT + extra] = offset(hot * HOT + slots + extra)


def paths(half, heads):
    order = tuple(range(half.bit_length() - 1))
    if heads // half % 2:
        return [(0, heads, order)]
    return [(0, heads // 2, order), (heads // 2, heads // 2, order[::-1])]


def share_of(index, half, heads):
    pieces = []
    for start, count, order in paths(half, heads):
        for bit in order:
            count //= 2
            start += index // (1 << bit) % 2 * count
        pieces.append((start, count))
    return pieces


def columns_of(piece):
    start, count = piece
    wide = count * HEAD_DIM
    if isinstance(start, int):
        return pl.ds(start * HEAD_DIM, wide)
    return pl.ds(pl.multiple_of(start * HEAD_DIM, wide), wide)


def copied(copies, sems):
    copies = [pltpu.make_async_copy(*pair, sems.at[at]) for at, pair in enumerate(copies)]
    for copy in copies:
        copy.start()
    for copy in copies:
        copy.wait()


def message(info, queries, peer, out, wide, extras, start, count, with_extras):
    slots, _, held = out.shape
    hot = info[info.shape[0] - 1]
    copies = []
    for slot in range(slots):
        window = jnp.maximum(info[peer * HOT + slot], 0)
        source = queries.at[window, :, pl.ds(start, count)]
        copies.append((source, out.at[slot, :, pl.ds(0, count)]))
    half = queries.shape[2] // wide
    for extra in range(extras if held > count else 0):
        at = 0
        for first, size in share_of(peer, half, queries.shape[2] // HEAD_DIM):
            window = info[hot * HOT + slots + extra]
            if with_extras is not None:
                window = jnp.where(with_extras, window, jnp.maximum(info[peer * HOT + extra], 0))
                first = jnp.where(with_extras, first, (start + count) // HEAD_DIM + at)
            source = queries.at[window, :, columns_of((first, size))]
            target = out.at[extra, :, pl.ds(count + at * HEAD_DIM, size * HEAD_DIM)]
            copies.append((source, target))
            at += size
    return copies


def far_copies(info, queries, steps, far, rest, wide, extras):
    half = queries.shape[2] // wide
    me = lax.axis_index("pos")
    away = jnp.logical_not(on_hot_half(info, 2 * half))
    chans = queries.shape[2]
    copies = []
    for step, out, other in zip(steps, far, rest):
        peer = jnp.bitwise_xor(me, step)
        copies += message(info, queries, peer, out, wide, extras, 0, chans - wide, away)
        copies += message(info, queries, peer, other, wide, extras, chans - wide, wide, None)
    return copies


def pack_kernel(extras, rows, wide, blocks, sites, queries, _, info, near, *refs):
    half, slots, _, _ = near.shape
    outs, (sems, blocks_held, sites_held, pair) = refs[:-4], refs[-4:]
    count = len(outs) // 2
    copied([(blocks, blocks_held), (sites, sites_held)], pair)
    route(info, 2 * half, slots, extras, rows, blocks_held, sites_held)
    base = jnp.bitwise_and(lax.axis_index("pos"), half)
    chans = queries.shape[2]
    steps = range(half, half + count)
    copies = far_copies(info, queries, steps, outs[:count], outs[count:], wide, extras)
    for at in range(half):
        copies += message(info, queries, base + at, near.at[at], wide, extras, 0, chans, None)
    copied(copies, sems)


def far_shapes(queries, slots, wide, count):
    _, tokens, chans = queries.shape
    return [jax.ShapeDtypeStruct((slots, tokens, chans), queries.dtype)] * count + [
        jax.ShapeDtypeStruct((slots, tokens, wide), queries.dtype)
    ] * count


def pack(blocks, sites, queries, tail, rows, half, slots, extras, wide, count):
    windows, tokens, chans = queries.shape
    scalars = pl.BlockSpec(memory_space=pltpu.SMEM)
    vector = pl.BlockSpec(memory_space=pltpu.VMEM)
    anywhere = pl.BlockSpec(memory_space=pl.ANY)
    info, near, *far = pl.pallas_call(
        functools.partial(pack_kernel, extras, rows, wide),
        in_specs=[anywhere] * 4,
        out_specs=[scalars] + [vector] * (1 + 2 * count),
        out_shape=[
            jax.ShapeDtypeStruct((2 * half * HOT + AHEAD,), jnp.int32),
            jax.ShapeDtypeStruct((half, slots, tokens, chans + wide), queries.dtype),
        ]
        + far_shapes(queries, slots, wide, count),
        scratch_shapes=[
            pltpu.SemaphoreType.DMA(((half + count) * (slots + 2 * extras) + count * slots,)),
            pltpu.SMEM((windows,), jnp.int32),
            pltpu.SMEM((windows,), jnp.int32),
            pltpu.SemaphoreType.DMA((2,)),
        ],
        compiler_params=pltpu.CompilerParams(vmem_limit_bytes=PACK_VMEM * MIB),
        cost_estimate=cost(PACK_FLOPS),
        name="pack",
    )(blocks, sites, queries, tail)
    return info, near, far[:count], far[count:]


def placed(info, out, sems, pieces):
    def each(act):
        at = 0
        for peer, result, start, count, column, whether in pieces:
            for slot in range(result.shape[0]):
                window = info[peer * HOT + slot]
                source = result.at[slot, :, pl.ds(start, count)]
                target = out.at[jnp.maximum(window, 0), :, pl.ds(column, count)]
                copy = pltpu.make_async_copy(source, target, sems.at[at])
                pl.when(jnp.logical_and(window >= 0, whether))(functools.partial(act, copy))
                at += 1

    each(lambda copy: copy.start())
    return lambda: each(lambda copy: copy.wait())


def unpack_early_kernel(wide, info, near, *refs):
    half = near.shape[0]
    results, (_, out, near_sems, sems) = refs[:half], refs[half:]
    me = lax.axis_index("pos")
    base = jnp.bitwise_and(me, half)
    home = on_hot_half(info, 2 * half)
    chans = out.shape[2]
    split = chans - 2 * wide
    pieces = [(base + at, near.at[at], 0, chans, 0, True) for at in range(half)]
    near_wait = placed(info, out, near_sems, pieces)
    pieces = []
    for at, result in enumerate(results):
        peer = jnp.bitwise_xor(me, half + at)
        pieces.append((peer, result, 0, split, 0, True))
        pieces.append((peer, result, split, wide, split, jnp.logical_not(home)))
    placed(info, out, sems, pieces)()
    near_wait()


def unpack_early(info, near, results, after, shape, wide):
    anywhere = pl.BlockSpec(memory_space=pl.ANY)
    half, slots, _, _ = near.shape
    return pl.pallas_call(
        functools.partial(unpack_early_kernel, wide),
        in_specs=[pl.BlockSpec(memory_space=pltpu.SMEM)]
        + [pl.BlockSpec(memory_space=pltpu.VMEM)] * (1 + half)
        + [anywhere],
        out_specs=anywhere,
        out_shape=jax.ShapeDtypeStruct(shape, near.dtype),
        scratch_shapes=[
            pltpu.SemaphoreType.DMA((half * slots,)),
            pltpu.SemaphoreType.DMA((2 * half * slots,)),
        ],
        compiler_params=pltpu.CompilerParams(vmem_limit_bytes=16 * MIB),
        cost_estimate=cost(1000),
        name="unpack_early",
    )(info, near, *results, after)


def unpack_kernel(wide, step, info, result, _, out, sems, extra_sems):
    extras = extra_sems.shape[0] // 2
    half = out.shape[2] // wide
    slots = HOT - extras
    split = out.shape[2] - 2 * wide
    peer = jnp.bitwise_xor(lax.axis_index("pos"), step)
    home = on_hot_half(info, 2 * half)
    pieces = [
        (peer, result, 0, wide, split + wide, True),
        (peer, result, wide, wide, split, home),
    ]
    wait = placed(info, out, sems, pieces)
    share = share_of(peer, half, out.shape[2] // HEAD_DIM)
    sources = [result.at[extra, :, pl.ds(wide, wide)] for extra in range(extras)]
    extra_wait = placed_extra(info, out, extra_sems, sources, share, jnp.logical_not(home))
    wait()
    extra_wait()


def placed_extra(info, out, sems, sources, share, whether):
    extras = len(sources)
    hot = info[info.shape[0] - 1]

    def each(act):
        for extra, source in enumerate(sources):
            window = info[hot * HOT + HOT - extras + extra]
            at = 0
            for place, piece in enumerate(share):
                part = source.at[:, pl.ds(at * HEAD_DIM, piece[1] * HEAD_DIM)]
                target = out.at[window, :, columns_of(piece)]
                copy = pltpu.make_async_copy(part, target, sems.at[2 * extra + place])
                pl.when(whether)(functools.partial(act, copy))
                at += piece[1]

    each(lambda copy: copy.start())
    return lambda: each(lambda copy: copy.wait())


def unpack_extra_kernel(info, near, _, out, *sems):
    half, extras, _, _ = near.shape
    home = on_hot_half(info, 2 * half)
    waits = []
    for at in range(half):
        sources = [near.at[at, extra] for extra in range(extras)]
        share = share_of(at, half, out.shape[2] // HEAD_DIM)
        waits.append(placed_extra(info, out, sems[at], sources, share, home))
    for wait in waits:
        wait()


def unpack(kernel, name, info, result, so_far, semaphores):
    anywhere = pl.BlockSpec(memory_space=pl.ANY)
    return pl.pallas_call(
        kernel,
        in_specs=[
            pl.BlockSpec(memory_space=pltpu.SMEM),
            pl.BlockSpec(memory_space=pltpu.VMEM),
            anywhere,
        ],
        out_specs=anywhere,
        out_shape=jax.ShapeDtypeStruct(so_far.shape, so_far.dtype),
        input_output_aliases={2: 0},
        scratch_shapes=[pltpu.SemaphoreType.DMA((count,)) for count in semaphores],
        compiler_params=pltpu.CompilerParams(vmem_limit_bytes=16 * MIB),
        cost_estimate=cost(UNPACK_FLOPS),
        name=name,
    )(info, result, so_far)


def exchanged(value, step):
    peers = lax.axis_size("pos")
    if step == 0:
        return value
    return lax.ppermute(value, "pos", [(i, i ^ step) for i in range(peers)])


def exchanged_near(value):
    peers = lax.axis_size("pos")
    half = peers // 2
    groups = [list(range(half)), list(range(half, peers))]
    return lax.all_to_all(value, "pos", 0, 0, axis_index_groups=groups, tiled=True)


def shards(gate_stream, key_stream, value_stream, filters, temps, queries, blocks, sites):
    rows, chans = gate_stream.shape
    taps = filters.shape[1]
    peers = lax.axis_size("pos")
    me = lax.axis_index("pos").astype(jnp.int32)
    windows = blocks.shape[0]
    heads = chans // HEAD_DIM
    extras = 2
    slots = HOT - extras
    half = peers // 2

    last = slice(rows - taps, rows)
    tail = key_stream[last].astype(jnp.float32) * value_stream[last].astype(jnp.float32)
    tail = tail.astype(jnp.bfloat16)
    earlier = lax.ppermute(tail, "pos", [(i, i + 1) for i in range(peers - 1)])
    wide = chans // half
    share = heads // half
    info, near, far, rest = pack(
        blocks, sites, queries, tail, rows, half, slots, extras, wide, half
    )
    far = [exchanged(sent, half + at) for at, sent in enumerate(far)]
    near = exchanged_near(near)
    hyena_out, valued, keyed = mix(
        gate_stream, key_stream, value_stream, earlier, filters, info
    )
    own = (info, temps, keyed, valued)

    ways = paths(half, heads)

    def halved(stage, sources, after):
        moved, kept_rows = cut(stage, ways, info, sources, after)
        pairs = []
        for (_, _, order), out, stays in zip(ways, moved, kept_rows):
            pairs += [stays, exchanged(out, 1 << order[stage])]
        return pairs, moved[0]

    def first(at, after):
        kernel = functools.partial(first_kernel, share)
        arrays = [far[at], rest[at]]
        result, back = attend(
            kernel, "attend_first", [heads - share, share], *own, [], after, arrays
        )
        sent.append(exchanged(result, half + at))
        kept.append(back)
        return result

    def second(at, count, after):
        kernel = functools.partial(second_kernel, share, at, count)
        some = slice(at, at + count)
        arrays = far[some] + sent[some] + kept[some]
        scratch = [pltpu.VMEM((count,) + kept[at].shape, jnp.bfloat16)]
        results = attend(
            kernel, "attend_second", [2 * share] * count, *own, [extra], after, arrays, scratch
        )
        late.extend(exchanged(result, half + at + more) for more, result in enumerate(results))
        return results[0]

    sent, kept, late = [], [], []
    hot_rows, after = halved(0, [valued], valued)
    after = first(0, after)
    (near_results,) = attend(near_kernel, "attend_near", [heads], *own, [], after, [near])
    near_out, after = exchanged_near(near_results), near_results
    for stage in range(1, half.bit_length() - 1):
        hot_rows, after = halved(stage, hot_rows, after)
    for at in range(1, half):
        after = first(at, after)
    near_extra, extra = attend_extra(ways, info, temps, hot_rows, after, near, far, wide)
    near_extra, after = exchanged_near(near_extra), extra
    for at in range(half):
        after = second(at, 1, after)
    so_far = unpack_early(info, near_out, sent, after, queries.shape, wide)
    kernel = unpack_extra_kernel
    so_far = unpack(kernel, "unpack_extra", info, near_extra, so_far, [2 * extras] * half)
    for at, result in enumerate(late):
        kernel = functools.partial(unpack_kernel, wide, half + at)
        so_far = unpack(kernel, "unpack", info, result, so_far, [2 * slots, 2 * extras])
    return (hyena_out, so_far)


def solution(mesh):
    placed = (
        P(("groups", "pos"), "mp"),
        P(("groups", "pos"), "mp"),
        P(("groups", "pos"), "mp"),
        P("mp", None),
        P("mp"),
        P("groups", "pos", "mp"),
        P("groups"),
        P("groups"),
    )
    return jax.shard_map(
        shards,
        mesh=mesh,
        in_specs=placed,
        out_specs=(P(("groups", "pos"), "mp"), P("groups", "pos", "mp")),
        check_vma=False,
    )
```

time: 148 us -> 136 us (0.919)
  Pallas kernels: 62.9 us -> 54 us
  local copies, waits for them, and re-layouts: 12 us -> 5.75 us
  starting transfers between devices: 46.2 us -> 49.8 us
    pallas_call x9, Pallas kernels: 32.9 us -> 20.6 us  [attend(): pl.pallas_call(kernel, in_specs=[scalars, scalars, vector, vector] + [vec...]
    unnamed x62 -> x38, local copies, waits for them, and re-layouts: 12 us -> 5.75 us
    all_to_all x3, starting transfers between devices: 12.1 us -> 16.8 us  [exchanged_near(): lax.all_to_all(value, 'pos', 0, 0, axis_index_groups=groups, tiled=True)]
    all_to_all x3, waiting for transfers between devices: 5.96 us -> 3.06 us  [exchanged_near(): lax.all_to_all(value, 'pos', 0, 0, axis_index_groups=groups, tiled=True)]
    ppermute x12 -> x16, waiting for transfers between devices: 16.3 us -> 19 us  [exchanged(): return lax.ppermute(value, 'pos', [(i, i ^ step) for i in range(peers)])]
    pallas_call x6 -> x10, Pallas kernels: 23.5 us -> 25.7 us  [the longest x1 8.18 us: mix(): pl.pallas_call(mix_later_kernel, in_specs=ins + [anywhere], out_specs=out...]
    ppermute x12 -> x16, starting transfers between devices: 29.2 us -> 27.4 us  [exchanged(): return lax.ppermute(value, 'pos', [(i, i ^ step) for i in range(peers)])]
  transfers between devices with their start and end apart: 16 -> 20, of which waited for: 6 -> 4; matrix products, arithmetic and copies ran while one was open for 0% -> 0% of each run, Pallas kernels for 41% -> 39%
where the time goes in v5:
time: 136 us; the launch traced here: 135 us
  Pallas kernels  54 us (40%)
  starting transfers between devices  49.8 us (37%)
  waiting for transfers between devices  22.1 us (16%)
  local copies, waits for them, and re-layouts  5.75 us (4%)
  other arithmetic  2.12 us (2%)
    ppermute x16, starting transfers between devices, exchanged(): return lax.ppermute(value, 'pos', [(i, i ^ step) for i in range(peers)])  27.4 us
    pallas_call x9, Pallas kernels, attend(): pl.pallas_call(kernel, in_specs=[scalars, scalars, vector, vector] + [vec...  20.6 us
    ppermute x16, waiting for transfers between devices, exchanged(): return lax.ppermute(value, 'pos', [(i, i ^ step) for i in range(peers)])  19 us
    all_to_all x3, starting transfers between devices, exchanged_near(): lax.all_to_all(value, 'pos', 0, 0, axis_index_groups=groups, tiled=True)  16.8 us
    pallas_call x1, Pallas kernels, mix(): pl.pallas_call(mix_later_kernel, in_specs=ins + [anywhere], out_specs=out...  8.18 us
    pallas_call x5, Pallas kernels, unpack(): pl.pallas_call(kernel, in_specs=[pl.BlockSpec(memory_space=pltpu.SMEM), p...  6.96 us
    unnamed x38, local copies, waits for them, and re-layouts  5.75 us
    ppermute x1, starting transfers between devices, shards(): earlier = lax.ppermute(tail, 'pos', [(i, i + 1) for i in range(peers - 1)])  5.66 us
  transfers between devices with their start and end apart: 20, of which 4 were waited for; matrix products, arithmetic and copies ran while one was open for 0% of the time, Pallas kernels for 39%

profile of v5, /device:TPU:0, one launch (start us, length us, event | category | flops | bytes accessed | tf_op | source)
XLA Modules:
  0.0 134.6 jit_solution(18036720318242802188)
XLA Ops:
  0.6 2.1 %multiply_convert_fusion._ = bf16[128,2048]{1,0:T(8,128)(2,1)} fusion(bf16[512,2048]{1,0:T(8,128)(2,1)} %value.3, bf16[512,2048]{1,0:T(8,128)(2,1)} %key.3), kind=kLoop, calls=%fused_computation | loop fusion | flops 1048576 | bytes 1572864 | tf_op jit(solution)/shard_map/convert_element_type | solution.py:691
  2.8 5.7 %collective-permute-start = (bf16[128,2048]{1,0:T(8,128)(2,1)}, bf16[128,2048]{1,0:T(8,128)(2,1)}, u32[]{:S(2)}, u32[]{:S(2)}) collective-permute-start(bf16[128,2048]{1,0:T(8,128)(2,1)} %multiply_convert_fusion._), channel_id=1, source_target_pairs={{0,2},{2,4},{4,6},{6,8},{8,10},{10,12},{12,14},{1,3},{3,5},{5,7},{... | collective-permute-start | bytes 1572872 | tf_op jit(solution)/shard_map/ppermute | solution.py:692
  8.4 5.1 %pack.1 = (s32[48]{0:T(128)}, bf16[4,2,32,2560]{3,2,1,0:T(8,128)(2,1)}, bf16[2,32,2048]{2,1,0:T(8,128)(2,1)}, bf16[2,32,2048]{2,1,0:T(8,128)(2,1)}, bf16[2,32,20...) custom-call(s32[16]{0:T(128)} %blocks.1, ...), custom_call_target="tpu_custom_call" | custom-call | flops 21474836480 | bytes 1000 | tf_op jit(solution)/shard_map/pack/pallas_call | solution.py:518
  13.5 4.4 %all-to-all-start = ((bf16[4,2,32,2560]{3,2,1,0:T(8,128)(2,1)}), bf16[4,2,32,2560]{3,2,1,0:T(8,128)(2,1)}, u32[]{:S(2)}, u32[]{:S(2)}) async-start(bf16[4,2,32,2560]{3,2,1,0:T(8,128)(2,1)} %get-tuple-element.50), calls=%async_computation | async-start | bytes 2621440 | tf_op jit(solution)/shard_map/all_to_all | solution.py:675
  18.0 1.9 %collective-permute-start.3 = (bf16[2,32,2048]{2,1,0:T(8,128)(2,1)}, bf16[2,32,2048]{2,1,0:T(8,128)(2,1)}, u32[]{:S(2)}, u32[]{:S(2)}) collective-permute-start(bf16[2,32,2048]{2,1,0:T(8,128)(2,1)} %get-tuple-element.47), channel_id=1, source_target_pairs={{0,8},{2,10},{4,12},{6,14},{8,0},{10,2},{12,4},{14,6},{1,9},{3,11}... | collective-permute-start | bytes 786440 | tf_op jit(solution)/shard_map/ppermute | solution.py:668
  19.8 2.5 %collective-permute-start.6 = (bf16[2,32,2048]{2,1,0:T(8,128)(2,1)}, bf16[2,32,2048]{2,1,0:T(8,128)(2,1)}, u32[]{:S(2)}, u32[]{:S(2)}) collective-permute-start(bf16[2,32,2048]{2,1,0:T(8,128)(2,1)} %get-tuple-element.55), channel_id=1, source_target_pairs={{0,10},{2,8},{4,14},{6,12},{8,2},{10,0},{12,6},{14,4},{1,11},{3,9}... | collective-permute-start | bytes 786440 | tf_op jit(solution)/shard_map/ppermute | solution.py:668
  22.3 2.7 %collective-permute-start.7 = (bf16[2,32,2048]{2,1,0:T(8,128)(2,1)}, bf16[2,32,2048]{2,1,0:T(8,128)(2,1)}, u32[]{:S(2)}, u32[]{:S(2)}) collective-permute-start(bf16[2,32,2048]{2,1,0:T(8,128)(2,1)} %get-tuple-element.58), channel_id=1, source_target_pairs={{0,12},{2,14},{4,8},{6,10},{8,4},{10,6},{12,0},{14,2},{1,13},{3,15... | collective-permute-start | bytes 786440 | tf_op jit(solution)/shard_map/ppermute | solution.py:668
  26.6 8.2 %mix_later.1 = (bf16[512,2048]{1,0:T(8,128)(2,1)}, bf16[16,512,128]{2,1,0:T(8,128)(2,1)S(1)}, bf16[16,128,512]{2,1,0:T(8,128)(2,1)S(1)}) custom-call(bf16[512,2048]{1,0:T(8,128)(2,1)} %gate.3, bf16[512,2048]{1,0:T(8,128)(2,1)} %key.3, bf16[512,2048]{1,0:T(8,128)(2,1)} %value.3, f32[2048,128]{1,0:T(8,128)S(1)} %copy-done.1, bf16[512,256]{1,0:T(8,128)(2,1)S(1)} %copy-done.3, ...), custom_call_target="tpu_custom_call" | custom-call | flops 107374182400 | bytes 1000 | tf_op jit(solution)/shard_map/mix_later/pallas_call | solution.py:129
  34.8 4.6 %mix_first.1 = (bf16[512,2048]{1,0:T(8,128)(2,1)}, bf16[16,512,128]{2,1,0:T(8,128)(2,1)S(1)}, bf16[16,128,512]{2,1,0:T(8,128)(2,1)S(1)}) custom-call(bf16[512,2048]{1,0:T(8,128)(2,1)} %gate.3, bf16[512,2048]{1,0:T(8,128)(2,1)} %key.3, bf16[512,2048]{1,0:T(8,128)(2,1)} %value.3, ...), custom_call_target="tpu_custom_call", output_to_operand_aliasing={{0}: (7, {}), {1}: (8, {}), {2}: (9, {})} | custom-call | flops 107374182400 | bytes 1000 | tf_op jit(solution)/shard_map/mix_first/pallas_call | solution.py:133
  39.4 1.7 %cut.2 = (bf16[4,512,128]{2,1,0:T(8,128)(2,1)}, bf16[4,512,128]{2,1,0:T(8,128)(2,1)}, bf16[4,512,128]{2,1,0:T(8,128)(2,1)S(1)}, bf16[4,512,128]{2,1,0:T(8,128)(2,1)S(1)}) custom-call(s32[48]{0:T(128)S(1)} %copy-done, bf16[16,512,128]{2,1,0:T(8,128)(2,1)S(1)} %get-tuple-element.42.refs_0_.refs_1_.rows, ...), custom_call_target="tpu_custom_call" | custom-call | flops 1000 | bytes 1000 | tf_op jit(solution)/shard_map/cut/pallas_call | solution.py:322
  41.2 1.8 %collective-permute-start.1 = (bf16[4,512,128]{2,1,0:T(8,128)(2,1)}, bf16[4,512,128]{2,1,0:T(8,128)(2,1)}, u32[]{:S(2)}, u32[]{:S(2)}) collective-permute-start(bf16[4,512,128]{2,1,0:T(8,128)(2,1)} %get-tuple-element.44._), channel_id=1, source_target_pairs={{0,2},{2,0},{4,6},{6,4},{8,10},{10,8},{12,14},{14,12},{1,3},{3,1},... | collective-permute-start | bytes 1572872 | tf_op jit(solution)/shard_map/ppermute | solution.py:668
  43.0 1.9 %attend_first.4 = (bf16[2,32,1536]{2,1,0:T(8,128)(2,1)S(1)}, bf16[2,32,512]{2,1,0:T(8,128)(2,1)S(1)}) custom-call(s32[48]{0:T(128)S(1)} %copy-done, f32[16]{0:T(128)S(1)} %copy-done.2, bf16[16,128,512]{2,1,0:T(8,128)(2,1)S(1)} %get-tuple-element.41.keys, bf16[16,512,128]{2,1,0:T(8,128)(2,1)S(1)} %get-tuple-element.42.refs_0_.refs_1_.rows, ...), custom_call_target="tpu_custom_call" | custom-call | flops 21474836480 | bytes 1000 | tf_op jit(solution)/shard_map/attend_first/pallas_call | solution.py:271
  45.0 3.1 %all-to-all-done.near.refs_5_ = bf16[4,2,32,2560]{3,2,1,0:T(8,128)(2,1)} async-done(((bf16[4,2,32,2560]{3,2,1,0:T(8,128)(2,1)}), bf16[4,2,32,2560]{3,2,1,0:T(8,128)(2,1)}, u32[]{:S(2)}, u32[]{:S(2)}) %all-to-all-start) | async-done | bytes 1310752 | tf_op jit(solution)/shard_map/all_to_all | solution.py:675
  49.6 5.7 %attend_near.1.refs_4_ = bf16[4,2,32,2048]{3,2,1,0:T(8,128)(2,1)} custom-call(s32[48]{0:T(128)S(1)} %copy-done, f32[16]{0:T(128)S(1)} %copy-done.2, bf16[16,128,512]{2,1,0:T(8,128)(2,1)S(1)} %copy-done.6, bf16[16,512,128]{2,1,0:T(8,128)(2,1)S(1)} %get-tuple-element.42.refs_0_.refs_1_.rows, bf16[2,32,1536]{2,1,0:T(8,128)(2,1)S(1)} %get-tuple-element.49._, ...), custom_call_target="tpu_custom_call" | custom-call | flops 21474836480 | bytes 1000 | tf_op jit(solution)/shard_map/attend_near/pallas_call | solution.py:271
  55.3 4.3 %all-to-all-start.2 = ((bf16[4,2,32,2048]{3,2,1,0:T(8,128)(2,1)}), bf16[4,2,32,2048]{3,2,1,0:T(8,128)(2,1)}, u32[]{:S(2)}, u32[]{:S(2)}) async-start(bf16[4,2,32,2048]{3,2,1,0:T(8,128)(2,1)} %attend_near.1.refs_4_), calls=%async_computation.2 | async-start | bytes 2097152 | tf_op jit(solution)/shard_map/all_to_all | solution.py:675
  59.6 9.7 %collective-permute-done.2.refs_3_ = bf16[4,512,128]{2,1,0:T(8,128)(2,1)} collective-permute-done((bf16[4,512,128]{2,1,0:T(8,128)(2,1)}, bf16[4,512,128]{2,1,0:T(8,128)(2,1)}, u32[]{:S(2)}, u32[]{:S(2)}) %collective-permute-start.2) | collective-permute-done | bytes 524320 | tf_op jit(solution)/shard_map/ppermute | solution.py:668
  69.3 2.2 %collective-permute-start.9 = (bf16[2,32,1536]{2,1,0:T(8,128)(2,1)S(1)}, bf16[2,32,1536]{2,1,0:T(8,128)(2,1)S(1)}, u32[]{:S(2)}, u32[]{:S(2)}) collective-permute-start(bf16[2,32,1536]{2,1,0:T(8,128)(2,1)S(1)} %get-tuple-element.49._), channel_id=1, source_target_pairs={{0,8},{2,10},{4,12},{6,14},{8,0},{10,2},{12,4},{14,6},{1,9},{3,11}... | collective-permute-start | bytes 589832 | tf_op jit(solution)/shard_map/ppermute | solution.py:668
  72.9 2.0 %collective-permute-start.4 = (bf16[2,512,128]{2,1,0:T(8,128)(2,1)S(1)}, bf16[2,512,128]{2,1,0:T(8,128)(2,1)S(1)}, u32[]{:S(2)}, u32[]{:S(2)}) collective-permute-start(bf16[2,512,128]{2,1,0:T(8,128)(2,1)S(1)} %get-tuple-element.52._), channel_id=1, source_target_pairs={{0,4},{2,6},{4,0},{6,2},{8,12},{10,14},{12,8},{14,10},{1,5},{3,7},... | collective-permute-start | bytes 786440 | tf_op jit(solution)/shard_map/ppermute | solution.py:668
  74.9 2.0 %attend_first.5 = (bf16[2,32,1536]{2,1,0:T(8,128)(2,1)S(1)}, bf16[2,32,512]{2,1,0:T(8,128)(2,1)S(1)}) custom-call(s32[48]{0:T(128)S(1)} %copy-done, f32[16]{0:T(128)S(1)} %copy-done.2, bf16[16,128,512]{2,1,0:T(8,128)(2,1)S(1)} %copy-done.7, bf16[16,512,128]{2,1,0:T(8,128)(2,1)S(1)} %get-tuple-element.42.refs_0_.refs_1_.rows, ...), custom_call_target="tpu_custom_call" | custom-call | flops 21474836480 | bytes 1000 | tf_op jit(solution)/shard_map/attend_first/pallas_call | solution.py:271
  78.1 2.0 %attend_first.6 = (bf16[2,32,1536]{2,1,0:T(8,128)(2,1)S(1)}, bf16[2,32,512]{2,1,0:T(8,128)(2,1)S(1)}) custom-call(s32[48]{0:T(128)S(1)} %copy-done, f32[16]{0:T(128)S(1)} %copy-done.2, bf16[16,128,512]{2,1,0:T(8,128)(2,1)S(1)} %copy-done.7, bf16[16,512,128]{2,1,0:T(8,128)(2,1)S(1)} %get-tuple-element.42.refs_0_.refs_1_.rows, ...), custom_call_target="tpu_custom_call" | custom-call | flops 21474836480 | bytes 1000 | tf_op jit(solution)/shard_map/attend_first/pallas_call | solution.py:271
  80.1 2.7 %collective-permute-start.11 = (bf16[2,32,1536]{2,1,0:T(8,128)(2,1)S(1)}, bf16[2,32,1536]{2,1,0:T(8,128)(2,1)S(1)}, u32[]{:S(2)}, u32[]{:S(2)}) collective-permute-start(bf16[2,32,1536]{2,1,0:T(8,128)(2,1)S(1)} %get-tuple-element.60._), channel_id=1, source_target_pairs={{0,12},{2,14},{4,8},{6,10},{8,4},{10,6},{12,0},{14,2},{1,13},{3,15... | collective-permute-start | bytes 589832 | tf_op jit(solution)/shard_map/ppermute | solution.py:668
  82.9 2.0 %attend_first.7 = (bf16[2,32,1536]{2,1,0:T(8,128)(2,1)S(1)}, bf16[2,32,512]{2,1,0:T(8,128)(2,1)S(1)}) custom-call(s32[48]{0:T(128)S(1)} %copy-done, f32[16]{0:T(128)S(1)} %copy-done.2, bf16[16,128,512]{2,1,0:T(8,128)(2,1)S(1)} %copy-done.7, bf16[16,512,128]{2,1,0:T(8,128)(2,1)S(1)} %get-tuple-element.42.refs_0_.refs_1_.rows, ...), custom_call_target="tpu_custom_call" | custom-call | flops 21474836480 | bytes 1000 | tf_op jit(solution)/shard_map/attend_first/pallas_call | solution.py:271
  85.5 4.2 %collective-permute-done.5.refs_3_ = bf16[2,512,128]{2,1,0:T(8,128)(2,1)S(1)} collective-permute-done((bf16[2,512,128]{2,1,0:T(8,128)(2,1)S(1)}, bf16[2,512,128]{2,1,0:T(8,128)(2,1)S(1)}, u32[]{:S(2)}, u32[]{:S(2)}) %collective-permute-start.5) | collective-permute-done | bytes 262176 | tf_op jit(solution)/shard_map/ppermute | solution.py:668
  89.7 2.5 %collective-permute-start.12 = (bf16[2,32,1536]{2,1,0:T(8,128)(2,1)S(1)}, bf16[2,32,1536]{2,1,0:T(8,128)(2,1)S(1)}, u32[]{:S(2)}, u32[]{:S(2)}) collective-permute-start(bf16[2,32,1536]{2,1,0:T(8,128)(2,1)S(1)} %get-tuple-element.63.refs_4_), channel_id=1, source_target_pairs={{0,14},{2,12},{4,10},{6,8},{8,6},{10,4},{12,2},{14,0},{1,15},{3,13... | collective-permute-start | bytes 589832 | tf_op jit(solution)/shard_map/ppermute | solution.py:668
  92.2 5.0 %collective-permute-done.4.refs_1_ = bf16[2,512,128]{2,1,0:T(8,128)(2,1)S(1)} collective-permute-done((bf16[2,512,128]{2,1,0:T(8,128)(2,1)S(1)}, bf16[2,512,128]{2,1,0:T(8,128)(2,1)S(1)}, u32[]{:S(2)}, u32[]{:S(2)}) %collective-permute-start.4) | collective-permute-done | bytes 262176 | tf_op jit(solution)/shard_map/ppermute | solution.py:668
  97.3 3.0 %attend_extra.1 = (bf16[4,2,32,512]{3,2,1,0:T(8,128)(2,1)}, bf16[4,2,32,512]{3,2,1,0:T(8,128)(2,1)S(1)}) custom-call(s32[48]{0:T(128)S(1)} %copy-done, f32[16]{0:T(128)S(1)} %copy-done.2, bf16[2,512,128]{2,1,0:T(8,128)(2,1)S(1)} %get-tuple-element.51.refs_0_, bf16[2,512,128]{2,1,0:T(8,128)(2,1)S(1)} %collective-permute-done.4.refs_1_, ...), custom_call_target="tpu_custom_call" | custom-call | flops 21474836480 | bytes 1000 | tf_op jit(solution)/shard_map/attend_extra/pallas_call | solution.py:367
  101.8 2.1 %attend_second.5._ = bf16[2,32,1024]{2,1,0:T(8,128)(2,1)} custom-call(s32[48]{0:T(128)S(1)} %copy-done, f32[16]{0:T(128)S(1)} %copy-done.2, bf16[16,128,512]{2,1,0:T(8,128)(2,1)S(1)} %copy-done.7, bf16[16,512,128]{2,1,0:T(8,128)(2,1)S(1)} %get-tuple-element.42.refs_0_.refs_1_.rows, bf16[4,2,32,512]{3,2,1,0:T(8,128)(2,1)S(1)} %get-tuple-element.64.extra._, ...), custom_call_target="tpu_custom_call" | custom-call | flops 21474836480 | bytes 1000 | tf_op jit(solution)/shard_map/attend_second/pallas_call | solution.py:271
  103.9 2.9 %collective-permute-start.15 = (bf16[2,32,1024]{2,1,0:T(8,128)(2,1)}, bf16[2,32,1024]{2,1,0:T(8,128)(2,1)}, u32[]{:S(2)}, u32[]{:S(2)}) collective-permute-start(bf16[2,32,1024]{2,1,0:T(8,128)(2,1)} %attend_second.5._), channel_id=1, source_target_pairs={{0,10},{2,8},{4,14},{6,12},{8,2},{10,0},{12,6},{14,4},{1,11},{3,9}... | collective-permute-start | bytes 393224 | tf_op jit(solution)/shard_map/ppermute | solution.py:668
  106.8 2.1 %attend_second.6._ = bf16[2,32,1024]{2,1,0:T(8,128)(2,1)} custom-call(s32[48]{0:T(128)S(1)} %copy-done, f32[16]{0:T(128)S(1)} %copy-done.2, bf16[16,128,512]{2,1,0:T(8,128)(2,1)S(1)} %copy-done.7, bf16[16,512,128]{2,1,0:T(8,128)(2,1)S(1)} %get-tuple-element.42.refs_0_.refs_1_.rows, bf16[4,2,32,512]{3,2,1,0:T(8,128)(2,1)S(1)} %get-tuple-element.64.extra._, ...), custom_call_target="tpu_custom_call" | custom-call | flops 21474836480 | bytes 1000 | tf_op jit(solution)/shard_map/attend_second/pallas_call | solution.py:271
  109.9 8.1 %all-to-all-start.1 = ((bf16[4,2,32,512]{3,2,1,0:T(8,128)(2,1)}), bf16[4,2,32,512]{3,2,1,0:T(8,128)(2,1)S(1)}, u32[]{:S(2)}, u32[]{:S(2)}) async-start(bf16[4,2,32,512]{3,2,1,0:T(8,128)(2,1)} %get-tuple-element.69), calls=%async_computation.1 | async-start | bytes 524288 | tf_op jit(solution)/shard_map/all_to_all | solution.py:675
  121.9 3.1 %collective-permute-start.13 = (bf16[2,32,1024]{2,1,0:T(8,128)(2,1)S(1)}, bf16[2,32,1024]{2,1,0:T(8,128)(2,1)S(1)}, u32[]{:S(2)}, u32[]{:S(2)}) collective-permute-start(bf16[2,32,1024]{2,1,0:T(8,128)(2,1)S(1)} %attend_second.7.refs_4_), channel_id=1, source_target_pairs={{0,14},{2,12},{4,10},{6,8},{8,6},{10,4},{12,2},{14,0},{1,15},{3,13... | collective-permute-start | bytes 393224 | tf_op jit(solution)/shard_map/ppermute | solution.py:668
  125.0 2.6 %unpack_early.1._ = bf16[16,32,2048]{2,1,0:T(8,128)(2,1)} custom-call(s32[48]{0:T(128)S(1)} %copy-done, bf16[4,2,32,2048]{3,2,1,0:T(8,128)(2,1)} %all-to-all-done.2.near, bf16[2,32,1536]{2,1,0:T(8,128)(2,1)S(1)} %collective-permute-done.9.refs_1_.refs_0_, bf16[2,32,1536]{2,1,0:T(8,128)(2,1)S(1)} %collective-permute-done.10.refs_1_, ...), custom_call_target="tpu_custom_call" | custom-call | flops 1000 | bytes 1000 | tf_op jit(solution)/shard_map/unpack_early/pallas_call | solution.py:578
  (68 shorter events, 20.1 us)
Async XLA Ops:
  2.8 32.1 %collective-permute-start = (bf16[128,2048]{1,0:T(8,128)(2,1)}, bf16[128,2048]{1,0:T(8,128)(2,1)}, u32[]{:S(2)}, u32[]{:S(2)}) collective-permute-start(bf16[128,2048]{1,0:T(8,128)(2,1)} %multiply_convert_fusion._), channel_id=1, source_target_pairs={{0,2},{2,4},{4,6},{6,8},{8,10},{10,12},{12,14},{1,3},{3,5},{5,7},{... | collective-permute-start | bytes 1572872 | tf_op jit(solution)/shard_map/ppermute | solution.py:692
  13.5 12.2 %copy-start = (s32[48]{0:T(128)S(1)}, s32[48]{0:T(128)}, u32[]{:S(2)}) copy-start(s32[48]{0:T(128)} %get-tuple-element.36._.info) | copy-start | bytes 580
  13.5 12.2 %copy-start.1 = (f32[2048,128]{1,0:T(8,128)S(1)}, f32[2048,128]{1,0:T(8,128)}, u32[]{:S(2)}) copy-start(f32[2048,128]{1,0:T(8,128)} %filters.3) | copy-start | bytes 3145732
  13.5 12.2 %copy-start.4 = (bf16[256,256]{1,0:T(8,128)(2,1)S(1)}, bf16[256,256]{1,0:T(8,128)(2,1)}, u32[]{:S(2)}) copy-start(bf16[256,256]{1,0:T(8,128)(2,1)} %constant.5.clone.inverse) | copy-start | bytes 393220
  13.5 34.5 %all-to-all-start = ((bf16[4,2,32,2560]{3,2,1,0:T(8,128)(2,1)}), bf16[4,2,32,2560]{3,2,1,0:T(8,128)(2,1)}, u32[]{:S(2)}, u32[]{:S(2)}) async-start(bf16[4,2,32,2560]{3,2,1,0:T(8,128)(2,1)} %get-tuple-element.50), calls=%async_computation | async-start | bytes 2621440 | tf_op jit(solution)/shard_map/all_to_all | solution.py:675
  18.0 23.3 %collective-permute-start.3 = (bf16[2,32,2048]{2,1,0:T(8,128)(2,1)}, bf16[2,32,2048]{2,1,0:T(8,128)(2,1)}, u32[]{:S(2)}, u32[]{:S(2)}) collective-permute-start(bf16[2,32,2048]{2,1,0:T(8,128)(2,1)} %get-tuple-element.47), channel_id=1, source_target_pairs={{0,8},{2,10},{4,12},{6,14},{8,0},{10,2},{12,4},{14,6},{1,9},{3,11}... | collective-permute-start | bytes 786440 | tf_op jit(solution)/shard_map/ppermute | solution.py:668
  19.8 55.1 %collective-permute-start.6 = (bf16[2,32,2048]{2,1,0:T(8,128)(2,1)}, bf16[2,32,2048]{2,1,0:T(8,128)(2,1)}, u32[]{:S(2)}, u32[]{:S(2)}) collective-permute-start(bf16[2,32,2048]{2,1,0:T(8,128)(2,1)} %get-tuple-element.55), channel_id=1, source_target_pairs={{0,10},{2,8},{4,14},{6,12},{8,2},{10,0},{12,6},{14,4},{1,11},{3,9}... | collective-permute-start | bytes 786440 | tf_op jit(solution)/shard_map/ppermute | solution.py:668
  22.3 55.8 %collective-permute-start.7 = (bf16[2,32,2048]{2,1,0:T(8,128)(2,1)}, bf16[2,32,2048]{2,1,0:T(8,128)(2,1)}, u32[]{:S(2)}, u32[]{:S(2)}) collective-permute-start(bf16[2,32,2048]{2,1,0:T(8,128)(2,1)} %get-tuple-element.58), channel_id=1, source_target_pairs={{0,12},{2,14},{4,8},{6,10},{8,4},{10,6},{12,0},{14,2},{1,13},{3,15... | collective-permute-start | bytes 786440 | tf_op jit(solution)/shard_map/ppermute | solution.py:668
  25.0 57.9 %collective-permute-start.8 = (bf16[2,32,2048]{2,1,0:T(8,128)(2,1)}, bf16[2,32,2048]{2,1,0:T(8,128)(2,1)}, u32[]{:S(2)}, u32[]{:S(2)}) collective-permute-start(bf16[2,32,2048]{2,1,0:T(8,128)(2,1)} %get-tuple-element.61), channel_id=1, source_target_pairs={{0,14},{2,12},{4,10},{6,8},{8,6},{10,4},{12,2},{14,0},{1,15},{3,13... | collective-permute-start | bytes 786440 | tf_op jit(solution)/shard_map/ppermute | solution.py:668
  39.4 3.6 %copy-start.5 = (bf16[16,128,512]{2,1,0:T(8,128)(2,1)}, bf16[16,128,512]{2,1,0:T(8,128)(2,1)S(1)}, u32[]{:S(2)}) copy-start(bf16[16,128,512]{2,1,0:T(8,128)(2,1)S(1)} %get-tuple-element.41.keys) | copy-start | bytes 6291460
  39.4 3.6 %copy-start.2 = (f32[16]{0:T(128)S(1)}, f32[16]{0:T(128)}, u32[]{:S(2)}) copy-start(f32[16]{0:T(128)} %temps.19) | copy-start | bytes 196
  39.4 3.6 %copy-start.15 = (bf16[2,32,512]{2,1,0:T(8,128)(2,1)S(1)}, bf16[2,32,512]{2,1,0:T(8,128)(2,1)}, u32[]{:S(2)}) copy-start(bf16[2,32,512]{2,1,0:T(8,128)(2,1)} %get-tuple-element.48.rest) | copy-start | bytes 196612
  41.1 28.2 %collective-permute-start.2 = (bf16[4,512,128]{2,1,0:T(8,128)(2,1)}, bf16[4,512,128]{2,1,0:T(8,128)(2,1)}, u32[]{:S(2)}, u32[]{:S(2)}) collective-permute-start(bf16[4,512,128]{2,1,0:T(8,128)(2,1)} %get-tuple-element.46), channel_id=1, source_target_pairs={{0,4},{2,6},{4,0},{6,2},{8,12},{10,14},{12,8},{14,10},{1,5},{3,7},... | collective-permute-start | bytes 1572872 | tf_op jit(solution)/shard_map/ppermute | solution.py:668
  41.2 30.3 %collective-permute-start.1 = (bf16[4,512,128]{2,1,0:T(8,128)(2,1)}, bf16[4,512,128]{2,1,0:T(8,128)(2,1)}, u32[]{:S(2)}, u32[]{:S(2)}) collective-permute-start(bf16[4,512,128]{2,1,0:T(8,128)(2,1)} %get-tuple-element.44._), channel_id=1, source_target_pairs={{0,2},{2,0},{4,6},{6,4},{8,10},{10,8},{12,14},{14,12},{1,3},{3,1},... | collective-permute-start | bytes 1572872 | tf_op jit(solution)/shard_map/ppermute | solution.py:668
  45.0 10.3 %copy-start.11 = (bf16[2,32,512]{2,1,0:T(8,128)(2,1)}, bf16[2,32,512]{2,1,0:T(8,128)(2,1)S(1)}, u32[]{:S(2)}) copy-start(bf16[2,32,512]{2,1,0:T(8,128)(2,1)S(1)} %get-tuple-element.65.refs_2_) | copy-start | bytes 196612
  55.3 54.6 %all-to-all-start.2 = ((bf16[4,2,32,2048]{3,2,1,0:T(8,128)(2,1)}), bf16[4,2,32,2048]{3,2,1,0:T(8,128)(2,1)}, u32[]{:S(2)}, u32[]{:S(2)}) async-start(bf16[4,2,32,2048]{3,2,1,0:T(8,128)(2,1)} %attend_near.1.refs_4_), calls=%async_computation.2 | async-start | bytes 2097152 | tf_op jit(solution)/shard_map/all_to_all | solution.py:675
  59.6 15.3 %copy-start.7 = (bf16[16,128,512]{2,1,0:T(8,128)(2,1)S(1)}, bf16[16,128,512]{2,1,0:T(8,128)(2,1)}, u32[]{:S(2)}) copy-start(bf16[16,128,512]{2,1,0:T(8,128)(2,1)} %copy-done.5) | copy-start | bytes 6291460
  59.6 15.3 %copy-start.16 = (bf16[2,32,512]{2,1,0:T(8,128)(2,1)S(1)}, bf16[2,32,512]{2,1,0:T(8,128)(2,1)}, u32[]{:S(2)}) copy-start(bf16[2,32,512]{2,1,0:T(8,128)(2,1)} %get-tuple-element.56.rest) | copy-start | bytes 196612
  69.3 30.9 %collective-permute-start.9 = (bf16[2,32,1536]{2,1,0:T(8,128)(2,1)S(1)}, bf16[2,32,1536]{2,1,0:T(8,128)(2,1)S(1)}, u32[]{:S(2)}, u32[]{:S(2)}) collective-permute-start(bf16[2,32,1536]{2,1,0:T(8,128)(2,1)S(1)} %get-tuple-element.49._), channel_id=1, source_target_pairs={{0,8},{2,10},{4,12},{6,14},{8,0},{10,2},{12,4},{14,6},{1,9},{3,11}... | collective-permute-start | bytes 589832 | tf_op jit(solution)/shard_map/ppermute | solution.py:668
  72.9 24.4 %collective-permute-start.4 = (bf16[2,512,128]{2,1,0:T(8,128)(2,1)S(1)}, bf16[2,512,128]{2,1,0:T(8,128)(2,1)S(1)}, u32[]{:S(2)}, u32[]{:S(2)}) collective-permute-start(bf16[2,512,128]{2,1,0:T(8,128)(2,1)S(1)} %get-tuple-element.52._), channel_id=1, source_target_pairs={{0,4},{2,6},{4,0},{6,2},{8,12},{10,14},{12,8},{14,10},{1,5},{3,7},... | collective-permute-start | bytes 786440 | tf_op jit(solution)/shard_map/ppermute | solution.py:668
  76.9 24.9 %collective-permute-start.10 = (bf16[2,32,1536]{2,1,0:T(8,128)(2,1)S(1)}, bf16[2,32,1536]{2,1,0:T(8,128)(2,1)S(1)}, u32[]{:S(2)}, u32[]{:S(2)}) collective-permute-start(bf16[2,32,1536]{2,1,0:T(8,128)(2,1)S(1)} %get-tuple-element.57._), channel_id=1, source_target_pairs={{0,10},{2,8},{4,14},{6,12},{8,2},{10,0},{12,6},{14,4},{1,11},{3,9}... | collective-permute-start | bytes 589832 | tf_op jit(solution)/shard_map/ppermute | solution.py:668
  78.1 4.8 %copy-start.17 = (bf16[2,32,512]{2,1,0:T(8,128)(2,1)S(1)}, bf16[2,32,512]{2,1,0:T(8,128)(2,1)}, u32[]{:S(2)}) copy-start(bf16[2,32,512]{2,1,0:T(8,128)(2,1)} %get-tuple-element.62.rest) | copy-start | bytes 196612
  80.1 26.7 %collective-permute-start.11 = (bf16[2,32,1536]{2,1,0:T(8,128)(2,1)S(1)}, bf16[2,32,1536]{2,1,0:T(8,128)(2,1)S(1)}, u32[]{:S(2)}, u32[]{:S(2)}) collective-permute-start(bf16[2,32,1536]{2,1,0:T(8,128)(2,1)S(1)} %get-tuple-element.60._), channel_id=1, source_target_pairs={{0,12},{2,14},{4,8},{6,10},{8,4},{10,6},{12,0},{14,2},{1,13},{3,15... | collective-permute-start | bytes 589832 | tf_op jit(solution)/shard_map/ppermute | solution.py:668
  82.9 6.9 %collective-permute-start.5 = (bf16[2,512,128]{2,1,0:T(8,128)(2,1)S(1)}, bf16[2,512,128]{2,1,0:T(8,128)(2,1)S(1)}, u32[]{:S(2)}, u32[]{:S(2)}) collective-permute-start(bf16[2,512,128]{2,1,0:T(8,128)(2,1)S(1)} %get-tuple-element.54), channel_id=1, source_target_pairs={{0,2},{2,0},{4,6},{6,4},{8,10},{10,8},{12,14},{14,12},{1,3},{3,1},... | collective-permute-start | bytes 786440 | tf_op jit(solution)/shard_map/ppermute | solution.py:668
  89.7 28.2 %collective-permute-start.12 = (bf16[2,32,1536]{2,1,0:T(8,128)(2,1)S(1)}, bf16[2,32,1536]{2,1,0:T(8,128)(2,1)S(1)}, u32[]{:S(2)}, u32[]{:S(2)}) collective-permute-start(bf16[2,32,1536]{2,1,0:T(8,128)(2,1)S(1)} %get-tuple-element.63.refs_4_), channel_id=1, source_target_pairs={{0,14},{2,12},{4,10},{6,8},{8,6},{10,4},{12,2},{14,0},{1,15},{3,13... | collective-permute-start | bytes 589832 | tf_op jit(solution)/shard_map/ppermute | solution.py:668
  100.2 6.6 %copy-start.9 = (bf16[4,2,32,512]{3,2,1,0:T(8,128)(2,1)}, bf16[4,2,32,512]{3,2,1,0:T(8,128)(2,1)S(1)}, u32[]{:S(2)}) copy-start(bf16[4,2,32,512]{3,2,1,0:T(8,128)(2,1)S(1)} %get-tuple-element.64.extra._) | copy-start | bytes 786436
  101.7 26.6 %collective-permute-start.16 = (bf16[2,32,1024]{2,1,0:T(8,128)(2,1)S(1)}, bf16[2,32,1024]{2,1,0:T(8,128)(2,1)}, u32[]{:S(2)}, u32[]{:S(2)}) collective-permute-start(bf16[2,32,1024]{2,1,0:T(8,128)(2,1)S(1)} %attend_second.4._), channel_id=1, source_target_pairs={{0,8},{2,10},{4,12},{6,14},{8,0},{10,2},{12,4},{14,6},{1,9},{3,11}... | collective-permute-start | bytes 393224 | tf_op jit(solution)/shard_map/ppermute | solution.py:668
  103.9 26.1 %collective-permute-start.15 = (bf16[2,32,1024]{2,1,0:T(8,128)(2,1)}, bf16[2,32,1024]{2,1,0:T(8,128)(2,1)}, u32[]{:S(2)}, u32[]{:S(2)}) collective-permute-start(bf16[2,32,1024]{2,1,0:T(8,128)(2,1)} %attend_second.5._), channel_id=1, source_target_pairs={{0,10},{2,8},{4,14},{6,12},{8,2},{10,0},{12,6},{14,4},{1,11},{3,9}... | collective-permute-start | bytes 393224 | tf_op jit(solution)/shard_map/ppermute | solution.py:668
  106.8 11.2 %copy-start.14 = (bf16[2,32,512]{2,1,0:T(8,128)(2,1)S(1)}, bf16[2,32,512]{2,1,0:T(8,128)(2,1)}, u32[]{:S(2)}) copy-start(bf16[2,32,512]{2,1,0:T(8,128)(2,1)} %copy-done.13) | copy-start | bytes 196612
  108.9 22.8 %collective-permute-start.14 = (bf16[2,32,1024]{2,1,0:T(8,128)(2,1)}, bf16[2,32,1024]{2,1,0:T(8,128)(2,1)}, u32[]{:S(2)}, u32[]{:S(2)}) collective-permute-start(bf16[2,32,1024]{2,1,0:T(8,128)(2,1)} %attend_second.6._), channel_id=1, source_target_pairs={{0,12},{2,14},{4,8},{6,10},{8,4},{10,6},{12,0},{14,2},{1,13},{3,15... | collective-permute-start | bytes 393224 | tf_op jit(solution)/shard_map/ppermute | solution.py:668
  109.9 17.7 %all-to-all-start.1 = ((bf16[4,2,32,512]{3,2,1,0:T(8,128)(2,1)}), bf16[4,2,32,512]{3,2,1,0:T(8,128)(2,1)S(1)}, u32[]{:S(2)}, u32[]{:S(2)}) async-start(bf16[4,2,32,512]{3,2,1,0:T(8,128)(2,1)} %get-tuple-element.69), calls=%async_computation.1 | async-start | bytes 524288 | tf_op jit(solution)/shard_map/all_to_all | solution.py:675
  121.9 11.4 %collective-permute-start.13 = (bf16[2,32,1024]{2,1,0:T(8,128)(2,1)S(1)}, bf16[2,32,1024]{2,1,0:T(8,128)(2,1)S(1)}, u32[]{:S(2)}, u32[]{:S(2)}) collective-permute-start(bf16[2,32,1024]{2,1,0:T(8,128)(2,1)S(1)} %attend_second.7.refs_4_), channel_id=1, source_target_pairs={{0,14},{2,12},{4,10},{6,8},{8,6},{10,4},{12,2},{14,0},{1,15},{3,13... | collective-permute-start | bytes 393224 | tf_op jit(solution)/shard_map/ppermute | solution.py:668
  (7 other events, 11.9 us)

commit v6 on v5

--- a/solution.py
+++ b/solution.py
@@ -121,7 +121,7 @@
             jax.ShapeDtypeStruct((heads, rows, HEAD_DIM), jnp.bfloat16),
             jax.ShapeDtypeStruct((heads, HEAD_DIM, rows), jnp.bfloat16),
         ],
-        compiler_params=pltpu.CompilerParams(vmem_limit_bytes=48 * MIB),
+        compiler_params=pltpu.CompilerParams(vmem_limit_bytes=24 * MIB),
         cost_estimate=cost(MIX_FLOPS),
     )
     arrays = (gate, key, value, filters, forward, inverse)
@@ -475,6 +475,10 @@
     return copies
 
 
+def far_steps(half):
+    return [half + at for at in (*range(half // 2, half), *range(half // 2))]
+
+
 def far_copies(info, queries, steps, far, rest, wide, extras):
     half = queries.shape[2] // wide
     me = lax.axis_index("pos")
@@ -496,7 +500,7 @@
     route(info, 2 * half, slots, extras, rows, blocks_held, sites_held)
     base = jnp.bitwise_and(lax.axis_index("pos"), half)
     chans = queries.shape[2]
-    steps = range(half, half + count)
+    steps = far_steps(half)
     copies = far_copies(info, queries, steps, outs[:count], outs[count:], wide, extras)
     for at in range(half):
         copies += message(info, queries, base + at, near.at[at], wide, extras, 0, chans, None)
@@ -565,7 +569,7 @@
     near_wait = placed(info, out, near_sems, pieces)
     pieces = []
     for at, result in enumerate(results):
-        peer = jnp.bitwise_xor(me, half + at)
+        peer = jnp.bitwise_xor(me, far_steps(half)[at])
         pieces.append((peer, result, 0, split, 0, True))
         pieces.append((peer, result, split, wide, split, jnp.logical_not(home)))
     placed(info, out, sems, pieces)()
@@ -592,23 +596,26 @@
     )(info, near, *results, after)
 
 
-def unpack_kernel(wide, step, info, result, _, out, sems, extra_sems):
-    extras = extra_sems.shape[0] // 2
+def unpack_kernel(wide, steps, info, *refs):
+    results, out, semaphores = refs[: len(steps)], refs[len(steps) + 1], refs[len(steps) + 2 :]
     half = out.shape[2] // wide
-    slots = HOT - extras
     split = out.shape[2] - 2 * wide
-    peer = jnp.bitwise_xor(lax.axis_index("pos"), step)
     home = on_hot_half(info, 2 * half)
-    pieces = [
-        (peer, result, 0, wide, split + wide, True),
-        (peer, result, wide, wide, split, home),
-    ]
-    wait = placed(info, out, sems, pieces)
-    share = share_of(peer, half, out.shape[2] // HEAD_DIM)
-    sources = [result.at[extra, :, pl.ds(wide, wide)] for extra in range(extras)]
-    extra_wait = placed_extra(info, out, extra_sems, sources, share, jnp.logical_not(home))
-    wait()
-    extra_wait()
+    waits = []
+    for step, result, sems, extra_sems in zip(steps, results, semaphores[::2], semaphores[1::2]):
+        extras = extra_sems.shape[0] // 2
+        peer = jnp.bitwise_xor(lax.axis_index("pos"), step)
+        pieces = [
+            (peer, result, 0, wide, split + wide, True),
+            (peer, result, wide, wide, split, home),
+        ]
+        waits.append(placed(info, out, sems, pieces))
+        share = share_of(peer, half, out.shape[2] // HEAD_DIM)
+        sources = [result.at[extra, :, pl.ds(wide, wide)] for extra in range(extras)]
+        away = jnp.logical_not(home)
+        waits.append(placed_extra(info, out, extra_sems, sources, share, away))
+    for wait in waits:
+        wait()
 
 
 def placed_extra(info, out, sems, sources, share, whether):
@@ -642,23 +649,20 @@
         wait()
 
 
-def unpack(kernel, name, info, result, so_far, semaphores):
+def unpack(kernel, name, info, results, so_far, semaphores):
     anywhere = pl.BlockSpec(memory_space=pl.ANY)
+    vector = pl.BlockSpec(memory_space=pltpu.VMEM)
     return pl.pallas_call(
         kernel,
-        in_specs=[
-            pl.BlockSpec(memory_space=pltpu.SMEM),
-            pl.BlockSpec(memory_space=pltpu.VMEM),
-            anywhere,
-        ],
+        in_specs=[pl.BlockSpec(memory_space=pltpu.SMEM)] + [vector] * len(results) + [anywhere],
         out_specs=anywhere,
         out_shape=jax.ShapeDtypeStruct(so_far.shape, so_far.dtype),
-        input_output_aliases={2: 0},
+        input_output_aliases={1 + len(results): 0},
         scratch_shapes=[pltpu.SemaphoreType.DMA((count,)) for count in semaphores],
         compiler_params=pltpu.CompilerParams(vmem_limit_bytes=16 * MIB),
         cost_estimate=cost(UNPACK_FLOPS),
         name=name,
-    )(info, result, so_far)
+    )(info, *results, so_far)
 
 
 def exchanged(value, step):
@@ -695,7 +699,7 @@
     info, near, far, rest = pack(
         blocks, sites, queries, tail, rows, half, slots, extras, wide, half
     )
-    far = [exchanged(sent, half + at) for at, sent in enumerate(far)]
+    far = [exchanged(sent, step) for step, sent in zip(far_steps(half), far)]
     near = exchanged_near(near)
     hyena_out, valued, keyed = mix(
         gate_stream, key_stream, value_stream, earlier, filters, info
@@ -717,7 +721,7 @@
         result, back = attend(
             kernel, "attend_first", [heads - share, share], *own, [], after, arrays
         )
-        sent.append(exchanged(result, half + at))
+        sent.append(exchanged(result, far_steps(half)[at]))
         kept.append(back)
         return result
 
@@ -729,7 +733,9 @@
         results = attend(
             kernel, "attend_second", [2 * share] * count, *own, [extra], after, arrays, scratch
         )
-        late.extend(exchanged(result, half + at + more) for more, result in enumerate(results))
+        late.extend(
+            exchanged(result, far_steps(half)[at + more]) for more, result in enumerate(results)
+        )
         return results[0]
 
     sent, kept, late = [], [], []
@@ -746,11 +752,12 @@
     for at in range(half):
         after = second(at, 1, after)
     so_far = unpack_early(info, near_out, sent, after, queries.shape, wide)
-    kernel = unpack_extra_kernel
-    so_far = unpack(kernel, "unpack_extra", info, near_extra, so_far, [2 * extras] * half)
-    for at, result in enumerate(late):
-        kernel = functools.partial(unpack_kernel, wide, half + at)
-        so_far = unpack(kernel, "unpack", info, result, so_far, [2 * slots, 2 * extras])
+    count = [2 * extras] * half
+    so_far = unpack(unpack_extra_kernel, "unpack_extra", info, [near_extra], so_far, count)
+    for at in range(0, half, 2):
+        kernel = functools.partial(unpack_kernel, wide, far_steps(half)[at : at + 2])
+        results = late[at : at + 2]
+        so_far = unpack(kernel, "unpack", info, results, so_far, [2 * slots, 2 * extras] * 2)
     return (hyena_out, so_far)
 
 

time: 136 us -> 133 us (0.978)
  local copies, waits for them, and re-layouts: 5.75 us -> 10.5 us
  Pallas kernels: 54 us -> 49.9 us
  waiting for transfers between devices: 22.1 us -> 20.2 us
  starting transfers between devices: 49.8 us -> 48.1 us
    unnamed x38 -> x52, local copies, waits for them, and re-layouts: 5.75 us -> 10.5 us
    all_to_all x3, starting transfers between devices: 16.8 us -> 12.8 us  [exchanged_near(): lax.all_to_all(value, 'pos', 0, 0, axis_index_groups=groups, tiled=True)]
    pallas_call x5 -> x3, Pallas kernels: 6.96 us -> 4.33 us  [unpack(): pl.pallas_call(kernel, in_specs=[pl.BlockSpec(memory_space=pltpu.SMEM)] +...]
    ppermute x16, starting transfers between devices: 27.4 us -> 29.7 us  [exchanged(): return lax.ppermute(value, 'pos', [(i, i ^ step) for i in range(peers)])]
    all_to_all x3, waiting for transfers between devices: 3.06 us -> 1.58 us  [exchanged_near(): lax.all_to_all(value, 'pos', 0, 0, axis_index_groups=groups, tiled=True)]
  transfers between devices with their start and end apart: 20 -> 20, of which waited for: 4 -> 4; matrix products, arithmetic and copies ran while one was open for 0% -> 0% of each run, Pallas kernels for 39% -> 36%
where the time goes in v6:
time: 133 us; the launch traced here: 132 us
  Pallas kernels  49.9 us (38%)
  starting transfers between devices  48.1 us (36%)
  waiting for transfers between devices  20.2 us (15%)
  local copies, waits for them, and re-layouts  10.5 us (8%)
  other arithmetic  2.12 us (2%)
    ppermute x16, starting transfers between devices, exchanged(): return lax.ppermute(value, 'pos', [(i, i ^ step) for i in range(peers)])  29.7 us
    pallas_call x9, Pallas kernels, attend(): pl.pallas_call(kernel, in_specs=[scalars, scalars, vector, vector] + [vec...  20.6 us
    ppermute x16, waiting for transfers between devices, exchanged(): return lax.ppermute(value, 'pos', [(i, i ^ step) for i in range(peers)])  18.7 us
    all_to_all x3, starting transfers between devices, exchanged_near(): lax.all_to_all(value, 'pos', 0, 0, axis_index_groups=groups, tiled=True)  12.8 us
    unnamed x52, local copies, waits for them, and re-layouts  10.5 us
    pallas_call x1, Pallas kernels, mix(): pl.pallas_call(mix_later_kernel, in_specs=ins + [anywhere], out_specs=out...  6.83 us
    ppermute x1, starting transfers between devices, shards(): earlier = lax.ppermute(tail, 'pos', [(i, i + 1) for i in range(peers - 1)])  5.67 us
    pallas_call x1, Pallas kernels, pack(): pl.pallas_call(functools.partial(pack_kernel, extras, rows, wide), in_spe...  5.07 us
  transfers between devices with their start and end apart: 20, of which 4 were waited for; matrix products, arithmetic and copies ran while one was open for 0% of the time, Pallas kernels for 36%

profile of v6, /device:TPU:0, one launch (start us, length us, event | category | flops | bytes accessed | tf_op | source)
XLA Modules:
  0.0 131.8 jit_solution(16121505058975469161)
XLA Ops:
  0.6 2.1 %multiply_convert_fusion._ = bf16[128,2048]{1,0:T(8,128)(2,1)} fusion(bf16[512,2048]{1,0:T(8,128)(2,1)} %value.3, bf16[512,2048]{1,0:T(8,128)(2,1)} %key.3), kind=kLoop, calls=%fused_computation | loop fusion | flops 1048576 | bytes 1572864 | tf_op jit(solution)/shard_map/convert_element_type | solution.py:695
  2.8 5.7 %collective-permute-start = (bf16[128,2048]{1,0:T(8,128)(2,1)}, bf16[128,2048]{1,0:T(8,128)(2,1)}, u32[]{:S(2)}, u32[]{:S(2)}) collective-permute-start(bf16[128,2048]{1,0:T(8,128)(2,1)} %multiply_convert_fusion._), channel_id=1, source_target_pairs={{0,2},{2,4},{4,6},{6,8},{8,10},{10,12},{12,14},{1,3},{3,5},{5,7},{... | collective-permute-start | bytes 1572872 | tf_op jit(solution)/shard_map/ppermute | solution.py:696
  8.4 5.1 %pack.1 = (s32[48]{0:T(128)}, bf16[4,2,32,2560]{3,2,1,0:T(8,128)(2,1)}, bf16[2,32,2048]{2,1,0:T(8,128)(2,1)}, bf16[2,32,2048]{2,1,0:T(8,128)(2,1)}, bf16[2,32,20...) custom-call(s32[16]{0:T(128)} %blocks.1, ...), custom_call_target="tpu_custom_call" | custom-call | flops 21474836480 | bytes 1000 | tf_op jit(solution)/shard_map/pack/pallas_call | solution.py:522
  13.5 4.5 %all-to-all-start = ((bf16[4,2,32,2560]{3,2,1,0:T(8,128)(2,1)}), bf16[4,2,32,2560]{3,2,1,0:T(8,128)(2,1)}, u32[]{:S(2)}, u32[]{:S(2)}) async-start(bf16[4,2,32,2560]{3,2,1,0:T(8,128)(2,1)} %get-tuple-element.50), calls=%async_computation | async-start | bytes 2621440 | tf_op jit(solution)/shard_map/all_to_all | solution.py:679
  18.0 3.2 %collective-permute-start.3 = (bf16[2,32,2048]{2,1,0:T(8,128)(2,1)}, bf16[2,32,2048]{2,1,0:T(8,128)(2,1)}, u32[]{:S(2)}, u32[]{:S(2)}) collective-permute-start(bf16[2,32,2048]{2,1,0:T(8,128)(2,1)} %get-tuple-element.47), channel_id=1, source_target_pairs={{0,12},{2,14},{4,8},{6,10},{8,4},{10,6},{12,0},{14,2},{1,13},{3,15... | collective-permute-start | bytes 786440 | tf_op jit(solution)/shard_map/ppermute | solution.py:672
  21.2 2.0 %collective-permute-start.6 = (bf16[2,32,2048]{2,1,0:T(8,128)(2,1)}, bf16[2,32,2048]{2,1,0:T(8,128)(2,1)}, u32[]{:S(2)}, u32[]{:S(2)}) collective-permute-start(bf16[2,32,2048]{2,1,0:T(8,128)(2,1)} %get-tuple-element.55), channel_id=1, source_target_pairs={{0,14},{2,12},{4,10},{6,8},{8,6},{10,4},{12,2},{14,0},{1,15},{3,13... | collective-permute-start | bytes 786440 | tf_op jit(solution)/shard_map/ppermute | solution.py:672
  23.2 2.5 %collective-permute-start.8 = (bf16[2,32,2048]{2,1,0:T(8,128)(2,1)}, bf16[2,32,2048]{2,1,0:T(8,128)(2,1)}, u32[]{:S(2)}, u32[]{:S(2)}) collective-permute-start(bf16[2,32,2048]{2,1,0:T(8,128)(2,1)} %get-tuple-element.61), channel_id=1, source_target_pairs={{0,10},{2,8},{4,14},{6,12},{8,2},{10,0},{12,6},{14,4},{1,11},{3,9}... | collective-permute-start | bytes 786440 | tf_op jit(solution)/shard_map/ppermute | solution.py:672
  31.5 6.8 %mix_later.1 = (bf16[512,2048]{1,0:T(8,128)(2,1)}, bf16[16,512,128]{2,1,0:T(8,128)(2,1)S(1)}, bf16[16,128,512]{2,1,0:T(8,128)(2,1)S(1)}) custom-call(bf16[512,2048]{1,0:T(8,128)(2,1)S(1)} %copy-done.5, bf16[512,2048]{1,0:T(8,128)(2,1)S(1)} %copy-done, bf16[512,2048]{1,0:T(8,128)(2,1)S(1)} %copy-done.2, f32[2048,128]{1,0:T(8,128)S(1)} %copy-done.7, ...), custom_call_target="tpu_custom_call" | custom-call | flops 107374182400 | bytes 1000 | tf_op jit(solution)/shard_map/mix_later/pallas_call | solution.py:129
  38.3 4.4 %mix_first.1 = (bf16[512,2048]{1,0:T(8,128)(2,1)}, bf16[16,512,128]{2,1,0:T(8,128)(2,1)S(1)}, bf16[16,128,512]{2,1,0:T(8,128)(2,1)S(1)}) custom-call(bf16[512,2048]{1,0:T(8,128)(2,1)S(1)} %copy-done.6, bf16[512,2048]{1,0:T(8,128)(2,1)S(1)} %copy-done.1, bf16[512,2048]{1,0:T(8,128)(2,1)S(1)} %copy-done.3, ...), custom_call_target="tpu_custom_call", output_to_operand_aliasing={{0}: (7, {}), {1}: (8, {}), {2}: (9, {})} | custom-call | flops 107374182400 | bytes 1000 | tf_op jit(solution)/shard_map/mix_first/pallas_call | solution.py:133
  42.8 1.7 %cut.2 = (bf16[4,512,128]{2,1,0:T(8,128)(2,1)}, bf16[4,512,128]{2,1,0:T(8,128)(2,1)}, bf16[4,512,128]{2,1,0:T(8,128)(2,1)S(1)}, bf16[4,512,128]{2,1,0:T(8,128)(2,1)S(1)}) custom-call(s32[48]{0:T(128)S(1)} %copy-done.4, bf16[16,512,128]{2,1,0:T(8,128)(2,1)S(1)} %get-tuple-element.42.refs_0_.refs_1_.rows, ...), custom_call_target="tpu_custom_call" | custom-call | flops 1000 | bytes 1000 | tf_op jit(solution)/shard_map/cut/pallas_call | solution.py:322
  46.7 2.0 %attend_first.4 = (bf16[2,32,1536]{2,1,0:T(8,128)(2,1)S(1)}, bf16[2,32,512]{2,1,0:T(8,128)(2,1)S(1)}) custom-call(s32[48]{0:T(128)S(1)} %copy-done.4, f32[16]{0:T(128)S(1)} %copy-done.8, bf16[16,128,512]{2,1,0:T(8,128)(2,1)S(1)} %get-tuple-element.41.keys, bf16[16,512,128]{2,1,0:T(8,128)(2,1)S(1)} %get-tuple-element.42.refs_0_.refs_1_.rows, ...), custom_call_target="tpu_custom_call" | custom-call | flops 21474836480 | bytes 1000 | tf_op jit(solution)/shard_map/attend_first/pallas_call | solution.py:271
  51.9 5.7 %attend_near.1.refs_4_ = bf16[4,2,32,2048]{3,2,1,0:T(8,128)(2,1)} custom-call(s32[48]{0:T(128)S(1)} %copy-done.4, f32[16]{0:T(128)S(1)} %copy-done.8, bf16[16,128,512]{2,1,0:T(8,128)(2,1)S(1)} %copy-done.13, bf16[16,512,128]{2,1,0:T(8,128)(2,1)S(1)} %get-tuple-element.42.refs_0_.refs_1_.rows, bf16[2,32,1536]{2,1,0:T(8,128)(2,1)S(1)} %get-tuple-element.49._, ...), custom_call_target="tpu_custom_call" | custom-call | flops 21474836480 | bytes 1000 | tf_op jit(solution)/shard_map/attend_near/pallas_call | solution.py:271
  57.5 4.2 %all-to-all-start.2 = ((bf16[4,2,32,2048]{3,2,1,0:T(8,128)(2,1)}), bf16[4,2,32,2048]{3,2,1,0:T(8,128)(2,1)}, u32[]{:S(2)}, u32[]{:S(2)}) async-start(bf16[4,2,32,2048]{3,2,1,0:T(8,128)(2,1)} %attend_near.1.refs_4_), calls=%async_computation.2 | async-start | bytes 2097152 | tf_op jit(solution)/shard_map/all_to_all | solution.py:679
  61.8 7.8 %collective-permute-done.2.refs_3_ = bf16[4,512,128]{2,1,0:T(8,128)(2,1)} collective-permute-done((bf16[4,512,128]{2,1,0:T(8,128)(2,1)}, bf16[4,512,128]{2,1,0:T(8,128)(2,1)}, u32[]{:S(2)}, u32[]{:S(2)}) %collective-permute-start.2) | collective-permute-done | bytes 524320 | tf_op jit(solution)/shard_map/ppermute | solution.py:672
  72.0 1.6 %collective-permute-start.4 = (bf16[2,512,128]{2,1,0:T(8,128)(2,1)S(1)}, bf16[2,512,128]{2,1,0:T(8,128)(2,1)S(1)}, u32[]{:S(2)}, u32[]{:S(2)}) collective-permute-start(bf16[2,512,128]{2,1,0:T(8,128)(2,1)S(1)} %get-tuple-element.52._), channel_id=1, source_target_pairs={{0,4},{2,6},{4,0},{6,2},{8,12},{10,14},{12,8},{14,10},{1,5},{3,7},... | collective-permute-start | bytes 786440 | tf_op jit(solution)/shard_map/ppermute | solution.py:672
  73.6 2.0 %attend_first.5 = (bf16[2,32,1536]{2,1,0:T(8,128)(2,1)S(1)}, bf16[2,32,512]{2,1,0:T(8,128)(2,1)S(1)}) custom-call(s32[48]{0:T(128)S(1)} %copy-done.4, f32[16]{0:T(128)S(1)} %copy-done.8, bf16[16,128,512]{2,1,0:T(8,128)(2,1)S(1)} %copy-done.14, bf16[16,512,128]{2,1,0:T(8,128)(2,1)S(1)} %get-tuple-element.42.refs_0_.refs_1_.rows, ...), custom_call_target="tpu_custom_call" | custom-call | flops 21474836480 | bytes 1000 | tf_op jit(solution)/shard_map/attend_first/pallas_call | solution.py:271
  75.6 2.5 %collective-permute-start.10 = (bf16[2,32,1536]{2,1,0:T(8,128)(2,1)S(1)}, bf16[2,32,1536]{2,1,0:T(8,128)(2,1)S(1)}, u32[]{:S(2)}, u32[]{:S(2)}) collective-permute-start(bf16[2,32,1536]{2,1,0:T(8,128)(2,1)S(1)} %get-tuple-element.57._), channel_id=1, source_target_pairs={{0,14},{2,12},{4,10},{6,8},{8,6},{10,4},{12,2},{14,0},{1,15},{3,13... | collective-permute-start | bytes 589832 | tf_op jit(solution)/shard_map/ppermute | solution.py:672
  78.1 2.0 %attend_first.6 = (bf16[2,32,1536]{2,1,0:T(8,128)(2,1)S(1)}, bf16[2,32,512]{2,1,0:T(8,128)(2,1)S(1)}) custom-call(s32[48]{0:T(128)S(1)} %copy-done.4, f32[16]{0:T(128)S(1)} %copy-done.8, bf16[16,128,512]{2,1,0:T(8,128)(2,1)S(1)} %copy-done.14, bf16[16,512,128]{2,1,0:T(8,128)(2,1)S(1)} %get-tuple-element.42.refs_0_.refs_1_.rows, ...), custom_call_target="tpu_custom_call" | custom-call | flops 21474836480 | bytes 1000 | tf_op jit(solution)/shard_map/attend_first/pallas_call | solution.py:271
  80.1 2.5 %collective-permute-start.11 = (bf16[2,32,1536]{2,1,0:T(8,128)(2,1)S(1)}, bf16[2,32,1536]{2,1,0:T(8,128)(2,1)S(1)}, u32[]{:S(2)}, u32[]{:S(2)}) collective-permute-start(bf16[2,32,1536]{2,1,0:T(8,128)(2,1)S(1)} %get-tuple-element.60._), channel_id=1, source_target_pairs={{0,8},{2,10},{4,12},{6,14},{8,0},{10,2},{12,4},{14,6},{1,9},{3,11}... | collective-permute-start | bytes 589832 | tf_op jit(solution)/shard_map/ppermute | solution.py:672
  82.6 2.0 %attend_first.7 = (bf16[2,32,1536]{2,1,0:T(8,128)(2,1)S(1)}, bf16[2,32,512]{2,1,0:T(8,128)(2,1)S(1)}) custom-call(s32[48]{0:T(128)S(1)} %copy-done.4, f32[16]{0:T(128)S(1)} %copy-done.8, bf16[16,128,512]{2,1,0:T(8,128)(2,1)S(1)} %copy-done.14, bf16[16,512,128]{2,1,0:T(8,128)(2,1)S(1)} %get-tuple-element.42.refs_0_.refs_1_.rows, ...), custom_call_target="tpu_custom_call" | custom-call | flops 21474836480 | bytes 1000 | tf_op jit(solution)/shard_map/attend_first/pallas_call | solution.py:271
  85.2 3.8 %collective-permute-done.5.refs_3_ = bf16[2,512,128]{2,1,0:T(8,128)(2,1)S(1)} collective-permute-done((bf16[2,512,128]{2,1,0:T(8,128)(2,1)S(1)}, bf16[2,512,128]{2,1,0:T(8,128)(2,1)S(1)}, u32[]{:S(2)}, u32[]{:S(2)}) %collective-permute-start.5) | collective-permute-done | bytes 262176 | tf_op jit(solution)/shard_map/ppermute | solution.py:672
  90.5 7.0 %collective-permute-done.4.refs_1_ = bf16[2,512,128]{2,1,0:T(8,128)(2,1)S(1)} collective-permute-done((bf16[2,512,128]{2,1,0:T(8,128)(2,1)S(1)}, bf16[2,512,128]{2,1,0:T(8,128)(2,1)S(1)}, u32[]{:S(2)}, u32[]{:S(2)}) %collective-permute-start.4) | collective-permute-done | bytes 262176 | tf_op jit(solution)/shard_map/ppermute | solution.py:672
  97.5 3.0 %attend_extra.1 = (bf16[4,2,32,512]{3,2,1,0:T(8,128)(2,1)}, bf16[4,2,32,512]{3,2,1,0:T(8,128)(2,1)S(1)}) custom-call(s32[48]{0:T(128)S(1)} %copy-done.4, f32[16]{0:T(128)S(1)} %copy-done.8, bf16[2,512,128]{2,1,0:T(8,128)(2,1)S(1)} %get-tuple-element.51.refs_0_, bf16[2,512,128]{2,1,0:T(8,128)(2,1)S(1)} %collective-permute-done.4.refs_1_, ...), custom_call_target="tpu_custom_call" | custom-call | flops 21474836480 | bytes 1000 | tf_op jit(solution)/shard_map/attend_extra/pallas_call | solution.py:367
  102.0 1.8 %collective-permute-start.15 = (bf16[2,32,1024]{2,1,0:T(8,128)(2,1)S(1)}, bf16[2,32,1024]{2,1,0:T(8,128)(2,1)}, u32[]{:S(2)}, u32[]{:S(2)}) collective-permute-start(bf16[2,32,1024]{2,1,0:T(8,128)(2,1)S(1)} %attend_second.4._), channel_id=1, source_target_pairs={{0,12},{2,14},{4,8},{6,10},{8,4},{10,6},{12,0},{14,2},{1,13},{3,15... | collective-permute-start | bytes 393224 | tf_op jit(solution)/shard_map/ppermute | solution.py:672
  103.8 2.1 %attend_second.5._ = bf16[2,32,1024]{2,1,0:T(8,128)(2,1)} custom-call(s32[48]{0:T(128)S(1)} %copy-done.4, f32[16]{0:T(128)S(1)} %copy-done.8, bf16[16,128,512]{2,1,0:T(8,128)(2,1)S(1)} %copy-done.14, bf16[16,512,128]{2,1,0:T(8,128)(2,1)S(1)} %get-tuple-element.42.refs_0_.refs_1_.rows, bf16[4,2,32,512]{3,2,1,0:T(8,128)(2,1)S(1)} %get-tuple-element.64.extra._, ...), custom_call_target="tpu_custom_call" | custom-call | flops 21474836480 | bytes 1000 | tf_op jit(solution)/shard_map/attend_second/pallas_call | solution.py:271
  105.9 4.9 %collective-permute-start.16 = (bf16[2,32,1024]{2,1,0:T(8,128)(2,1)}, bf16[2,32,1024]{2,1,0:T(8,128)(2,1)}, u32[]{:S(2)}, u32[]{:S(2)}) collective-permute-start(bf16[2,32,1024]{2,1,0:T(8,128)(2,1)} %attend_second.5._), channel_id=1, source_target_pairs={{0,14},{2,12},{4,10},{6,8},{8,6},{10,4},{12,2},{14,0},{1,15},{3,13... | collective-permute-start | bytes 393224 | tf_op jit(solution)/shard_map/ppermute | solution.py:672
  110.9 2.1 %attend_second.6._ = bf16[2,32,1024]{2,1,0:T(8,128)(2,1)} custom-call(s32[48]{0:T(128)S(1)} %copy-done.4, f32[16]{0:T(128)S(1)} %copy-done.8, bf16[16,128,512]{2,1,0:T(8,128)(2,1)S(1)} %copy-done.14, bf16[16,512,128]{2,1,0:T(8,128)(2,1)S(1)} %get-tuple-element.42.refs_0_.refs_1_.rows, bf16[4,2,32,512]{3,2,1,0:T(8,128)(2,1)S(1)} %get-tuple-element.64.extra._, ...), custom_call_target="tpu_custom_call" | custom-call | flops 21474836480 | bytes 1000 | tf_op jit(solution)/shard_map/attend_second/pallas_call | solution.py:271
  113.0 4.1 %all-to-all-start.1 = ((bf16[4,2,32,512]{3,2,1,0:T(8,128)(2,1)}), bf16[4,2,32,512]{3,2,1,0:T(8,128)(2,1)S(1)}, u32[]{:S(2)}, u32[]{:S(2)}) async-start(bf16[4,2,32,512]{3,2,1,0:T(8,128)(2,1)} %get-tuple-element.69), calls=%async_computation.1 | async-start | bytes 524288 | tf_op jit(solution)/shard_map/all_to_all | solution.py:679
  121.0 3.8 %collective-permute-start.14 = (bf16[2,32,1024]{2,1,0:T(8,128)(2,1)S(1)}, bf16[2,32,1024]{2,1,0:T(8,128)(2,1)S(1)}, u32[]{:S(2)}, u32[]{:S(2)}) collective-permute-start(bf16[2,32,1024]{2,1,0:T(8,128)(2,1)S(1)} %attend_second.7.refs_4_), channel_id=1, source_target_pairs={{0,10},{2,8},{4,14},{6,12},{8,2},{10,0},{12,6},{14,4},{1,11},{3,9}... | collective-permute-start | bytes 393224 | tf_op jit(solution)/shard_map/ppermute | solution.py:672
  124.8 2.6 %unpack_early.1._ = bf16[16,32,2048]{2,1,0:T(8,128)(2,1)} custom-call(s32[48]{0:T(128)S(1)} %copy-done.4, bf16[4,2,32,2048]{3,2,1,0:T(8,128)(2,1)} %all-to-all-done.2.near, bf16[2,32,1536]{2,1,0:T(8,128)(2,1)S(1)} %collective-permute-done.9.refs_1_.refs_0_, bf16[2,32,1536]{2,1,0:T(8,128)(2,1)S(1)} %collective-permute-done.10.refs_1_, ...), custom_call_target="tpu_custom_call" | custom-call | flops 1000 | bytes 1000 | tf_op jit(solution)/shard_map/unpack_early/pallas_call | solution.py:582
  128.1 1.8 %unpack.2.refs_2_ = bf16[16,32,2048]{2,1,0:T(8,128)(2,1)} custom-call(s32[48]{0:T(128)S(1)} %copy-done.4, bf16[2,32,1024]{2,1,0:T(8,128)(2,1)} %collective-permute-done.15.refs_0_, bf16[2,32,1024]{2,1,0:T(8,128)(2,1)} %collective-permute-done.16.refs_1_, bf16[16,32,2048]{2,1,0:T(8,128)(2,1)} %unpack_extra.1.refs_2_), custom_call_target="tpu_custom_call", output_to_operand_aliasing={{}: (3, {})} | custom-call | flops 21474836480 | bytes 1000 | tf_op jit(solution)/shard_map/unpack/pallas_call | solution.py:655
  130.0 1.8 %unpack.3 = bf16[16,32,2048]{2,1,0:T(8,128)(2,1)} custom-call(s32[48]{0:T(128)S(1)} %copy-done.4, bf16[2,32,1024]{2,1,0:T(8,128)(2,1)} %collective-permute-done.12.refs_0_, bf16[2,32,1024]{2,1,0:T(8,128)(2,1)S(1)} %collective-permute-done.14.refs_1_, bf16[16,32,2048]{2,1,0:T(8,128)(2,1)} %unpack.2.refs_2_), custom_call_target="tpu_custom_call", output_to_operand_aliasing={{}: (3, {})} | custom-call | flops 21474836480 | bytes 1000 | tf_op jit(solution)/shard_map/unpack/pallas_call | solution.py:655
  (80 shorter events, 22.0 us)
Async XLA Ops:
  2.8 35.5 %collective-permute-start = (bf16[128,2048]{1,0:T(8,128)(2,1)}, bf16[128,2048]{1,0:T(8,128)(2,1)}, u32[]{:S(2)}, u32[]{:S(2)}) collective-permute-start(bf16[128,2048]{1,0:T(8,128)(2,1)} %multiply_convert_fusion._), channel_id=1, source_target_pairs={{0,2},{2,4},{4,6},{6,8},{8,10},{10,12},{12,14},{1,3},{3,5},{5,7},{... | collective-permute-start | bytes 1572872 | tf_op jit(solution)/shard_map/ppermute | solution.py:696
  13.5 12.2 %copy-start.4 = (s32[48]{0:T(128)S(1)}, s32[48]{0:T(128)}, u32[]{:S(2)}) copy-start(s32[48]{0:T(128)} %get-tuple-element.36._.info) | copy-start | bytes 580
  13.5 12.2 %copy-start.7 = (f32[2048,128]{1,0:T(8,128)S(1)}, f32[2048,128]{1,0:T(8,128)}, u32[]{:S(2)}) copy-start(f32[2048,128]{1,0:T(8,128)} %filters.3) | copy-start | bytes 3145732
  13.5 12.2 %copy-start.11 = (bf16[256,256]{1,0:T(8,128)(2,1)S(1)}, bf16[256,256]{1,0:T(8,128)(2,1)}, u32[]{:S(2)}) copy-start(bf16[256,256]{1,0:T(8,128)(2,1)} %constant.5.clone.inverse) | copy-start | bytes 393220
  13.5 36.7 %all-to-all-start = ((bf16[4,2,32,2560]{3,2,1,0:T(8,128)(2,1)}), bf16[4,2,32,2560]{3,2,1,0:T(8,128)(2,1)}, u32[]{:S(2)}, u32[]{:S(2)}) async-start(bf16[4,2,32,2560]{3,2,1,0:T(8,128)(2,1)} %get-tuple-element.50), calls=%async_computation | async-start | bytes 2621440 | tf_op jit(solution)/shard_map/all_to_all | solution.py:679
  18.0 27.3 %collective-permute-start.3 = (bf16[2,32,2048]{2,1,0:T(8,128)(2,1)}, bf16[2,32,2048]{2,1,0:T(8,128)(2,1)}, u32[]{:S(2)}, u32[]{:S(2)}) collective-permute-start(bf16[2,32,2048]{2,1,0:T(8,128)(2,1)} %get-tuple-element.47), channel_id=1, source_target_pairs={{0,12},{2,14},{4,8},{6,10},{8,4},{10,6},{12,0},{14,2},{1,13},{3,15... | collective-permute-start | bytes 786440 | tf_op jit(solution)/shard_map/ppermute | solution.py:672
  21.2 52.4 %collective-permute-start.6 = (bf16[2,32,2048]{2,1,0:T(8,128)(2,1)}, bf16[2,32,2048]{2,1,0:T(8,128)(2,1)}, u32[]{:S(2)}, u32[]{:S(2)}) collective-permute-start(bf16[2,32,2048]{2,1,0:T(8,128)(2,1)} %get-tuple-element.55), channel_id=1, source_target_pairs={{0,14},{2,12},{4,10},{6,8},{8,6},{10,4},{12,2},{14,0},{1,15},{3,13... | collective-permute-start | bytes 786440 | tf_op jit(solution)/shard_map/ppermute | solution.py:672
  23.2 54.8 %collective-permute-start.7 = (bf16[2,32,2048]{2,1,0:T(8,128)(2,1)}, bf16[2,32,2048]{2,1,0:T(8,128)(2,1)}, u32[]{:S(2)}, u32[]{:S(2)}) collective-permute-start(bf16[2,32,2048]{2,1,0:T(8,128)(2,1)} %get-tuple-element.58), channel_id=1, source_target_pairs={{0,8},{2,10},{4,12},{6,14},{8,0},{10,2},{12,4},{14,6},{1,9},{3,11}... | collective-permute-start | bytes 786440 | tf_op jit(solution)/shard_map/ppermute | solution.py:672
  23.2 59.3 %collective-permute-start.8 = (bf16[2,32,2048]{2,1,0:T(8,128)(2,1)}, bf16[2,32,2048]{2,1,0:T(8,128)(2,1)}, u32[]{:S(2)}, u32[]{:S(2)}) collective-permute-start(bf16[2,32,2048]{2,1,0:T(8,128)(2,1)} %get-tuple-element.61), channel_id=1, source_target_pairs={{0,10},{2,8},{4,14},{6,12},{8,2},{10,0},{12,6},{14,4},{1,11},{3,9}... | collective-permute-start | bytes 786440 | tf_op jit(solution)/shard_map/ppermute | solution.py:672
  31.5 6.8 %copy-start.1 = (bf16[512,2048]{1,0:T(8,128)(2,1)S(1)}, bf16[512,2048]{1,0:T(8,128)(2,1)}, u32[]{:S(2)}) copy-start(bf16[512,2048]{1,0:T(8,128)(2,1)} %key.3) | copy-start | bytes 6291460
  31.5 6.8 %copy-start.3 = (bf16[512,2048]{1,0:T(8,128)(2,1)S(1)}, bf16[512,2048]{1,0:T(8,128)(2,1)}, u32[]{:S(2)}) copy-start(bf16[512,2048]{1,0:T(8,128)(2,1)} %value.3) | copy-start | bytes 6291460
  31.5 6.8 %copy-start.6 = (bf16[512,2048]{1,0:T(8,128)(2,1)S(1)}, bf16[512,2048]{1,0:T(8,128)(2,1)}, u32[]{:S(2)}) copy-start(bf16[512,2048]{1,0:T(8,128)(2,1)} %gate.3) | copy-start | bytes 6291460
  31.5 6.9 %copy-start.10 = (bf16[512,256]{1,0:T(8,128)(2,1)S(1)}, bf16[512,256]{1,0:T(8,128)(2,1)}, u32[]{:S(2)}) copy-start(bf16[512,256]{1,0:T(8,128)(2,1)} %constant.4.clone.forward) | copy-start | bytes 786436
  44.5 25.2 %collective-permute-start.2 = (bf16[4,512,128]{2,1,0:T(8,128)(2,1)}, bf16[4,512,128]{2,1,0:T(8,128)(2,1)}, u32[]{:S(2)}, u32[]{:S(2)}) collective-permute-start(bf16[4,512,128]{2,1,0:T(8,128)(2,1)} %get-tuple-element.46), channel_id=1, source_target_pairs={{0,4},{2,6},{4,0},{6,2},{8,12},{10,14},{12,8},{14,10},{1,5},{3,7},... | collective-permute-start | bytes 1572872 | tf_op jit(solution)/shard_map/ppermute | solution.py:672
  45.3 25.4 %collective-permute-start.1 = (bf16[4,512,128]{2,1,0:T(8,128)(2,1)}, bf16[4,512,128]{2,1,0:T(8,128)(2,1)}, u32[]{:S(2)}, u32[]{:S(2)}) collective-permute-start(bf16[4,512,128]{2,1,0:T(8,128)(2,1)} %get-tuple-element.44._), channel_id=1, source_target_pairs={{0,2},{2,0},{4,6},{6,4},{8,10},{10,8},{12,14},{14,12},{1,3},{3,1},... | collective-permute-start | bytes 1572872 | tf_op jit(solution)/shard_map/ppermute | solution.py:672
  48.7 8.8 %copy-start.18 = (bf16[2,32,512]{2,1,0:T(8,128)(2,1)}, bf16[2,32,512]{2,1,0:T(8,128)(2,1)S(1)}, u32[]{:S(2)}) copy-start(bf16[2,32,512]{2,1,0:T(8,128)(2,1)S(1)} %get-tuple-element.65.refs_2_) | copy-start | bytes 196612
  57.5 55.4 %all-to-all-start.2 = ((bf16[4,2,32,2048]{3,2,1,0:T(8,128)(2,1)}), bf16[4,2,32,2048]{3,2,1,0:T(8,128)(2,1)}, u32[]{:S(2)}, u32[]{:S(2)}) async-start(bf16[4,2,32,2048]{3,2,1,0:T(8,128)(2,1)} %attend_near.1.refs_4_), calls=%async_computation.2 | async-start | bytes 2097152 | tf_op jit(solution)/shard_map/all_to_all | solution.py:679
  61.8 11.8 %copy-start.14 = (bf16[16,128,512]{2,1,0:T(8,128)(2,1)S(1)}, bf16[16,128,512]{2,1,0:T(8,128)(2,1)}, u32[]{:S(2)}) copy-start(bf16[16,128,512]{2,1,0:T(8,128)(2,1)} %copy-done.12) | copy-start | bytes 6291460
  61.8 11.8 %copy-start.23 = (bf16[2,32,512]{2,1,0:T(8,128)(2,1)S(1)}, bf16[2,32,512]{2,1,0:T(8,128)(2,1)}, u32[]{:S(2)}) copy-start(bf16[2,32,512]{2,1,0:T(8,128)(2,1)} %get-tuple-element.56.rest) | copy-start | bytes 196612
  69.6 30.8 %collective-permute-start.9 = (bf16[2,32,1536]{2,1,0:T(8,128)(2,1)S(1)}, bf16[2,32,1536]{2,1,0:T(8,128)(2,1)S(1)}, u32[]{:S(2)}, u32[]{:S(2)}) collective-permute-start(bf16[2,32,1536]{2,1,0:T(8,128)(2,1)S(1)} %get-tuple-element.49._), channel_id=1, source_target_pairs={{0,12},{2,14},{4,8},{6,10},{8,4},{10,6},{12,0},{14,2},{1,13},{3,15... | collective-permute-start | bytes 589832 | tf_op jit(solution)/shard_map/ppermute | solution.py:672
  72.0 25.5 %collective-permute-start.4 = (bf16[2,512,128]{2,1,0:T(8,128)(2,1)S(1)}, bf16[2,512,128]{2,1,0:T(8,128)(2,1)S(1)}, u32[]{:S(2)}, u32[]{:S(2)}) collective-permute-start(bf16[2,512,128]{2,1,0:T(8,128)(2,1)S(1)} %get-tuple-element.52._), channel_id=1, source_target_pairs={{0,4},{2,6},{4,0},{6,2},{8,12},{10,14},{12,8},{14,10},{1,5},{3,7},... | collective-permute-start | bytes 786440 | tf_op jit(solution)/shard_map/ppermute | solution.py:672
  75.6 28.2 %collective-permute-start.10 = (bf16[2,32,1536]{2,1,0:T(8,128)(2,1)S(1)}, bf16[2,32,1536]{2,1,0:T(8,128)(2,1)S(1)}, u32[]{:S(2)}, u32[]{:S(2)}) collective-permute-start(bf16[2,32,1536]{2,1,0:T(8,128)(2,1)S(1)} %get-tuple-element.57._), channel_id=1, source_target_pairs={{0,14},{2,12},{4,10},{6,8},{8,6},{10,4},{12,2},{14,0},{1,15},{3,13... | collective-permute-start | bytes 589832 | tf_op jit(solution)/shard_map/ppermute | solution.py:672
  80.1 30.8 %collective-permute-start.11 = (bf16[2,32,1536]{2,1,0:T(8,128)(2,1)S(1)}, bf16[2,32,1536]{2,1,0:T(8,128)(2,1)S(1)}, u32[]{:S(2)}, u32[]{:S(2)}) collective-permute-start(bf16[2,32,1536]{2,1,0:T(8,128)(2,1)S(1)} %get-tuple-element.60._), channel_id=1, source_target_pairs={{0,8},{2,10},{4,12},{6,14},{8,0},{10,2},{12,4},{14,6},{1,9},{3,11}... | collective-permute-start | bytes 589832 | tf_op jit(solution)/shard_map/ppermute | solution.py:672
  82.6 6.4 %collective-permute-start.5 = (bf16[2,512,128]{2,1,0:T(8,128)(2,1)S(1)}, bf16[2,512,128]{2,1,0:T(8,128)(2,1)S(1)}, u32[]{:S(2)}, u32[]{:S(2)}) collective-permute-start(bf16[2,512,128]{2,1,0:T(8,128)(2,1)S(1)} %get-tuple-element.54), channel_id=1, source_target_pairs={{0,2},{2,0},{4,6},{6,4},{8,10},{10,8},{12,14},{14,12},{1,3},{3,1},... | collective-permute-start | bytes 786440 | tf_op jit(solution)/shard_map/ppermute | solution.py:672
  88.9 28.1 %collective-permute-start.13 = (bf16[2,32,1536]{2,1,0:T(8,128)(2,1)S(1)}, bf16[2,32,1536]{2,1,0:T(8,128)(2,1)S(1)}, u32[]{:S(2)}, u32[]{:S(2)}) collective-permute-start(bf16[2,32,1536]{2,1,0:T(8,128)(2,1)S(1)} %get-tuple-element.63.refs_4_), channel_id=1, source_target_pairs={{0,10},{2,8},{4,14},{6,12},{8,2},{10,0},{12,6},{14,4},{1,11},{3,9}... | collective-permute-start | bytes 589832 | tf_op jit(solution)/shard_map/ppermute | solution.py:672
  100.5 10.4 %copy-start.16 = (bf16[4,2,32,512]{3,2,1,0:T(8,128)(2,1)}, bf16[4,2,32,512]{3,2,1,0:T(8,128)(2,1)S(1)}, u32[]{:S(2)}) copy-start(bf16[4,2,32,512]{3,2,1,0:T(8,128)(2,1)S(1)} %get-tuple-element.64.extra._) | copy-start | bytes 786436
  102.0 26.1 %collective-permute-start.15 = (bf16[2,32,1024]{2,1,0:T(8,128)(2,1)S(1)}, bf16[2,32,1024]{2,1,0:T(8,128)(2,1)}, u32[]{:S(2)}, u32[]{:S(2)}) collective-permute-start(bf16[2,32,1024]{2,1,0:T(8,128)(2,1)S(1)} %attend_second.4._), channel_id=1, source_target_pairs={{0,12},{2,14},{4,8},{6,10},{8,4},{10,6},{12,0},{14,2},{1,13},{3,15... | collective-permute-start | bytes 393224 | tf_op jit(solution)/shard_map/ppermute | solution.py:672
  105.9 22.2 %collective-permute-start.16 = (bf16[2,32,1024]{2,1,0:T(8,128)(2,1)}, bf16[2,32,1024]{2,1,0:T(8,128)(2,1)}, u32[]{:S(2)}, u32[]{:S(2)}) collective-permute-start(bf16[2,32,1024]{2,1,0:T(8,128)(2,1)} %attend_second.5._), channel_id=1, source_target_pairs={{0,14},{2,12},{4,10},{6,8},{8,6},{10,4},{12,2},{14,0},{1,15},{3,13... | collective-permute-start | bytes 393224 | tf_op jit(solution)/shard_map/ppermute | solution.py:672
  110.9 6.2 %copy-start.21 = (bf16[2,32,512]{2,1,0:T(8,128)(2,1)S(1)}, bf16[2,32,512]{2,1,0:T(8,128)(2,1)}, u32[]{:S(2)}) copy-start(bf16[2,32,512]{2,1,0:T(8,128)(2,1)} %copy-done.20) | copy-start | bytes 196612
  113.0 17.0 %collective-permute-start.12 = (bf16[2,32,1024]{2,1,0:T(8,128)(2,1)}, bf16[2,32,1024]{2,1,0:T(8,128)(2,1)}, u32[]{:S(2)}, u32[]{:S(2)}) collective-permute-start(bf16[2,32,1024]{2,1,0:T(8,128)(2,1)} %attend_second.6._), channel_id=1, source_target_pairs={{0,8},{2,10},{4,12},{6,14},{8,0},{10,2},{12,4},{14,6},{1,9},{3,11}... | collective-permute-start | bytes 393224 | tf_op jit(solution)/shard_map/ppermute | solution.py:672
  113.0 14.4 %all-to-all-start.1 = ((bf16[4,2,32,512]{3,2,1,0:T(8,128)(2,1)}), bf16[4,2,32,512]{3,2,1,0:T(8,128)(2,1)S(1)}, u32[]{:S(2)}, u32[]{:S(2)}) async-start(bf16[4,2,32,512]{3,2,1,0:T(8,128)(2,1)} %get-tuple-element.69), calls=%async_computation.1 | async-start | bytes 524288 | tf_op jit(solution)/shard_map/all_to_all | solution.py:679
  121.0 9.0 %collective-permute-start.14 = (bf16[2,32,1024]{2,1,0:T(8,128)(2,1)S(1)}, bf16[2,32,1024]{2,1,0:T(8,128)(2,1)S(1)}, u32[]{:S(2)}, u32[]{:S(2)}) collective-permute-start(bf16[2,32,1024]{2,1,0:T(8,128)(2,1)S(1)} %attend_second.7.refs_4_), channel_id=1, source_target_pairs={{0,10},{2,8},{4,14},{6,12},{8,2},{10,0},{12,6},{14,4},{1,11},{3,9}... | collective-permute-start | bytes 393224 | tf_op jit(solution)/shard_map/ppermute | solution.py:672
  (14 other events, 34.2 us)

commit v7 on v6

--- a/solution.py
+++ b/solution.py
@@ -476,7 +476,8 @@
 
 
 def far_steps(half):
-    return [half + at for at in (*range(half // 2, half), *range(half // 2))]
+    order = [at for pair in zip(range(half // 2, half), range(half // 2)) for at in pair]
+    return [half + at for at in order]
 
 
 def far_copies(info, queries, steps, far, rest, wide, extras):

time: 133 us -> 133 us (level)
    ppermute x16, waiting for transfers between devices: 18.7 us -> 20.3 us  [exchanged(): return lax.ppermute(value, 'pos', [(i, i ^ step) for i in range(peers)])]
    all_to_all x3, waiting for transfers between devices: 1.58 us -> 0.01 us  [exchanged_near(): lax.all_to_all(value, 'pos', 0, 0, axis_index_groups=groups, tiled=True)]
  transfers between devices with their start and end apart: 20 -> 20, of which waited for: 4 -> 6; matrix products, arithmetic and copies ran while one was open for 0% -> 0% of each run, Pallas kernels for 36% -> 37%
where the time goes in v7:
time: 133 us; the launch traced here: 132 us
  Pallas kernels  50.4 us (38%)
  starting transfers between devices  47.5 us (36%)
  waiting for transfers between devices  20.3 us (15%)
  local copies, waits for them, and re-layouts  10.6 us (8%)
  other arithmetic  2.12 us (2%)
    ppermute x16, starting transfers between devices, exchanged(): return lax.ppermute(value, 'pos', [(i, i ^ step) for i in range(peers)])  29.4 us
    pallas_call x9, Pallas kernels, attend(): pl.pallas_call(kernel, in_specs=[scalars, scalars, vector, vector] + [vec...  20.6 us
    ppermute x16, waiting for transfers between devices, exchanged(): return lax.ppermute(value, 'pos', [(i, i ^ step) for i in range(peers)])  20.3 us
    all_to_all x3, starting transfers between devices, exchanged_near(): lax.all_to_all(value, 'pos', 0, 0, axis_index_groups=groups, tiled=True)  12.4 us
    unnamed x52, local copies, waits for them, and re-layouts  10.6 us
    pallas_call x1, Pallas kernels, mix(): pl.pallas_call(mix_later_kernel, in_specs=ins + [anywhere], out_specs=out...  6.83 us
    ppermute x1, starting transfers between devices, shards(): earlier = lax.ppermute(tail, 'pos', [(i, i + 1) for i in range(peers - 1)])  5.67 us
    pallas_call x1, Pallas kernels, pack(): pl.pallas_call(functools.partial(pack_kernel, extras, rows, wide), in_spe...  5.07 us
  transfers between devices with their start and end apart: 20, of which 6 were waited for; matrix products, arithmetic and copies ran while one was open for 0% of the time, Pallas kernels for 37%

profile of v7, /device:TPU:0, one launch (start us, length us, event | category | flops | bytes accessed | tf_op | source)
XLA Modules:
  0.0 131.9 jit_solution(12906321423089782449)
XLA Ops:
  0.6 2.1 %multiply_convert_fusion._ = bf16[128,2048]{1,0:T(8,128)(2,1)} fusion(bf16[512,2048]{1,0:T(8,128)(2,1)} %value.3, bf16[512,2048]{1,0:T(8,128)(2,1)} %key.3), kind=kLoop, calls=%fused_computation | loop fusion | flops 1048576 | bytes 1572864 | tf_op jit(solution)/shard_map/convert_element_type | solution.py:696
  2.8 5.7 %collective-permute-start = (bf16[128,2048]{1,0:T(8,128)(2,1)}, bf16[128,2048]{1,0:T(8,128)(2,1)}, u32[]{:S(2)}, u32[]{:S(2)}) collective-permute-start(bf16[128,2048]{1,0:T(8,128)(2,1)} %multiply_convert_fusion._), channel_id=1, source_target_pairs={{0,2},{2,4},{4,6},{6,8},{8,10},{10,12},{12,14},{1,3},{3,5},{5,7},{... | collective-permute-start | bytes 1572872 | tf_op jit(solution)/shard_map/ppermute | solution.py:697
  8.4 5.1 %pack.1 = (s32[48]{0:T(128)}, bf16[4,2,32,2560]{3,2,1,0:T(8,128)(2,1)}, bf16[2,32,2048]{2,1,0:T(8,128)(2,1)}, bf16[2,32,2048]{2,1,0:T(8,128)(2,1)}, bf16[2,32,20...) custom-call(s32[16]{0:T(128)} %blocks.1, ...), custom_call_target="tpu_custom_call" | custom-call | flops 21474836480 | bytes 1000 | tf_op jit(solution)/shard_map/pack/pallas_call | solution.py:523
  13.5 4.5 %all-to-all-start = ((bf16[4,2,32,2560]{3,2,1,0:T(8,128)(2,1)}), bf16[4,2,32,2560]{3,2,1,0:T(8,128)(2,1)}, u32[]{:S(2)}, u32[]{:S(2)}) async-start(bf16[4,2,32,2560]{3,2,1,0:T(8,128)(2,1)} %get-tuple-element.50), calls=%async_computation | async-start | bytes 2621440 | tf_op jit(solution)/shard_map/all_to_all | solution.py:680
  18.0 3.2 %collective-permute-start.3 = (bf16[2,32,2048]{2,1,0:T(8,128)(2,1)}, bf16[2,32,2048]{2,1,0:T(8,128)(2,1)}, u32[]{:S(2)}, u32[]{:S(2)}) collective-permute-start(bf16[2,32,2048]{2,1,0:T(8,128)(2,1)} %get-tuple-element.47), channel_id=1, source_target_pairs={{0,12},{2,14},{4,8},{6,10},{8,4},{10,6},{12,0},{14,2},{1,13},{3,15... | collective-permute-start | bytes 786440 | tf_op jit(solution)/shard_map/ppermute | solution.py:673
  21.4 2.7 %collective-permute-start.7 = (bf16[2,32,2048]{2,1,0:T(8,128)(2,1)}, bf16[2,32,2048]{2,1,0:T(8,128)(2,1)}, u32[]{:S(2)}, u32[]{:S(2)}) collective-permute-start(bf16[2,32,2048]{2,1,0:T(8,128)(2,1)} %get-tuple-element.58), channel_id=1, source_target_pairs={{0,14},{2,12},{4,10},{6,8},{8,6},{10,4},{12,2},{14,0},{1,15},{3,13... | collective-permute-start | bytes 786440 | tf_op jit(solution)/shard_map/ppermute | solution.py:673
  30.8 6.8 %mix_later.1 = (bf16[512,2048]{1,0:T(8,128)(2,1)}, bf16[16,512,128]{2,1,0:T(8,128)(2,1)S(1)}, bf16[16,128,512]{2,1,0:T(8,128)(2,1)S(1)}) custom-call(bf16[512,2048]{1,0:T(8,128)(2,1)S(1)} %copy-done.5, bf16[512,2048]{1,0:T(8,128)(2,1)S(1)} %copy-done, bf16[512,2048]{1,0:T(8,128)(2,1)S(1)} %copy-done.2, f32[2048,128]{1,0:T(8,128)S(1)} %copy-done.7, ...), custom_call_target="tpu_custom_call" | custom-call | flops 107374182400 | bytes 1000 | tf_op jit(solution)/shard_map/mix_later/pallas_call | solution.py:129
  37.7 4.4 %mix_first.1 = (bf16[512,2048]{1,0:T(8,128)(2,1)}, bf16[16,512,128]{2,1,0:T(8,128)(2,1)S(1)}, bf16[16,128,512]{2,1,0:T(8,128)(2,1)S(1)}) custom-call(bf16[512,2048]{1,0:T(8,128)(2,1)S(1)} %copy-done.6, bf16[512,2048]{1,0:T(8,128)(2,1)S(1)} %copy-done.1, bf16[512,2048]{1,0:T(8,128)(2,1)S(1)} %copy-done.3, ...), custom_call_target="tpu_custom_call", output_to_operand_aliasing={{0}: (7, {}), {1}: (8, {}), {2}: (9, {})} | custom-call | flops 107374182400 | bytes 1000 | tf_op jit(solution)/shard_map/mix_first/pallas_call | solution.py:133
  42.1 1.7 %cut.2 = (bf16[4,512,128]{2,1,0:T(8,128)(2,1)}, bf16[4,512,128]{2,1,0:T(8,128)(2,1)}, bf16[4,512,128]{2,1,0:T(8,128)(2,1)S(1)}, bf16[4,512,128]{2,1,0:T(8,128)(2,1)S(1)}) custom-call(s32[48]{0:T(128)S(1)} %copy-done.4, bf16[16,512,128]{2,1,0:T(8,128)(2,1)S(1)} %get-tuple-element.42.refs_0_.refs_1_.rows, ...), custom_call_target="tpu_custom_call" | custom-call | flops 1000 | bytes 1000 | tf_op jit(solution)/shard_map/cut/pallas_call | solution.py:322
  43.8 1.7 %collective-permute-start.2 = (bf16[4,512,128]{2,1,0:T(8,128)(2,1)}, bf16[4,512,128]{2,1,0:T(8,128)(2,1)}, u32[]{:S(2)}, u32[]{:S(2)}) collective-permute-start(bf16[4,512,128]{2,1,0:T(8,128)(2,1)} %get-tuple-element.46), channel_id=1, source_target_pairs={{0,4},{2,6},{4,0},{6,2},{8,12},{10,14},{12,8},{14,10},{1,5},{3,7},... | collective-permute-start | bytes 1572872 | tf_op jit(solution)/shard_map/ppermute | solution.py:673
  46.9 2.0 %attend_first.4 = (bf16[2,32,1536]{2,1,0:T(8,128)(2,1)S(1)}, bf16[2,32,512]{2,1,0:T(8,128)(2,1)S(1)}) custom-call(s32[48]{0:T(128)S(1)} %copy-done.4, f32[16]{0:T(128)S(1)} %copy-done.8, bf16[16,128,512]{2,1,0:T(8,128)(2,1)S(1)} %get-tuple-element.41.keys, bf16[16,512,128]{2,1,0:T(8,128)(2,1)S(1)} %get-tuple-element.42.refs_0_.refs_1_.rows, ...), custom_call_target="tpu_custom_call" | custom-call | flops 21474836480 | bytes 1000 | tf_op jit(solution)/shard_map/attend_first/pallas_call | solution.py:271
  48.9 1.6 %copy-done.13 = bf16[16,128,512]{2,1,0:T(8,128)(2,1)S(1)} copy-done((bf16[16,128,512]{2,1,0:T(8,128)(2,1)S(1)}, bf16[16,128,512]{2,1,0:T(8,128)(2,1)}, u32[]{:S(2)}) %copy-start.13) | copy-done | bytes 2097176
  50.5 5.7 %attend_near.1.refs_4_ = bf16[4,2,32,2048]{3,2,1,0:T(8,128)(2,1)} custom-call(s32[48]{0:T(128)S(1)} %copy-done.4, f32[16]{0:T(128)S(1)} %copy-done.8, bf16[16,128,512]{2,1,0:T(8,128)(2,1)S(1)} %copy-done.13, bf16[16,512,128]{2,1,0:T(8,128)(2,1)S(1)} %get-tuple-element.42.refs_0_.refs_1_.rows, bf16[2,32,1536]{2,1,0:T(8,128)(2,1)S(1)} %get-tuple-element.49._, ...), custom_call_target="tpu_custom_call" | custom-call | flops 21474836480 | bytes 1000 | tf_op jit(solution)/shard_map/attend_near/pallas_call | solution.py:271
  56.2 4.2 %all-to-all-start.2 = ((bf16[4,2,32,2048]{3,2,1,0:T(8,128)(2,1)}), bf16[4,2,32,2048]{3,2,1,0:T(8,128)(2,1)}, u32[]{:S(2)}, u32[]{:S(2)}) async-start(bf16[4,2,32,2048]{3,2,1,0:T(8,128)(2,1)} %attend_near.1.refs_4_), calls=%async_computation.2 | async-start | bytes 2097152 | tf_op jit(solution)/shard_map/all_to_all | solution.py:680
  60.5 8.7 %collective-permute-done.2.refs_3_ = bf16[4,512,128]{2,1,0:T(8,128)(2,1)} collective-permute-done((bf16[4,512,128]{2,1,0:T(8,128)(2,1)}, bf16[4,512,128]{2,1,0:T(8,128)(2,1)}, u32[]{:S(2)}, u32[]{:S(2)}) %collective-permute-start.2) | collective-permute-done | bytes 524320 | tf_op jit(solution)/shard_map/ppermute | solution.py:673
  70.6 5.8 %collective-permute-done.1.refs_1_ = bf16[4,512,128]{2,1,0:T(8,128)(2,1)} collective-permute-done((bf16[4,512,128]{2,1,0:T(8,128)(2,1)}, bf16[4,512,128]{2,1,0:T(8,128)(2,1)}, u32[]{:S(2)}, u32[]{:S(2)}) %collective-permute-start.1) | collective-permute-done | bytes 524320 | tf_op jit(solution)/shard_map/ppermute | solution.py:673
  77.9 2.0 %attend_first.5 = (bf16[2,32,1536]{2,1,0:T(8,128)(2,1)S(1)}, bf16[2,32,512]{2,1,0:T(8,128)(2,1)S(1)}) custom-call(s32[48]{0:T(128)S(1)} %copy-done.4, f32[16]{0:T(128)S(1)} %copy-done.8, bf16[16,128,512]{2,1,0:T(8,128)(2,1)S(1)} %copy-done.14, bf16[16,512,128]{2,1,0:T(8,128)(2,1)S(1)} %get-tuple-element.42.refs_0_.refs_1_.rows, ...), custom_call_target="tpu_custom_call" | custom-call | flops 21474836480 | bytes 1000 | tf_op jit(solution)/shard_map/attend_first/pallas_call | solution.py:271
  80.0 2.0 %attend_first.6 = (bf16[2,32,1536]{2,1,0:T(8,128)(2,1)S(1)}, bf16[2,32,512]{2,1,0:T(8,128)(2,1)S(1)}) custom-call(s32[48]{0:T(128)S(1)} %copy-done.4, f32[16]{0:T(128)S(1)} %copy-done.8, bf16[16,128,512]{2,1,0:T(8,128)(2,1)S(1)} %copy-done.14, bf16[16,512,128]{2,1,0:T(8,128)(2,1)S(1)} %get-tuple-element.42.refs_0_.refs_1_.rows, ...), custom_call_target="tpu_custom_call" | custom-call | flops 21474836480 | bytes 1000 | tf_op jit(solution)/shard_map/attend_first/pallas_call | solution.py:271
  82.0 4.2 %collective-permute-start.11 = (bf16[2,32,1536]{2,1,0:T(8,128)(2,1)S(1)}, bf16[2,32,1536]{2,1,0:T(8,128)(2,1)S(1)}, u32[]{:S(2)}, u32[]{:S(2)}) collective-permute-start(bf16[2,32,1536]{2,1,0:T(8,128)(2,1)S(1)} %get-tuple-element.60._), channel_id=1, source_target_pairs={{0,14},{2,12},{4,10},{6,8},{8,6},{10,4},{12,2},{14,0},{1,15},{3,13... | collective-permute-start | bytes 589832 | tf_op jit(solution)/shard_map/ppermute | solution.py:673
  86.2 1.6 %collective-permute-start.5 = (bf16[2,512,128]{2,1,0:T(8,128)(2,1)S(1)}, bf16[2,512,128]{2,1,0:T(8,128)(2,1)S(1)}, u32[]{:S(2)}, u32[]{:S(2)}) collective-permute-start(bf16[2,512,128]{2,1,0:T(8,128)(2,1)S(1)} %get-tuple-element.54), channel_id=1, source_target_pairs={{0,2},{2,0},{4,6},{6,4},{8,10},{10,8},{12,14},{14,12},{1,3},{3,1},... | collective-permute-start | bytes 786440 | tf_op jit(solution)/shard_map/ppermute | solution.py:673
  87.8 1.9 %attend_first.7 = (bf16[2,32,1536]{2,1,0:T(8,128)(2,1)S(1)}, bf16[2,32,512]{2,1,0:T(8,128)(2,1)S(1)}) custom-call(s32[48]{0:T(128)S(1)} %copy-done.4, f32[16]{0:T(128)S(1)} %copy-done.8, bf16[16,128,512]{2,1,0:T(8,128)(2,1)S(1)} %copy-done.14, bf16[16,512,128]{2,1,0:T(8,128)(2,1)S(1)} %get-tuple-element.42.refs_0_.refs_1_.rows, ...), custom_call_target="tpu_custom_call" | custom-call | flops 21474836480 | bytes 1000 | tf_op jit(solution)/shard_map/attend_first/pallas_call | solution.py:271
  90.4 3.5 %collective-permute-done.5.refs_3_ = bf16[2,512,128]{2,1,0:T(8,128)(2,1)S(1)} collective-permute-done((bf16[2,512,128]{2,1,0:T(8,128)(2,1)S(1)}, bf16[2,512,128]{2,1,0:T(8,128)(2,1)S(1)}, u32[]{:S(2)}, u32[]{:S(2)}) %collective-permute-start.5) | collective-permute-done | bytes 262176 | tf_op jit(solution)/shard_map/ppermute | solution.py:673
  95.1 3.0 %attend_extra.1 = (bf16[4,2,32,512]{3,2,1,0:T(8,128)(2,1)}, bf16[4,2,32,512]{3,2,1,0:T(8,128)(2,1)S(1)}) custom-call(s32[48]{0:T(128)S(1)} %copy-done.4, f32[16]{0:T(128)S(1)} %copy-done.8, bf16[2,512,128]{2,1,0:T(8,128)(2,1)S(1)} %get-tuple-element.51.refs_0_, bf16[2,512,128]{2,1,0:T(8,128)(2,1)S(1)} %collective-permute-done.4.refs_1_, ...), custom_call_target="tpu_custom_call" | custom-call | flops 21474836480 | bytes 1000 | tf_op jit(solution)/shard_map/attend_extra/pallas_call | solution.py:367
  99.6 1.8 %collective-permute-start.15 = (bf16[2,32,1024]{2,1,0:T(8,128)(2,1)S(1)}, bf16[2,32,1024]{2,1,0:T(8,128)(2,1)}, u32[]{:S(2)}, u32[]{:S(2)}) collective-permute-start(bf16[2,32,1024]{2,1,0:T(8,128)(2,1)S(1)} %attend_second.4._), channel_id=1, source_target_pairs={{0,12},{2,14},{4,8},{6,10},{8,4},{10,6},{12,0},{14,2},{1,13},{3,15... | collective-permute-start | bytes 393224 | tf_op jit(solution)/shard_map/ppermute | solution.py:673
  101.4 2.1 %attend_second.5._ = bf16[2,32,1024]{2,1,0:T(8,128)(2,1)} custom-call(s32[48]{0:T(128)S(1)} %copy-done.4, f32[16]{0:T(128)S(1)} %copy-done.8, bf16[16,128,512]{2,1,0:T(8,128)(2,1)S(1)} %copy-done.14, bf16[16,512,128]{2,1,0:T(8,128)(2,1)S(1)} %get-tuple-element.42.refs_0_.refs_1_.rows, bf16[4,2,32,512]{3,2,1,0:T(8,128)(2,1)S(1)} %get-tuple-element.64.extra._, ...), custom_call_target="tpu_custom_call" | custom-call | flops 21474836480 | bytes 1000 | tf_op jit(solution)/shard_map/attend_second/pallas_call | solution.py:271
  103.8 2.1 %attend_second.6._ = bf16[2,32,1024]{2,1,0:T(8,128)(2,1)} custom-call(s32[48]{0:T(128)S(1)} %copy-done.4, f32[16]{0:T(128)S(1)} %copy-done.8, bf16[16,128,512]{2,1,0:T(8,128)(2,1)S(1)} %copy-done.14, bf16[16,512,128]{2,1,0:T(8,128)(2,1)S(1)} %get-tuple-element.42.refs_0_.refs_1_.rows, bf16[4,2,32,512]{3,2,1,0:T(8,128)(2,1)S(1)} %get-tuple-element.64.extra._, ...), custom_call_target="tpu_custom_call" | custom-call | flops 21474836480 | bytes 1000 | tf_op jit(solution)/shard_map/attend_second/pallas_call | solution.py:271
  105.9 7.1 %collective-permute-start.12 = (bf16[2,32,1024]{2,1,0:T(8,128)(2,1)}, bf16[2,32,1024]{2,1,0:T(8,128)(2,1)}, u32[]{:S(2)}, u32[]{:S(2)}) collective-permute-start(bf16[2,32,1024]{2,1,0:T(8,128)(2,1)} %attend_second.6._), channel_id=1, source_target_pairs={{0,14},{2,12},{4,10},{6,8},{8,6},{10,4},{12,2},{14,0},{1,15},{3,13... | collective-permute-start | bytes 393224 | tf_op jit(solution)/shard_map/ppermute | solution.py:673
  113.1 3.7 %all-to-all-start.1 = ((bf16[4,2,32,512]{3,2,1,0:T(8,128)(2,1)}), bf16[4,2,32,512]{3,2,1,0:T(8,128)(2,1)S(1)}, u32[]{:S(2)}, u32[]{:S(2)}) async-start(bf16[4,2,32,512]{3,2,1,0:T(8,128)(2,1)} %get-tuple-element.69), calls=%async_computation.1 | async-start | bytes 524288 | tf_op jit(solution)/shard_map/all_to_all | solution.py:680
  121.4 2.6 %collective-permute-start.14 = (bf16[2,32,1024]{2,1,0:T(8,128)(2,1)S(1)}, bf16[2,32,1024]{2,1,0:T(8,128)(2,1)S(1)}, u32[]{:S(2)}, u32[]{:S(2)}) collective-permute-start(bf16[2,32,1024]{2,1,0:T(8,128)(2,1)S(1)} %attend_second.7.refs_4_), channel_id=1, source_target_pairs={{0,10},{2,8},{4,14},{6,12},{8,2},{10,0},{12,6},{14,4},{1,11},{3,9}... | collective-permute-start | bytes 393224 | tf_op jit(solution)/shard_map/ppermute | solution.py:673
  123.9 2.5 %unpack_early.1._ = bf16[16,32,2048]{2,1,0:T(8,128)(2,1)} custom-call(s32[48]{0:T(128)S(1)} %copy-done.4, bf16[4,2,32,2048]{3,2,1,0:T(8,128)(2,1)} %all-to-all-done.2.near, bf16[2,32,1536]{2,1,0:T(8,128)(2,1)S(1)} %collective-permute-done.9.refs_1_.refs_0_, bf16[2,32,1536]{2,1,0:T(8,128)(2,1)S(1)} %collective-permute-done.10.refs_1_, ...), custom_call_target="tpu_custom_call" | custom-call | flops 1000 | bytes 1000 | tf_op jit(solution)/shard_map/unpack_early/pallas_call | solution.py:583
  127.9 1.8 %unpack.2.refs_2_ = bf16[16,32,2048]{2,1,0:T(8,128)(2,1)} custom-call(s32[48]{0:T(128)S(1)} %copy-done.4, bf16[2,32,1024]{2,1,0:T(8,128)(2,1)} %collective-permute-done.15.refs_0_, bf16[2,32,1024]{2,1,0:T(8,128)(2,1)} %collective-permute-done.16.refs_1_, bf16[16,32,2048]{2,1,0:T(8,128)(2,1)} %unpack_extra.1.refs_2_), custom_call_target="tpu_custom_call", output_to_operand_aliasing={{}: (3, {})} | custom-call | flops 21474836480 | bytes 1000 | tf_op jit(solution)/shard_map/unpack/pallas_call | solution.py:656
  130.1 1.8 %unpack.3 = bf16[16,32,2048]{2,1,0:T(8,128)(2,1)} custom-call(s32[48]{0:T(128)S(1)} %copy-done.4, bf16[2,32,1024]{2,1,0:T(8,128)(2,1)} %collective-permute-done.12.refs_0_, bf16[2,32,1024]{2,1,0:T(8,128)(2,1)S(1)} %collective-permute-done.14.refs_1_, bf16[16,32,2048]{2,1,0:T(8,128)(2,1)} %unpack.2.refs_2_), custom_call_target="tpu_custom_call", output_to_operand_aliasing={{}: (3, {})} | custom-call | flops 21474836480 | bytes 1000 | tf_op jit(solution)/shard_map/unpack/pallas_call | solution.py:656
  (80 shorter events, 21.3 us)
Async XLA Ops:
  2.8 34.9 %collective-permute-start = (bf16[128,2048]{1,0:T(8,128)(2,1)}, bf16[128,2048]{1,0:T(8,128)(2,1)}, u32[]{:S(2)}, u32[]{:S(2)}) collective-permute-start(bf16[128,2048]{1,0:T(8,128)(2,1)} %multiply_convert_fusion._), channel_id=1, source_target_pairs={{0,2},{2,4},{4,6},{6,8},{8,10},{10,12},{12,14},{1,3},{3,5},{5,7},{... | collective-permute-start | bytes 1572872 | tf_op jit(solution)/shard_map/ppermute | solution.py:697
  13.5 11.5 %copy-start.4 = (s32[48]{0:T(128)S(1)}, s32[48]{0:T(128)}, u32[]{:S(2)}) copy-start(s32[48]{0:T(128)} %get-tuple-element.36._.info) | copy-start | bytes 580
  13.5 11.5 %copy-start.7 = (f32[2048,128]{1,0:T(8,128)S(1)}, f32[2048,128]{1,0:T(8,128)}, u32[]{:S(2)}) copy-start(f32[2048,128]{1,0:T(8,128)} %filters.3) | copy-start | bytes 3145732
  13.5 11.5 %copy-start.11 = (bf16[256,256]{1,0:T(8,128)(2,1)S(1)}, bf16[256,256]{1,0:T(8,128)(2,1)}, u32[]{:S(2)}) copy-start(bf16[256,256]{1,0:T(8,128)(2,1)} %constant.5.clone.inverse) | copy-start | bytes 393220
  13.5 35.4 %all-to-all-start = ((bf16[4,2,32,2560]{3,2,1,0:T(8,128)(2,1)}), bf16[4,2,32,2560]{3,2,1,0:T(8,128)(2,1)}, u32[]{:S(2)}, u32[]{:S(2)}) async-start(bf16[4,2,32,2560]{3,2,1,0:T(8,128)(2,1)} %get-tuple-element.50), calls=%async_computation | async-start | bytes 2621440 | tf_op jit(solution)/shard_map/all_to_all | solution.py:680
  18.0 27.5 %collective-permute-start.3 = (bf16[2,32,2048]{2,1,0:T(8,128)(2,1)}, bf16[2,32,2048]{2,1,0:T(8,128)(2,1)}, u32[]{:S(2)}, u32[]{:S(2)}) collective-permute-start(bf16[2,32,2048]{2,1,0:T(8,128)(2,1)} %get-tuple-element.47), channel_id=1, source_target_pairs={{0,12},{2,14},{4,8},{6,10},{8,4},{10,6},{12,0},{14,2},{1,13},{3,15... | collective-permute-start | bytes 786440 | tf_op jit(solution)/shard_map/ppermute | solution.py:673
  21.2 56.6 %collective-permute-start.6 = (bf16[2,32,2048]{2,1,0:T(8,128)(2,1)}, bf16[2,32,2048]{2,1,0:T(8,128)(2,1)}, u32[]{:S(2)}, u32[]{:S(2)}) collective-permute-start(bf16[2,32,2048]{2,1,0:T(8,128)(2,1)} %get-tuple-element.55), channel_id=1, source_target_pairs={{0,8},{2,10},{4,12},{6,14},{8,0},{10,2},{12,4},{14,6},{1,9},{3,11}... | collective-permute-start | bytes 786440 | tf_op jit(solution)/shard_map/ppermute | solution.py:673
  21.4 58.5 %collective-permute-start.7 = (bf16[2,32,2048]{2,1,0:T(8,128)(2,1)}, bf16[2,32,2048]{2,1,0:T(8,128)(2,1)}, u32[]{:S(2)}, u32[]{:S(2)}) collective-permute-start(bf16[2,32,2048]{2,1,0:T(8,128)(2,1)} %get-tuple-element.58), channel_id=1, source_target_pairs={{0,14},{2,12},{4,10},{6,8},{8,6},{10,4},{12,2},{14,0},{1,15},{3,13... | collective-permute-start | bytes 786440 | tf_op jit(solution)/shard_map/ppermute | solution.py:673
  24.1 62.1 %collective-permute-start.8 = (bf16[2,32,2048]{2,1,0:T(8,128)(2,1)}, bf16[2,32,2048]{2,1,0:T(8,128)(2,1)}, u32[]{:S(2)}, u32[]{:S(2)}) collective-permute-start(bf16[2,32,2048]{2,1,0:T(8,128)(2,1)} %get-tuple-element.61), channel_id=1, source_target_pairs={{0,10},{2,8},{4,14},{6,12},{8,2},{10,0},{12,6},{14,4},{1,11},{3,9}... | collective-permute-start | bytes 786440 | tf_op jit(solution)/shard_map/ppermute | solution.py:673
  30.8 6.8 %copy-start.1 = (bf16[512,2048]{1,0:T(8,128)(2,1)S(1)}, bf16[512,2048]{1,0:T(8,128)(2,1)}, u32[]{:S(2)}) copy-start(bf16[512,2048]{1,0:T(8,128)(2,1)} %key.3) | copy-start | bytes 6291460
  30.8 6.8 %copy-start.3 = (bf16[512,2048]{1,0:T(8,128)(2,1)S(1)}, bf16[512,2048]{1,0:T(8,128)(2,1)}, u32[]{:S(2)}) copy-start(bf16[512,2048]{1,0:T(8,128)(2,1)} %value.3) | copy-start | bytes 6291460
  30.8 6.9 %copy-start.6 = (bf16[512,2048]{1,0:T(8,128)(2,1)S(1)}, bf16[512,2048]{1,0:T(8,128)(2,1)}, u32[]{:S(2)}) copy-start(bf16[512,2048]{1,0:T(8,128)(2,1)} %gate.3) | copy-start | bytes 6291460
  30.8 6.9 %copy-start.10 = (bf16[512,256]{1,0:T(8,128)(2,1)S(1)}, bf16[512,256]{1,0:T(8,128)(2,1)}, u32[]{:S(2)}) copy-start(bf16[512,256]{1,0:T(8,128)(2,1)} %constant.4.clone.forward) | copy-start | bytes 786436
  43.8 25.4 %collective-permute-start.2 = (bf16[4,512,128]{2,1,0:T(8,128)(2,1)}, bf16[4,512,128]{2,1,0:T(8,128)(2,1)}, u32[]{:S(2)}, u32[]{:S(2)}) collective-permute-start(bf16[4,512,128]{2,1,0:T(8,128)(2,1)} %get-tuple-element.46), channel_id=1, source_target_pairs={{0,4},{2,6},{4,0},{6,2},{8,12},{10,14},{12,8},{14,10},{1,5},{3,7},... | collective-permute-start | bytes 1572872 | tf_op jit(solution)/shard_map/ppermute | solution.py:673
  45.5 31.0 %collective-permute-start.1 = (bf16[4,512,128]{2,1,0:T(8,128)(2,1)}, bf16[4,512,128]{2,1,0:T(8,128)(2,1)}, u32[]{:S(2)}, u32[]{:S(2)}) collective-permute-start(bf16[4,512,128]{2,1,0:T(8,128)(2,1)} %get-tuple-element.44._), channel_id=1, source_target_pairs={{0,2},{2,0},{4,6},{6,4},{8,10},{10,8},{12,14},{14,12},{1,3},{3,1},... | collective-permute-start | bytes 1572872 | tf_op jit(solution)/shard_map/ppermute | solution.py:673
  48.9 7.3 %copy-start.18 = (bf16[2,32,512]{2,1,0:T(8,128)(2,1)}, bf16[2,32,512]{2,1,0:T(8,128)(2,1)S(1)}, u32[]{:S(2)}) copy-start(bf16[2,32,512]{2,1,0:T(8,128)(2,1)S(1)} %get-tuple-element.65.refs_2_) | copy-start | bytes 196612
  56.2 56.9 %all-to-all-start.2 = ((bf16[4,2,32,2048]{3,2,1,0:T(8,128)(2,1)}), bf16[4,2,32,2048]{3,2,1,0:T(8,128)(2,1)}, u32[]{:S(2)}, u32[]{:S(2)}) async-start(bf16[4,2,32,2048]{3,2,1,0:T(8,128)(2,1)} %attend_near.1.refs_4_), calls=%async_computation.2 | async-start | bytes 2097152 | tf_op jit(solution)/shard_map/all_to_all | solution.py:680
  60.5 17.4 %copy-start.14 = (bf16[16,128,512]{2,1,0:T(8,128)(2,1)S(1)}, bf16[16,128,512]{2,1,0:T(8,128)(2,1)}, u32[]{:S(2)}) copy-start(bf16[16,128,512]{2,1,0:T(8,128)(2,1)} %copy-done.12) | copy-start | bytes 6291460
  60.5 17.4 %copy-start.23 = (bf16[2,32,512]{2,1,0:T(8,128)(2,1)S(1)}, bf16[2,32,512]{2,1,0:T(8,128)(2,1)}, u32[]{:S(2)}) copy-start(bf16[2,32,512]{2,1,0:T(8,128)(2,1)} %get-tuple-element.56.rest) | copy-start | bytes 196612
  69.2 28.8 %collective-permute-start.9 = (bf16[2,32,1536]{2,1,0:T(8,128)(2,1)S(1)}, bf16[2,32,1536]{2,1,0:T(8,128)(2,1)S(1)}, u32[]{:S(2)}, u32[]{:S(2)}) collective-permute-start(bf16[2,32,1536]{2,1,0:T(8,128)(2,1)S(1)} %get-tuple-element.49._), channel_id=1, source_target_pairs={{0,12},{2,14},{4,8},{6,10},{8,4},{10,6},{12,0},{14,2},{1,13},{3,15... | collective-permute-start | bytes 589832 | tf_op jit(solution)/shard_map/ppermute | solution.py:673
  77.7 17.3 %collective-permute-start.4 = (bf16[2,512,128]{2,1,0:T(8,128)(2,1)S(1)}, bf16[2,512,128]{2,1,0:T(8,128)(2,1)S(1)}, u32[]{:S(2)}, u32[]{:S(2)}) collective-permute-start(bf16[2,512,128]{2,1,0:T(8,128)(2,1)S(1)} %get-tuple-element.52._), channel_id=1, source_target_pairs={{0,4},{2,6},{4,0},{6,2},{8,12},{10,14},{12,8},{14,10},{1,5},{3,7},... | collective-permute-start | bytes 786440 | tf_op jit(solution)/shard_map/ppermute | solution.py:673
  79.9 21.5 %collective-permute-start.10 = (bf16[2,32,1536]{2,1,0:T(8,128)(2,1)S(1)}, bf16[2,32,1536]{2,1,0:T(8,128)(2,1)S(1)}, u32[]{:S(2)}, u32[]{:S(2)}) collective-permute-start(bf16[2,32,1536]{2,1,0:T(8,128)(2,1)S(1)} %get-tuple-element.57._), channel_id=1, source_target_pairs={{0,8},{2,10},{4,12},{6,14},{8,0},{10,2},{12,4},{14,6},{1,9},{3,11}... | collective-permute-start | bytes 589832 | tf_op jit(solution)/shard_map/ppermute | solution.py:673
  80.0 7.8 %copy-start.24 = (bf16[2,32,512]{2,1,0:T(8,128)(2,1)S(1)}, bf16[2,32,512]{2,1,0:T(8,128)(2,1)}, u32[]{:S(2)}) copy-start(bf16[2,32,512]{2,1,0:T(8,128)(2,1)} %get-tuple-element.62.rest) | copy-start | bytes 196612
  82.0 21.9 %collective-permute-start.11 = (bf16[2,32,1536]{2,1,0:T(8,128)(2,1)S(1)}, bf16[2,32,1536]{2,1,0:T(8,128)(2,1)S(1)}, u32[]{:S(2)}, u32[]{:S(2)}) collective-permute-start(bf16[2,32,1536]{2,1,0:T(8,128)(2,1)S(1)} %get-tuple-element.60._), channel_id=1, source_target_pairs={{0,14},{2,12},{4,10},{6,8},{8,6},{10,4},{12,2},{14,0},{1,15},{3,13... | collective-permute-start | bytes 589832 | tf_op jit(solution)/shard_map/ppermute | solution.py:673
  86.2 7.7 %collective-permute-start.5 = (bf16[2,512,128]{2,1,0:T(8,128)(2,1)S(1)}, bf16[2,512,128]{2,1,0:T(8,128)(2,1)S(1)}, u32[]{:S(2)}, u32[]{:S(2)}) collective-permute-start(bf16[2,512,128]{2,1,0:T(8,128)(2,1)S(1)} %get-tuple-element.54), channel_id=1, source_target_pairs={{0,2},{2,0},{4,6},{6,4},{8,10},{10,8},{12,14},{14,12},{1,3},{3,1},... | collective-permute-start | bytes 786440 | tf_op jit(solution)/shard_map/ppermute | solution.py:673
  93.9 23.5 %collective-permute-start.13 = (bf16[2,32,1536]{2,1,0:T(8,128)(2,1)S(1)}, bf16[2,32,1536]{2,1,0:T(8,128)(2,1)S(1)}, u32[]{:S(2)}, u32[]{:S(2)}) collective-permute-start(bf16[2,32,1536]{2,1,0:T(8,128)(2,1)S(1)} %get-tuple-element.63.refs_4_), channel_id=1, source_target_pairs={{0,10},{2,8},{4,14},{6,12},{8,2},{10,0},{12,6},{14,4},{1,11},{3,9}... | collective-permute-start | bytes 589832 | tf_op jit(solution)/shard_map/ppermute | solution.py:673
  99.6 28.3 %collective-permute-start.15 = (bf16[2,32,1024]{2,1,0:T(8,128)(2,1)S(1)}, bf16[2,32,1024]{2,1,0:T(8,128)(2,1)}, u32[]{:S(2)}, u32[]{:S(2)}) collective-permute-start(bf16[2,32,1024]{2,1,0:T(8,128)(2,1)S(1)} %attend_second.4._), channel_id=1, source_target_pairs={{0,12},{2,14},{4,8},{6,10},{8,4},{10,6},{12,0},{14,2},{1,13},{3,15... | collective-permute-start | bytes 393224 | tf_op jit(solution)/shard_map/ppermute | solution.py:673
  103.5 24.4 %collective-permute-start.16 = (bf16[2,32,1024]{2,1,0:T(8,128)(2,1)}, bf16[2,32,1024]{2,1,0:T(8,128)(2,1)}, u32[]{:S(2)}, u32[]{:S(2)}) collective-permute-start(bf16[2,32,1024]{2,1,0:T(8,128)(2,1)} %attend_second.5._), channel_id=1, source_target_pairs={{0,8},{2,10},{4,12},{6,14},{8,0},{10,2},{12,4},{14,6},{1,9},{3,11}... | collective-permute-start | bytes 393224 | tf_op jit(solution)/shard_map/ppermute | solution.py:673
  103.8 13.6 %copy-start.21 = (bf16[2,32,512]{2,1,0:T(8,128)(2,1)S(1)}, bf16[2,32,512]{2,1,0:T(8,128)(2,1)}, u32[]{:S(2)}) copy-start(bf16[2,32,512]{2,1,0:T(8,128)(2,1)} %copy-done.20) | copy-start | bytes 196612
  105.9 24.2 %collective-permute-start.12 = (bf16[2,32,1024]{2,1,0:T(8,128)(2,1)}, bf16[2,32,1024]{2,1,0:T(8,128)(2,1)}, u32[]{:S(2)}, u32[]{:S(2)}) collective-permute-start(bf16[2,32,1024]{2,1,0:T(8,128)(2,1)} %attend_second.6._), channel_id=1, source_target_pairs={{0,14},{2,12},{4,10},{6,8},{8,6},{10,4},{12,2},{14,0},{1,15},{3,13... | collective-permute-start | bytes 393224 | tf_op jit(solution)/shard_map/ppermute | solution.py:673
  113.1 13.4 %all-to-all-start.1 = ((bf16[4,2,32,512]{3,2,1,0:T(8,128)(2,1)}), bf16[4,2,32,512]{3,2,1,0:T(8,128)(2,1)S(1)}, u32[]{:S(2)}, u32[]{:S(2)}) async-start(bf16[4,2,32,512]{3,2,1,0:T(8,128)(2,1)} %get-tuple-element.69), calls=%async_computation.1 | async-start | bytes 524288 | tf_op jit(solution)/shard_map/all_to_all | solution.py:680
  121.4 8.7 %collective-permute-start.14 = (bf16[2,32,1024]{2,1,0:T(8,128)(2,1)S(1)}, bf16[2,32,1024]{2,1,0:T(8,128)(2,1)S(1)}, u32[]{:S(2)}, u32[]{:S(2)}) collective-permute-start(bf16[2,32,1024]{2,1,0:T(8,128)(2,1)S(1)} %attend_second.7.refs_4_), channel_id=1, source_target_pairs={{0,10},{2,8},{4,14},{6,12},{8,2},{10,0},{12,6},{14,4},{1,11},{3,9}... | collective-permute-start | bytes 393224 | tf_op jit(solution)/shard_map/ppermute | solution.py:673
  (14 other events, 35.8 us)
